TPU v7x, 32 devices: a whole 2x2x4 slice. The times are simulated.
32 devices in a mesh: tm: 32 (over z, y, x, core), chan: 1.
Axes of the slice: x: 2, y: 2, z: 4, core: 2. Of those that a mesh axis runs over, the one named last changes fastest.
Arguments:
- signal: bfloat16 [384, 4096], P('chan', 'tm'), may hold values from -6 to 6
- codes_init: float32 [128, 4096], P(None, 'tm'), may hold values from -2 to 2
- dictionary_init: float32 [128, 36864], P(None, 'chan'), may hold values from -6 to 6
- threshold: float32 [128], replicated, may hold values from 0.05 to 0.5
- plan: int32 [8], replicated, may hold values from 0 to 7, each once
Outputs:
- sparse_codes: float32 [128, 4096], P(None, 'tm')
- dictionary: float32 [128, 36864], P(None, 'chan')
- residual: float32 [384, 4096], P('chan', 'tm')
Inputs may be any that keep to these rules, and one draw needn't show every extreme that they name: `plan`: every atom block from 0 to 7 appears exactly once.
All inputs are finite; a program needn't handle non-finite values.
Results may differ from a plain program's by a relative error of at most 0.013.
Values may be sent and summed in bfloat16 or wider, within the bound.
No kernel may reach another device: no remote copies, remote signals or barrier semaphores. Data moves between devices by JAX's collectives and lax.ppermute only.
A program may use at most 128 MiB of HBM per device.

v0:
```python
import jax
import jax.numpy as jnp
from jax import lax
from jax.sharding import PartitionSpec as P

C = 384
K = 128
L = 96
BLOCK_ATOMS = 16
INNER = 2
OUTER = 2


code_rate = 0.3
move_rate = 0.5
tiny_eps = 1e-06


def shifted(shard, axis, by):
    peers = lax.axis_size(axis)
    pairs = [(i, i + by) for i in range(peers) if 0 <= i + by < peers]
    return lax.ppermute(shard, axis, pairs)


def renew_atoms(old_atoms, across, mean_sq, spread):
    return (old_atoms + move_rate * across / jnp.sqrt(spread)[:, None]) / jnp.sqrt(mean_sq + 0.25)[
        :, None
    ]


def shards(signal, codes_init, dictionary_init, threshold, plan):
    segment = signal.shape[1]
    local_chan = signal.shape[0]
    unit_scale = (C * L) ** (-0.5)
    entries = C * L
    limit = threshold[:, None]

    def convolve(atom_cube, code_low):
        code_edge = shifted(code_low[:, segment - (L - 1) :], "tm", 1)
        extended = jnp.concatenate([code_edge, code_low], axis=1)
        lagged = jnp.stack(
            [extended[:, L - 1 - offset : L - 1 - offset + segment] for offset in range(L)], axis=1
        )
        return unit_scale * jnp.einsum(
            "kcl,klt->ct", atom_cube, lagged, preferred_element_type=jnp.float32
        )

    def resid_columns(resid_low):
        resid_edge = shifted(resid_low[:, : L - 1], "tm", -1)
        extended = jnp.concatenate([resid_low, resid_edge], axis=1)
        lagged = jnp.stack([extended[:, offset : offset + segment] for offset in range(L)], axis=1)
        return lagged.reshape(local_chan * L, segment)

    code_state = codes_init
    dictionary = dictionary_init
    residual = signal.astype(jnp.float32)
    for outer_step in range(OUTER):
        dict_low = dictionary.astype(jnp.bfloat16)
        atom_cube = dict_low.reshape(K, local_chan, L)
        for inner_step in range(INNER):
            code_low = code_state.astype(jnp.bfloat16)
            residual = signal.astype(jnp.float32) - convolve(atom_cube, code_low)
            lagged = resid_columns(residual.astype(jnp.bfloat16))
            partial_value = unit_scale * jnp.dot(
                dict_low, lagged, preferred_element_type=jnp.float32
            )
            scores = lax.psum(partial_value.astype(jnp.bfloat16), "chan").astype(jnp.float32)
            stepped = code_state + code_rate * scores
            code_state = stepped - jnp.clip(stepped, -limit, limit)
        code_low = code_state.astype(jnp.bfloat16)
        residual = signal.astype(jnp.float32) - convolve(atom_cube, code_low)
        lagged = resid_columns(residual.astype(jnp.bfloat16))
        first_row = plan[outer_step] * BLOCK_ATOMS
        code_block = lax.dynamic_slice_in_dim(code_low, first_row, BLOCK_ATOMS, 0)
        local_grad = lax.dot_general(
            code_block, lagged, (((1,), (1,)), ((), ())), preferred_element_type=jnp.float32
        )
        old_atoms = lax.dynamic_slice_in_dim(dictionary, first_row, BLOCK_ATOMS, 0)
        gradient = lax.psum(local_grad, "tm")
        dot_sum, square_sum = lax.psum(
            (jnp.sum(gradient * old_atoms, axis=1), jnp.sum(old_atoms * old_atoms, axis=1)), "chan"
        )
        mean_sq = square_sum / entries + tiny_eps
        along_coef = dot_sum / entries / mean_sq
        across = gradient - along_coef[:, None] * old_atoms
        spread = lax.psum(jnp.sum(across * across, axis=1), "chan") / entries + tiny_eps
        renewed = renew_atoms(old_atoms, across, mean_sq, spread)
        dictionary = lax.dynamic_update_slice_in_dim(dictionary, renewed, first_row, 0)
    return (code_state, dictionary, residual)


def solution(mesh):
    placed = (P("chan", "tm"), P(None, "tm"), P(None, "chan"), P(), P())
    return jax.shard_map(
        shards,
        mesh=mesh,
        in_specs=placed,
        out_specs=(P(None, "tm"), P(None, "chan"), P("chan", "tm")),
        check_vma=False,
    )
```

profile of v0, /device:TPU:0, one launch (start us, length us, event | category | flops | bytes accessed | tf_op | source)
XLA Modules:
  0.0 1001.4 jit_solution(14871638666821467310)
XLA Ops:
  7.2 14.5 %copy.1097 = f32[128,36864]{1,0:T(8,128)} copy(f32[128,36864]{1,0:T(8,128)} %param.7) | data formatting | bytes 37748736
  24.4 14.6 %copy.25 = bf16[128,36864]{0,1:T(8,128)(2,1)} copy(f32[128,36864]{1,0:T(8,128)} %copy.1097) | data formatting | bytes 28311552 | tf_op args[2]
  38.9 13.3 %copy.26 = bf16[128,384,96]{1,0,2:T(8,128)(2,1)} copy(bf16[128,384,96]{0,2,1:T(8,128)(2,1)} %bitcast.4314) | data formatting | bytes 18874368 | tf_op jit(solution)/shard_map/reshape | solution.py:59
  54.6 6.2 constant_dynamic-update-slice_fusion.191
  129.5 12.7 %copy.27 = bf16[384,96,128]{2,1,0:T(8,128)(2,1)} copy(bf16[384,96,128]{0,2,1:T(8,128)(2,1)} %constant_dynamic-update-slice_fusion.96) | data formatting | bytes 18874368 | tf_op jit(solution)/shard_map/stack | solution.py:51
  142.2 9.2 constant_dynamic-update-slice_fusion.287
  228.5 13.1 %copy.32 = bf16[384,96,128]{2,1,0:T(8,128)(2,1)} copy(bf16[384,96,128]{0,2,1:T(8,128)(2,1)} %constant_dynamic-update-slice_fusion.288) | data formatting | bytes 18874368 | tf_op jit(solution)/shard_map/stack | solution.py:51
  241.6 9.1 fusion.28
  259.3 6.2 constant_dynamic-update-slice_fusion.575
  332.7 12.8 %copy.36 = bf16[384,96,128]{2,1,0:T(8,128)(2,1)} copy(bf16[384,96,128]{0,2,1:T(8,128)(2,1)} %constant_dynamic-update-slice_fusion.480) | data formatting | bytes 18874368 | tf_op jit(solution)/shard_map/stack | solution.py:51
  345.5 7.7 fusion.2118
  353.5 143.3 %all-reduce.3.cloned.1.call-done = f32[16,36864]{1,0:T(8,128)} async-done(((f32[16,36864]{1,0:T(8,128)}), f32[16,36864]{1,0:T(8,128)}) %all-reduce.3.cloned.1.call-update) | async-done | bytes 2359312 | tf_op jit(solution)/shard_map/psum | solution.py:79
  506.4 11.2 %convert_element_type.88 = bf16[128,36864]{1,0:T(8,128)(2,1)} convert(f32[128,36864]{1,0:T(8,128)} %divide_dynamic-update-slice_fusion.1) | non-fusion elementwise | flops 4718592 | bytes 28311552 | tf_op jit(solution)/shard_map/convert_element_type | solution.py:58
  517.5 12.7 %copy.37 = bf16[128,36864]{0,1:T(8,128)(2,1)} copy(bf16[128,36864]{1,0:T(8,128)(2,1)} %convert_element_type.88) | data formatting | bytes 18874368 | tf_op jit(solution)/shard_map/convert_element_type | solution.py:58
  530.2 13.3 %copy.38 = bf16[128,384,96]{1,0,2:T(8,128)(2,1)} copy(bf16[128,384,96]{0,2,1:T(8,128)(2,1)} %bitcast.4321) | data formatting | bytes 18874368 | tf_op jit(solution)/shard_map/reshape | solution.py:59
  543.6 6.2 constant_dynamic-update-slice_fusion.671
  616.3 12.7 %copy.39 = bf16[384,96,128]{2,1,0:T(8,128)(2,1)} copy(bf16[384,96,128]{0,2,1:T(8,128)(2,1)} %constant_dynamic-update-slice_fusion.576) | data formatting | bytes 18874368 | tf_op jit(solution)/shard_map/stack | solution.py:51
  629.0 10.2 %constant_dynamic-update-slice_fusion.767 = (bf16[128,96,128]{0,2,1:T(8,128)(2,1)S(1)}, bf16[128,128]{0,1:T(8,128)(2,1)S(1)}, f32[128,128]{0,1:T(8,128)S(1)}) fusion(bf16[128,36864]{1,0:T(8,128)(2,1)} %convert_element_type.88, bf16[36864,128]{1,0:T(8,128)(2,1)} %bitcast.4319, f32[128]{0:T(128)S(1)} %neg.3, f32[128]{0:T(128)S(1)} %copy-done.7, ...), kind=kOutput, calls=%fused_computation.1341 | convolution fusion | flops 1208172544 | bytes 19137536 | tf_op jit(solution)/shard_map/dot_general | solution.py:64
  719.4 13.1 %copy.41 = bf16[384,96,128]{2,1,0:T(8,128)(2,1)} copy(bf16[384,96,128]{0,2,1:T(8,128)(2,1)} %constant_dynamic-update-slice_fusion.768) | data formatting | bytes 18874368 | tf_op jit(solution)/shard_map/stack | solution.py:51
  732.5 10.1 %constant_dynamic-update-slice_fusion.959 = (bf16[128,96,128]{0,2,1:T(8,128)(2,1)S(1)}, bf16[128,128]{0,1:T(8,128)(2,1)S(1)}, f32[128,128]{0,1:T(8,128)S(1)}) fusion(f32[128]{0:T(128)S(1)} %neg.3, f32[128]{0:T(128)S(1)} %copy-done.7, f32[128,128]{0,1:T(8,128)S(1)} %get-tuple-element.40, bf16[128,36864]{1,0:T(8,128)(2,1)} %convert_element_type.88, ...), kind=kOutput, calls=%fused_computation.1533 | convolution fusion | flops 1208107008 | bytes 19072000 | tf_op jit(solution)/shard_map/dot_general | solution.py:64
  750.9 6.2 constant_dynamic-update-slice_fusion.1055
  823.5 12.8 %copy.43 = bf16[384,96,128]{2,1,0:T(8,128)(2,1)} copy(bf16[384,96,128]{0,2,1:T(8,128)(2,1)} %constant_dynamic-update-slice_fusion.960) | data formatting | bytes 18874368 | tf_op jit(solution)/shard_map/stack | solution.py:51
  836.3 7.8 fusion.2116
  845.7 138.9 %all-reduce.5.cloned.1.call-done = f32[16,36864]{1,0:T(8,128)} async-done(((f32[16,36864]{1,0:T(8,128)}), f32[16,36864]{1,0:T(8,128)}) %all-reduce.5.cloned.1.call-update) | async-done | bytes 2359312 | tf_op jit(solution)/shard_map/psum | solution.py:79
  (1128 shorter events, 465.5 us)
Async XLA Ops:
  7.2 17.1 %copy-start.5 = (bf16[384,128]{1,0:T(8,128)(2,1)S(1)}, bf16[384,128]{1,0:T(8,128)(2,1)}, u32[]{:S(2)}) copy-start(bf16[384,128]{1,0:T(8,128)(2,1)} %param.5) | copy-start | bytes 294916
  7.2 14.5 %copy-start.6 = (f32[128,128]{1,0:T(8,128)S(1)}, f32[128,128]{1,0:T(8,128)}, u32[]{:S(2)}) copy-start(f32[128,128]{1,0:T(8,128)} %param.6) | copy-start | bytes 196612
  7.2 489.6 %all-reduce.3.cloned.1.call-start = ((), (), s32[]{:S(2)}) async-start(), calls=%async_computation | async-start | bytes 4718592 | tf_op jit(solution)/shard_map/psum | solution.py:79
  21.9 30.4 %collective-permute-start = (bf16[128,95]{0,1:T(8,128)(2,1)S(1)}, bf16[128,95]{0,1:T(8,128)(2,1)S(1)}, u32[]{:S(2)}, u32[]{:S(2)}) collective-permute-start(bf16[128,95]{0,1:T(8,128)(2,1)S(1)} %slice.4328), channel_id=1, source_target_pairs={{0,1},{1,2},{2,3},{3,4},{4,5},{5,6},{6,7},{7,8},{8,9},{9,10},{10,1... | collective-permute-start | bytes 72968 | tf_op jit(solution)/shard_map/ppermute | solution.py:22
  54.6 7.5 copy-start.7
  60.8 5.3 collective-permute-start.1
  142.2 17.3 %slice-start = ((s8[9437184]{0:T(1024)(128)(4,1)}), s8[4194304]{0:T(1024)(128)(4,1)S(1)}, s32[]{:S(2)}) async-start(s8[9437184]{0:T(1024)(128)(4,1)} %bitcast.4312), calls=%async_computation.2 | async-start | bytes 8388608
  142.2 17.3 %slice-start.1 = ((s8[9437184]{0:T(1024)(128)(4,1)}), s8[4194304]{0:T(1024)(128)(4,1)S(1)}, s32[]{:S(2)}) async-start(s8[9437184]{0:T(1024)(128)(4,1)} %bitcast.4312), calls=%async_computation.3 | async-start | bytes 8388608
  142.2 17.4 %slice-start.2 = ((s8[9437184]{0:T(1024)(128)(4,1)}), s8[1048576]{0:T(1024)(128)(4,1)S(1)}, s32[]{:S(2)}) async-start(s8[9437184]{0:T(1024)(128)(4,1)} %bitcast.4312), calls=%async_computation.4 | async-start | bytes 2097152
  151.4 5.8 collective-permute-start.2
  162.0 3.2 collective-permute-start.3
  250.8 8.4 copy-start.3
  250.9 6.0 collective-permute-start.4
  259.3 8.2 copy-start.8
  266.2 3.4 collective-permute-start.5
  353.3 631.3 %all-reduce.5.cloned.1.call-start = ((), (), s32[]{:S(2)}) async-start(), calls=%async_computation.1 | async-start | bytes 4718592 | tf_op jit(solution)/shard_map/psum | solution.py:79
  496.8 5.8 copy-start.1
  549.8 3.2 collective-permute-start.6
  616.3 12.7 %copy-start.4 = (f32[128,128]{0,1:T(8,128)S(1)}, f32[128,128]{0,1:T(8,128)}, u32[]{:S(2)}) copy-start(f32[128,128]{0,1:T(8,128)} %copy-done.3) | copy-start | bytes 196612
  639.2 5.2 collective-permute-start.7
  652.9 3.2 collective-permute-start.8
  742.6 5.9 collective-permute-start.9
  757.2 3.2 collective-permute-start.10
  836.3 8.5 copy-start.2
  (1 other events, 5.8 us)
Sparse Core Ops, SparseCore 0:
  353.4 143.3 all-reduce.2
  844.2 140.3 all-reduce.4
where the time goes:
time: 1010 us; the launch traced here: 1000 us
  other arithmetic  420 us (42%)
  waiting for transfers between devices  296 us (29%)
  local copies, waits for them, and re-layouts  149 us (15%)
  matrix products  87.6 us (9%)
  starting transfers between devices  31 us (3%)
  between operations  17.9 us (2%)
    unnamed x1037, other arithmetic  386 us
    psum x2, waiting for transfers between devices, shards(): gradient = lax.psum(local_grad, 'tm')  282 us
    another operation x6, local copies, waits for them, and re-layouts, resid_columns(): jnp.stack([extended[:, offset:offset + segment] for offset in range(L)],...  77.1 us
    dot_general x4, matrix products, shards(): jnp.dot(dict_low, lagged, preferred_element_type=jnp.float32)  38.6 us
    dot_general x6, matrix products, convolve(): jnp.einsum('kcl,klt->ct', atom_cube, lagged, preferred_element_type=jnp.f...  33.5 us
    unnamed x30, local copies, waits for them, and re-layouts  30.9 us
    ppermute x11, starting transfers between devices, shifted(): return lax.ppermute(shard, axis, pairs)  30.7 us
    reshape x2, local copies, waits for them, and re-layouts, shards(): atom_cube = dict_low.reshape(K, local_chan, L)  26.6 us
  transfers between devices with their start and end apart: 13, of which 12 were waited for; matrix products, arithmetic and copies ran while one was open for 3% of the time, Pallas kernels for 0%

commit v1 on v0

--- a/solution.py
+++ b/solution.py
@@ -1,6 +1,10 @@
+import functools
+
 import jax
 import jax.numpy as jnp
 from jax import lax
+from jax.experimental import pallas as pl
+from jax.experimental.pallas import tpu as pltpu
 from jax.sharding import PartitionSpec as P
 
 C = 384
@@ -10,10 +14,18 @@
 INNER = 2
 OUTER = 2
 
-
 code_rate = 0.3
 move_rate = 0.5
 tiny_eps = 1e-06
+
+ROWS = 16
+COARSE = L // ROWS
+FINE = 4
+LANES = 128
+VMEM_BYTES = 56 * 1024 * 1024
+
+NN = (((1,), (0,)), ((), ()))
+NT = (((1,), (1,)), ((), ()))
 
 
 def shifted(shard, axis, by):
@@ -22,13 +34,449 @@
     return lax.ppermute(shard, axis, pairs)
 
 
+def by_tap(columns_ref, turned_ref):
+    width = columns_ref.shape[1]
+    for start in range(0, width, 384):
+        turned_ref[start : start + 384, :] = columns_ref[:, start : start + 384].T
+
+
+def layout_kernel(dict_ref, taps_ref, turned_ref):
+    by_tap(dict_ref, turned_ref)
+    for tap in range(L):
+        taps_ref[tap] = turned_ref[pl.ds(tap, ROWS, stride=L), :].astype(jnp.bfloat16)
+
+
+def layout(dictionary, channels):
+    steps = channels // ROWS
+    return pl.pallas_call(
+        layout_kernel,
+        grid=(steps,),
+        in_specs=[pl.BlockSpec((K, ROWS * L), lambda i: (0, i))],
+        out_specs=pl.BlockSpec((L, ROWS, K), lambda i: (0, i, 0)),
+        out_shape=jax.ShapeDtypeStruct((L, channels, K), jnp.bfloat16),
+        scratch_shapes=[pltpu.VMEM((ROWS * L, K), jnp.float32)],
+        compiler_params=pltpu.CompilerParams(vmem_limit_bytes=VMEM_BYTES),
+        name="layout",
+    )(dictionary)
+
+
+def patch_kernel(row_ref, atoms_ref, taps_ref, out_ref, columns_ref, turned_ref):
+    first_row = pl.multiple_of(row_ref[0], BLOCK_ATOMS)
+
+    @pl.when(pl.program_id(0) == 0)
+    def _():
+        columns_ref[...] = jnp.zeros_like(columns_ref)
+
+    columns_ref[pl.ds(first_row, BLOCK_ATOMS), :] = atoms_ref[...]
+    by_tap(columns_ref, turned_ref)
+    lane = lax.broadcasted_iota(jnp.int32, (ROWS, K), 1)
+    renewed = (lane >= first_row) & (lane < first_row + BLOCK_ATOMS)
+    for tap in range(L):
+        fresh = turned_ref[pl.ds(tap, ROWS, stride=L), :]
+        kept = taps_ref[tap].astype(jnp.float32)
+        out_ref[tap] = jnp.where(renewed, fresh, kept).astype(jnp.bfloat16)
+
+
+def patch(first_row, atoms, taps):
+    channels = taps.shape[1]
+    steps = channels // ROWS
+    return pl.pallas_call(
+        patch_kernel,
+        grid_spec=pltpu.PrefetchScalarGridSpec(
+            num_scalar_prefetch=1,
+            grid=(steps,),
+            in_specs=[
+                pl.BlockSpec((BLOCK_ATOMS, ROWS * L), lambda i, r: (0, i)),
+                pl.BlockSpec((L, ROWS, K), lambda i, r: (0, i, 0)),
+            ],
+            out_specs=pl.BlockSpec((L, ROWS, K), lambda i, r: (0, i, 0)),
+            scratch_shapes=[
+                pltpu.VMEM((K, ROWS * L), jnp.float32),
+                pltpu.VMEM((ROWS * L, K), jnp.float32),
+            ],
+        ),
+        out_shape=jax.ShapeDtypeStruct(taps.shape, jnp.bfloat16),
+        input_output_aliases={2: 0},
+        compiler_params=pltpu.CompilerParams(vmem_limit_bytes=VMEM_BYTES),
+        name="patch",
+    )(first_row, atoms, taps)
+
+
+def extents():
+    reach = [(L, 0)]
+    for _ in range(INNER):
+        reach.insert(0, (reach[0][0] + L, reach[0][1] + L))
+    return reach
+
+
+def hops_of(reach, segment):
+    return -(-reach // segment)
+
+
+def codes_kernel(
+    segment,
+    peers,
+    code_hops,
+    signal_hops,
+    place_ref,
+    limit_ref,
+    *refs,
+):
+    code_refs = refs[: len(code_hops)]
+    signal_refs = refs[len(code_hops) : len(code_hops) + len(signal_hops)]
+    taps_hbm, codes_out, resid_out, payload_out = refs[len(code_hops) + len(signal_hops) :][:4]
+    taps, zf, zb, sf, rb, zz, rr, fine, acc, tall, sems = refs[len(code_hops) + len(signal_hops) + 4 :]
+    channels = taps.shape[2]
+    tiles = channels // LANES
+    scale = (C * L) ** (-0.5)
+    base = place_ref[0]
+    first_row = pl.multiple_of(place_ref[1], BLOCK_ATOMS)
+    total_time = peers * segment
+    reach = extents()
+    z_left, z_right = reach[0]
+    s_left, s_right = z_left - L, z_right
+    passes = ROWS // FINE
+
+    def tap_copy(step):
+        return pltpu.make_async_copy(
+            taps_hbm.at[:, pl.ds(step * FINE, FINE)],
+            taps.at[:, pl.ds(step * FINE, FINE)],
+            sems.at[step],
+        )
+
+    for step in range(passes):
+        tap_copy(step).start()
+
+    for hop, ref in zip(code_hops, code_refs):
+        low = max(-z_left, hop * segment)
+        high = min(segment + z_right, (hop + 1) * segment)
+        piece = ref[...].T
+        zf[low + z_left : high + z_left, :] = piece[low - hop * segment : high - hop * segment]
+    for hop, ref in zip(signal_hops, signal_refs):
+        low = max(-s_left, hop * segment)
+        high = min(segment + s_right, (hop + 1) * segment)
+        piece = ref[...].astype(jnp.float32).T
+        sf[low + s_left : high + s_left, :] = piece[low - hop * segment : high - hop * segment]
+    zb[...] = zf[...].astype(jnp.bfloat16)
+
+    def moment(start, count, width):
+        return base + start + lax.broadcasted_iota(jnp.int32, (count, width), 0)
+
+    def convolve(start, count, wait):
+        rows = count + ROWS
+        for coarse in range(COARSE):
+            begin = start - ROWS - ROWS * coarse + z_left
+            zz[:rows, coarse * K : (coarse + 1) * K] = zb[begin : begin + rows, :]
+        acc[:, :count, :] = jnp.zeros((tiles, count, LANES), jnp.float32)
+
+        def one_pass(step, carry):
+            if wait:
+                tap_copy(step).wait()
+            for pair in range(FINE // 2):
+                fine_lag = step * FINE + 2 * pair
+                weights = jnp.concatenate(
+                    [
+                        jnp.concatenate([taps[m, fine_lag + j] for m in range(COARSE)], axis=1)
+                        for j in range(2)
+                    ],
+                    axis=0,
+                )
+                product = lax.dot_general(
+                    zz[:rows, :], weights, NT, preferred_element_type=jnp.float32
+                )
+                for j in range(2):
+                    for tile in range(tiles):
+                        column = j * channels + tile * LANES
+                        fine[2 * pair + j, tile, :rows, :] = product[:, column : column + LANES]
+            for tile in range(tiles):
+                total = acc[tile, :count, :]
+                for j in range(FINE):
+                    total += fine[j, tile, pl.ds(ROWS - step * FINE - j, count), :]
+                acc[tile, :count, :] = total
+            return carry
+
+        lax.fori_loop(0, passes, one_pass, 0)
+
+    def correlate(start, count):
+        rows = count + ROWS
+        for coarse in range(COARSE):
+            begin = start + ROWS * coarse + s_left
+            rr[:rows, coarse * channels : (coarse + 1) * channels] = rb[begin : begin + rows, :]
+        acc[0, :count, :] = jnp.zeros((count, LANES), jnp.float32)
+
+        def one_pass(step, carry):
+            for pair in range(FINE // 2):
+                fine_lag = step * FINE + 2 * pair
+                weights = jnp.concatenate(
+                    [
+                        jnp.concatenate([taps[m, fine_lag + j] for m in range(COARSE)], axis=0)
+                        for j in range(2)
+                    ],
+                    axis=1,
+                )
+                product = lax.dot_general(
+                    rr[:rows, :], weights, NN, preferred_element_type=jnp.float32
+                )
+                for j in range(2):
+                    fine[2 * pair + j, 0, :rows, :] = product[:, j * K : (j + 1) * K]
+            total = acc[0, :count, :]
+            for j in range(FINE):
+                total += fine[j, 0, pl.ds(step * FINE + j, count), :]
+            acc[0, :count, :] = total
+            return carry
+
+        lax.fori_loop(0, passes, one_pass, 0)
+
+    limit = limit_ref[...]
+    for step in range(INNER):
+        left, right = reach[step + 1]
+        start, count = -left, left + segment + right + L
+        convolve(start, count, step == 0)
+        inside = moment(start, count, LANES) < total_time
+        for tile in range(tiles):
+            column = slice(tile * LANES, (tile + 1) * LANES)
+            value = sf[start + s_left : start + s_left + count, column] - scale * acc[tile, :count, :]
+            rb[start + s_left : start + s_left + count, column] = jnp.where(
+                inside, value, 0.0
+            ).astype(jnp.bfloat16)
+        count = left + segment + right
+        correlate(start, count)
+        window = slice(start + z_left, start + z_left + count)
+        stepped = zf[window, :] + code_rate * (scale * acc[0, :count, :])
+        state = stepped - jnp.clip(stepped, -limit, limit)
+        state = jnp.where(moment(start, count, K) >= 0, state, 0.0)
+        zf[window, :] = state
+        zb[window, :] = state.astype(jnp.bfloat16)
+
+    convolve(0, segment, False)
+    for tile in range(tiles):
+        column = slice(tile * LANES, (tile + 1) * LANES)
+        value = sf[s_left : s_left + segment, column] - scale * acc[tile, :segment, :]
+        value = value.T
+        resid_out[column, :] = value
+        tall[column, :] = value
+    codes_out[...] = zf[z_left : z_left + segment, :].T
+    block = codes_out[pl.ds(first_row, BLOCK_ATOMS), :].astype(jnp.bfloat16)
+    share = channels // peers
+    share_rows = payload_out.shape[1] - BLOCK_ATOMS
+    for peer in range(peers):
+        payload_out[peer, :share_rows, :] = tall[peer * share : peer * share + share_rows, :].astype(
+            jnp.bfloat16
+        )
+        payload_out[peer, share_rows:, :] = block
+
+
+def run_codes(place, limit, codes, signals, taps, segment, peers):
+    code_hops, signal_hops = tuple(codes), tuple(signals)
+    channels = taps.shape[1]
+    share = channels // peers
+    share_rows = -(-share // ROWS) * ROWS
+    reach = extents()
+    z_rows = reach[0][0] + segment + reach[0][1]
+    s_rows = z_rows - L
+    longest = s_rows + ROWS
+    scored = reach[1][0] + segment + reach[1][1] + ROWS
+    whole = lambda: pl.BlockSpec(memory_space=pltpu.VMEM)
+    return pl.pallas_call(
+        functools.partial(codes_kernel, segment, peers, code_hops, signal_hops),
+        in_specs=[pl.BlockSpec(memory_space=pltpu.SMEM), whole()]
+        + [whole() for _ in code_hops + signal_hops]
+        + [pl.BlockSpec(memory_space=pl.ANY)],
+        out_specs=[whole(), whole(), whole()],
+        out_shape=[
+            jax.ShapeDtypeStruct((K, segment), jnp.float32),
+            jax.ShapeDtypeStruct((channels, segment), jnp.float32),
+            jax.ShapeDtypeStruct((peers, share_rows + BLOCK_ATOMS, segment), jnp.bfloat16),
+        ],
+        scratch_shapes=[
+            pltpu.VMEM((COARSE, ROWS, channels, K), jnp.bfloat16),
+            pltpu.VMEM((z_rows, K), jnp.float32),
+            pltpu.VMEM((z_rows, K), jnp.bfloat16),
+            pltpu.VMEM((s_rows, channels), jnp.float32),
+            pltpu.VMEM((s_rows, channels), jnp.bfloat16),
+            pltpu.VMEM((longest, COARSE * K), jnp.bfloat16),
+            pltpu.VMEM((scored, COARSE * channels), jnp.bfloat16),
+            pltpu.VMEM((FINE, channels // LANES, longest, LANES), jnp.float32),
+            pltpu.VMEM((channels // LANES, s_rows, LANES), jnp.float32),
+            pltpu.VMEM((channels + ROWS, segment), jnp.float32),
+            pltpu.SemaphoreType.DMA((ROWS // FINE,)),
+        ],
+        compiler_params=pltpu.CompilerParams(vmem_limit_bytes=VMEM_BYTES),
+        name="codes",
+    )(
+        place,
+        limit,
+        *codes.values(),
+        *signals.values(),
+        taps.reshape(COARSE, ROWS, channels, K),
+    )
+
+
+def gradient_kernel(share, source_ref, blocks_ref, out_ref, rf, zf, rr, zz):
+    peers, rows, segment = blocks_ref.shape
+    share_rows = rows - BLOCK_ATOMS
+    span = peers * segment
+    rf[:, span:] = jnp.zeros((share_rows, LANES), jnp.float32)
+    zf[:, :LANES] = jnp.zeros((BLOCK_ATOMS, LANES), jnp.float32)
+    for peer in range(peers):
+        column = peer * segment
+        rf[:, column : column + segment] = blocks_ref[peer, :share_rows, :].astype(jnp.float32)
+        zf[:, LANES + column : LANES + column + segment] = blocks_ref[peer, share_rows:, :].astype(
+            jnp.float32
+        )
+    for lag in range(ROWS):
+        rr[lag * share_rows : (lag + 1) * share_rows, :] = rf[:, lag : lag + span].astype(jnp.bfloat16)
+    for coarse in range(COARSE):
+        begin = LANES - ROWS * coarse
+        zz[coarse * BLOCK_ATOMS : (coarse + 1) * BLOCK_ATOMS, :] = zf[:, begin : begin + span].astype(
+            jnp.bfloat16
+        )
+    lagged = lax.dot_general(zz[...], rr[...], NT, preferred_element_type=jnp.float32)
+    lagged = lagged.astype(jnp.bfloat16)
+    wide = ROWS * share_rows
+    entries = share * L
+    total = jnp.zeros((BLOCK_ATOMS, entries), jnp.float32)
+    for coarse in range(COARSE):
+        row = lax.broadcasted_iota(jnp.int32, (wide, entries), 0) + coarse * wide
+        chosen = (row == source_ref[...]).astype(jnp.float32).astype(jnp.bfloat16)
+        total += lax.dot_general(
+            lagged[coarse * BLOCK_ATOMS : (coarse + 1) * BLOCK_ATOMS, :],
+            chosen,
+            NN,
+            preferred_element_type=jnp.float32,
+        )
+    out_ref[...] = total.astype(jnp.bfloat16)
+
+
+def share_gradient(blocks, share):
+    peers, rows, segment = blocks.shape
+    share_rows = rows - BLOCK_ATOMS
+    span = peers * segment
+    entry = jnp.arange(share * L, dtype=jnp.int32)
+    channel, tap = entry // L, entry % L
+    source = (tap // ROWS) * (ROWS * share_rows) + (tap % ROWS) * share_rows + channel
+    return pl.pallas_call(
+        functools.partial(gradient_kernel, share),
+        out_shape=jax.ShapeDtypeStruct((BLOCK_ATOMS, share * L), jnp.bfloat16),
+        scratch_shapes=[
+            pltpu.VMEM((share_rows, span + LANES), jnp.float32),
+            pltpu.VMEM((BLOCK_ATOMS, LANES + span), jnp.float32),
+            pltpu.VMEM((ROWS * share_rows, span), jnp.bfloat16),
+            pltpu.VMEM((COARSE * BLOCK_ATOMS, span), jnp.bfloat16),
+        ],
+        compiler_params=pltpu.CompilerParams(vmem_limit_bytes=VMEM_BYTES),
+        name="gradient",
+    )(source[None, :], blocks)
+
+
+def renew_kernel(row_ref, grad_ref, dict_hbm, out_hbm, atoms_ref, old, across, sems):
+    first_row = pl.multiple_of(row_ref[0], BLOCK_ATOMS)
+    peers, _, width = grad_ref.shape
+    entries = C * L
+    fetch = pltpu.make_async_copy(dict_hbm.at[pl.ds(first_row, BLOCK_ATOMS)], old, sems.at[0])
+    fetch.start()
+    fetch.wait()
+
+    def column(peer):
+        return pl.ds(pl.multiple_of(peer * width, LANES), width)
+
+    zeros = jnp.zeros((BLOCK_ATOMS, width), jnp.float32)
+
+    def sums(peer, carry):
+        square, dot = carry
+        before = old[:, column(peer)]
+        return square + before * before, dot + grad_ref[peer].astype(jnp.float32) * before
+
+    square, dot = lax.fori_loop(0, peers, sums, (zeros, zeros))
+    mean_sq = jnp.sum(square, axis=1, keepdims=True) / entries + tiny_eps
+    along = jnp.sum(dot, axis=1, keepdims=True) / entries / mean_sq
+
+    def project(peer, square):
+        value = grad_ref[peer].astype(jnp.float32) - along * old[:, column(peer)]
+        across[:, column(peer)] = value
+        return square + value * value
+
+    square = lax.fori_loop(0, peers, project, zeros)
+    spread = jnp.sum(square, axis=1, keepdims=True) / entries + tiny_eps
+    step = move_rate / jnp.sqrt(spread)
+    norm = 1.0 / jnp.sqrt(mean_sq + 0.25)
+
+    def renew(peer, carry):
+        atoms_ref[:, column(peer)] = (old[:, column(peer)] + step * across[:, column(peer)]) * norm
+        return carry
+
+    lax.fori_loop(0, peers, renew, 0)
+    store = pltpu.make_async_copy(atoms_ref, out_hbm.at[pl.ds(first_row, BLOCK_ATOMS)], sems.at[1])
+    store.start()
+    store.wait()
+
+
+def renew(first_row, gradient, dictionary):
+    width = dictionary.shape[1]
+    return pl.pallas_call(
+        renew_kernel,
+        in_specs=[
+            pl.BlockSpec(memory_space=pltpu.SMEM),
+            pl.BlockSpec(memory_space=pltpu.VMEM),
+            pl.BlockSpec(memory_space=pl.ANY),
+        ],
+        out_specs=[pl.BlockSpec(memory_space=pl.ANY), pl.BlockSpec(memory_space=pltpu.VMEM)],
+        out_shape=[
+            jax.ShapeDtypeStruct(dictionary.shape, jnp.float32),
+            jax.ShapeDtypeStruct((BLOCK_ATOMS, width), jnp.float32),
+        ],
+        scratch_shapes=[
+            pltpu.VMEM((BLOCK_ATOMS, width), jnp.float32),
+            pltpu.VMEM((BLOCK_ATOMS, width), jnp.float32),
+            pltpu.SemaphoreType.DMA((2,)),
+        ],
+        input_output_aliases={2: 0},
+        compiler_params=pltpu.CompilerParams(vmem_limit_bytes=VMEM_BYTES),
+        name="renew",
+    )(first_row, gradient, dictionary)
+
+
+def whole_channels(signal, codes_init, dictionary_init, threshold, plan):
+    channels, segment = signal.shape
+    peers = lax.axis_size("tm")
+    share = channels // peers
+    limit = threshold[None, :]
+    reach = extents()
+    z_left, z_right = reach[0]
+    s_left, s_right = z_left - L, z_right
+
+    def window(shard, left, right):
+        hops = range(-hops_of(left, segment), hops_of(right, segment) + 1)
+        return {hop: shard if hop == 0 else shifted(shard, "tm", -hop) for hop in hops}
+
+    base = lax.axis_index("tm") * segment
+    signals = window(signal, s_left, s_right)
+    code_state = codes_init
+    dictionary = dictionary_init
+    taps = layout(dictionary, channels)
+    for outer_step in range(OUTER):
+        first_row = plan[outer_step] * BLOCK_ATOMS
+        place = jnp.stack([base, first_row]).astype(jnp.int32)
+        codes = window(code_state, z_left, z_right)
+        code_state, residual, payload = run_codes(
+            place, limit, codes, signals, taps, segment, peers
+        )
+        blocks = lax.all_to_all(payload, "tm", 0, 0, tiled=True)
+        piece = share_gradient(blocks, share)
+        gradient = lax.all_gather(piece, "tm")
+        dictionary, atoms = renew(first_row[None].astype(jnp.int32), gradient, dictionary)
+        if outer_step + 1 < OUTER:
+            taps = patch(first_row[None].astype(jnp.int32), atoms, taps)
+    return code_state, dictionary, residual
+
+
 def renew_atoms(old_atoms, across, mean_sq, spread):
     return (old_atoms + move_rate * across / jnp.sqrt(spread)[:, None]) / jnp.sqrt(mean_sq + 0.25)[
         :, None
     ]
 
 
-def shards(signal, codes_init, dictionary_init, threshold, plan):
+def split_channels(signal, codes_init, dictionary_init, threshold, plan):
     segment = signal.shape[1]
     local_chan = signal.shape[0]
     unit_scale = (C * L) ** (-0.5)
@@ -89,6 +537,20 @@
     return (code_state, dictionary, residual)
 
 
+def shards(signal, codes_init, dictionary_init, threshold, plan):
+    channels, segment = signal.shape
+    peers = lax.axis_size("tm")
+    fits = (
+        lax.axis_size("chan") == 1
+        and segment % LANES == 0
+        and channels % LANES == 0
+        and channels % peers == 0
+        and (channels // peers * L) % LANES == 0
+    )
+    body = whole_channels if fits else split_channels
+    return body(signal, codes_init, dictionary_init, threshold, plan)
+
+
 def solution(mesh):
     placed = (P("chan", "tm"), P(None, "tm"), P(None, "chan"), P(), P())
     return jax.shard_map(

time: 1010 us -> 334 us (0.33)
  other arithmetic: 420 us -> 1.84 us
  waiting for transfers between devices: 296 us -> 108 us
  Pallas kernels: 0 us -> 132 us
  local copies, waits for them, and re-layouts: 149 us -> 17.2 us
  matrix products: 87.6 us -> 0 us
  blocking collectives: 0 us -> 14.3 us
  starting transfers between devices: 31 us -> 43.4 us
    unnamed x1037 -> x0, other arithmetic: 386 us -> none
    psum x2 -> x0, waiting for transfers between devices: 282 us -> none  [shards(): gradient = lax.psum(local_grad, 'tm')]
    pallas_call x0 -> x8, Pallas kernels: none -> 132 us  [the longest x2 56.3 us: run_codes(): pl.pallas_call(functools.partial(codes_kernel, segment, peers, code_hops,...]
    all_gather x0 -> x2, waiting for transfers between devices: none -> 89.3 us  [whole_channels(): gradient = lax.all_gather(piece, 'tm')]
    dot_general x12 -> x0, matrix products: 87.6 us -> none  [the longest x4 38.6 us: shards(): jnp.dot(dict_low, lagged, preferred_element_type=jnp.float32)]
    another operation x6 -> x0, local copies, waits for them, and re-layouts: 77.1 us -> none  [resid_columns(): jnp.stack([extended[:, offset:offset + segment] for offset in range(L)],...]
    reshape x2 -> x0, local copies, waits for them, and re-layouts: 26.6 us -> none  [shards(): atom_cube = dict_low.reshape(K, local_chan, L)]
    all_to_all x0 -> x1, blocking collectives: none -> 14.3 us  [whole_channels(): blocks = lax.all_to_all(payload, 'tm', 0, 0, tiled=True)]
  transfers between devices with their start and end apart: 13 -> 17, of which waited for: 12 -> 4; matrix products, arithmetic and copies ran while one was open for 3% -> 1% of each run, Pallas kernels for 0% -> 18%
where the time goes in v1:
time: 334 us; the launch traced here: 332 us
  Pallas kernels  132 us (40%)
  waiting for transfers between devices  108 us (32%)
  starting transfers between devices  43.4 us (13%)
  local copies, waits for them, and re-layouts  17.2 us (5%)
  between operations  15.7 us (5%)
  blocking collectives  14.3 us (4%)
    all_gather x2, waiting for transfers between devices, whole_channels(): gradient = lax.all_gather(piece, 'tm')  89.3 us
    pallas_call x2, Pallas kernels, run_codes(): pl.pallas_call(functools.partial(codes_kernel, segment, peers, code_hops,...  56.3 us
    ppermute x14, starting transfers between devices, shifted(): return lax.ppermute(shard, axis, pairs)  35.6 us
    pallas_call x1, Pallas kernels, layout(): pl.pallas_call(layout_kernel, grid=(steps,), in_specs=[pl.BlockSpec((K, R...  26.7 us
    pallas_call x1, Pallas kernels, patch(): pl.pallas_call(patch_kernel, grid_spec=pltpu.PrefetchScalarGridSpec(num_s...  26.2 us
    unnamed x37, local copies, waits for them, and re-layouts  16.6 us
    pallas_call x2, Pallas kernels, renew(): pl.pallas_call(renew_kernel, in_specs=[pl.BlockSpec(memory_space=pltpu.SM...  15.5 us
    all_to_all x1, blocking collectives, whole_channels(): blocks = lax.all_to_all(payload, 'tm', 0, 0, tiled=True)  14.3 us
  transfers between devices with their start and end apart: 17, of which 4 were waited for; matrix products, arithmetic and copies ran while one was open for 1% of the time, Pallas kernels for 18%

profile of v1, /device:TPU:0, one launch (start us, length us, event | category | flops | bytes accessed | tf_op | source)
XLA Modules:
  0.0 332.3 jit_solution(9695865850043995637)
XLA Ops:
  7.2 14.5 %copy.15.dict_ref.dict_hbm = f32[128,36864]{1,0:T(8,128)} copy(f32[128,36864]{1,0:T(8,128)} %param.7) | data formatting | bytes 37748736
  21.7 4.3 %collective-permute-start = (f32[128,128]{1,0:T(8,128)S(1)}, f32[128,128]{1,0:T(8,128)S(1)}, u32[]{:S(2)}, u32[]{:S(2)}) collective-permute-start(f32[128,128]{1,0:T(8,128)S(1)} %copy-done.6), channel_id=1, source_target_pairs={{0,3},{1,4},{2,5},{3,6},{4,7},{5,8},{6,9},{7,10},{8,11},{9,12},{10... | collective-permute-start | bytes 196616 | tf_op jit(solution)/shard_map/ppermute | solution.py:34
  26.0 3.4 %collective-permute-start.1 = (f32[128,128]{1,0:T(8,128)S(1)}, f32[128,128]{1,0:T(8,128)S(1)}, u32[]{:S(2)}, u32[]{:S(2)}) collective-permute-start(f32[128,128]{1,0:T(8,128)S(1)} %copy-done.6), channel_id=1, source_target_pairs={{0,2},{1,3},{2,4},{3,5},{4,6},{5,7},{6,8},{7,9},{8,10},{9,11},{10,... | collective-permute-start | bytes 196616 | tf_op jit(solution)/shard_map/ppermute | solution.py:34
  29.4 2.3 collective-permute-start.2
  31.7 1.3 collective-permute-start.3
  33.1 5.3 %collective-permute-start.5 = (bf16[384,128]{1,0:T(8,128)(2,1)S(1)}, bf16[384,128]{1,0:T(8,128)(2,1)S(1)}, u32[]{:S(2)}, u32[]{:S(2)}) collective-permute-start(bf16[384,128]{1,0:T(8,128)(2,1)S(1)} %copy-done.1), channel_id=1, source_target_pairs={{0,2},{1,3},{2,4},{3,5},{4,6},{5,7},{6,8},{7,9},{8,10},{9,11},{10,... | collective-permute-start | bytes 294920 | tf_op jit(solution)/shard_map/ppermute | solution.py:34
  38.4 26.7 %layout.1.taps_ref = bf16[96,384,128]{2,1,0:T(8,128)(2,1)} custom-call(f32[128,36864]{1,0:T(8,128)} %copy.15.dict_ref.dict_hbm), custom_call_target="tpu_custom_call" | custom-call | tf_op jit(solution)/shard_map/layout/pallas_call | solution.py:51
  66.4 1.5 collective-permute-start.6
  72.4 8.3 %collective-permute-done.4.refs_5_ = f32[128,128]{1,0:T(8,128)S(1)} collective-permute-done((f32[128,128]{1,0:T(8,128)S(1)}, f32[128,128]{1,0:T(8,128)S(1)}, u32[]{:S(2)}, u32[]{:S(2)}) %collective-permute-start.4) | collective-permute-done | bytes 65568 | tf_op jit(solution)/shard_map/ppermute | solution.py:34
  81.5 28.1 %codes.2 = (f32[128,128]{1,0:T(8,128)}, f32[384,128]{1,0:T(8,128)}, bf16[32,32,128]{2,1,0:T(8,128)(2,1)}) custom-call(s32[2]{0:T(128)} %pad_add_fusion.1.place_ref, f32[1,128]{1,0:T(1,128)} %bitcast.10, f32[128,128]{1,0:T(8,128)} %copy-done.7, f32[128,128]{1,0:T(8,128)} %copy-done.8, f32[128,128]{1,0:T(8,128)} %copy-done.9, f32[128,128]{1,0:T(8,128)} %refs_3_.1, ...), custom_call_target="tpu_custom_call" | custom-call | tf_op jit(solution)/shard_map/codes/pallas_call | solution.py:280
  109.7 7.8 %all-to-all-start = ((bf16[32,32,128]{2,1,0:T(8,128)(2,1)}), bf16[32,32,128]{2,1,0:T(8,128)(2,1)S(1)}, u32[]{:S(2)}, u32[]{:S(2)}) async-start(bf16[32,32,128]{2,1,0:T(8,128)(2,1)} %get-tuple-element.12), calls=%async_computation | async-start | bytes 524288 | tf_op jit(solution)/shard_map/all_to_all | solution.py:464
  118.1 9.9 %all-to-all-done.blocks_ref = bf16[32,32,128]{2,1,0:T(8,128)(2,1)S(1)} async-done(((bf16[32,32,128]{2,1,0:T(8,128)(2,1)}), bf16[32,32,128]{2,1,0:T(8,128)(2,1)S(1)}, u32[]{:S(2)}, u32[]{:S(2)}) %all-to-all-start) | async-done | bytes 262176 | tf_op jit(solution)/shard_map/all_to_all | solution.py:464
  128.7 3.8 %gradient.2 = bf16[16,1152]{1,0:T(8,128)(2,1)} custom-call(s32[1,1152]{1,0:T(1,128)} %fusion.source_ref, bf16[32,32,128]{2,1,0:T(8,128)(2,1)} %copy-done), custom_call_target="tpu_custom_call" | custom-call | tf_op jit(solution)/shard_map/gradient/pallas_call | solution.py:358
  133.2 2.2 collective-permute-start.10
  135.4 2.2 collective-permute-start.11
  140.2 6.6 %collective-permute-start.9 = (f32[128,128]{1,0:T(8,128)}, f32[128,128]{1,0:T(8,128)S(1)}, u32[]{:S(2)}, u32[]{:S(2)}) collective-permute-start(f32[128,128]{1,0:T(8,128)} %get-tuple-element.11.refs_3_), channel_id=1, source_target_pairs={{0,3},{1,4},{2,5},{3,6},{4,7},{5,8},{6,9},{7,10},{8,11},{9,12},{10... | collective-permute-start | bytes 196616 | tf_op jit(solution)/shard_map/ppermute | solution.py:34
  147.4 37.3 %all-gather.5.cloned.1.call-done = bf16[512,1152]{1,0:T(8,128)(2,1)} async-done(((bf16[16,1152]{1,0:T(8,128)(2,1)}), bf16[512,1152]{1,0:T(8,128)(2,1)}) %all-gather.5.cloned.1.call-update) | async-done | bytes 1179664 | tf_op jit(solution)/shard_map/all_gather | solution.py:466
  184.7 7.7 %renew.2 = (f32[128,36864]{1,0:T(8,128)}, f32[16,36864]{1,0:T(8,128)}) custom-call(s32[1]{0:T(128)S(6)} %mul.39.row_ref, bf16[32,16,1152]{2,1,0:T(8,128)(2,1)} %bitcast.8, f32[128,36864]{1,0:T(8,128)} %copy.15.dict_ref.dict_hbm), custom_call_target="tpu_custom_call", output_to_operand_aliasing={{0}: (2, {})} | custom-call | tf_op jit(solution)/shard_map/renew/pallas_call | solution.py:416
  192.4 26.2 %patch.1 = bf16[96,384,128]{2,1,0:T(8,128)(2,1)} custom-call(s32[1]{0:T(128)S(6)} %mul.39.row_ref, f32[16,36864]{1,0:T(8,128)} %get-tuple-element.13.atoms_ref, bf16[96,384,128]{2,1,0:T(8,128)(2,1)} %layout.1.taps_ref), custom_call_target="tpu_custom_call", output_to_operand_aliasing={{}: (2, {})} | custom-call | tf_op jit(solution)/shard_map/patch/pallas_call | solution.py:83
  219.4 28.1 %codes.3 = (f32[128,128]{1,0:T(8,128)}, f32[384,128]{1,0:T(8,128)}, bf16[32,32,128]{2,1,0:T(8,128)(2,1)}) custom-call(s32[2]{0:T(128)} %pad_add_fusion.place_ref, f32[1,128]{1,0:T(1,128)} %bitcast.11, f32[128,128]{1,0:T(8,128)} %copy-done.15, f32[128,128]{1,0:T(8,128)} %copy-done.11, f32[128,128]{1,0:T(8,128)} %copy-done.12, ...), custom_call_target="tpu_custom_call" | custom-call | tf_op jit(solution)/shard_map/codes/pallas_call | solution.py:280
  247.5 14.3 %all_to_all.10.blocks_ref = bf16[32,32,128]{2,1,0:T(8,128)(2,1)} all-to-all(bf16[32,32,128]{2,1,0:T(8,128)(2,1)} %get-tuple-element.15), channel_id=1, replica_groups=mesh['tm'=32,'chan'=1] {'tm'}, dimensions={0} | all-to-all | bytes 524288 | tf_op jit(solution)/shard_map/all_to_all | solution.py:464
  261.8 3.8 %gradient.3 = bf16[16,1152]{1,0:T(8,128)(2,1)} custom-call(s32[1,1152]{1,0:T(1,128)} %fusion.source_ref, bf16[32,32,128]{2,1,0:T(8,128)(2,1)} %all_to_all.10.blocks_ref), custom_call_target="tpu_custom_call" | custom-call | tf_op jit(solution)/shard_map/gradient/pallas_call | solution.py:358
  265.7 52.0 %all-gather.7.cloned.1.call-done = bf16[512,1152]{1,0:T(8,128)(2,1)} async-done(((bf16[16,1152]{1,0:T(8,128)(2,1)}), bf16[512,1152]{1,0:T(8,128)(2,1)}) %all-gather.7.cloned.1.call-update) | async-done | bytes 1179664 | tf_op jit(solution)/shard_map/all_gather | solution.py:466
  317.7 7.8 %renew.3 = (f32[128,36864]{1,0:T(8,128)}, f32[16,36864]{1,0:T(8,128)}) custom-call(s32[1]{0:T(128)S(6)} %mul.38.row_ref, bf16[32,16,1152]{2,1,0:T(8,128)(2,1)} %bitcast.9, f32[128,36864]{1,0:T(8,128)} %get-tuple-element.16.dict_hbm), custom_call_target="tpu_custom_call", output_to_operand_aliasing={{0}: (2, {})} | custom-call | tf_op jit(solution)/shard_map/renew/pallas_call | solution.py:416
  (62 shorter events, 11.1 us)
Async XLA Ops:
  7.2 25.9 %copy-start.1 = (bf16[384,128]{1,0:T(8,128)(2,1)S(1)}, bf16[384,128]{1,0:T(8,128)(2,1)}, u32[]{:S(2)}) copy-start(bf16[384,128]{1,0:T(8,128)(2,1)} %refs_8_.3) | copy-start | bytes 294916
  7.2 14.5 %copy-start.6 = (f32[128,128]{1,0:T(8,128)S(1)}, f32[128,128]{1,0:T(8,128)}, u32[]{:S(2)}) copy-start(f32[128,128]{1,0:T(8,128)} %refs_3_.1) | copy-start | bytes 196612
  21.7 44.6 %collective-permute-start = (f32[128,128]{1,0:T(8,128)S(1)}, f32[128,128]{1,0:T(8,128)S(1)}, u32[]{:S(2)}, u32[]{:S(2)}) collective-permute-start(f32[128,128]{1,0:T(8,128)S(1)} %copy-done.6), channel_id=1, source_target_pairs={{0,3},{1,4},{2,5},{3,6},{4,7},{5,8},{6,9},{7,10},{8,11},{9,12},{10... | collective-permute-start | bytes 196616 | tf_op jit(solution)/shard_map/ppermute | solution.py:34
  26.0 41.9 %collective-permute-start.1 = (f32[128,128]{1,0:T(8,128)S(1)}, f32[128,128]{1,0:T(8,128)S(1)}, u32[]{:S(2)}, u32[]{:S(2)}) collective-permute-start(f32[128,128]{1,0:T(8,128)S(1)} %copy-done.6), channel_id=1, source_target_pairs={{0,2},{1,3},{2,4},{3,5},{4,6},{5,7},{6,8},{7,9},{8,10},{9,11},{10,... | collective-permute-start | bytes 196616 | tf_op jit(solution)/shard_map/ppermute | solution.py:34
  29.4 39.8 %collective-permute-start.2 = (f32[128,128]{1,0:T(8,128)S(1)}, f32[128,128]{1,0:T(8,128)S(1)}, u32[]{:S(2)}, u32[]{:S(2)}) collective-permute-start(f32[128,128]{1,0:T(8,128)S(1)} %copy-done.6), channel_id=1, source_target_pairs={{0,1},{1,2},{2,3},{3,4},{4,5},{5,6},{6,7},{7,8},{8,9},{9,10},{10,1... | collective-permute-start | bytes 196616 | tf_op jit(solution)/shard_map/ppermute | solution.py:34
  31.7 38.8 %collective-permute-start.3 = (f32[128,128]{1,0:T(8,128)S(1)}, f32[128,128]{1,0:T(8,128)S(1)}, u32[]{:S(2)}, u32[]{:S(2)}) collective-permute-start(f32[128,128]{1,0:T(8,128)S(1)} %copy-done.6), channel_id=1, source_target_pairs={{1,0},{2,1},{3,2},{4,3},{5,4},{6,5},{7,6},{8,7},{9,8},{10,9},{11,1... | collective-permute-start | bytes 196616 | tf_op jit(solution)/shard_map/ppermute | solution.py:34
  33.1 47.7 %collective-permute-start.5 = (bf16[384,128]{1,0:T(8,128)(2,1)S(1)}, bf16[384,128]{1,0:T(8,128)(2,1)S(1)}, u32[]{:S(2)}, u32[]{:S(2)}) collective-permute-start(bf16[384,128]{1,0:T(8,128)(2,1)S(1)} %copy-done.1), channel_id=1, source_target_pairs={{0,2},{1,3},{2,4},{3,5},{4,6},{5,7},{6,8},{7,9},{8,10},{9,11},{10,... | collective-permute-start | bytes 294920 | tf_op jit(solution)/shard_map/ppermute | solution.py:34
  38.4 26.7 %copy-start.17 = (s32[8]{0:T(128)S(1)}, s32[8]{0:T(128)}, u32[]{:S(2)}) copy-start(s32[8]{0:T(128)} %param.9) | copy-start | bytes 100
  66.3 14.5 %copy-start.7 = (f32[128,128]{1,0:T(8,128)}, f32[128,128]{1,0:T(8,128)S(1)}, u32[]{:S(2)}) copy-start(f32[128,128]{1,0:T(8,128)S(1)} %collective-permute-done.refs_0_) | copy-start | bytes 196612
  66.4 14.4 %collective-permute-start.6 = (bf16[384,128]{1,0:T(8,128)(2,1)S(1)}, bf16[384,128]{1,0:T(8,128)(2,1)S(1)}, u32[]{:S(2)}, u32[]{:S(2)}) collective-permute-start(bf16[384,128]{1,0:T(8,128)(2,1)S(1)} %copy-done.1), channel_id=1, source_target_pairs={{0,1},{1,2},{2,3},{3,4},{4,5},{5,6},{6,7},{7,8},{8,9},{9,10},{10,1... | collective-permute-start | bytes 294920 | tf_op jit(solution)/shard_map/ppermute | solution.py:34
  67.9 12.9 %copy-start.8 = (f32[128,128]{1,0:T(8,128)}, f32[128,128]{1,0:T(8,128)S(1)}, u32[]{:S(2)}) copy-start(f32[128,128]{1,0:T(8,128)S(1)} %collective-permute-done.1.refs_1_) | copy-start | bytes 196612
  67.9 12.9 %collective-permute-start.7 = (bf16[384,128]{1,0:T(8,128)(2,1)S(1)}, bf16[384,128]{1,0:T(8,128)(2,1)S(1)}, u32[]{:S(2)}, u32[]{:S(2)}) collective-permute-start(bf16[384,128]{1,0:T(8,128)(2,1)S(1)} %copy-done.1), channel_id=1, source_target_pairs={{1,0},{2,1},{3,2},{4,3},{5,4},{6,5},{7,6},{8,7},{9,8},{10,9},{11,1... | collective-permute-start | bytes 294920 | tf_op jit(solution)/shard_map/ppermute | solution.py:34
  69.2 11.6 %copy-start.9 = (f32[128,128]{1,0:T(8,128)}, f32[128,128]{1,0:T(8,128)S(1)}, u32[]{:S(2)}) copy-start(f32[128,128]{1,0:T(8,128)S(1)} %collective-permute-done.2.refs_2_) | copy-start | bytes 196612
  69.2 11.6 %collective-permute-start.8 = (bf16[384,128]{1,0:T(8,128)(2,1)S(1)}, bf16[384,128]{1,0:T(8,128)(2,1)S(1)}, u32[]{:S(2)}, u32[]{:S(2)}) collective-permute-start(bf16[384,128]{1,0:T(8,128)(2,1)S(1)} %copy-done.1), channel_id=1, source_target_pairs={{2,0},{3,1},{4,2},{5,3},{6,4},{7,5},{8,6},{9,7},{10,8},{11,9},{12,... | collective-permute-start | bytes 294920 | tf_op jit(solution)/shard_map/ppermute | solution.py:34
  70.5 10.3 %copy-start.10 = (f32[128,128]{1,0:T(8,128)}, f32[128,128]{1,0:T(8,128)S(1)}, u32[]{:S(2)}) copy-start(f32[128,128]{1,0:T(8,128)S(1)} %collective-permute-done.3.refs_4_) | copy-start | bytes 196612
  70.5 10.2 %collective-permute-start.4 = (f32[128,128]{1,0:T(8,128)S(1)}, f32[128,128]{1,0:T(8,128)S(1)}, u32[]{:S(2)}, u32[]{:S(2)}) collective-permute-start(f32[128,128]{1,0:T(8,128)S(1)} %copy-done.6), channel_id=1, source_target_pairs={{2,0},{3,1},{4,2},{5,3},{6,4},{7,5},{8,6},{9,7},{10,8},{11,9},{12,... | collective-permute-start | bytes 196616 | tf_op jit(solution)/shard_map/ppermute | solution.py:34
  109.7 18.4 %all-to-all-start = ((bf16[32,32,128]{2,1,0:T(8,128)(2,1)}), bf16[32,32,128]{2,1,0:T(8,128)(2,1)S(1)}, u32[]{:S(2)}, u32[]{:S(2)}) async-start(bf16[32,32,128]{2,1,0:T(8,128)(2,1)} %get-tuple-element.12), calls=%async_computation | async-start | bytes 524288 | tf_op jit(solution)/shard_map/all_to_all | solution.py:464
  117.4 67.3 %all-gather.5.cloned.1.call-start = ((), (), s32[]{:S(2)}) async-start(), calls=%async_computation.2 | async-start | bytes 1216512 | tf_op jit(solution)/shard_map/all_gather | solution.py:466
  132.6 185.0 %all-gather.7.cloned.1.call-start = ((), (), s32[]{:S(2)}) async-start(), calls=%async_computation.3 | async-start | bytes 1216512 | tf_op jit(solution)/shard_map/all_gather | solution.py:466
  133.2 85.4 %collective-permute-start.10 = (f32[128,128]{1,0:T(8,128)}, f32[128,128]{1,0:T(8,128)S(1)}, u32[]{:S(2)}, u32[]{:S(2)}) collective-permute-start(f32[128,128]{1,0:T(8,128)} %get-tuple-element.11.refs_3_), channel_id=1, source_target_pairs={{0,2},{1,3},{2,4},{3,5},{4,6},{5,7},{6,8},{7,9},{8,10},{9,11},{10,... | collective-permute-start | bytes 196616 | tf_op jit(solution)/shard_map/ppermute | solution.py:34
  135.4 83.2 %collective-permute-start.11 = (f32[128,128]{1,0:T(8,128)}, f32[128,128]{1,0:T(8,128)S(1)}, u32[]{:S(2)}, u32[]{:S(2)}) collective-permute-start(f32[128,128]{1,0:T(8,128)} %get-tuple-element.11.refs_3_), channel_id=1, source_target_pairs={{0,1},{1,2},{2,3},{3,4},{4,5},{5,6},{6,7},{7,8},{8,9},{9,10},{10,1... | collective-permute-start | bytes 196616 | tf_op jit(solution)/shard_map/ppermute | solution.py:34
  137.6 81.0 %collective-permute-start.12 = (f32[128,128]{1,0:T(8,128)}, f32[128,128]{1,0:T(8,128)S(1)}, u32[]{:S(2)}, u32[]{:S(2)}) collective-permute-start(f32[128,128]{1,0:T(8,128)} %get-tuple-element.11.refs_3_), channel_id=1, source_target_pairs={{1,0},{2,1},{3,2},{4,3},{5,4},{6,5},{7,6},{8,7},{9,8},{10,9},{11,1... | collective-permute-start | bytes 196616 | tf_op jit(solution)/shard_map/ppermute | solution.py:34
  138.9 79.8 %collective-permute-start.13 = (f32[128,128]{1,0:T(8,128)}, f32[128,128]{1,0:T(8,128)S(1)}, u32[]{:S(2)}, u32[]{:S(2)}) collective-permute-start(f32[128,128]{1,0:T(8,128)} %get-tuple-element.11.refs_3_), channel_id=1, source_target_pairs={{2,0},{3,1},{4,2},{5,3},{6,4},{7,5},{8,6},{9,7},{10,8},{11,9},{12,... | collective-permute-start | bytes 196616 | tf_op jit(solution)/shard_map/ppermute | solution.py:34
  140.2 78.5 %collective-permute-start.9 = (f32[128,128]{1,0:T(8,128)}, f32[128,128]{1,0:T(8,128)S(1)}, u32[]{:S(2)}, u32[]{:S(2)}) collective-permute-start(f32[128,128]{1,0:T(8,128)} %get-tuple-element.11.refs_3_), channel_id=1, source_target_pairs={{0,3},{1,4},{2,5},{3,6},{4,7},{5,8},{6,9},{7,10},{8,11},{9,12},{10... | collective-permute-start | bytes 196616 | tf_op jit(solution)/shard_map/ppermute | solution.py:34
  (11 other events, 7.4 us)
Sparse Core Ops, SparseCore 0:
  132.7 51.9 all-gather.4
  265.8 51.8 all-gather.6

commit v2 on v1

--- a/solution.py
+++ b/solution.py
@@ -20,6 +20,7 @@
 
 ROWS = 16
 COARSE = L // ROWS
+STRIDE = L + 1
 FINE = 4
 LANES = 128
 VMEM_BYTES = 56 * 1024 * 1024
@@ -36,14 +37,17 @@
 
 def by_tap(columns_ref, turned_ref):
     width = columns_ref.shape[1]
-    for start in range(0, width, 384):
-        turned_ref[start : start + 384, :] = columns_ref[:, start : start + 384].T
+    for start in range(0, width, 4 * L):
+        turned = columns_ref[:, start : start + 4 * L].T
+        for q in range(4):
+            row = (start // L + q) * STRIDE
+            turned_ref[row : row + L, :] = turned[q * L : (q + 1) * L]
 
 
 def layout_kernel(dict_ref, taps_ref, turned_ref):
     by_tap(dict_ref, turned_ref)
     for tap in range(L):
-        taps_ref[tap] = turned_ref[pl.ds(tap, ROWS, stride=L), :].astype(jnp.bfloat16)
+        taps_ref[tap] = turned_ref[pl.ds(tap, ROWS, stride=STRIDE), :].astype(jnp.bfloat16)
 
 
 def layout(dictionary, channels):
@@ -54,52 +58,10 @@
         in_specs=[pl.BlockSpec((K, ROWS * L), lambda i: (0, i))],
         out_specs=pl.BlockSpec((L, ROWS, K), lambda i: (0, i, 0)),
         out_shape=jax.ShapeDtypeStruct((L, channels, K), jnp.bfloat16),
-        scratch_shapes=[pltpu.VMEM((ROWS * L, K), jnp.float32)],
+        scratch_shapes=[pltpu.VMEM((ROWS * STRIDE, K), jnp.float32)],
         compiler_params=pltpu.CompilerParams(vmem_limit_bytes=VMEM_BYTES),
         name="layout",
     )(dictionary)
-
-
-def patch_kernel(row_ref, atoms_ref, taps_ref, out_ref, columns_ref, turned_ref):
-    first_row = pl.multiple_of(row_ref[0], BLOCK_ATOMS)
-
-    @pl.when(pl.program_id(0) == 0)
-    def _():
-        columns_ref[...] = jnp.zeros_like(columns_ref)
-
-    columns_ref[pl.ds(first_row, BLOCK_ATOMS), :] = atoms_ref[...]
-    by_tap(columns_ref, turned_ref)
-    lane = lax.broadcasted_iota(jnp.int32, (ROWS, K), 1)
-    renewed = (lane >= first_row) & (lane < first_row + BLOCK_ATOMS)
-    for tap in range(L):
-        fresh = turned_ref[pl.ds(tap, ROWS, stride=L), :]
-        kept = taps_ref[tap].astype(jnp.float32)
-        out_ref[tap] = jnp.where(renewed, fresh, kept).astype(jnp.bfloat16)
-
-
-def patch(first_row, atoms, taps):
-    channels = taps.shape[1]
-    steps = channels // ROWS
-    return pl.pallas_call(
-        patch_kernel,
-        grid_spec=pltpu.PrefetchScalarGridSpec(
-            num_scalar_prefetch=1,
-            grid=(steps,),
-            in_specs=[
-                pl.BlockSpec((BLOCK_ATOMS, ROWS * L), lambda i, r: (0, i)),
-                pl.BlockSpec((L, ROWS, K), lambda i, r: (0, i, 0)),
-            ],
-            out_specs=pl.BlockSpec((L, ROWS, K), lambda i, r: (0, i, 0)),
-            scratch_shapes=[
-                pltpu.VMEM((K, ROWS * L), jnp.float32),
-                pltpu.VMEM((ROWS * L, K), jnp.float32),
-            ],
-        ),
-        out_shape=jax.ShapeDtypeStruct(taps.shape, jnp.bfloat16),
-        input_output_aliases={2: 0},
-        compiler_params=pltpu.CompilerParams(vmem_limit_bytes=VMEM_BYTES),
-        name="patch",
-    )(first_row, atoms, taps)
 
 
 def extents():
@@ -113,19 +75,25 @@
     return -(-reach // segment)
 
 
-def codes_kernel(
-    segment,
-    peers,
-    code_hops,
-    signal_hops,
-    place_ref,
-    limit_ref,
-    *refs,
-):
-    code_refs = refs[: len(code_hops)]
-    signal_refs = refs[len(code_hops) : len(code_hops) + len(signal_hops)]
-    taps_hbm, codes_out, resid_out, payload_out = refs[len(code_hops) + len(signal_hops) :][:4]
-    taps, zf, zb, sf, rb, zz, rr, fine, acc, tall, sems = refs[len(code_hops) + len(signal_hops) + 4 :]
+def codes_kernel(segment, peers, code_hops, signal_hops, packed, atoms_count, copies, *refs):
+    refs = list(refs)
+
+    def take(count):
+        taken = refs[:count]
+        del refs[:count]
+        return taken
+
+    place_ref, limit_ref = take(2)
+    code_refs = take(len(code_hops))
+    signal_refs = take(len(signal_hops))
+    atoms_refs = take(atoms_count)
+    (taps_hbm,) = take(1)
+    dict_hbm = take(1) if copies else None
+    codes_out, resid_out, payload_out = take(3)
+    dict_out = take(1) if copies else None
+    taps, zf, zb, sf, rb, zz, rr, fine, acc, tall, sems = take(11)
+    copy_sems = take(1) if copies else None
+    columns, turned = take(2) if atoms_count else (None, None)
     channels = taps.shape[2]
     tiles = channels // LANES
     scale = (C * L) ** (-0.5)
@@ -147,15 +115,27 @@
     for step in range(passes):
         tap_copy(step).start()
 
+    def dict_copy(step):
+        rows = pl.ds(step * BLOCK_ATOMS, BLOCK_ATOMS)
+        return pltpu.make_async_copy(dict_hbm[0].at[rows], dict_out[0].at[rows], copy_sems[0].at[step])
+
+    if copies:
+        for step in range(K // BLOCK_ATOMS):
+            dict_copy(step).start()
+
     for hop, ref in zip(code_hops, code_refs):
         low = max(-z_left, hop * segment)
         high = min(segment + z_right, (hop + 1) * segment)
-        piece = ref[...].T
+        if hop in packed:
+            piece = ref[channels : channels + K, :].astype(jnp.float32)
+            piece = (piece + ref[channels + K :, :].astype(jnp.float32)).T
+        else:
+            piece = ref[...].T
         zf[low + z_left : high + z_left, :] = piece[low - hop * segment : high - hop * segment]
     for hop, ref in zip(signal_hops, signal_refs):
         low = max(-s_left, hop * segment)
         high = min(segment + s_right, (hop + 1) * segment)
-        piece = ref[...].astype(jnp.float32).T
+        piece = ref[:channels, :].astype(jnp.float32).T
         sf[low + s_left : high + s_left, :] = piece[low - hop * segment : high - hop * segment]
     zb[...] = zf[...].astype(jnp.bfloat16)
 
@@ -227,11 +207,35 @@
 
         lax.fori_loop(0, passes, one_pass, 0)
 
+    if atoms_count:
+        for step in range(passes):
+            tap_copy(step).wait()
+    for index in range(atoms_count):
+        row = pl.multiple_of(place_ref[2 + index], BLOCK_ATOMS)
+        lane = lax.broadcasted_iota(jnp.int32, (ROWS, K), 1)
+        renewed = (lane >= row) & (lane < row + BLOCK_ATOMS)
+        columns[...] = jnp.zeros_like(columns)
+
+        def patch(group, carry):
+            part = pl.ds(pl.multiple_of(group * (ROWS * L), LANES), ROWS * L)
+            columns[pl.ds(row, BLOCK_ATOMS), :] = atoms_refs[index][:, part]
+            by_tap(columns, turned)
+            own = pl.ds(pl.multiple_of(group * ROWS, ROWS), ROWS)
+            for tap in range(L):
+                fresh = turned[pl.ds(tap, ROWS, stride=STRIDE), :]
+                kept = taps[tap // ROWS, tap % ROWS, own, :].astype(jnp.float32)
+                taps[tap // ROWS, tap % ROWS, own, :] = jnp.where(renewed, fresh, kept).astype(
+                    jnp.bfloat16
+                )
+            return carry
+
+        lax.fori_loop(0, channels // ROWS, patch, 0)
+
     limit = limit_ref[...]
     for step in range(INNER):
         left, right = reach[step + 1]
         start, count = -left, left + segment + right + L
-        convolve(start, count, step == 0)
+        convolve(start, count, step == 0 and not atoms_count)
         inside = moment(start, count, LANES) < total_time
         for tile in range(tiles):
             column = slice(tile * LANES, (tile + 1) * LANES)
@@ -264,9 +268,12 @@
             jnp.bfloat16
         )
         payload_out[peer, share_rows:, :] = block
-
-
-def run_codes(place, limit, codes, signals, taps, segment, peers):
+    if copies:
+        for step in range(K // BLOCK_ATOMS):
+            dict_copy(step).wait()
+
+
+def run_codes(place, limit, codes, signals, packed, atoms, taps, dictionary, segment, peers):
     code_hops, signal_hops = tuple(codes), tuple(signals)
     channels = taps.shape[1]
     share = channels // peers
@@ -276,18 +283,28 @@
     s_rows = z_rows - L
     longest = s_rows + ROWS
     scored = reach[1][0] + segment + reach[1][1] + ROWS
+    copies = dictionary is not None
     whole = lambda: pl.BlockSpec(memory_space=pltpu.VMEM)
+    remote = lambda: pl.BlockSpec(memory_space=pl.ANY)
+    patching = [
+        pltpu.VMEM((K, ROWS * L), jnp.float32),
+        pltpu.VMEM((ROWS * STRIDE, K), jnp.float32),
+    ]
     return pl.pallas_call(
-        functools.partial(codes_kernel, segment, peers, code_hops, signal_hops),
+        functools.partial(
+            codes_kernel, segment, peers, code_hops, signal_hops, packed, len(atoms), copies
+        ),
         in_specs=[pl.BlockSpec(memory_space=pltpu.SMEM), whole()]
         + [whole() for _ in code_hops + signal_hops]
-        + [pl.BlockSpec(memory_space=pl.ANY)],
-        out_specs=[whole(), whole(), whole()],
+        + [whole() for _ in atoms]
+        + [remote()] * (1 + copies),
+        out_specs=[whole(), whole(), whole()] + [remote()] * copies,
         out_shape=[
             jax.ShapeDtypeStruct((K, segment), jnp.float32),
             jax.ShapeDtypeStruct((channels, segment), jnp.float32),
             jax.ShapeDtypeStruct((peers, share_rows + BLOCK_ATOMS, segment), jnp.bfloat16),
-        ],
+        ]
+        + ([jax.ShapeDtypeStruct(dictionary.shape, jnp.float32)] if copies else []),
         scratch_shapes=[
             pltpu.VMEM((COARSE, ROWS, channels, K), jnp.bfloat16),
             pltpu.VMEM((z_rows, K), jnp.float32),
@@ -300,7 +317,9 @@
             pltpu.VMEM((channels // LANES, s_rows, LANES), jnp.float32),
             pltpu.VMEM((channels + ROWS, segment), jnp.float32),
             pltpu.SemaphoreType.DMA((ROWS // FINE,)),
-        ],
+        ]
+        + ([pltpu.SemaphoreType.DMA((K // BLOCK_ATOMS,))] if copies else [])
+        + (patching if atoms else []),
         compiler_params=pltpu.CompilerParams(vmem_limit_bytes=VMEM_BYTES),
         name="codes",
     )(
@@ -308,7 +327,9 @@
         limit,
         *codes.values(),
         *signals.values(),
+        *atoms,
         taps.reshape(COARSE, ROWS, channels, K),
+        *([dictionary] if copies else []),
     )
 
 
@@ -369,12 +390,36 @@
     )(source[None, :], blocks)
 
 
-def renew_kernel(row_ref, grad_ref, dict_hbm, out_hbm, atoms_ref, old, across, sems):
-    first_row = pl.multiple_of(row_ref[0], BLOCK_ATOMS)
-    peers, _, width = grad_ref.shape
+def gather_pieces(piece):
+    peers = lax.axis_size("tm")
+    held = piece[None]
+    bit = peers // 2
+    while bit > 1:
+        came = lax.ppermute(held, "tm", [(i, i ^ bit) for i in range(peers)])
+        held = jnp.concatenate([held, came], axis=0)
+        bit //= 2
+    return held, lax.ppermute(held, "tm", [(i, i ^ 1) for i in range(peers)])
+
+
+def renew_kernel(place_ref, held_hbm, came_hbm, dict_hbm, out_hbm, atoms_ref, grad, old, across, sems):
+    me = place_ref[0]
+    first_row = pl.multiple_of(place_ref[1], BLOCK_ATOMS)
+    peers, _, width = grad.shape
+    half = peers // 2
     entries = C * L
-    fetch = pltpu.make_async_copy(dict_hbm.at[pl.ds(first_row, BLOCK_ATOMS)], old, sems.at[0])
+    fetch = pltpu.make_async_copy(dict_hbm.at[pl.ds(first_row, BLOCK_ATOMS)], old, sems.at[peers])
     fetch.start()
+    pieces = []
+    for slot in range(half):
+        flips = sum(((slot >> i) & 1) * (half >> i) for i in range(half.bit_length() - 1))
+        for source, extra in ((held_hbm, 0), (came_hbm, 1)):
+            owner = me ^ (flips + extra)
+            pieces.append(
+                pltpu.make_async_copy(source.at[slot], grad.at[owner], sems.at[2 * slot + extra])
+            )
+            pieces[-1].start()
+    for piece in pieces:
+        piece.wait()
     fetch.wait()
 
     def column(peer):
@@ -385,14 +430,14 @@
     def sums(peer, carry):
         square, dot = carry
         before = old[:, column(peer)]
-        return square + before * before, dot + grad_ref[peer].astype(jnp.float32) * before
+        return square + before * before, dot + grad[peer].astype(jnp.float32) * before
 
     square, dot = lax.fori_loop(0, peers, sums, (zeros, zeros))
     mean_sq = jnp.sum(square, axis=1, keepdims=True) / entries + tiny_eps
     along = jnp.sum(dot, axis=1, keepdims=True) / entries / mean_sq
 
     def project(peer, square):
-        value = grad_ref[peer].astype(jnp.float32) - along * old[:, column(peer)]
+        value = grad[peer].astype(jnp.float32) - along * old[:, column(peer)]
         across[:, column(peer)] = value
         return square + value * value
 
@@ -406,34 +451,34 @@
         return carry
 
     lax.fori_loop(0, peers, renew, 0)
-    store = pltpu.make_async_copy(atoms_ref, out_hbm.at[pl.ds(first_row, BLOCK_ATOMS)], sems.at[1])
+    store = pltpu.make_async_copy(atoms_ref, out_hbm.at[pl.ds(first_row, BLOCK_ATOMS)], sems.at[peers])
     store.start()
     store.wait()
 
 
-def renew(first_row, gradient, dictionary):
-    width = dictionary.shape[1]
+def renew(place, held, came, dictionary):
+    channels_taps = dictionary.shape[1]
+    peers = 2 * held.shape[0]
+    width = held.shape[2]
+    remote = pl.BlockSpec(memory_space=pl.ANY)
     return pl.pallas_call(
         renew_kernel,
-        in_specs=[
-            pl.BlockSpec(memory_space=pltpu.SMEM),
-            pl.BlockSpec(memory_space=pltpu.VMEM),
-            pl.BlockSpec(memory_space=pl.ANY),
-        ],
-        out_specs=[pl.BlockSpec(memory_space=pl.ANY), pl.BlockSpec(memory_space=pltpu.VMEM)],
+        in_specs=[pl.BlockSpec(memory_space=pltpu.SMEM), remote, remote, remote],
+        out_specs=[remote, pl.BlockSpec(memory_space=pltpu.VMEM)],
         out_shape=[
             jax.ShapeDtypeStruct(dictionary.shape, jnp.float32),
-            jax.ShapeDtypeStruct((BLOCK_ATOMS, width), jnp.float32),
+            jax.ShapeDtypeStruct((BLOCK_ATOMS, channels_taps), jnp.float32),
         ],
         scratch_shapes=[
-            pltpu.VMEM((BLOCK_ATOMS, width), jnp.float32),
-            pltpu.VMEM((BLOCK_ATOMS, width), jnp.float32),
-            pltpu.SemaphoreType.DMA((2,)),
+            pltpu.VMEM((peers, BLOCK_ATOMS, width), jnp.bfloat16),
+            pltpu.VMEM((BLOCK_ATOMS, channels_taps), jnp.float32),
+            pltpu.VMEM((BLOCK_ATOMS, channels_taps), jnp.float32),
+            pltpu.SemaphoreType.DMA((peers + 1,)),
         ],
-        input_output_aliases={2: 0},
+        input_output_aliases={3: 0},
         compiler_params=pltpu.CompilerParams(vmem_limit_bytes=VMEM_BYTES),
         name="renew",
-    )(first_row, gradient, dictionary)
+    )(place, held, came, dictionary)
 
 
 def whole_channels(signal, codes_init, dictionary_init, threshold, plan):
@@ -445,28 +490,47 @@
     z_left, z_right = reach[0]
     s_left, s_right = z_left - L, z_right
 
-    def window(shard, left, right):
-        hops = range(-hops_of(left, segment), hops_of(right, segment) + 1)
-        return {hop: shard if hop == 0 else shifted(shard, "tm", -hop) for hop in hops}
-
-    base = lax.axis_index("tm") * segment
-    signals = window(signal, s_left, s_right)
+    def hops(left, right):
+        return [h for h in range(-hops_of(left, segment), hops_of(right, segment) + 1) if h]
+
+    index = lax.axis_index("tm").astype(jnp.int32)
+    code_hops, signal_hops = hops(z_left, z_right), hops(s_left, s_right)
+    high = lax.reduce_precision(codes_init, exponent_bits=8, mantissa_bits=7)
+    bundle = jnp.concatenate(
+        [signal, high.astype(jnp.bfloat16), (codes_init - high).astype(jnp.bfloat16)], axis=0
+    )
+    bundles = {hop: shifted(bundle, "tm", -hop) for hop in signal_hops}
+    signals = {0: signal, **bundles}
     code_state = codes_init
     dictionary = dictionary_init
     taps = layout(dictionary, channels)
-    for outer_step in range(OUTER):
-        first_row = plan[outer_step] * BLOCK_ATOMS
-        place = jnp.stack([base, first_row]).astype(jnp.int32)
-        codes = window(code_state, z_left, z_right)
-        code_state, residual, payload = run_codes(
-            place, limit, codes, signals, taps, segment, peers
-        )
+    first_rows = [plan[step].astype(jnp.int32) * BLOCK_ATOMS for step in range(OUTER)]
+    renewed = []
+    for step in range(OUTER):
+        packed = tuple(bundles) if step == 0 else ()
+        codes = {0: code_state}
+        for hop in code_hops:
+            codes[hop] = bundles[hop] if hop in packed else shifted(code_state, "tm", -hop)
+        place = jnp.stack([index * segment, first_rows[step], *first_rows[:step]])
+        results = run_codes(
+            place,
+            limit,
+            codes,
+            signals,
+            packed,
+            renewed,
+            taps,
+            dictionary if step == 0 else None,
+            segment,
+            peers,
+        )
+        code_state, residual, payload = results[:3]
+        if step == 0:
+            dictionary = results[3]
         blocks = lax.all_to_all(payload, "tm", 0, 0, tiled=True)
-        piece = share_gradient(blocks, share)
-        gradient = lax.all_gather(piece, "tm")
-        dictionary, atoms = renew(first_row[None].astype(jnp.int32), gradient, dictionary)
-        if outer_step + 1 < OUTER:
-            taps = patch(first_row[None].astype(jnp.int32), atoms, taps)
+        held, came = gather_pieces(share_gradient(blocks, share))
+        dictionary, atoms = renew(jnp.stack([index, first_rows[step]]), held, came, dictionary)
+        renewed = renewed + [atoms]
     return code_state, dictionary, residual
 
 
@@ -546,6 +610,8 @@
         and channels % LANES == 0
         and channels % peers == 0
         and (channels // peers * L) % LANES == 0
+        and peers > 1
+        and peers & (peers - 1) == 0
     )
     body = whole_channels if fits else split_channels
     return body(signal, codes_init, dictionary_init, threshold, plan)

time: 334 us -> 785 us (2.35)
  Pallas kernels: 132 us -> 660 us
  waiting for transfers between devices: 108 us -> 45.2 us
  between operations: 15.7 us -> 2.43 us
  local copies, waits for them, and re-layouts: 17.2 us -> 6.03 us
    pallas_call x2, Pallas kernels: 56.3 us -> 616 us  [run_codes(): pl.pallas_call(functools.partial(codes_kernel, segment, peers, code_hops,...]
    all_gather x2 -> x0, waiting for transfers between devices: 89.3 us -> none  [whole_channels(): gradient = lax.all_gather(piece, 'tm')]
    ppermute x0 -> x10, waiting for transfers between devices: none -> 35.3 us  [the longest x8 33.9 us: gather_pieces(): came = lax.ppermute(held, 'tm', [(i, i ^ bit) for i in range(peers)])]
    pallas_call x1 -> x0, Pallas kernels: 26.2 us -> none  [patch(): pl.pallas_call(patch_kernel, grid_spec=pltpu.PrefetchScalarGridSpec(num_s...]
    unnamed x37 -> x38, local copies, waits for them, and re-layouts: 16.6 us -> 4.6 us
    ppermute x14 -> x10, starting transfers between devices: 35.6 us -> 26.1 us  [shifted(): return lax.ppermute(shard, axis, pairs)]
    ppermute x14 -> x10, waiting for transfers between devices: 8.35 us -> 0.03 us  [shifted(): return lax.ppermute(shard, axis, pairs)]
  transfers between devices with their start and end apart: 17 -> 21, of which waited for: 4 -> 10; matrix products, arithmetic and copies ran while one was open for 1% -> 1% of each run, Pallas kernels for 18% -> 4%
where the time goes in v2:
time: 785 us; the launch traced here: 784 us
  Pallas kernels  660 us (84%)
  waiting for transfers between devices  45.2 us (6%)
  starting transfers between devices  41 us (5%)
  blocking collectives  19 us (2%)
  other arithmetic  9.6 us (1%)
    pallas_call x2, Pallas kernels, run_codes(): pl.pallas_call(functools.partial(codes_kernel, segment, peers, code_hops,...  616 us
    ppermute x8, waiting for transfers between devices, gather_pieces(): came = lax.ppermute(held, 'tm', [(i, i ^ bit) for i in range(peers)])  33.9 us
    ppermute x10, starting transfers between devices, shifted(): return lax.ppermute(shard, axis, pairs)  26.1 us
    pallas_call x1, Pallas kernels, layout(): pl.pallas_call(layout_kernel, grid=(steps,), in_specs=[pl.BlockSpec((K, R...  21.2 us
    all_to_all x1, blocking collectives, whole_channels(): blocks = lax.all_to_all(payload, 'tm', 0, 0, tiled=True)  19 us
  transfers between devices with their start and end apart: 21, of which 10 were waited for; matrix products, arithmetic and copies ran while one was open for 1% of the time, Pallas kernels for 4%

profile of v2, /device:TPU:0, one launch (start us, length us, event | category | flops | bytes accessed | tf_op | source)
XLA Modules:
  0.0 783.6 jit_solution(8571952544735106858)
XLA Ops:
  2.4 4.9 collective-permute-start.1
  7.3 1.5 collective-permute-start.2
  11.3 6.5 collective-permute-start
  19.3 21.2 %layout.1 = bf16[96,384,128]{2,1,0:T(8,128)(2,1)} custom-call(f32[128,36864]{1,0:T(8,128)} %refs_14_.1), custom_call_target="tpu_custom_call" | custom-call | tf_op jit(solution)/shard_map/layout/pallas_call | solution.py:55
  42.5 575.2 %codes.2 = (f32[128,128]{1,0:T(8,128)}, f32[384,128]{1,0:T(8,128)}, bf16[32,32,128]{2,1,0:T(8,128)(2,1)}, f32[128,36864]{1,0:T(8,128)}) custom-call(s32[2]{0:T(128)} %pad_add_fusion.1.refs_0_, f32[1,128]{1,0:T(1,128)} %bitcast.18, f32[128,128]{1,0:T(8,128)} %refs_2_.1, f32[128,128]{1,0:T(8,128)} %copy-done.14, bf16[640,128]{1,0:T(8,128)(2,1)} %copy-done, ...), custom_call_target="tpu_custom_call" | custom-call | tf_op jit(solution)/shard_map/codes/pallas_call | solution.py:293
  617.8 7.2 all-to-all-start
  625.6 9.9 %all-to-all-done.blocks_ref = bf16[32,32,128]{2,1,0:T(8,128)(2,1)S(1)} async-done(((bf16[32,32,128]{2,1,0:T(8,128)(2,1)}), bf16[32,32,128]{2,1,0:T(8,128)(2,1)S(1)}, u32[]{:S(2)}, u32[]{:S(2)}) %all-to-all-start) | async-done | bytes 262176 | tf_op jit(solution)/shard_map/all_to_all | solution.py:530
  636.3 3.8 gradient.2
  640.4 4.8 collective-permute-done.10
  647.8 2.6 collective-permute-done.11
  652.5 3.9 collective-permute-done.12
  658.3 5.7 collective-permute-done.13
  665.3 3.0 collective-permute-start.5
  668.4 3.6 collective-permute-start.6
  674.6 1.5 collective-permute-start.9
  676.8 7.6 renew.2
  685.1 41.0 %codes.3 = (f32[128,128]{1,0:T(8,128)}, f32[384,128]{1,0:T(8,128)}, bf16[32,32,128]{2,1,0:T(8,128)(2,1)}) custom-call(s32[3]{0:T(128)} %pad_add_fusion.refs_0_, f32[1,128]{1,0:T(1,128)} %bitcast.19, f32[128,128]{1,0:T(8,128)} %get-tuple-element.12.refs_2_, f32[128,128]{1,0:T(8,128)} %copy-done.9, f32[128,128]{1,0:T(8,128)} %copy-done.10, ...), custom_call_target="tpu_custom_call" | custom-call | tf_op jit(solution)/shard_map/codes/pallas_call | solution.py:293
  726.1 19.0 %all_to_all.10.blocks_ref = bf16[32,32,128]{2,1,0:T(8,128)(2,1)} all-to-all(bf16[32,32,128]{2,1,0:T(8,128)(2,1)} %get-tuple-element.17), channel_id=1, replica_groups=mesh['tm'=32,'chan'=1] {'tm'}, dimensions={0} | all-to-all | bytes 524288 | tf_op jit(solution)/shard_map/all_to_all | solution.py:530
  745.1 3.8 gradient.3
  749.3 4.8 collective-permute-done.15
  756.6 2.6 collective-permute-done.16
  761.4 3.9 collective-permute-done.17
  767.2 5.7 collective-permute-done.18
  775.8 7.6 renew.3
  (80 shorter events, 29.9 us)
Async XLA Ops:
  2.4 39.3 %collective-permute-start.1 = (bf16[640,128]{1,0:T(8,128)(2,1)S(1)}, bf16[640,128]{1,0:T(8,128)(2,1)S(1)}, u32[]{:S(2)}, u32[]{:S(2)}) collective-permute-start(bf16[640,128]{1,0:T(8,128)(2,1)S(1)} %pad_maximum_fusion.2), channel_id=1, source_target_pairs={{0,2},{1,3},{2,4},{3,5},{4,6},{5,7},{6,8},{7,9},{8,10},{9,11},{10,... | collective-permute-start | bytes 491528 | tf_op jit(solution)/shard_map/ppermute | solution.py:35
  7.3 34.5 %collective-permute-start.2 = (bf16[640,128]{1,0:T(8,128)(2,1)S(1)}, bf16[640,128]{1,0:T(8,128)(2,1)S(1)}, u32[]{:S(2)}, u32[]{:S(2)}) collective-permute-start(bf16[640,128]{1,0:T(8,128)(2,1)S(1)} %pad_maximum_fusion.2), channel_id=1, source_target_pairs={{0,1},{1,2},{2,3},{3,4},{4,5},{5,6},{6,7},{7,8},{8,9},{9,10},{10,1... | collective-permute-start | bytes 491528 | tf_op jit(solution)/shard_map/ppermute | solution.py:35
  8.7 33.0 %collective-permute-start.3 = (bf16[640,128]{1,0:T(8,128)(2,1)S(1)}, bf16[640,128]{1,0:T(8,128)(2,1)S(1)}, u32[]{:S(2)}, u32[]{:S(2)}) collective-permute-start(bf16[640,128]{1,0:T(8,128)(2,1)S(1)} %pad_maximum_fusion.2), channel_id=1, source_target_pairs={{1,0},{2,1},{3,2},{4,3},{5,4},{6,5},{7,6},{8,7},{9,8},{10,9},{11,1... | collective-permute-start | bytes 491528 | tf_op jit(solution)/shard_map/ppermute | solution.py:35
  10.0 31.7 %collective-permute-start.4 = (bf16[640,128]{1,0:T(8,128)(2,1)S(1)}, bf16[640,128]{1,0:T(8,128)(2,1)S(1)}, u32[]{:S(2)}, u32[]{:S(2)}) collective-permute-start(bf16[640,128]{1,0:T(8,128)(2,1)S(1)} %pad_maximum_fusion.2), channel_id=1, source_target_pairs={{2,0},{3,1},{4,2},{5,3},{6,4},{7,5},{8,6},{9,7},{10,8},{11,9},{12,... | collective-permute-start | bytes 491528 | tf_op jit(solution)/shard_map/ppermute | solution.py:35
  11.3 30.4 %collective-permute-start = (f32[128,128]{1,0:T(8,128)}, f32[128,128]{1,0:T(8,128)S(1)}, u32[]{:S(2)}, u32[]{:S(2)}) collective-permute-start(f32[128,128]{1,0:T(8,128)} %refs_2_.1), channel_id=1, source_target_pairs={{0,3},{1,4},{2,5},{3,6},{4,7},{5,8},{6,9},{7,10},{8,11},{9,12},{10... | collective-permute-start | bytes 196616 | tf_op jit(solution)/shard_map/ppermute | solution.py:35
  617.8 17.8 %all-to-all-start = ((bf16[32,32,128]{2,1,0:T(8,128)(2,1)}), bf16[32,32,128]{2,1,0:T(8,128)(2,1)S(1)}, u32[]{:S(2)}, u32[]{:S(2)}) async-start(bf16[32,32,128]{2,1,0:T(8,128)(2,1)} %get-tuple-element.13), calls=%async_computation | async-start | bytes 524288 | tf_op jit(solution)/shard_map/all_to_all | solution.py:530
  640.1 5.1 collective-permute-start.10
  646.0 4.4 collective-permute-start.11
  651.2 5.2 collective-permute-start.12
  657.2 6.8 collective-permute-start.13
  664.0 12.7 %copy-start.5 = (bf16[16,16,1152]{2,1,0:T(8,128)(2,1)}, bf16[16,16,1152]{2,1,0:T(8,128)(2,1)S(1)}, u32[]{:S(2)}) copy-start(bf16[16,16,1152]{2,1,0:T(8,128)(2,1)S(1)} %constant_dynamic-update-slice_fusion.held_hbm) | copy-start | bytes 1769476
  664.0 10.5 %collective-permute-start.14 = (bf16[16,16,1152]{2,1,0:T(8,128)(2,1)S(1)}, bf16[16,16,1152]{2,1,0:T(8,128)(2,1)S(1)}, u32[]{:S(2)}, u32[]{:S(2)}) collective-permute-start(bf16[16,16,1152]{2,1,0:T(8,128)(2,1)S(1)} %constant_dynamic-update-slice_fusion.held_hbm), channel_id=1, source_target_pairs={{0,1},{1,0},{2,3},{3,2},{4,5},{5,4},{6,7},{7,6},{8,9},{9,8},{10,11... | collective-permute-start | bytes 1769480 | tf_op jit(solution)/shard_map/ppermute | solution.py:401
  665.3 19.0 %collective-permute-start.5 = (f32[128,128]{1,0:T(8,128)}, f32[128,128]{1,0:T(8,128)S(1)}, u32[]{:S(2)}, u32[]{:S(2)}) collective-permute-start(f32[128,128]{1,0:T(8,128)} %get-tuple-element.12.refs_2_), channel_id=1, source_target_pairs={{0,3},{1,4},{2,5},{3,6},{4,7},{5,8},{6,9},{7,10},{8,11},{9,12},{10... | collective-permute-start | bytes 196616 | tf_op jit(solution)/shard_map/ppermute | solution.py:35
  668.4 16.0 %collective-permute-start.6 = (f32[128,128]{1,0:T(8,128)}, f32[128,128]{1,0:T(8,128)S(1)}, u32[]{:S(2)}, u32[]{:S(2)}) collective-permute-start(f32[128,128]{1,0:T(8,128)} %get-tuple-element.12.refs_2_), channel_id=1, source_target_pairs={{0,2},{1,3},{2,4},{3,5},{4,6},{5,7},{6,8},{7,9},{8,10},{9,11},{10,... | collective-permute-start | bytes 196616 | tf_op jit(solution)/shard_map/ppermute | solution.py:35
  672.0 12.4 %collective-permute-start.7 = (f32[128,128]{1,0:T(8,128)}, f32[128,128]{1,0:T(8,128)S(1)}, u32[]{:S(2)}, u32[]{:S(2)}) collective-permute-start(f32[128,128]{1,0:T(8,128)} %get-tuple-element.12.refs_2_), channel_id=1, source_target_pairs={{0,1},{1,2},{2,3},{3,4},{4,5},{5,6},{6,7},{7,8},{8,9},{9,10},{10,1... | collective-permute-start | bytes 196616 | tf_op jit(solution)/shard_map/ppermute | solution.py:35
  673.3 11.1 %collective-permute-start.8 = (f32[128,128]{1,0:T(8,128)}, f32[128,128]{1,0:T(8,128)S(1)}, u32[]{:S(2)}, u32[]{:S(2)}) collective-permute-start(f32[128,128]{1,0:T(8,128)} %get-tuple-element.12.refs_2_), channel_id=1, source_target_pairs={{1,0},{2,1},{3,2},{4,3},{5,4},{6,5},{7,6},{8,7},{9,8},{10,9},{11,1... | collective-permute-start | bytes 196616 | tf_op jit(solution)/shard_map/ppermute | solution.py:35
  674.6 2.2 copy-start.7
  674.6 9.8 %collective-permute-start.9 = (f32[128,128]{1,0:T(8,128)}, f32[128,128]{1,0:T(8,128)S(1)}, u32[]{:S(2)}, u32[]{:S(2)}) collective-permute-start(f32[128,128]{1,0:T(8,128)} %get-tuple-element.12.refs_2_), channel_id=1, source_target_pairs={{2,0},{3,1},{4,2},{5,3},{6,4},{7,5},{8,6},{9,7},{10,8},{11,9},{12,... | collective-permute-start | bytes 196616 | tf_op jit(solution)/shard_map/ppermute | solution.py:35
  749.0 5.1 collective-permute-start.15
  754.8 4.4 collective-permute-start.16
  760.0 5.2 collective-permute-start.17
  766.1 6.8 collective-permute-start.18
  772.9 2.1 copy-start.6
  772.9 2.1 collective-permute-start.19
  (12 other events, 8.2 us)

commit v3 on v0

--- a/solution.py
+++ b/solution.py
@@ -1,6 +1,10 @@
+import functools
+
 import jax
 import jax.numpy as jnp
 from jax import lax
+from jax.experimental import pallas as pl
+from jax.experimental.pallas import tpu as pltpu
 from jax.sharding import PartitionSpec as P
 
 C = 384
@@ -10,10 +14,19 @@
 INNER = 2
 OUTER = 2
 
-
 code_rate = 0.3
 move_rate = 0.5
 tiny_eps = 1e-06
+
+ROWS = 16
+COARSE = L // ROWS
+STRIDE = L + 1
+FINE = 4
+LANES = 128
+VMEM_BYTES = 56 * 1024 * 1024
+
+NN = (((1,), (0,)), ((), ()))
+NT = (((1,), (1,)), ((), ()))
 
 
 def shifted(shard, axis, by):
@@ -22,13 +35,496 @@
     return lax.ppermute(shard, axis, pairs)
 
 
+def turn(columns_ref, start, turned_ref):
+    for quad in range(ROWS // 4):
+        part = pl.ds(start + quad * 4 * L, 4 * L)
+        turned = columns_ref[:, part].T
+        for q in range(4):
+            row = (quad * 4 + q) * STRIDE
+            turned_ref[row : row + L, :] = turned[q * L : (q + 1) * L]
+
+
+def layout_kernel(dict_ref, taps_ref, copy_hbm, even, odd, sem):
+    width = dict_ref.shape[1]
+    column = pl.multiple_of(pl.program_id(0) * width, LANES)
+    copy = pltpu.make_async_copy(dict_ref, copy_hbm.at[:, pl.ds(column, width)], sem)
+    copy.start()
+    groups = width // (ROWS * L)
+    turn(dict_ref, 0, even)
+    for group in range(groups):
+        now, later = (even, odd) if group % 2 == 0 else (odd, even)
+        if group + 1 < groups:
+            turn(dict_ref, (group + 1) * ROWS * L, later)
+        for tap in range(L):
+            taps_ref[tap, group * ROWS : (group + 1) * ROWS, :] = now[
+                pl.ds(tap, ROWS, stride=STRIDE), :
+            ].astype(jnp.bfloat16)
+    copy.wait()
+
+
+def layout(dictionary, channels):
+    block = 4 * ROWS
+    return pl.pallas_call(
+        layout_kernel,
+        grid=(channels // block,),
+        in_specs=[pl.BlockSpec((K, block * L), lambda i: (0, i))],
+        out_specs=[
+            pl.BlockSpec((L, block, K), lambda i: (0, i, 0)),
+            pl.BlockSpec(memory_space=pl.ANY),
+        ],
+        out_shape=[
+            jax.ShapeDtypeStruct((L, channels, K), jnp.bfloat16),
+            jax.ShapeDtypeStruct(dictionary.shape, jnp.float32),
+        ],
+        scratch_shapes=[
+            pltpu.VMEM((ROWS * STRIDE, K), jnp.float32),
+            pltpu.VMEM((ROWS * STRIDE, K), jnp.float32),
+            pltpu.SemaphoreType.DMA,
+        ],
+        compiler_params=pltpu.CompilerParams(vmem_limit_bytes=VMEM_BYTES),
+        name="layout",
+    )(dictionary)
+
+
+def fetch_taps(taps_hbm, taps, sems):
+    copies = [
+        pltpu.make_async_copy(
+            taps_hbm.at[:, pl.ds(lag, FINE)], taps.at[:, pl.ds(lag, FINE)], sems.at[lag // FINE]
+        )
+        for lag in range(0, ROWS, FINE)
+    ]
+    for copy in copies:
+        copy.start()
+    return [copy.wait for copy in copies]
+
+
+def convolve(zb, begin, count, taps, zz, fine, acc, waits):
+    channels = taps.shape[2]
+    tiles = channels // LANES
+    rows = count + ROWS
+    for coarse in range(COARSE):
+        first = begin - ROWS - ROWS * coarse
+        zz[:rows, coarse * K : (coarse + 1) * K] = zb[first : first + rows, :]
+    for lag in range(0, ROWS, FINE):
+        if waits:
+            waits[lag // FINE]()
+        slot = lag // FINE % 2 * FINE
+        for pair in range(0, FINE, 2):
+            weights = jnp.concatenate(
+                [
+                    jnp.concatenate([taps[m, lag + pair + j] for m in range(COARSE)], axis=1)
+                    for j in range(2)
+                ],
+                axis=0,
+            )
+            product = lax.dot_general(zz[:rows, :], weights, NT, preferred_element_type=jnp.float32)
+            for j in range(2):
+                for tile in range(tiles):
+                    column = j * channels + tile * LANES
+                    fine[slot + pair + j, tile, :rows, :] = product[:, column : column + LANES]
+        for tile in range(tiles):
+            total = None if lag == 0 else acc[tile, :count, :]
+            for j in range(FINE):
+                first = ROWS - lag - j
+                part = fine[slot + j, tile, first : first + count, :]
+                total = part if total is None else total + part
+            acc[tile, :count, :] = total
+
+
+def correlate(rb, count, taps, rr, fine, acc):
+    channels = taps.shape[2]
+    rows = count + ROWS
+    for coarse in range(COARSE):
+        first = ROWS * coarse
+        rr[:rows, coarse * channels : (coarse + 1) * channels] = rb[first : first + rows, :]
+    for lag in range(0, ROWS, FINE):
+        slot = lag // FINE % 2 * FINE
+        for pair in range(0, FINE, 2):
+            weights = jnp.concatenate(
+                [
+                    jnp.concatenate([taps[m, lag + pair + j] for m in range(COARSE)], axis=0)
+                    for j in range(2)
+                ],
+                axis=1,
+            )
+            product = lax.dot_general(rr[:rows, :], weights, NN, preferred_element_type=jnp.float32)
+            for j in range(2):
+                fine[slot + pair + j, 0, :rows, :] = product[:, j * K : (j + 1) * K]
+        total = None if lag == 0 else acc[0, :count, :]
+        for j in range(FINE):
+            part = fine[slot + j, 0, lag + j : lag + j + count, :]
+            total = part if total is None else total + part
+        acc[0, :count, :] = total
+
+
+def patch_taps(row, atoms_ref, taps, columns, even, odd):
+    channels = taps.shape[2]
+    lane = lax.broadcasted_iota(jnp.int32, (ROWS, K), 1)
+    renewed = (lane >= row) & (lane < row + BLOCK_ATOMS)
+    columns[...] = jnp.zeros_like(columns)
+
+    def patch(step, carry):
+        width = 2 * ROWS * L
+        part = pl.ds(pl.multiple_of(step * width, LANES), width)
+        columns[pl.ds(row, BLOCK_ATOMS), :] = atoms_ref[:, part]
+        turn(columns, 0, even)
+        turn(columns, ROWS * L, odd)
+        for half, turned in ((0, even), (1, odd)):
+            own = pl.ds(pl.multiple_of((2 * step + half) * ROWS, ROWS), ROWS)
+            for tap in range(L):
+                fresh = turned[pl.ds(tap, ROWS, stride=STRIDE), :]
+                kept = taps[tap // ROWS, tap % ROWS, own, :].astype(jnp.float32)
+                taps[tap // ROWS, tap % ROWS, own, :] = jnp.where(renewed, fresh, kept).astype(
+                    jnp.bfloat16
+                )
+        return carry
+
+    lax.fori_loop(0, channels // (2 * ROWS), patch, 0)
+
+
+def put_codes(zb, own, left, right):
+    segment = own.shape[1]
+    zb[:L, :] = left[...].astype(jnp.float32).T[segment - L :].astype(jnp.bfloat16)
+    zb[L : L + segment, :] = own[...].T.astype(jnp.bfloat16)
+    if right is not None:
+        zb[L + segment :, :] = right[:K, :].astype(jnp.float32).T[:L].astype(jnp.bfloat16)
+
+
+def iterate_kernel(total_time, patching, place_ref, limit_ref, *refs):
+    code_ref, left_ref, right_ref, signal_ref, next_ref = refs[:5]
+    refs = refs[5:]
+    if patching:
+        atoms_ref, refs = refs[0], refs[1:]
+    taps_hbm, state_out, low_out = refs[:3]
+    refs = refs[3:]
+    if patching:
+        taps_out, refs = refs[0], refs[1:]
+    taps, zb, rb, zz, rr, fine, acc, sems = refs[:8]
+    channels, segment = signal_ref.shape
+    tiles = channels // LANES
+    scale = (C * L) ** (-0.5)
+    waits = fetch_taps(taps_hbm, taps, sems)
+    put_codes(zb, code_ref, left_ref, right_ref)
+    if patching:
+        columns, even, odd, out_sem = refs[8:]
+        for wait in waits:
+            wait()
+        waits = None
+        patch_taps(pl.multiple_of(place_ref[1], BLOCK_ATOMS), atoms_ref, taps, columns, even, odd)
+        store = pltpu.make_async_copy(taps, taps_out, out_sem)
+        store.start()
+    reach = segment + L
+    convolve(zb, L, reach, taps, zz, fine, acc, waits)
+    moment = place_ref[0] + lax.broadcasted_iota(jnp.int32, (reach, LANES), 0)
+    inside = moment < total_time
+    for tile in range(tiles):
+        column = slice(tile * LANES, (tile + 1) * LANES)
+        first = signal_ref[column, :].astype(jnp.float32).T
+        second = next_ref[K + tile * LANES : K + (tile + 1) * LANES, :].astype(jnp.float32).T[:L]
+        value = jnp.concatenate([first, second], axis=0) - scale * acc[tile, :reach, :]
+        rb[:, column] = jnp.where(inside, value, 0.0).astype(jnp.bfloat16)
+    correlate(rb, segment, taps, rr, fine, acc)
+    limit = limit_ref[...]
+    stepped = code_ref[...].T + code_rate * (scale * acc[0, :segment, :])
+    state = (stepped - jnp.clip(stepped, -limit, limit)).T
+    state_out[...] = state
+    low_out[...] = state.astype(jnp.bfloat16)
+    if patching:
+        store.wait()
+
+
+def iterate(place, limit, code, left, right, signal, following, taps, atoms, peers):
+    channels, segment = signal.shape
+    patching = atoms is not None
+    reach = segment + L
+    whole = pl.BlockSpec(memory_space=pltpu.VMEM)
+    remote = pl.BlockSpec(memory_space=pl.ANY)
+    cube = (COARSE, ROWS, channels, K)
+    return pl.pallas_call(
+        functools.partial(iterate_kernel, peers * segment, patching),
+        in_specs=[pl.BlockSpec(memory_space=pltpu.SMEM)] + [whole] * (6 + patching) + [remote],
+        out_specs=[whole, whole] + [remote] * patching,
+        out_shape=[
+            jax.ShapeDtypeStruct((K, segment), jnp.float32),
+            jax.ShapeDtypeStruct((K, segment), jnp.bfloat16),
+        ]
+        + [jax.ShapeDtypeStruct(cube, jnp.bfloat16)] * patching,
+        scratch_shapes=[
+            pltpu.VMEM(cube, jnp.bfloat16),
+            pltpu.VMEM((L + reach, K), jnp.bfloat16),
+            pltpu.VMEM((reach, channels), jnp.bfloat16),
+            pltpu.VMEM((reach + ROWS, COARSE * K), jnp.bfloat16),
+            pltpu.VMEM((segment + ROWS, COARSE * channels), jnp.bfloat16),
+            pltpu.VMEM((2 * FINE, channels // LANES, reach + ROWS, LANES), jnp.float32),
+            pltpu.VMEM((channels // LANES, reach, LANES), jnp.float32),
+            pltpu.SemaphoreType.DMA((ROWS // FINE,)),
+        ]
+        + [
+            pltpu.VMEM((K, 2 * ROWS * L), jnp.float32),
+            pltpu.VMEM((ROWS * STRIDE, K), jnp.float32),
+            pltpu.VMEM((ROWS * STRIDE, K), jnp.float32),
+            pltpu.SemaphoreType.DMA,
+        ]
+        * patching,
+        compiler_params=pltpu.CompilerParams(vmem_limit_bytes=VMEM_BYTES),
+        name="iterate",
+    )(place, limit, code, left, right, signal, following, *([atoms] * patching), taps)
+
+
+def finish_kernel(
+    peers, place_ref, code_ref, left_ref, signal_ref, taps_hbm, resid_out, payload_out, taps, zb, zz, fine, acc, tall, sems
+):
+    channels, segment = signal_ref.shape
+    scale = (C * L) ** (-0.5)
+    waits = fetch_taps(taps_hbm, taps, sems)
+    put_codes(zb, code_ref, left_ref, None)
+    convolve(zb, L, segment, taps, zz, fine, acc, waits)
+    for tile in range(channels // LANES):
+        column = slice(tile * LANES, (tile + 1) * LANES)
+        value = signal_ref[column, :].astype(jnp.float32) - scale * acc[tile, :segment, :].T
+        resid_out[column, :] = value
+        tall[column, :] = value
+    row = pl.multiple_of(place_ref[0], BLOCK_ATOMS)
+    block = code_ref[pl.ds(row, BLOCK_ATOMS), :].astype(jnp.bfloat16)
+    share = channels // peers
+    share_rows = payload_out.shape[1] - BLOCK_ATOMS
+    tall[channels:, :] = jnp.zeros((tall.shape[0] - channels, segment), jnp.float32)
+    for peer in range(peers):
+        part = tall[peer * share : peer * share + share_rows, :]
+        payload_out[peer, :share_rows, :] = part.astype(jnp.bfloat16)
+        payload_out[peer, share_rows:, :] = block
+
+
+def finish(place, code, left, signal, taps, peers):
+    channels, segment = signal.shape
+    share = channels // peers
+    share_rows = -(-share // ROWS) * ROWS
+    whole = pl.BlockSpec(memory_space=pltpu.VMEM)
+    return pl.pallas_call(
+        functools.partial(finish_kernel, peers),
+        in_specs=[pl.BlockSpec(memory_space=pltpu.SMEM), whole, whole, whole]
+        + [pl.BlockSpec(memory_space=pl.ANY)],
+        out_specs=[whole, whole],
+        out_shape=[
+            jax.ShapeDtypeStruct((channels, segment), jnp.float32),
+            jax.ShapeDtypeStruct((peers, share_rows + BLOCK_ATOMS, segment), jnp.bfloat16),
+        ],
+        scratch_shapes=[
+            pltpu.VMEM((COARSE, ROWS, channels, K), jnp.bfloat16),
+            pltpu.VMEM((L + segment, K), jnp.bfloat16),
+            pltpu.VMEM((segment + ROWS, COARSE * K), jnp.bfloat16),
+            pltpu.VMEM((2 * FINE, channels // LANES, segment + ROWS, LANES), jnp.float32),
+            pltpu.VMEM((channels // LANES, segment, LANES), jnp.float32),
+            pltpu.VMEM((channels + ROWS, segment), jnp.float32),
+            pltpu.SemaphoreType.DMA((ROWS // FINE,)),
+        ],
+        compiler_params=pltpu.CompilerParams(vmem_limit_bytes=VMEM_BYTES),
+        name="finish",
+    )(place, code, left, signal, taps)
+
+
+def gradient_kernel(share, source_ref, blocks_ref, out_ref, rf, zf, rr, zz):
+    peers, rows, segment = blocks_ref.shape
+    share_rows = rows - BLOCK_ATOMS
+    span = peers * segment
+    rf[:, span:] = jnp.zeros((share_rows, LANES), jnp.float32)
+    zf[:, :LANES] = jnp.zeros((BLOCK_ATOMS, LANES), jnp.float32)
+    for peer in range(peers):
+        column = peer * segment
+        rf[:, column : column + segment] = blocks_ref[peer, :share_rows, :].astype(jnp.float32)
+        zf[:, LANES + column : LANES + column + segment] = blocks_ref[peer, share_rows:, :].astype(
+            jnp.float32
+        )
+    for lag in range(ROWS):
+        rr[lag * share_rows : (lag + 1) * share_rows, :] = rf[:, lag : lag + span].astype(jnp.bfloat16)
+    for coarse in range(COARSE):
+        begin = LANES - ROWS * coarse
+        zz[coarse * BLOCK_ATOMS : (coarse + 1) * BLOCK_ATOMS, :] = zf[:, begin : begin + span].astype(
+            jnp.bfloat16
+        )
+    lagged = lax.dot_general(zz[...], rr[...], NT, preferred_element_type=jnp.float32)
+    lagged = lagged.astype(jnp.bfloat16)
+    wide = ROWS * share_rows
+    entries = share * L
+    total = jnp.zeros((BLOCK_ATOMS, entries), jnp.float32)
+    for coarse in range(COARSE):
+        row = lax.broadcasted_iota(jnp.int32, (wide, entries), 0) + coarse * wide
+        chosen = (row == source_ref[...]).astype(jnp.float32).astype(jnp.bfloat16)
+        total += lax.dot_general(
+            lagged[coarse * BLOCK_ATOMS : (coarse + 1) * BLOCK_ATOMS, :],
+            chosen,
+            NN,
+            preferred_element_type=jnp.float32,
+        )
+    out_ref[...] = total.astype(jnp.bfloat16)
+
+
+def share_gradient(blocks, share):
+    peers, rows, segment = blocks.shape
+    share_rows = rows - BLOCK_ATOMS
+    span = peers * segment
+    entry = jnp.arange(share * L, dtype=jnp.int32)
+    channel, tap = entry // L, entry % L
+    source = (tap // ROWS) * (ROWS * share_rows) + (tap % ROWS) * share_rows + channel
+    return pl.pallas_call(
+        functools.partial(gradient_kernel, share),
+        out_shape=jax.ShapeDtypeStruct((BLOCK_ATOMS, share * L), jnp.bfloat16),
+        scratch_shapes=[
+            pltpu.VMEM((share_rows, span + LANES), jnp.float32),
+            pltpu.VMEM((BLOCK_ATOMS, LANES + span), jnp.float32),
+            pltpu.VMEM((ROWS * share_rows, span), jnp.bfloat16),
+            pltpu.VMEM((COARSE * BLOCK_ATOMS, span), jnp.bfloat16),
+        ],
+        compiler_params=pltpu.CompilerParams(vmem_limit_bytes=VMEM_BYTES),
+        name="gradient",
+    )(source[None, :], blocks)
+
+
+def gather_steps(peers):
+    bits = [1 << i for i in range(peers.bit_length() - 2, 0, -1)]
+    steps = []
+    for first in range(0, len(bits), 2):
+        pair = bits[first : first + 2]
+        steps.append(pair + [sum(pair)] if len(pair) == 2 else pair)
+    return steps
+
+
+def gather_slots(peers):
+    flips = [0]
+    for masks in gather_steps(peers):
+        flips = [f ^ m for m in [0] + masks for f in flips]
+    return flips
+
+
+def gather_pieces(piece):
+    peers = lax.axis_size("tm")
+
+    def exchanged(shard, mask):
+        return lax.ppermute(shard, "tm", [(i, i ^ mask) for i in range(peers)])
+
+    held = piece[None]
+    for masks in gather_steps(peers):
+        held = jnp.concatenate([held] + [exchanged(held, mask) for mask in masks], axis=0)
+    return held, exchanged(held, 1)
+
+
+def renew_kernel(place_ref, held_hbm, came_hbm, dict_hbm, out_hbm, atoms_ref, grad, old, across, sems):
+    me = place_ref[0]
+    first_row = pl.multiple_of(place_ref[1], BLOCK_ATOMS)
+    peers, _, width = grad.shape
+    entries = C * L
+    fetch = pltpu.make_async_copy(dict_hbm.at[pl.ds(first_row, BLOCK_ATOMS)], old, sems.at[peers])
+    fetch.start()
+    pieces = []
+    for slot, flips in enumerate(gather_slots(peers)):
+        for source, extra in ((held_hbm, 0), (came_hbm, 1)):
+            owner = me ^ (flips + extra)
+            pieces.append(
+                pltpu.make_async_copy(source.at[slot], grad.at[owner], sems.at[2 * slot + extra])
+            )
+            pieces[-1].start()
+    for piece in pieces:
+        piece.wait()
+    fetch.wait()
+
+    def column(peer):
+        return pl.ds(pl.multiple_of(peer * width, LANES), width)
+
+    zeros = jnp.zeros((BLOCK_ATOMS, width), jnp.float32)
+
+    def sums(peer, carry):
+        square, dot = carry
+        before = old[:, column(peer)]
+        return square + before * before, dot + grad[peer].astype(jnp.float32) * before
+
+    square, dot = lax.fori_loop(0, peers, sums, (zeros, zeros))
+    mean_sq = jnp.sum(square, axis=1, keepdims=True) / entries + tiny_eps
+    along = jnp.sum(dot, axis=1, keepdims=True) / entries / mean_sq
+
+    def project(peer, square):
+        value = grad[peer].astype(jnp.float32) - along * old[:, column(peer)]
+        across[:, column(peer)] = value
+        return square + value * value
+
+    square = lax.fori_loop(0, peers, project, zeros)
+    spread = jnp.sum(square, axis=1, keepdims=True) / entries + tiny_eps
+    step = move_rate / jnp.sqrt(spread)
+    norm = 1.0 / jnp.sqrt(mean_sq + 0.25)
+
+    def renew(peer, carry):
+        atoms_ref[:, column(peer)] = (old[:, column(peer)] + step * across[:, column(peer)]) * norm
+        return carry
+
+    lax.fori_loop(0, peers, renew, 0)
+    store = pltpu.make_async_copy(atoms_ref, out_hbm.at[pl.ds(first_row, BLOCK_ATOMS)], sems.at[peers])
+    store.start()
+    store.wait()
+
+
+def renew(place, held, came, dictionary):
+    channels_taps = dictionary.shape[1]
+    peers = 2 * held.shape[0]
+    width = held.shape[2]
+    remote = pl.BlockSpec(memory_space=pl.ANY)
+    return pl.pallas_call(
+        renew_kernel,
+        in_specs=[pl.BlockSpec(memory_space=pltpu.SMEM), remote, remote, remote],
+        out_specs=[remote, pl.BlockSpec(memory_space=pltpu.VMEM)],
+        out_shape=[
+            jax.ShapeDtypeStruct(dictionary.shape, jnp.float32),
+            jax.ShapeDtypeStruct((BLOCK_ATOMS, channels_taps), jnp.float32),
+        ],
+        scratch_shapes=[
+            pltpu.VMEM((peers, BLOCK_ATOMS, width), jnp.bfloat16),
+            pltpu.VMEM((BLOCK_ATOMS, channels_taps), jnp.float32),
+            pltpu.VMEM((BLOCK_ATOMS, channels_taps), jnp.float32),
+            pltpu.SemaphoreType.DMA((peers + 1,)),
+        ],
+        input_output_aliases={3: 0},
+        compiler_params=pltpu.CompilerParams(vmem_limit_bytes=VMEM_BYTES),
+        name="renew",
+    )(place, held, came, dictionary)
+
+
+def whole_channels(signal, codes_init, dictionary_init, threshold, plan):
+    channels, segment = signal.shape
+    peers = lax.axis_size("tm")
+    limit = threshold[None, :]
+    index = lax.axis_index("tm").astype(jnp.int32)
+    first_rows = [plan[step].astype(jnp.int32) * BLOCK_ATOMS for step in range(OUTER)]
+    low = codes_init.astype(jnp.bfloat16)
+    following = shifted(jnp.concatenate([low, signal], axis=0), "tm", -1)
+    left, right = shifted(low, "tm", 1), following
+    taps, dictionary = layout(dictionary_init, channels)
+    taps = taps.reshape(COARSE, ROWS, channels, K)
+    code_state, atoms = codes_init, None
+    for step in range(OUTER):
+        place = jnp.stack([index * segment, first_rows[step - 1] if step else first_rows[0]])
+        for inner in range(INNER):
+            fresh = atoms if inner == 0 else None
+            results = iterate(
+                place, limit, code_state, left, right, signal, following, taps, fresh, peers
+            )
+            code_state, low = results[:2]
+            if fresh is not None:
+                taps = results[2]
+            left = shifted(low, "tm", 1)
+            if step + 1 < OUTER or inner + 1 < INNER:
+                right = shifted(low, "tm", -1)
+        residual, payload = finish(first_rows[step][None], code_state, left, signal, taps, peers)
+        blocks = lax.all_to_all(payload, "tm", 0, 0, tiled=True)
+        held, came = gather_pieces(share_gradient(blocks, channels // peers))
+        dictionary, atoms = renew(jnp.stack([index, first_rows[step]]), held, came, dictionary)
+    return code_state, dictionary, residual
+
+
 def renew_atoms(old_atoms, across, mean_sq, spread):
     return (old_atoms + move_rate * across / jnp.sqrt(spread)[:, None]) / jnp.sqrt(mean_sq + 0.25)[
         :, None
     ]
 
 
-def shards(signal, codes_init, dictionary_init, threshold, plan):
+def split_channels(signal, codes_init, dictionary_init, threshold, plan):
     segment = signal.shape[1]
     local_chan = signal.shape[0]
     unit_scale = (C * L) ** (-0.5)
@@ -89,6 +585,23 @@
     return (code_state, dictionary, residual)
 
 
+def shards(signal, codes_init, dictionary_init, threshold, plan):
+    channels, segment = signal.shape
+    peers = lax.axis_size("tm")
+    fits = (
+        lax.axis_size("chan") == 1
+        and segment % LANES == 0
+        and channels % (4 * ROWS) == 0
+        and channels % LANES == 0
+        and channels % peers == 0
+        and (channels // peers * L) % LANES == 0
+        and peers > 1
+        and peers & (peers - 1) == 0
+    )
+    body = whole_channels if fits else split_channels
+    return body(signal, codes_init, dictionary_init, threshold, plan)
+
+
 def solution(mesh):
     placed = (P("chan", "tm"), P(None, "tm"), P(None, "chan"), P(), P())
     return jax.shard_map(

time: 1010 us -> 222 us (0.22)
  other arithmetic: 420 us -> 5.79 us
  waiting for transfers between devices: 296 us -> 27.1 us
  local copies, waits for them, and re-layouts: 149 us -> 9.15 us
  Pallas kernels: 0 us -> 101 us
  matrix products: 87.6 us -> 0 us
  starting transfers between devices: 31 us -> 53.5 us
  blocking collectives: 0 us -> 21.7 us
  between operations: 17.9 us -> 2.44 us
    unnamed x1037 -> x0, other arithmetic: 386 us -> none
    psum x2 -> x0, waiting for transfers between devices: 282 us -> none  [shards(): gradient = lax.psum(local_grad, 'tm')]
    pallas_call x0 -> x11, Pallas kernels: none -> 101 us  [the longest x4 45 us: iterate(): pl.pallas_call(functools.partial(iterate_kernel, peers * segment, patchin...]
    dot_general x12 -> x0, matrix products: 87.6 us -> none  [the longest x4 38.6 us: shards(): jnp.dot(dict_low, lagged, preferred_element_type=jnp.float32)]
    another operation x6 -> x0, local copies, waits for them, and re-layouts: 77.1 us -> none  [resid_columns(): jnp.stack([extended[:, offset:offset + segment] for offset in range(L)],...]
    reshape x2 -> x0, local copies, waits for them, and re-layouts: 26.6 us -> none  [shards(): atom_cube = dict_low.reshape(K, local_chan, L)]
    unnamed x30 -> x40, local copies, waits for them, and re-layouts: 30.9 us -> 7.79 us
    all_to_all x0 -> x1, blocking collectives: none -> 21.7 us  [whole_channels(): blocks = lax.all_to_all(payload, 'tm', 0, 0, tiled=True)]
  transfers between devices with their start and end apart: 13 -> 24, of which waited for: 12 -> 13; matrix products, arithmetic and copies ran while one was open for 3% -> 3% of each run, Pallas kernels for 0% -> 12%
where the time goes in v3:
time: 222 us; the launch traced here: 221 us
  Pallas kernels  101 us (45%)
  starting transfers between devices  53.5 us (24%)
  waiting for transfers between devices  27.1 us (12%)
  blocking collectives  21.7 us (10%)
  local copies, waits for them, and re-layouts  9.15 us (4%)
  other arithmetic  5.79 us (3%)
  between operations  2.44 us (1%)
    pallas_call x4, Pallas kernels, iterate(): pl.pallas_call(functools.partial(iterate_kernel, peers * segment, patchin...  45 us
    ppermute x9, starting transfers between devices, shifted(): return lax.ppermute(shard, axis, pairs)  25.1 us
    all_to_all x1, blocking collectives, whole_channels(): blocks = lax.all_to_all(payload, 'tm', 0, 0, tiled=True)  21.7 us
    pallas_call x1, Pallas kernels, layout(): pl.pallas_call(layout_kernel, grid=(channels // block,), in_specs=[pl.Blo...  18.7 us
    ppermute x14, starting transfers between devices, exchanged(): return lax.ppermute(shard, 'tm', [(i, i ^ mask) for i in range(peers)])  16 us
    pallas_call x2, Pallas kernels, renew(): pl.pallas_call(renew_kernel, in_specs=[pl.BlockSpec(memory_space=pltpu.SM...  15.3 us
    pallas_call x2, Pallas kernels, finish(): pl.pallas_call(functools.partial(finish_kernel, peers), in_specs=[pl.Bloc...  14.5 us
    ppermute x14, waiting for transfers between devices, exchanged(): return lax.ppermute(shard, 'tm', [(i, i ^ mask) for i in range(peers)])  14 us
  transfers between devices with their start and end apart: 24, of which 13 were waited for; matrix products, arithmetic and copies ran while one was open for 3% of the time, Pallas kernels for 12%

profile of v3, /device:TPU:0, one launch (start us, length us, event | category | flops | bytes accessed | tf_op | source)
XLA Modules:
  0.0 220.8 jit_solution(8433608422578355783)
XLA Ops:
  1.5 2.3 %collective-permute-start = (bf16[128,128]{1,0:T(8,128)(2,1)S(1)}, bf16[128,128]{1,0:T(8,128)(2,1)S(1)}, u32[]{:S(2)}, u32[]{:S(2)}) collective-permute-start(bf16[128,128]{1,0:T(8,128)(2,1)S(1)} %convert_element_type.3), channel_id=1, source_target_pairs={{0,1},{1,2},{2,3},{3,4},{4,5},{5,6},{6,7},{7,8},{8,9},{9,10},{10,1... | collective-permute-start | bytes 98312 | tf_op jit(solution)/shard_map/ppermute | solution.py:35
  8.6 18.7 %layout.1 = (bf16[96,384,128]{2,1,0:T(8,128)(2,1)}, f32[128,36864]{1,0:T(8,128)}) custom-call(f32[128,36864]{1,0:T(8,128)} %dict_ref.1), custom_call_target="tpu_custom_call" | custom-call | tf_op jit(solution)/shard_map/layout/pallas_call | solution.py:67
  28.0 8.4 %iterate.4 = (f32[128,128]{1,0:T(8,128)}, bf16[128,128]{1,0:T(8,128)(2,1)}) custom-call(s32[2]{0:T(128)} %pad_add_fusion.place_ref, f32[1,128]{1,0:T(1,128)} %bitcast.20, f32[128,128]{1,0:T(8,128)} %refs_0_.1, bf16[128,128]{1,0:T(8,128)(2,1)} %copy-done.7, bf16[512,128]{1,0:T(8,128)(2,1)} %copy-done, bf16[384,128]{1,0:T(8,128)(2,1)} %signal_ref.3, ...), custom_call_target="tpu_custom_call" | custom-call | tf_op jit(solution)/shard_map/iterate/pallas_call | solution.py:243
  37.7 5.8 %collective-permute-start.2 = (bf16[128,128]{1,0:T(8,128)(2,1)}, bf16[128,128]{1,0:T(8,128)(2,1)S(1)}, u32[]{:S(2)}, u32[]{:S(2)}) collective-permute-start(bf16[128,128]{1,0:T(8,128)(2,1)} %get-tuple-element.22), channel_id=1, source_target_pairs={{0,1},{1,2},{2,3},{3,4},{4,5},{5,6},{6,7},{7,8},{8,9},{9,10},{10,1... | collective-permute-start | bytes 98312 | tf_op jit(solution)/shard_map/ppermute | solution.py:35
  45.1 8.4 %iterate.5 = (f32[128,128]{1,0:T(8,128)}, bf16[128,128]{1,0:T(8,128)(2,1)}) custom-call(s32[2]{0:T(128)} %pad_add_fusion.place_ref, f32[1,128]{1,0:T(1,128)} %bitcast.21, f32[128,128]{1,0:T(8,128)} %get-tuple-element.21.refs_0_, bf16[128,128]{1,0:T(8,128)(2,1)} %copy-done.12, bf16[128,128]{1,0:T(8,128)(2,1)} %copy-done.10, bf16[384,128]{1,0:T(8,128)(2,1)} %signal_ref.3, ...), custom_call_target="tpu_custom_call" | custom-call | tf_op jit(solution)/shard_map/iterate/pallas_call | solution.py:243
  53.5 4.1 %collective-permute-start.4 = (bf16[128,128]{1,0:T(8,128)(2,1)}, bf16[128,128]{1,0:T(8,128)(2,1)S(1)}, u32[]{:S(2)}, u32[]{:S(2)}) collective-permute-start(bf16[128,128]{1,0:T(8,128)(2,1)} %get-tuple-element.24), channel_id=1, source_target_pairs={{0,1},{1,2},{2,3},{3,4},{4,5},{5,6},{6,7},{7,8},{8,9},{9,10},{10,1... | collective-permute-start | bytes 98312 | tf_op jit(solution)/shard_map/ppermute | solution.py:35
  59.3 7.2 %finish.2 = (f32[384,128]{1,0:T(8,128)}, bf16[32,32,128]{2,1,0:T(8,128)(2,1)}) custom-call(s32[1]{0:T(128)S(6)} %mul.39.place_ref, f32[128,128]{1,0:T(8,128)} %get-tuple-element.23.code_ref.refs_0_, bf16[128,128]{1,0:T(8,128)(2,1)} %copy-done.6, bf16[384,128]{1,0:T(8,128)(2,1)} %signal_ref.3, bf16[6,16,384,128]{3,2,1,0:T(8,128)(2,1)} %bitcast.10), custom_call_target="tpu_custom_call" | custom-call | tf_op jit(solution)/shard_map/finish/pallas_call | solution.py:303
  66.5 12.4 %all-to-all-start = ((bf16[32,32,128]{2,1,0:T(8,128)(2,1)}), bf16[32,32,128]{2,1,0:T(8,128)(2,1)S(1)}, u32[]{:S(2)}, u32[]{:S(2)}) async-start(bf16[32,32,128]{2,1,0:T(8,128)(2,1)} %get-tuple-element.25), calls=%async_computation | async-start | bytes 524288 | tf_op jit(solution)/shard_map/all_to_all | solution.py:515
  79.6 9.8 %all-to-all-done.blocks_ref = bf16[32,32,128]{2,1,0:T(8,128)(2,1)S(1)} async-done(((bf16[32,32,128]{2,1,0:T(8,128)(2,1)}), bf16[32,32,128]{2,1,0:T(8,128)(2,1)S(1)}, u32[]{:S(2)}, u32[]{:S(2)}) %all-to-all-start) | async-done | bytes 262176 | tf_op jit(solution)/shard_map/all_to_all | solution.py:515
  90.1 3.8 %gradient.2 = bf16[16,1152]{1,0:T(8,128)(2,1)} custom-call(s32[1,1152]{1,0:T(1,128)} %fusion.source_ref, bf16[32,32,128]{2,1,0:T(8,128)(2,1)} %copy-done.1), custom_call_target="tpu_custom_call" | custom-call | tf_op jit(solution)/shard_map/gradient/pallas_call | solution.py:369
  95.3 3.1 %collective-permute-start.6 = (bf16[1,16,1152]{2,1,0:T(8,128)(2,1)}, bf16[1,16,1152]{2,1,0:T(8,128)(2,1)S(1)}, u32[]{:S(2)}, u32[]{:S(2)}) collective-permute-start(bf16[1,16,1152]{2,1,0:T(8,128)(2,1)} %bitcast.18), channel_id=1, source_target_pairs={{0,16},{1,17},{2,18},{3,19},{4,20},{5,21},{6,22},{7,23},{8,24},{9,... | collective-permute-start | bytes 110600 | tf_op jit(solution)/shard_map/ppermute | solution.py:403
  105.1 4.7 %collective-permute-done.9 = bf16[4,16,1152]{2,1,0:T(8,128)(2,1)S(1)} collective-permute-done((bf16[4,16,1152]{2,1,0:T(8,128)(2,1)S(1)}, bf16[4,16,1152]{2,1,0:T(8,128)(2,1)S(1)}, u32[]{:S(2)}, u32[]{:S(2)}) %collective-permute-start.9) | collective-permute-done | bytes 147488 | tf_op jit(solution)/shard_map/ppermute | solution.py:403
  112.7 7.6 %renew.2 = (f32[128,36864]{1,0:T(8,128)}, f32[16,36864]{1,0:T(8,128)}) custom-call(s32[2]{0:T(128)} %pad_add_fusion.2.place_ref, bf16[16,16,1152]{2,1,0:T(8,128)(2,1)} %copy-done.2, bf16[16,16,1152]{2,1,0:T(8,128)(2,1)} %copy-done.4, f32[128,36864]{1,0:T(8,128)} %get-tuple-element.26.dict_hbm), custom_call_target="tpu_custom_call", output_to_operand_aliasing={{0}: (3, {})} | custom-call | tf_op jit(solution)/shard_map/renew/pallas_call | solution.py:469
  121.0 19.9 %iterate.6 = (f32[128,128]{1,0:T(8,128)}, bf16[128,128]{1,0:T(8,128)(2,1)}, bf16[6,16,384,128]{3,2,1,0:T(8,128)(2,1)}) custom-call(s32[2]{0:T(128)} %pad_add_fusion.place_ref, f32[1,128]{1,0:T(1,128)} %bitcast.22, f32[128,128]{1,0:T(8,128)} %get-tuple-element.23.code_ref.refs_0_, bf16[128,128]{1,0:T(8,128)(2,1)} %copy-done.6, bf16[128,128]{1,0:T(8,128)(2,1)} %copy-done.8, ...), custom_call_target="tpu_custom_call" | custom-call | tf_op jit(solution)/shard_map/iterate/pallas_call | solution.py:243
  142.2 3.5 %collective-permute-start.13 = (bf16[128,128]{1,0:T(8,128)(2,1)}, bf16[128,128]{1,0:T(8,128)(2,1)S(1)}, u32[]{:S(2)}, u32[]{:S(2)}) collective-permute-start(bf16[128,128]{1,0:T(8,128)(2,1)} %get-tuple-element.29), channel_id=1, source_target_pairs={{0,1},{1,2},{2,3},{3,4},{4,5},{5,6},{6,7},{7,8},{8,9},{9,10},{10,1... | collective-permute-start | bytes 98312 | tf_op jit(solution)/shard_map/ppermute | solution.py:35
  147.4 8.4 %iterate.7 = (f32[128,128]{1,0:T(8,128)}, bf16[128,128]{1,0:T(8,128)(2,1)}) custom-call(s32[2]{0:T(128)} %pad_add_fusion.place_ref, f32[1,128]{1,0:T(1,128)} %bitcast.23, f32[128,128]{1,0:T(8,128)} %get-tuple-element.28.refs_0_, bf16[128,128]{1,0:T(8,128)(2,1)} %copy-done.11, bf16[128,128]{1,0:T(8,128)(2,1)} %copy-done.9, bf16[384,128]{1,0:T(8,128)(2,1)} %signal_ref.3, ...), custom_call_target="tpu_custom_call" | custom-call | tf_op jit(solution)/shard_map/iterate/pallas_call | solution.py:243
  155.8 4.1 %collective-permute-start.15 = (bf16[128,128]{1,0:T(8,128)(2,1)}, bf16[128,128]{1,0:T(8,128)(2,1)S(1)}, u32[]{:S(2)}, u32[]{:S(2)}) collective-permute-start(bf16[128,128]{1,0:T(8,128)(2,1)} %get-tuple-element.32), channel_id=1, source_target_pairs={{0,1},{1,2},{2,3},{3,4},{4,5},{5,6},{6,7},{7,8},{8,9},{9,10},{10,1... | collective-permute-start | bytes 98312 | tf_op jit(solution)/shard_map/ppermute | solution.py:35
  161.4 7.2 %finish.3 = (f32[384,128]{1,0:T(8,128)}, bf16[32,32,128]{2,1,0:T(8,128)(2,1)}) custom-call(s32[1]{0:T(128)S(6)} %mul.42.place_ref, f32[128,128]{1,0:T(8,128)} %get-tuple-element.17.code_ref, bf16[128,128]{1,0:T(8,128)(2,1)} %copy-done.13, bf16[384,128]{1,0:T(8,128)(2,1)} %signal_ref.3, bf16[6,16,384,128]{3,2,1,0:T(8,128)(2,1)} %get-tuple-element.30.refs_5_.taps_hbm), custom_call_target="tpu_custom_call" | custom-call | tf_op jit(solution)/shard_map/finish/pallas_call | solution.py:303
  168.6 21.7 %all_to_all.10.blocks_ref = bf16[32,32,128]{2,1,0:T(8,128)(2,1)} all-to-all(bf16[32,32,128]{2,1,0:T(8,128)(2,1)} %get-tuple-element.33), channel_id=1, replica_groups=mesh['tm'=32,'chan'=1] {'tm'}, dimensions={0} | all-to-all | bytes 524288 | tf_op jit(solution)/shard_map/all_to_all | solution.py:515
  190.3 3.8 %gradient.3 = bf16[16,1152]{1,0:T(8,128)(2,1)} custom-call(s32[1,1152]{1,0:T(1,128)} %fusion.source_ref, bf16[32,32,128]{2,1,0:T(8,128)(2,1)} %all_to_all.10.blocks_ref), custom_call_target="tpu_custom_call" | custom-call | tf_op jit(solution)/shard_map/gradient/pallas_call | solution.py:369
  195.5 3.1 %collective-permute-start.16 = (bf16[1,16,1152]{2,1,0:T(8,128)(2,1)}, bf16[1,16,1152]{2,1,0:T(8,128)(2,1)S(1)}, u32[]{:S(2)}, u32[]{:S(2)}) collective-permute-start(bf16[1,16,1152]{2,1,0:T(8,128)(2,1)} %bitcast.14), channel_id=1, source_target_pairs={{0,16},{1,17},{2,18},{3,19},{4,20},{5,21},{6,22},{7,23},{8,24},{9,... | collective-permute-start | bytes 110600 | tf_op jit(solution)/shard_map/ppermute | solution.py:403
  205.3 4.7 %collective-permute-done.19 = bf16[4,16,1152]{2,1,0:T(8,128)(2,1)S(1)} collective-permute-done((bf16[4,16,1152]{2,1,0:T(8,128)(2,1)S(1)}, bf16[4,16,1152]{2,1,0:T(8,128)(2,1)S(1)}, u32[]{:S(2)}, u32[]{:S(2)}) %collective-permute-start.19) | collective-permute-done | bytes 147488 | tf_op jit(solution)/shard_map/ppermute | solution.py:403
  210.7 1.4 collective-permute-done.22.came_hbm
  212.9 7.6 %renew.3 = (f32[128,36864]{1,0:T(8,128)}, f32[16,36864]{1,0:T(8,128)}) custom-call(s32[2]{0:T(128)} %pad_add_fusion.1.place_ref, bf16[16,16,1152]{2,1,0:T(8,128)(2,1)} %copy-done.3, bf16[16,16,1152]{2,1,0:T(8,128)(2,1)} %copy-done.5, f32[128,36864]{1,0:T(8,128)} %get-tuple-element.34.dict_hbm), custom_call_target="tpu_custom_call", output_to_operand_aliasing={{0}: (3, {})} | custom-call | tf_op jit(solution)/shard_map/renew/pallas_call | solution.py:469
  (87 shorter events, 36.6 us)
Async XLA Ops:
  1.5 25.8 %collective-permute-start = (bf16[128,128]{1,0:T(8,128)(2,1)S(1)}, bf16[128,128]{1,0:T(8,128)(2,1)S(1)}, u32[]{:S(2)}, u32[]{:S(2)}) collective-permute-start(bf16[128,128]{1,0:T(8,128)(2,1)S(1)} %convert_element_type.3), channel_id=1, source_target_pairs={{0,1},{1,2},{2,3},{3,4},{4,5},{5,6},{6,7},{7,8},{8,9},{9,10},{10,1... | collective-permute-start | bytes 98312 | tf_op jit(solution)/shard_map/ppermute | solution.py:35
  4.7 22.6 %collective-permute-start.1 = (bf16[512,128]{1,0:T(8,128)(2,1)S(1)}, bf16[512,128]{1,0:T(8,128)(2,1)S(1)}, u32[]{:S(2)}, u32[]{:S(2)}) collective-permute-start(bf16[512,128]{1,0:T(8,128)(2,1)S(1)} %pad_maximum_fusion.2), channel_id=1, source_target_pairs={{1,0},{2,1},{3,2},{4,3},{5,4},{6,5},{7,6},{8,7},{9,8},{10,9},{11,1... | collective-permute-start | bytes 393224 | tf_op jit(solution)/shard_map/ppermute | solution.py:35
  36.4 7.1 %collective-permute-start.3 = (bf16[128,128]{1,0:T(8,128)(2,1)}, bf16[128,128]{1,0:T(8,128)(2,1)S(1)}, u32[]{:S(2)}, u32[]{:S(2)}) collective-permute-start(bf16[128,128]{1,0:T(8,128)(2,1)} %get-tuple-element.22), channel_id=1, source_target_pairs={{1,0},{2,1},{3,2},{4,3},{5,4},{6,5},{7,6},{8,7},{9,8},{10,9},{11,1... | collective-permute-start | bytes 98312 | tf_op jit(solution)/shard_map/ppermute | solution.py:35
  37.7 6.8 %collective-permute-start.2 = (bf16[128,128]{1,0:T(8,128)(2,1)}, bf16[128,128]{1,0:T(8,128)(2,1)S(1)}, u32[]{:S(2)}, u32[]{:S(2)}) collective-permute-start(bf16[128,128]{1,0:T(8,128)(2,1)} %get-tuple-element.22), channel_id=1, source_target_pairs={{0,1},{1,2},{2,3},{3,4},{4,5},{5,6},{6,7},{7,8},{8,9},{9,10},{10,1... | collective-permute-start | bytes 98312 | tf_op jit(solution)/shard_map/ppermute | solution.py:35
  53.5 5.2 %collective-permute-start.4 = (bf16[128,128]{1,0:T(8,128)(2,1)}, bf16[128,128]{1,0:T(8,128)(2,1)S(1)}, u32[]{:S(2)}, u32[]{:S(2)}) collective-permute-start(bf16[128,128]{1,0:T(8,128)(2,1)} %get-tuple-element.24), channel_id=1, source_target_pairs={{0,1},{1,2},{2,3},{3,4},{4,5},{5,6},{6,7},{7,8},{8,9},{9,10},{10,1... | collective-permute-start | bytes 98312 | tf_op jit(solution)/shard_map/ppermute | solution.py:35
  66.5 22.9 %all-to-all-start = ((bf16[32,32,128]{2,1,0:T(8,128)(2,1)}), bf16[32,32,128]{2,1,0:T(8,128)(2,1)S(1)}, u32[]{:S(2)}, u32[]{:S(2)}) async-start(bf16[32,32,128]{2,1,0:T(8,128)(2,1)} %get-tuple-element.25), calls=%async_computation | async-start | bytes 524288 | tf_op jit(solution)/shard_map/all_to_all | solution.py:515
  93.9 6.2 %collective-permute-start.8 = (bf16[1,16,1152]{2,1,0:T(8,128)(2,1)}, bf16[1,16,1152]{2,1,0:T(8,128)(2,1)S(1)}, u32[]{:S(2)}, u32[]{:S(2)}) collective-permute-start(bf16[1,16,1152]{2,1,0:T(8,128)(2,1)} %bitcast.16), channel_id=1, source_target_pairs={{0,24},{1,25},{2,26},{3,27},{4,28},{5,29},{6,30},{7,31},{8,16},{9,... | collective-permute-start | bytes 110600 | tf_op jit(solution)/shard_map/ppermute | solution.py:403
  95.3 4.9 %collective-permute-start.7 = (bf16[1,16,1152]{2,1,0:T(8,128)(2,1)}, bf16[1,16,1152]{2,1,0:T(8,128)(2,1)S(1)}, u32[]{:S(2)}, u32[]{:S(2)}) collective-permute-start(bf16[1,16,1152]{2,1,0:T(8,128)(2,1)} %bitcast.17), channel_id=1, source_target_pairs={{0,8},{1,9},{2,10},{3,11},{4,12},{5,13},{6,14},{7,15},{8,0},{9,1},... | collective-permute-start | bytes 110600 | tf_op jit(solution)/shard_map/ppermute | solution.py:403
  95.3 5.4 %collective-permute-start.6 = (bf16[1,16,1152]{2,1,0:T(8,128)(2,1)}, bf16[1,16,1152]{2,1,0:T(8,128)(2,1)S(1)}, u32[]{:S(2)}, u32[]{:S(2)}) collective-permute-start(bf16[1,16,1152]{2,1,0:T(8,128)(2,1)} %bitcast.18), channel_id=1, source_target_pairs={{0,16},{1,17},{2,18},{3,19},{4,20},{5,21},{6,22},{7,23},{8,24},{9,... | collective-permute-start | bytes 110600 | tf_op jit(solution)/shard_map/ppermute | solution.py:403
  101.5 8.3 %collective-permute-start.11 = (bf16[4,16,1152]{2,1,0:T(8,128)(2,1)S(1)}, bf16[4,16,1152]{2,1,0:T(8,128)(2,1)S(1)}, u32[]{:S(2)}, u32[]{:S(2)}) collective-permute-start(bf16[4,16,1152]{2,1,0:T(8,128)(2,1)S(1)} %pad_maximum_fusion), channel_id=1, source_target_pairs={{0,6},{1,7},{2,4},{3,5},{4,2},{5,3},{6,0},{7,1},{8,14},{9,15},{10,... | collective-permute-start | bytes 442376 | tf_op jit(solution)/shard_map/ppermute | solution.py:403
  102.7 7.0 %collective-permute-start.10 = (bf16[4,16,1152]{2,1,0:T(8,128)(2,1)S(1)}, bf16[4,16,1152]{2,1,0:T(8,128)(2,1)S(1)}, u32[]{:S(2)}, u32[]{:S(2)}) collective-permute-start(bf16[4,16,1152]{2,1,0:T(8,128)(2,1)S(1)} %pad_maximum_fusion), channel_id=1, source_target_pairs={{0,2},{1,3},{2,0},{3,1},{4,6},{5,7},{6,4},{7,5},{8,10},{9,11},{10,... | collective-permute-start | bytes 442376 | tf_op jit(solution)/shard_map/ppermute | solution.py:403
  103.9 5.9 %collective-permute-start.9 = (bf16[4,16,1152]{2,1,0:T(8,128)(2,1)S(1)}, bf16[4,16,1152]{2,1,0:T(8,128)(2,1)S(1)}, u32[]{:S(2)}, u32[]{:S(2)}) collective-permute-start(bf16[4,16,1152]{2,1,0:T(8,128)(2,1)S(1)} %pad_maximum_fusion), channel_id=1, source_target_pairs={{0,4},{1,5},{2,6},{3,7},{4,0},{5,1},{6,2},{7,3},{8,12},{9,13},{10,... | collective-permute-start | bytes 442376 | tf_op jit(solution)/shard_map/ppermute | solution.py:403
  109.8 2.1 collective-permute-start.12
  109.9 10.5 %collective-permute-start.5 = (bf16[128,128]{1,0:T(8,128)(2,1)}, bf16[128,128]{1,0:T(8,128)(2,1)S(1)}, u32[]{:S(2)}, u32[]{:S(2)}) collective-permute-start(bf16[128,128]{1,0:T(8,128)(2,1)} %get-tuple-element.24), channel_id=1, source_target_pairs={{1,0},{2,1},{3,2},{4,3},{5,4},{6,5},{7,6},{8,7},{9,8},{10,9},{11,1... | collective-permute-start | bytes 98312 | tf_op jit(solution)/shard_map/ppermute | solution.py:35
  140.9 4.9 %collective-permute-start.14 = (bf16[128,128]{1,0:T(8,128)(2,1)}, bf16[128,128]{1,0:T(8,128)(2,1)S(1)}, u32[]{:S(2)}, u32[]{:S(2)}) collective-permute-start(bf16[128,128]{1,0:T(8,128)(2,1)} %get-tuple-element.29), channel_id=1, source_target_pairs={{1,0},{2,1},{3,2},{4,3},{5,4},{6,5},{7,6},{8,7},{9,8},{10,9},{11,1... | collective-permute-start | bytes 98312 | tf_op jit(solution)/shard_map/ppermute | solution.py:35
  142.2 4.6 %collective-permute-start.13 = (bf16[128,128]{1,0:T(8,128)(2,1)}, bf16[128,128]{1,0:T(8,128)(2,1)S(1)}, u32[]{:S(2)}, u32[]{:S(2)}) collective-permute-start(bf16[128,128]{1,0:T(8,128)(2,1)} %get-tuple-element.29), channel_id=1, source_target_pairs={{0,1},{1,2},{2,3},{3,4},{4,5},{5,6},{6,7},{7,8},{8,9},{9,10},{10,1... | collective-permute-start | bytes 98312 | tf_op jit(solution)/shard_map/ppermute | solution.py:35
  155.8 5.0 %collective-permute-start.15 = (bf16[128,128]{1,0:T(8,128)(2,1)}, bf16[128,128]{1,0:T(8,128)(2,1)S(1)}, u32[]{:S(2)}, u32[]{:S(2)}) collective-permute-start(bf16[128,128]{1,0:T(8,128)(2,1)} %get-tuple-element.32), channel_id=1, source_target_pairs={{0,1},{1,2},{2,3},{3,4},{4,5},{5,6},{6,7},{7,8},{8,9},{9,10},{10,1... | collective-permute-start | bytes 98312 | tf_op jit(solution)/shard_map/ppermute | solution.py:35
  194.1 6.3 %collective-permute-start.18 = (bf16[1,16,1152]{2,1,0:T(8,128)(2,1)}, bf16[1,16,1152]{2,1,0:T(8,128)(2,1)S(1)}, u32[]{:S(2)}, u32[]{:S(2)}) collective-permute-start(bf16[1,16,1152]{2,1,0:T(8,128)(2,1)} %bitcast.12), channel_id=1, source_target_pairs={{0,24},{1,25},{2,26},{3,27},{4,28},{5,29},{6,30},{7,31},{8,16},{9,... | collective-permute-start | bytes 110600 | tf_op jit(solution)/shard_map/ppermute | solution.py:403
  195.5 4.9 %collective-permute-start.17 = (bf16[1,16,1152]{2,1,0:T(8,128)(2,1)}, bf16[1,16,1152]{2,1,0:T(8,128)(2,1)S(1)}, u32[]{:S(2)}, u32[]{:S(2)}) collective-permute-start(bf16[1,16,1152]{2,1,0:T(8,128)(2,1)} %bitcast.13), channel_id=1, source_target_pairs={{0,8},{1,9},{2,10},{3,11},{4,12},{5,13},{6,14},{7,15},{8,0},{9,1},... | collective-permute-start | bytes 110600 | tf_op jit(solution)/shard_map/ppermute | solution.py:403
  195.5 5.4 %collective-permute-start.16 = (bf16[1,16,1152]{2,1,0:T(8,128)(2,1)}, bf16[1,16,1152]{2,1,0:T(8,128)(2,1)S(1)}, u32[]{:S(2)}, u32[]{:S(2)}) collective-permute-start(bf16[1,16,1152]{2,1,0:T(8,128)(2,1)} %bitcast.14), channel_id=1, source_target_pairs={{0,16},{1,17},{2,18},{3,19},{4,20},{5,21},{6,22},{7,23},{8,24},{9,... | collective-permute-start | bytes 110600 | tf_op jit(solution)/shard_map/ppermute | solution.py:403
  201.7 8.3 %collective-permute-start.21 = (bf16[4,16,1152]{2,1,0:T(8,128)(2,1)S(1)}, bf16[4,16,1152]{2,1,0:T(8,128)(2,1)S(1)}, u32[]{:S(2)}, u32[]{:S(2)}) collective-permute-start(bf16[4,16,1152]{2,1,0:T(8,128)(2,1)S(1)} %pad_maximum_fusion.1), channel_id=1, source_target_pairs={{0,6},{1,7},{2,4},{3,5},{4,2},{5,3},{6,0},{7,1},{8,14},{9,15},{10,... | collective-permute-start | bytes 442376 | tf_op jit(solution)/shard_map/ppermute | solution.py:403
  202.9 7.0 %collective-permute-start.20 = (bf16[4,16,1152]{2,1,0:T(8,128)(2,1)S(1)}, bf16[4,16,1152]{2,1,0:T(8,128)(2,1)S(1)}, u32[]{:S(2)}, u32[]{:S(2)}) collective-permute-start(bf16[4,16,1152]{2,1,0:T(8,128)(2,1)S(1)} %pad_maximum_fusion.1), channel_id=1, source_target_pairs={{0,2},{1,3},{2,0},{3,1},{4,6},{5,7},{6,4},{7,5},{8,10},{9,11},{10,... | collective-permute-start | bytes 442376 | tf_op jit(solution)/shard_map/ppermute | solution.py:403
  204.1 5.9 %collective-permute-start.19 = (bf16[4,16,1152]{2,1,0:T(8,128)(2,1)S(1)}, bf16[4,16,1152]{2,1,0:T(8,128)(2,1)S(1)}, u32[]{:S(2)}, u32[]{:S(2)}) collective-permute-start(bf16[4,16,1152]{2,1,0:T(8,128)(2,1)S(1)} %pad_maximum_fusion.1), channel_id=1, source_target_pairs={{0,4},{1,5},{2,6},{3,7},{4,0},{5,1},{6,2},{7,3},{8,12},{9,13},{10,... | collective-permute-start | bytes 442376 | tf_op jit(solution)/shard_map/ppermute | solution.py:403
  210.0 2.1 collective-permute-start.22
  (14 other events, 12.9 us)

commit v4 on v3

--- a/solution.py
+++ b/solution.py
@@ -23,7 +23,7 @@
 STRIDE = L + 1
 FINE = 4
 LANES = 128
-VMEM_BYTES = 56 * 1024 * 1024
+VMEM_BYTES = 24 * 1024 * 1024
 
 NN = (((1,), (0,)), ((), ()))
 NT = (((1,), (1,)), ((), ()))
@@ -35,13 +35,36 @@
     return lax.ppermute(shard, axis, pairs)
 
 
+def resident(value):
+    return pltpu.with_memory_space_constraint(value, pltpu.VMEM)
+
+
+def vmem():
+    return pl.BlockSpec(memory_space=pltpu.VMEM)
+
+
 def turn(columns_ref, start, turned_ref):
-    for quad in range(ROWS // 4):
-        part = pl.ds(start + quad * 4 * L, 4 * L)
-        turned = columns_ref[:, part].T
-        for q in range(4):
-            row = (quad * 4 + q) * STRIDE
-            turned_ref[row : row + L, :] = turned[q * L : (q + 1) * L]
+    side = 2 * LANES
+    row = lax.broadcasted_iota(jnp.int32, (side, side), 0)
+    column = lax.broadcasted_iota(jnp.int32, (side, side), 1)
+    identity = (row == column).astype(jnp.float32).astype(jnp.bfloat16)
+    for first in range(0, ROWS * L, 2 * side):
+        pair = jnp.concatenate(
+            [columns_ref[:, pl.ds(start + first + half * side, side)] for half in range(2)], axis=0
+        ).astype(jnp.bfloat16)
+        turned = lax.dot_general(identity, pair, NT, preferred_element_type=jnp.float32)
+        for half in range(2):
+            entry = first + half * side
+            end = entry + side
+            begin = entry
+            while begin < end:
+                channel, tap = begin // L, begin % L
+                count = min(end - begin, L - tap)
+                target = channel * STRIDE + tap
+                turned_ref[target : target + count, :] = turned[
+                    begin - entry : begin - entry + count, half * K : (half + 1) * K
+                ]
+                begin += count
 
 
 def layout_kernel(dict_ref, taps_ref, copy_hbm, even, odd, sem):
@@ -55,8 +78,9 @@
         now, later = (even, odd) if group % 2 == 0 else (odd, even)
         if group + 1 < groups:
             turn(dict_ref, (group + 1) * ROWS * L, later)
+        own = pl.ds(pl.multiple_of((pl.program_id(0) * groups + group) * ROWS, ROWS), ROWS)
         for tap in range(L):
-            taps_ref[tap, group * ROWS : (group + 1) * ROWS, :] = now[
+            taps_ref[tap // ROWS, tap % ROWS, own, :] = now[
                 pl.ds(tap, ROWS, stride=STRIDE), :
             ].astype(jnp.bfloat16)
     copy.wait()
@@ -68,12 +92,9 @@
         layout_kernel,
         grid=(channels // block,),
         in_specs=[pl.BlockSpec((K, block * L), lambda i: (0, i))],
-        out_specs=[
-            pl.BlockSpec((L, block, K), lambda i: (0, i, 0)),
-            pl.BlockSpec(memory_space=pl.ANY),
-        ],
+        out_specs=[vmem(), pl.BlockSpec(memory_space=pl.ANY)],
         out_shape=[
-            jax.ShapeDtypeStruct((L, channels, K), jnp.bfloat16),
+            pltpu.VMEM((COARSE, ROWS, channels, K), jnp.bfloat16),
             jax.ShapeDtypeStruct(dictionary.shape, jnp.float32),
         ],
         scratch_shapes=[
@@ -86,19 +107,7 @@
     )(dictionary)
 
 
-def fetch_taps(taps_hbm, taps, sems):
-    copies = [
-        pltpu.make_async_copy(
-            taps_hbm.at[:, pl.ds(lag, FINE)], taps.at[:, pl.ds(lag, FINE)], sems.at[lag // FINE]
-        )
-        for lag in range(0, ROWS, FINE)
-    ]
-    for copy in copies:
-        copy.start()
-    return [copy.wait for copy in copies]
-
-
-def convolve(zb, begin, count, taps, zz, fine, acc, waits):
+def convolve(zb, begin, count, taps, zz, fine, acc):
     channels = taps.shape[2]
     tiles = channels // LANES
     rows = count + ROWS
@@ -106,8 +115,6 @@
         first = begin - ROWS - ROWS * coarse
         zz[:rows, coarse * K : (coarse + 1) * K] = zb[first : first + rows, :]
     for lag in range(0, ROWS, FINE):
-        if waits:
-            waits[lag // FINE]()
         slot = lag // FINE % 2 * FINE
         for pair in range(0, FINE, 2):
             weights = jnp.concatenate(
@@ -182,46 +189,54 @@
     lax.fori_loop(0, channels // (2 * ROWS), patch, 0)
 
 
-def put_codes(zb, own, left, right):
+def put_codes(zb, own, first_ref, second_ref, even):
     segment = own.shape[1]
-    zb[:L, :] = left[...].astype(jnp.float32).T[segment - L :].astype(jnp.bfloat16)
     zb[L : L + segment, :] = own[...].T.astype(jnp.bfloat16)
-    if right is not None:
-        zb[L + segment :, :] = right[:K, :].astype(jnp.float32).T[:L].astype(jnp.bfloat16)
+
+    def put(left, right):
+        zb[:L, :] = left[:K, :].astype(jnp.float32).T[segment - L :].astype(jnp.bfloat16)
+        if zb.shape[0] > L + segment:
+            zb[L + segment :, :] = right[:K, :].astype(jnp.float32).T[:L].astype(jnp.bfloat16)
+
+    pl.when(even)(lambda: put(second_ref, first_ref))
+    pl.when(jnp.logical_not(even))(lambda: put(first_ref, second_ref))
 
 
 def iterate_kernel(total_time, patching, place_ref, limit_ref, *refs):
-    code_ref, left_ref, right_ref, signal_ref, next_ref = refs[:5]
-    refs = refs[5:]
+    code_ref, first_ref, second_ref, signal_ref, next_first, next_second = refs[:6]
+    refs = refs[6:]
     if patching:
         atoms_ref, refs = refs[0], refs[1:]
-    taps_hbm, state_out, low_out = refs[:3]
+    taps, state_out, low_out = refs[:3]
     refs = refs[3:]
     if patching:
-        taps_out, refs = refs[0], refs[1:]
-    taps, zb, rb, zz, rr, fine, acc, sems = refs[:8]
+        taps, refs = refs[0], refs[1:]
+    zb, rb, zz, rr, fine, acc, beyond = refs[:7]
     channels, segment = signal_ref.shape
     tiles = channels // LANES
     scale = (C * L) ** (-0.5)
-    waits = fetch_taps(taps_hbm, taps, sems)
-    put_codes(zb, code_ref, left_ref, right_ref)
+    even = place_ref[2] == 0
+    put_codes(zb, code_ref, first_ref, second_ref, even)
+
+    def put(following):
+        for tile in range(tiles):
+            own = slice(K + tile * LANES, K + (tile + 1) * LANES)
+            turned = following[own, :].astype(jnp.float32).T
+            beyond[:, tile * LANES : (tile + 1) * LANES] = turned[:L]
+
+    pl.when(even)(lambda: put(next_first))
+    pl.when(jnp.logical_not(even))(lambda: put(next_second))
     if patching:
-        columns, even, odd, out_sem = refs[8:]
-        for wait in waits:
-            wait()
-        waits = None
-        patch_taps(pl.multiple_of(place_ref[1], BLOCK_ATOMS), atoms_ref, taps, columns, even, odd)
-        store = pltpu.make_async_copy(taps, taps_out, out_sem)
-        store.start()
+        columns, even_ref, odd_ref = refs[7:]
+        patch_taps(pl.multiple_of(place_ref[1], BLOCK_ATOMS), atoms_ref, taps, columns, even_ref, odd_ref)
     reach = segment + L
-    convolve(zb, L, reach, taps, zz, fine, acc, waits)
+    convolve(zb, L, reach, taps, zz, fine, acc)
     moment = place_ref[0] + lax.broadcasted_iota(jnp.int32, (reach, LANES), 0)
     inside = moment < total_time
     for tile in range(tiles):
         column = slice(tile * LANES, (tile + 1) * LANES)
-        first = signal_ref[column, :].astype(jnp.float32).T
-        second = next_ref[K + tile * LANES : K + (tile + 1) * LANES, :].astype(jnp.float32).T[:L]
-        value = jnp.concatenate([first, second], axis=0) - scale * acc[tile, :reach, :]
+        own = signal_ref[column, :].astype(jnp.float32).T
+        value = jnp.concatenate([own, beyond[:, column]], axis=0) - scale * acc[tile, :reach, :]
         rb[:, column] = jnp.where(inside, value, 0.0).astype(jnp.bfloat16)
     correlate(rb, segment, taps, rr, fine, acc)
     limit = limit_ref[...]
@@ -229,56 +244,49 @@
     state = (stepped - jnp.clip(stepped, -limit, limit)).T
     state_out[...] = state
     low_out[...] = state.astype(jnp.bfloat16)
-    if patching:
-        store.wait()
-
-
-def iterate(place, limit, code, left, right, signal, following, taps, atoms, peers):
+
+
+def iterate(place, limit, code, swapped, signal, following, taps, atoms, peers):
     channels, segment = signal.shape
     patching = atoms is not None
     reach = segment + L
-    whole = pl.BlockSpec(memory_space=pltpu.VMEM)
-    remote = pl.BlockSpec(memory_space=pl.ANY)
-    cube = (COARSE, ROWS, channels, K)
     return pl.pallas_call(
         functools.partial(iterate_kernel, peers * segment, patching),
-        in_specs=[pl.BlockSpec(memory_space=pltpu.SMEM)] + [whole] * (6 + patching) + [remote],
-        out_specs=[whole, whole] + [remote] * patching,
+        in_specs=[pl.BlockSpec(memory_space=pltpu.SMEM)] + [vmem()] * (8 + patching),
+        out_specs=[vmem()] * (2 + patching),
         out_shape=[
             jax.ShapeDtypeStruct((K, segment), jnp.float32),
             jax.ShapeDtypeStruct((K, segment), jnp.bfloat16),
         ]
-        + [jax.ShapeDtypeStruct(cube, jnp.bfloat16)] * patching,
+        + [pltpu.VMEM(taps.shape, jnp.bfloat16)] * patching,
         scratch_shapes=[
-            pltpu.VMEM(cube, jnp.bfloat16),
             pltpu.VMEM((L + reach, K), jnp.bfloat16),
             pltpu.VMEM((reach, channels), jnp.bfloat16),
             pltpu.VMEM((reach + ROWS, COARSE * K), jnp.bfloat16),
             pltpu.VMEM((segment + ROWS, COARSE * channels), jnp.bfloat16),
             pltpu.VMEM((2 * FINE, channels // LANES, reach + ROWS, LANES), jnp.float32),
             pltpu.VMEM((channels // LANES, reach, LANES), jnp.float32),
-            pltpu.SemaphoreType.DMA((ROWS // FINE,)),
+            pltpu.VMEM((L, channels), jnp.float32),
         ]
         + [
             pltpu.VMEM((K, 2 * ROWS * L), jnp.float32),
             pltpu.VMEM((ROWS * STRIDE, K), jnp.float32),
             pltpu.VMEM((ROWS * STRIDE, K), jnp.float32),
-            pltpu.SemaphoreType.DMA,
         ]
         * patching,
+        input_output_aliases={9: 2} if patching else {},
         compiler_params=pltpu.CompilerParams(vmem_limit_bytes=VMEM_BYTES),
         name="iterate",
-    )(place, limit, code, left, right, signal, following, *([atoms] * patching), taps)
+    )(place, limit, code, *swapped, signal, *following, *([resident(atoms)] if patching else []), resident(taps))
 
 
 def finish_kernel(
-    peers, place_ref, code_ref, left_ref, signal_ref, taps_hbm, resid_out, payload_out, taps, zb, zz, fine, acc, tall, sems
+    peers, place_ref, code_ref, first_ref, second_ref, signal_ref, taps, resid_out, payload_out, zb, zz, fine, acc, tall
 ):
     channels, segment = signal_ref.shape
     scale = (C * L) ** (-0.5)
-    waits = fetch_taps(taps_hbm, taps, sems)
-    put_codes(zb, code_ref, left_ref, None)
-    convolve(zb, L, segment, taps, zz, fine, acc, waits)
+    put_codes(zb, code_ref, first_ref, second_ref, place_ref[1] == 0)
+    convolve(zb, L, segment, taps, zz, fine, acc)
     for tile in range(channels // LANES):
         column = slice(tile * LANES, (tile + 1) * LANES)
         value = signal_ref[column, :].astype(jnp.float32) - scale * acc[tile, :segment, :].T
@@ -295,38 +303,39 @@
         payload_out[peer, share_rows:, :] = block
 
 
-def finish(place, code, left, signal, taps, peers):
+def finish(place, code, swapped, signal, taps, peers):
     channels, segment = signal.shape
     share = channels // peers
     share_rows = -(-share // ROWS) * ROWS
-    whole = pl.BlockSpec(memory_space=pltpu.VMEM)
     return pl.pallas_call(
         functools.partial(finish_kernel, peers),
-        in_specs=[pl.BlockSpec(memory_space=pltpu.SMEM), whole, whole, whole]
-        + [pl.BlockSpec(memory_space=pl.ANY)],
-        out_specs=[whole, whole],
+        in_specs=[pl.BlockSpec(memory_space=pltpu.SMEM)] + [vmem()] * 5,
+        out_specs=[vmem(), vmem()],
         out_shape=[
             jax.ShapeDtypeStruct((channels, segment), jnp.float32),
             jax.ShapeDtypeStruct((peers, share_rows + BLOCK_ATOMS, segment), jnp.bfloat16),
         ],
         scratch_shapes=[
-            pltpu.VMEM((COARSE, ROWS, channels, K), jnp.bfloat16),
             pltpu.VMEM((L + segment, K), jnp.bfloat16),
             pltpu.VMEM((segment + ROWS, COARSE * K), jnp.bfloat16),
             pltpu.VMEM((2 * FINE, channels // LANES, segment + ROWS, LANES), jnp.float32),
             pltpu.VMEM((channels // LANES, segment, LANES), jnp.float32),
             pltpu.VMEM((channels + ROWS, segment), jnp.float32),
-            pltpu.SemaphoreType.DMA((ROWS // FINE,)),
         ],
         compiler_params=pltpu.CompilerParams(vmem_limit_bytes=VMEM_BYTES),
         name="finish",
-    )(place, code, left, signal, taps)
-
-
-def gradient_kernel(share, source_ref, blocks_ref, out_ref, rf, zf, rr, zz):
+    )(place, code, *swapped, signal, resident(taps))
+
+
+def gradient_kernel(share, place_ref, source_ref, blocks_ref, dict_hbm, out_ref, rf, zf, rr, zz, old, sem):
     peers, rows, segment = blocks_ref.shape
     share_rows = rows - BLOCK_ATOMS
     span = peers * segment
+    entries = share * L
+    rows_of = pl.ds(pl.multiple_of(place_ref[1], BLOCK_ATOMS), BLOCK_ATOMS)
+    columns_of = pl.ds(pl.multiple_of(place_ref[0] * entries, LANES), entries)
+    fetch = pltpu.make_async_copy(dict_hbm.at[rows_of, columns_of], old, sem)
+    fetch.start()
     rf[:, span:] = jnp.zeros((share_rows, LANES), jnp.float32)
     zf[:, :LANES] = jnp.zeros((BLOCK_ATOMS, LANES), jnp.float32)
     for peer in range(peers):
@@ -343,23 +352,40 @@
             jnp.bfloat16
         )
     lagged = lax.dot_general(zz[...], rr[...], NT, preferred_element_type=jnp.float32)
-    lagged = lagged.astype(jnp.bfloat16)
     wide = ROWS * share_rows
-    entries = share * L
-    total = jnp.zeros((BLOCK_ATOMS, entries), jnp.float32)
+    parts = []
+    left = lagged
+    for _ in range(3):
+        parts.append(left.astype(jnp.bfloat16))
+        left = left - parts[-1].astype(jnp.float32)
+    total = jnp.zeros((3 * BLOCK_ATOMS, entries), jnp.float32)
     for coarse in range(COARSE):
         row = lax.broadcasted_iota(jnp.int32, (wide, entries), 0) + coarse * wide
         chosen = (row == source_ref[...]).astype(jnp.float32).astype(jnp.bfloat16)
         total += lax.dot_general(
-            lagged[coarse * BLOCK_ATOMS : (coarse + 1) * BLOCK_ATOMS, :],
+            jnp.concatenate(
+                [part[coarse * BLOCK_ATOMS : (coarse + 1) * BLOCK_ATOMS, :] for part in parts], axis=0
+            ),
             chosen,
             NN,
             preferred_element_type=jnp.float32,
         )
-    out_ref[...] = total.astype(jnp.bfloat16)
-
-
-def share_gradient(blocks, share):
+    gradient = total[:BLOCK_ATOMS] + total[BLOCK_ATOMS : 2 * BLOCK_ATOMS] + total[2 * BLOCK_ATOMS :]
+    fetch.wait()
+    before = old[...]
+    square = jnp.sum(before * before, axis=1, keepdims=True)
+    along = jnp.sum(gradient * before, axis=1, keepdims=True) / (square + tiny_eps)
+    out_ref[:, :entries] = (gradient - along * before).astype(jnp.bfloat16)
+    lane = lax.broadcasted_iota(jnp.int32, (BLOCK_ATOMS, LANES), 1)
+    terms = jnp.zeros((BLOCK_ATOMS, LANES), jnp.float32)
+    for i in range(3):
+        term = along.astype(jnp.bfloat16).astype(jnp.float32)
+        along = along - term
+        terms = jnp.where(lane == i, term, terms)
+    out_ref[:, entries:] = terms.astype(jnp.bfloat16)
+
+
+def share_gradient(place, blocks, dictionary, share):
     peers, rows, segment = blocks.shape
     share_rows = rows - BLOCK_ATOMS
     span = peers * segment
@@ -368,16 +394,19 @@
     source = (tap // ROWS) * (ROWS * share_rows) + (tap % ROWS) * share_rows + channel
     return pl.pallas_call(
         functools.partial(gradient_kernel, share),
-        out_shape=jax.ShapeDtypeStruct((BLOCK_ATOMS, share * L), jnp.bfloat16),
+        in_specs=[pl.BlockSpec(memory_space=pltpu.SMEM), vmem(), vmem(), pl.BlockSpec(memory_space=pl.ANY)],
+        out_shape=jax.ShapeDtypeStruct((BLOCK_ATOMS, share * L + LANES), jnp.bfloat16),
         scratch_shapes=[
             pltpu.VMEM((share_rows, span + LANES), jnp.float32),
             pltpu.VMEM((BLOCK_ATOMS, LANES + span), jnp.float32),
             pltpu.VMEM((ROWS * share_rows, span), jnp.bfloat16),
             pltpu.VMEM((COARSE * BLOCK_ATOMS, span), jnp.bfloat16),
+            pltpu.VMEM((BLOCK_ATOMS, share * L), jnp.float32),
+            pltpu.SemaphoreType.DMA,
         ],
         compiler_params=pltpu.CompilerParams(vmem_limit_bytes=VMEM_BYTES),
         name="gradient",
-    )(source[None, :], blocks)
+    )(place, source[None, :], blocks, dictionary)
 
 
 def gather_steps(peers):
@@ -408,82 +437,105 @@
     return held, exchanged(held, 1)
 
 
-def renew_kernel(place_ref, held_hbm, came_hbm, dict_hbm, out_hbm, atoms_ref, grad, old, across, sems):
+def recall_kernel(place_ref, dict_hbm, piece_ref, old_ref, mean_ref, sem):
+    del piece_ref
+    first_row = pl.multiple_of(place_ref[1], BLOCK_ATOMS)
+    fetch = pltpu.make_async_copy(dict_hbm.at[pl.ds(first_row, BLOCK_ATOMS)], old_ref, sem)
+    fetch.start()
+    fetch.wait()
+    width = 9 * LANES if old_ref.shape[1] % (9 * LANES) == 0 else LANES
+
+    def add(step, square):
+        before = old_ref[:, pl.ds(pl.multiple_of(step * width, LANES), width)]
+        return square + before * before
+
+    square = lax.fori_loop(
+        0, old_ref.shape[1] // width, add, jnp.zeros((BLOCK_ATOMS, width), jnp.float32)
+    )
+    mean_sq = jnp.sum(square, axis=1, keepdims=True) / (C * L) + tiny_eps
+    mean_ref[...] = jnp.broadcast_to(mean_sq, mean_ref.shape)
+
+
+def recall(place, dictionary, piece):
+    remote = pl.BlockSpec(memory_space=pl.ANY)
+    return pl.pallas_call(
+        recall_kernel,
+        in_specs=[pl.BlockSpec(memory_space=pltpu.SMEM), remote, remote],
+        out_specs=[vmem(), vmem()],
+        out_shape=[
+            pltpu.VMEM((BLOCK_ATOMS, dictionary.shape[1]), jnp.float32),
+            jax.ShapeDtypeStruct((BLOCK_ATOMS, LANES), jnp.float32),
+        ],
+        scratch_shapes=[pltpu.SemaphoreType.DMA],
+        compiler_params=pltpu.CompilerParams(vmem_limit_bytes=VMEM_BYTES),
+        name="recall",
+    )(place, dictionary, piece)
+
+
+def renew_kernel(place_ref, held_ref, came_ref, old, mean_ref, dict_hbm, out_hbm, atoms_ref, grad, sems):
+    del dict_hbm
     me = place_ref[0]
     first_row = pl.multiple_of(place_ref[1], BLOCK_ATOMS)
-    peers, _, width = grad.shape
+    half, _, wide = held_ref.shape
+    width = wide - LANES
     entries = C * L
-    fetch = pltpu.make_async_copy(dict_hbm.at[pl.ds(first_row, BLOCK_ATOMS)], old, sems.at[peers])
-    fetch.start()
-    pieces = []
-    for slot, flips in enumerate(gather_slots(peers)):
-        for source, extra in ((held_hbm, 0), (came_hbm, 1)):
+    shares = []
+    for slot, flips in enumerate(gather_slots(2 * half)):
+        for source, extra in ((held_ref, 0), (came_ref, 1)):
             owner = me ^ (flips + extra)
-            pieces.append(
-                pltpu.make_async_copy(source.at[slot], grad.at[owner], sems.at[2 * slot + extra])
-            )
-            pieces[-1].start()
-    for piece in pieces:
-        piece.wait()
-    fetch.wait()
-
-    def column(peer):
-        return pl.ds(pl.multiple_of(peer * width, LANES), width)
-
+            shares.append((source.at[slot], pl.ds(pl.multiple_of(owner * width, LANES), width)))
     zeros = jnp.zeros((BLOCK_ATOMS, width), jnp.float32)
-
-    def sums(peer, carry):
-        square, dot = carry
-        before = old[:, column(peer)]
-        return square + before * before, dot + grad[peer].astype(jnp.float32) * before
-
-    square, dot = lax.fori_loop(0, peers, sums, (zeros, zeros))
-    mean_sq = jnp.sum(square, axis=1, keepdims=True) / entries + tiny_eps
+    dot = zeros
+    for source, column in shares:
+        before = old[:, column]
+        along = jnp.sum(source[:, width:].astype(jnp.float32), axis=1, keepdims=True)
+        value = source[:, :width].astype(jnp.float32) + along * before
+        grad[:, column] = value
+        dot += value * before
+    mean_sq = mean_ref[:, :1]
     along = jnp.sum(dot, axis=1, keepdims=True) / entries / mean_sq
-
-    def project(peer, square):
-        value = grad[peer].astype(jnp.float32) - along * old[:, column(peer)]
-        across[:, column(peer)] = value
-        return square + value * value
-
-    square = lax.fori_loop(0, peers, project, zeros)
+    square = zeros
+    for _, column in shares:
+        value = grad[:, column] - along * old[:, column]
+        grad[:, column] = value
+        square += value * value
     spread = jnp.sum(square, axis=1, keepdims=True) / entries + tiny_eps
     step = move_rate / jnp.sqrt(spread)
     norm = 1.0 / jnp.sqrt(mean_sq + 0.25)
-
-    def renew(peer, carry):
-        atoms_ref[:, column(peer)] = (old[:, column(peer)] + step * across[:, column(peer)]) * norm
-        return carry
-
-    lax.fori_loop(0, peers, renew, 0)
-    store = pltpu.make_async_copy(atoms_ref, out_hbm.at[pl.ds(first_row, BLOCK_ATOMS)], sems.at[peers])
-    store.start()
-    store.wait()
-
-
-def renew(place, held, came, dictionary):
-    channels_taps = dictionary.shape[1]
-    peers = 2 * held.shape[0]
-    width = held.shape[2]
+    stores = []
+    for index, (_, column) in enumerate(shares):
+        atoms_ref[:, column] = (old[:, column] + step * grad[:, column]) * norm
+        stores.append(
+            pltpu.make_async_copy(
+                atoms_ref.at[:, column],
+                out_hbm.at[pl.ds(first_row, BLOCK_ATOMS), column],
+                sems.at[index],
+            )
+        )
+        stores[-1].start()
+    for store in stores:
+        store.wait()
+
+
+def renew(place, held, came, old, mean_sq, dictionary):
+    entries = dictionary.shape[1]
     remote = pl.BlockSpec(memory_space=pl.ANY)
     return pl.pallas_call(
         renew_kernel,
-        in_specs=[pl.BlockSpec(memory_space=pltpu.SMEM), remote, remote, remote],
-        out_specs=[remote, pl.BlockSpec(memory_space=pltpu.VMEM)],
+        in_specs=[pl.BlockSpec(memory_space=pltpu.SMEM)] + [vmem()] * 4 + [remote],
+        out_specs=[remote, vmem()],
         out_shape=[
             jax.ShapeDtypeStruct(dictionary.shape, jnp.float32),
-            jax.ShapeDtypeStruct((BLOCK_ATOMS, channels_taps), jnp.float32),
+            pltpu.VMEM((BLOCK_ATOMS, entries), jnp.float32),
         ],
         scratch_shapes=[
-            pltpu.VMEM((peers, BLOCK_ATOMS, width), jnp.bfloat16),
-            pltpu.VMEM((BLOCK_ATOMS, channels_taps), jnp.float32),
-            pltpu.VMEM((BLOCK_ATOMS, channels_taps), jnp.float32),
-            pltpu.SemaphoreType.DMA((peers + 1,)),
-        ],
-        input_output_aliases={3: 0},
+            pltpu.VMEM((BLOCK_ATOMS, entries), jnp.float32),
+            pltpu.SemaphoreType.DMA((2 * held.shape[0],)),
+        ],
+        input_output_aliases={5: 0},
         compiler_params=pltpu.CompilerParams(vmem_limit_bytes=VMEM_BYTES),
         name="renew",
-    )(place, held, came, dictionary)
+    )(place, held, came, resident(old), mean_sq, dictionary)
 
 
 def whole_channels(signal, codes_init, dictionary_init, threshold, plan):
@@ -492,29 +544,38 @@
     limit = threshold[None, :]
     index = lax.axis_index("tm").astype(jnp.int32)
     first_rows = [plan[step].astype(jnp.int32) * BLOCK_ATOMS for step in range(OUTER)]
+    even = index % 2
+
+    def swaps(shard):
+        ends = [range(first, peers - 1, 2) for first in (0, 1)]
+        pairs = [[p for i in end for p in ((i, i + 1), (i + 1, i))] for end in ends]
+        return [lax.ppermute(shard, "tm", pair) for pair in pairs]
+
     low = codes_init.astype(jnp.bfloat16)
-    following = shifted(jnp.concatenate([low, signal], axis=0), "tm", -1)
-    left, right = shifted(low, "tm", 1), following
+    following = swaps(jnp.concatenate([low, signal], axis=0))
+    swapped = following
     taps, dictionary = layout(dictionary_init, channels)
-    taps = taps.reshape(COARSE, ROWS, channels, K)
     code_state, atoms = codes_init, None
     for step in range(OUTER):
-        place = jnp.stack([index * segment, first_rows[step - 1] if step else first_rows[0]])
+        previous = first_rows[step - 1] if step else first_rows[0]
+        place = jnp.stack([index * segment, previous, even])
         for inner in range(INNER):
             fresh = atoms if inner == 0 else None
             results = iterate(
-                place, limit, code_state, left, right, signal, following, taps, fresh, peers
+                place, limit, code_state, swapped, signal, following, taps, fresh, peers
             )
             code_state, low = results[:2]
             if fresh is not None:
                 taps = results[2]
-            left = shifted(low, "tm", 1)
-            if step + 1 < OUTER or inner + 1 < INNER:
-                right = shifted(low, "tm", -1)
-        residual, payload = finish(first_rows[step][None], code_state, left, signal, taps, peers)
+            swapped = swaps(low)
+        place = jnp.stack([first_rows[step], even])
+        residual, payload = finish(place, code_state, swapped, signal, taps, peers)
         blocks = lax.all_to_all(payload, "tm", 0, 0, tiled=True)
-        held, came = gather_pieces(share_gradient(blocks, channels // peers))
-        dictionary, atoms = renew(jnp.stack([index, first_rows[step]]), held, came, dictionary)
+        place = jnp.stack([index, first_rows[step]])
+        piece = share_gradient(place, blocks, dictionary, channels // peers)
+        held, came = gather_pieces(piece)
+        old, mean_sq = recall(place, dictionary, piece)
+        dictionary, atoms = renew(place, held, came, old, mean_sq, dictionary)
     return code_state, dictionary, residual
 
 

time: 222 us -> 199 us (0.90)
  Pallas kernels: 101 us -> 70.6 us
  blocking collectives: 21.7 us -> 0 us
  local copies, waits for them, and re-layouts: 9.15 us -> 28.7 us
  waiting for transfers between devices: 27.1 us -> 40.7 us
  other arithmetic: 5.79 us -> 2.24 us
    all_to_all x1 -> x0, blocking collectives: 21.7 us -> none  [whole_channels(): blocks = lax.all_to_all(payload, 'tm', 0, 0, tiled=True)]
    unnamed x40 -> x36, local copies, waits for them, and re-layouts: 7.79 us -> 27.4 us
    pallas_call x4, Pallas kernels: 45 us -> 30 us  [iterate(): pl.pallas_call(functools.partial(iterate_kernel, peers * segment, patchin...]
    all_to_all x1 -> x2, waiting for transfers between devices: 9.76 us -> 20.8 us  [whole_channels(): blocks = lax.all_to_all(payload, 'tm', 0, 0, tiled=True)]
    pallas_call x2, Pallas kernels: 15.3 us -> 8.43 us  [renew(): pl.pallas_call(renew_kernel, in_specs=[pl.BlockSpec(memory_space=pltpu.SM...]
    pallas_call x2, Pallas kernels: 14.5 us -> 9.6 us  [finish(): pl.pallas_call(functools.partial(finish_kernel, peers), in_specs=[pl.Bloc...]
    pallas_call x1, Pallas kernels: 18.7 us -> 14.3 us  [layout(): pl.pallas_call(layout_kernel, grid=(channels // block,), in_specs=[pl.Blo...]
    all_to_all x1 -> x2, starting transfers between devices: 12.4 us -> 16.5 us  [whole_channels(): blocks = lax.all_to_all(payload, 'tm', 0, 0, tiled=True)]
  transfers between devices with their start and end apart: 24 -> 26, of which waited for: 13 -> 14; matrix products, arithmetic and copies ran while one was open for 3% -> 1% of each run, Pallas kernels for 12% -> 8%
where the time goes in v4:
time: 199 us; the launch traced here: 198 us
  Pallas kernels  70.6 us (35%)
  starting transfers between devices  53.8 us (27%)
  waiting for transfers between devices  40.7 us (20%)
  local copies, waits for them, and re-layouts  28.7 us (14%)
  between operations  2.48 us (1%)
  other arithmetic  2.24 us (1%)
    pallas_call x4, Pallas kernels, iterate(): pl.pallas_call(functools.partial(iterate_kernel, peers * segment, patchin...  30 us
    unnamed x36, local copies, waits for them, and re-layouts  27.4 us
    ppermute x10, starting transfers between devices, swaps(): return [lax.ppermute(shard, 'tm', pair) for pair in pairs]  21.1 us
    all_to_all x2, waiting for transfers between devices, whole_channels(): blocks = lax.all_to_all(payload, 'tm', 0, 0, tiled=True)  20.8 us
    ppermute x14, waiting for transfers between devices, exchanged(): return lax.ppermute(shard, 'tm', [(i, i ^ mask) for i in range(peers)])  17.2 us
    all_to_all x2, starting transfers between devices, whole_channels(): blocks = lax.all_to_all(payload, 'tm', 0, 0, tiled=True)  16.5 us
    ppermute x14, starting transfers between devices, exchanged(): return lax.ppermute(shard, 'tm', [(i, i ^ mask) for i in range(peers)])  16.2 us
    pallas_call x1, Pallas kernels, layout(): pl.pallas_call(layout_kernel, grid=(channels // block,), in_specs=[pl.Blo...  14.3 us
  transfers between devices with their start and end apart: 26, of which 14 were waited for; matrix products, arithmetic and copies ran while one was open for 1% of the time, Pallas kernels for 8%

profile of v4, /device:TPU:0, one launch (start us, length us, event | category | flops | bytes accessed | tf_op | source)
XLA Modules:
  0.0 198.5 jit_solution(16847325682201875334)
XLA Ops:
  3.1 4.4 %collective-permute-start = (bf16[512,128]{1,0:T(8,128)(2,1)S(1)}, bf16[512,128]{1,0:T(8,128)(2,1)S(1)}, u32[]{:S(2)}, u32[]{:S(2)}) collective-permute-start(bf16[512,128]{1,0:T(8,128)(2,1)S(1)} %pad_maximum_fusion.2), channel_id=1, source_target_pairs={{0,1},{1,0},{2,3},{3,2},{4,5},{5,4},{6,7},{7,6},{8,9},{9,8},{10,11... | collective-permute-start | bytes 393224 | tf_op jit(solution)/shard_map/ppermute | solution.py:552
  8.7 6.4 %copy-done.4 = f32[128,36864]{1,0:T(8,128)S(1)} copy-done((f32[128,36864]{1,0:T(8,128)S(1)}, f32[128,36864]{1,0:T(8,128)}, u32[]{:S(2)}) %copy-start.4) | copy-done | bytes 18874392
  15.1 14.3 %layout.1 = (bf16[6,16,384,128]{3,2,1,0:T(8,128)(2,1)S(1)}, f32[128,36864]{1,0:T(8,128)}) custom-call(f32[128,36864]{1,0:T(8,128)S(1)} %copy-done.4), custom_call_target="tpu_custom_call" | custom-call | tf_op jit(solution)/shard_map/layout/pallas_call | solution.py:91
  29.4 3.6 %copy-done.2 = bf16[6,16,384,128]{3,2,1,0:T(8,128)(2,1)} copy-done((bf16[6,16,384,128]{3,2,1,0:T(8,128)(2,1)}, bf16[6,16,384,128]{3,2,1,0:T(8,128)(2,1)S(1)}, u32[]{:S(2)}) %copy-start.2) | copy-done | bytes 9437208
  33.8 3.7 %copy-done.3 = bf16[6,16,384,128]{3,2,1,0:T(8,128)(2,1)S(1)} copy-done((bf16[6,16,384,128]{3,2,1,0:T(8,128)(2,1)S(1)}, bf16[6,16,384,128]{3,2,1,0:T(8,128)(2,1)}, u32[]{:S(2)}) %copy-start.3) | copy-done | bytes 9437208
  37.5 5.2 %iterate.4 = (f32[128,128]{1,0:T(8,128)S(1)}, bf16[128,128]{1,0:T(8,128)(2,1)S(1)}) custom-call(s32[3]{0:T(128)S(1)} %pad_add_fusion.place_ref, f32[1,128]{1,0:T(1,128)S(1)} %bitcast.18, f32[128,128]{1,0:T(8,128)S(1)} %copy-done.6, bf16[512,128]{1,0:T(8,128)(2,1)S(1)} %collective-permute-done.refs_1_.refs_4_, ...), custom_call_target="tpu_custom_call" | custom-call | tf_op jit(solution)/shard_map/iterate/pallas_call | solution.py:253
  47.2 5.2 %iterate.5 = (f32[128,128]{1,0:T(8,128)S(1)}, bf16[128,128]{1,0:T(8,128)(2,1)S(1)}) custom-call(s32[3]{0:T(128)S(1)} %pad_add_fusion.place_ref, f32[1,128]{1,0:T(1,128)S(1)} %bitcast.19, f32[128,128]{1,0:T(8,128)S(1)} %get-tuple-element.25.refs_0_, bf16[128,128]{1,0:T(8,128)(2,1)S(1)} %collective-permute-done.2.refs_1_, ...), custom_call_target="tpu_custom_call" | custom-call | tf_op jit(solution)/shard_map/iterate/pallas_call | solution.py:253
  53.0 3.7 %collective-permute-start.4 = (bf16[128,128]{1,0:T(8,128)(2,1)S(1)}, bf16[128,128]{1,0:T(8,128)(2,1)S(1)}, u32[]{:S(2)}, u32[]{:S(2)}) collective-permute-start(bf16[128,128]{1,0:T(8,128)(2,1)S(1)} %get-tuple-element.28), channel_id=1, source_target_pairs={{0,1},{1,0},{2,3},{3,2},{4,5},{5,4},{6,7},{7,6},{8,9},{9,8},{10,11... | collective-permute-start | bytes 98312 | tf_op jit(solution)/shard_map/ppermute | solution.py:552
  57.6 4.8 %finish.2 = (f32[384,128]{1,0:T(8,128)}, bf16[32,32,128]{2,1,0:T(8,128)(2,1)}) custom-call(s32[2]{0:T(128)S(1)} %pad_add_fusion.2.place_ref, f32[128,128]{1,0:T(8,128)S(1)} %get-tuple-element.27.code_ref.refs_0_, bf16[128,128]{1,0:T(8,128)(2,1)S(1)} %collective-permute-done.4.first_ref.refs_1_, ...), custom_call_target="tpu_custom_call" | custom-call | tf_op jit(solution)/shard_map/finish/pallas_call | solution.py:310
  62.4 9.2 %all-to-all-start = ((bf16[32,32,128]{2,1,0:T(8,128)(2,1)}), bf16[32,32,128]{2,1,0:T(8,128)(2,1)S(1)}, u32[]{:S(2)}, u32[]{:S(2)}) async-start(bf16[32,32,128]{2,1,0:T(8,128)(2,1)} %get-tuple-element.29), calls=%async_computation | async-start | bytes 524288 | tf_op jit(solution)/shard_map/all_to_all | solution.py:573
  71.7 10.3 %all-to-all-done.blocks_ref = bf16[32,32,128]{2,1,0:T(8,128)(2,1)S(1)} async-done(((bf16[32,32,128]{2,1,0:T(8,128)(2,1)}), bf16[32,32,128]{2,1,0:T(8,128)(2,1)S(1)}, u32[]{:S(2)}, u32[]{:S(2)}) %all-to-all-start) | async-done | bytes 262176 | tf_op jit(solution)/shard_map/all_to_all | solution.py:573
  82.0 6.4 %copy-done = f32[128,36864]{1,0:T(8,128)S(1)} copy-done((f32[128,36864]{1,0:T(8,128)S(1)}, f32[128,36864]{1,0:T(8,128)}, u32[]{:S(2)}) %copy-start) | copy-done | bytes 18874392
  101.7 5.4 %collective-permute-done.9 = bf16[4,16,1280]{2,1,0:T(8,128)(2,1)S(1)} collective-permute-done((bf16[4,16,1280]{2,1,0:T(8,128)(2,1)S(1)}, bf16[4,16,1280]{2,1,0:T(8,128)(2,1)S(1)}, u32[]{:S(2)}, u32[]{:S(2)}) %collective-permute-start.9) | collective-permute-done | bytes 163872 | tf_op jit(solution)/shard_map/ppermute | solution.py:432
  109.4 3.5 %renew.2 = (f32[128,36864]{1,0:T(8,128)}, f32[16,36864]{1,0:T(8,128)S(1)}) custom-call(s32[2]{0:T(128)S(1)} %pad_add_fusion.1.place_ref, bf16[16,16,1280]{2,1,0:T(8,128)(2,1)S(1)} %constant_dynamic-update-slice_fusion.held_ref, bf16[16,16,1280]{2,1,0:T(8,128)(2,1)S(1)} %collective-permute-done.12.came_ref, ...), custom_call_target="tpu_custom_call", output_to_operand_aliasing={{0}: (5, {})} | custom-call | tf_op jit(solution)/shard_map/renew/pallas_call | solution.py:523
  112.9 13.3 %iterate.6 = (f32[128,128]{1,0:T(8,128)S(1)}, bf16[128,128]{1,0:T(8,128)(2,1)S(1)}, bf16[6,16,384,128]{3,2,1,0:T(8,128)(2,1)S(1)}) custom-call(s32[3]{0:T(128)S(1)} %pad_add_fusion.place_ref, f32[1,128]{1,0:T(1,128)S(1)} %bitcast.20, f32[128,128]{1,0:T(8,128)S(1)} %get-tuple-element.27.code_ref.refs_0_, ...), custom_call_target="tpu_custom_call", output_to_operand_aliasing={{2}: (9, {})} | custom-call | tf_op jit(solution)/shard_map/iterate/pallas_call | solution.py:253
  126.9 3.1 %collective-permute-start.13 = (bf16[128,128]{1,0:T(8,128)(2,1)S(1)}, bf16[128,128]{1,0:T(8,128)(2,1)S(1)}, u32[]{:S(2)}, u32[]{:S(2)}) collective-permute-start(bf16[128,128]{1,0:T(8,128)(2,1)S(1)} %get-tuple-element.35), channel_id=1, source_target_pairs={{0,1},{1,0},{2,3},{3,2},{4,5},{5,4},{6,7},{7,6},{8,9},{9,8},{10,11... | collective-permute-start | bytes 98312 | tf_op jit(solution)/shard_map/ppermute | solution.py:552
  130.9 6.2 %iterate.7 = (f32[128,128]{1,0:T(8,128)}, bf16[128,128]{1,0:T(8,128)(2,1)S(1)}) custom-call(s32[3]{0:T(128)S(1)} %pad_add_fusion.place_ref, f32[1,128]{1,0:T(1,128)S(1)} %bitcast.21, f32[128,128]{1,0:T(8,128)S(1)} %get-tuple-element.34.refs_0_, bf16[128,128]{1,0:T(8,128)(2,1)S(1)} %collective-permute-done.13.refs_1_, ...), custom_call_target="tpu_custom_call" | custom-call | tf_op jit(solution)/shard_map/iterate/pallas_call | solution.py:253
  137.8 3.7 %collective-permute-start.15 = (bf16[128,128]{1,0:T(8,128)(2,1)S(1)}, bf16[128,128]{1,0:T(8,128)(2,1)S(1)}, u32[]{:S(2)}, u32[]{:S(2)}) collective-permute-start(bf16[128,128]{1,0:T(8,128)(2,1)S(1)} %get-tuple-element.38), channel_id=1, source_target_pairs={{0,1},{1,0},{2,3},{3,2},{4,5},{5,4},{6,7},{7,6},{8,9},{9,8},{10,11... | collective-permute-start | bytes 98312 | tf_op jit(solution)/shard_map/ppermute | solution.py:552
  143.2 4.8 %finish.3 = (f32[384,128]{1,0:T(8,128)}, bf16[32,32,128]{2,1,0:T(8,128)(2,1)}) custom-call(s32[2]{0:T(128)S(1)} %pad_add_fusion.4.place_ref, f32[128,128]{1,0:T(8,128)S(1)} %copy-done.7, bf16[128,128]{1,0:T(8,128)(2,1)S(1)} %collective-permute-done.15.first_ref, bf16[128,128]{1,0:T(8,128)(2,1)S(1)} %collective-permute-done.16.second_ref, ...), custom_call_target="tpu_custom_call" | custom-call | tf_op jit(solution)/shard_map/finish/pallas_call | solution.py:310
  148.1 7.3 %all-to-all-start.1 = ((bf16[32,32,128]{2,1,0:T(8,128)(2,1)}), bf16[32,32,128]{2,1,0:T(8,128)(2,1)S(1)}, u32[]{:S(2)}, u32[]{:S(2)}) async-start(bf16[32,32,128]{2,1,0:T(8,128)(2,1)} %get-tuple-element.39), calls=%async_computation.1 | async-start | bytes 524288 | tf_op jit(solution)/shard_map/all_to_all | solution.py:573
  155.5 10.5 %all-to-all-done.1.blocks_ref = bf16[32,32,128]{2,1,0:T(8,128)(2,1)S(1)} async-done(((bf16[32,32,128]{2,1,0:T(8,128)(2,1)}), bf16[32,32,128]{2,1,0:T(8,128)(2,1)S(1)}, u32[]{:S(2)}, u32[]{:S(2)}) %all-to-all-start.1) | async-done | bytes 262176 | tf_op jit(solution)/shard_map/all_to_all | solution.py:573
  166.0 6.4 %copy-done.1 = f32[128,36864]{1,0:T(8,128)S(1)} copy-done((f32[128,36864]{1,0:T(8,128)S(1)}, f32[128,36864]{1,0:T(8,128)}, u32[]{:S(2)}) %copy-start.1) | copy-done | bytes 18874392
  185.7 5.4 %collective-permute-done.20 = bf16[4,16,1280]{2,1,0:T(8,128)(2,1)S(1)} collective-permute-done((bf16[4,16,1280]{2,1,0:T(8,128)(2,1)S(1)}, bf16[4,16,1280]{2,1,0:T(8,128)(2,1)S(1)}, u32[]{:S(2)}, u32[]{:S(2)}) %collective-permute-start.20) | collective-permute-done | bytes 163872 | tf_op jit(solution)/shard_map/ppermute | solution.py:432
  193.3 4.9 %renew.3 = (f32[128,36864]{1,0:T(8,128)}, f32[16,36864]{1,0:T(8,128)}) custom-call(s32[2]{0:T(128)S(1)} %pad_add_fusion.3.place_ref, bf16[16,16,1280]{2,1,0:T(8,128)(2,1)S(1)} %constant_dynamic-update-slice_fusion.7.held_ref, bf16[16,16,1280]{2,1,0:T(8,128)(2,1)S(1)} %collective-permute-done.23.came_ref, ...), custom_call_target="tpu_custom_call", output_to_operand_aliasing={{0}: (5, {})} | custom-call | tf_op jit(solution)/shard_map/renew/pallas_call | solution.py:523
  (91 shorter events, 44.2 us)
Async XLA Ops:
  2.4 31.4 %collective-permute-start.1 = (bf16[512,128]{1,0:T(8,128)(2,1)S(1)}, bf16[512,128]{1,0:T(8,128)(2,1)S(1)}, u32[]{:S(2)}, u32[]{:S(2)}) collective-permute-start(bf16[512,128]{1,0:T(8,128)(2,1)S(1)} %pad_maximum_fusion.2), channel_id=1, source_target_pairs={{1,2},{2,1},{3,4},{4,3},{5,6},{6,5},{7,8},{8,7},{9,10},{10,9},{11,... | collective-permute-start | bytes 393224 | tf_op jit(solution)/shard_map/ppermute | solution.py:552
  3.1 30.7 %collective-permute-start = (bf16[512,128]{1,0:T(8,128)(2,1)S(1)}, bf16[512,128]{1,0:T(8,128)(2,1)S(1)}, u32[]{:S(2)}, u32[]{:S(2)}) collective-permute-start(bf16[512,128]{1,0:T(8,128)(2,1)S(1)} %pad_maximum_fusion.2), channel_id=1, source_target_pairs={{0,1},{1,0},{2,3},{3,2},{4,5},{5,4},{6,7},{7,6},{8,9},{9,8},{10,11... | collective-permute-start | bytes 393224 | tf_op jit(solution)/shard_map/ppermute | solution.py:552
  42.7 3.6 %collective-permute-start.3 = (bf16[128,128]{1,0:T(8,128)(2,1)S(1)}, bf16[128,128]{1,0:T(8,128)(2,1)S(1)}, u32[]{:S(2)}, u32[]{:S(2)}) collective-permute-start(bf16[128,128]{1,0:T(8,128)(2,1)S(1)} %get-tuple-element.26), channel_id=1, source_target_pairs={{1,2},{2,1},{3,4},{4,3},{5,6},{6,5},{7,8},{8,7},{9,10},{10,9},{11,... | collective-permute-start | bytes 98312 | tf_op jit(solution)/shard_map/ppermute | solution.py:552
  43.4 3.8 %collective-permute-start.2 = (bf16[128,128]{1,0:T(8,128)(2,1)S(1)}, bf16[128,128]{1,0:T(8,128)(2,1)S(1)}, u32[]{:S(2)}, u32[]{:S(2)}) collective-permute-start(bf16[128,128]{1,0:T(8,128)(2,1)S(1)} %get-tuple-element.26), channel_id=1, source_target_pairs={{0,1},{1,0},{2,3},{3,2},{4,5},{5,4},{6,7},{7,6},{8,9},{9,8},{10,11... | collective-permute-start | bytes 98312 | tf_op jit(solution)/shard_map/ppermute | solution.py:552
  52.4 4.4 %collective-permute-start.5 = (bf16[128,128]{1,0:T(8,128)(2,1)S(1)}, bf16[128,128]{1,0:T(8,128)(2,1)S(1)}, u32[]{:S(2)}, u32[]{:S(2)}) collective-permute-start(bf16[128,128]{1,0:T(8,128)(2,1)S(1)} %get-tuple-element.28), channel_id=1, source_target_pairs={{1,2},{2,1},{3,4},{4,3},{5,6},{6,5},{7,8},{8,7},{9,10},{10,9},{11,... | collective-permute-start | bytes 98312 | tf_op jit(solution)/shard_map/ppermute | solution.py:552
  53.0 4.6 %collective-permute-start.4 = (bf16[128,128]{1,0:T(8,128)(2,1)S(1)}, bf16[128,128]{1,0:T(8,128)(2,1)S(1)}, u32[]{:S(2)}, u32[]{:S(2)}) collective-permute-start(bf16[128,128]{1,0:T(8,128)(2,1)S(1)} %get-tuple-element.28), channel_id=1, source_target_pairs={{0,1},{1,0},{2,3},{3,2},{4,5},{5,4},{6,7},{7,6},{8,9},{9,8},{10,11... | collective-permute-start | bytes 98312 | tf_op jit(solution)/shard_map/ppermute | solution.py:552
  62.4 19.6 %all-to-all-start = ((bf16[32,32,128]{2,1,0:T(8,128)(2,1)}), bf16[32,32,128]{2,1,0:T(8,128)(2,1)S(1)}, u32[]{:S(2)}, u32[]{:S(2)}) async-start(bf16[32,32,128]{2,1,0:T(8,128)(2,1)} %get-tuple-element.29), calls=%async_computation | async-start | bytes 524288 | tf_op jit(solution)/shard_map/all_to_all | solution.py:573
  91.4 6.2 %collective-permute-start.8 = (bf16[1,16,1280]{2,1,0:T(8,128)(2,1)S(1)}, bf16[1,16,1280]{2,1,0:T(8,128)(2,1)S(1)}, u32[]{:S(2)}, u32[]{:S(2)}) collective-permute-start(bf16[1,16,1280]{2,1,0:T(8,128)(2,1)S(1)} %bitcast.14), channel_id=1, source_target_pairs={{0,24},{1,25},{2,26},{3,27},{4,28},{5,29},{6,30},{7,31},{8,16},{9,... | collective-permute-start | bytes 122888 | tf_op jit(solution)/shard_map/ppermute | solution.py:432
  92.8 4.8 %collective-permute-start.7 = (bf16[1,16,1280]{2,1,0:T(8,128)(2,1)S(1)}, bf16[1,16,1280]{2,1,0:T(8,128)(2,1)S(1)}, u32[]{:S(2)}, u32[]{:S(2)}) collective-permute-start(bf16[1,16,1280]{2,1,0:T(8,128)(2,1)S(1)} %bitcast.15), channel_id=1, source_target_pairs={{0,8},{1,9},{2,10},{3,11},{4,12},{5,13},{6,14},{7,15},{8,0},{9,1},... | collective-permute-start | bytes 122888 | tf_op jit(solution)/shard_map/ppermute | solution.py:432
  92.8 5.3 %collective-permute-start.6 = (bf16[1,16,1280]{2,1,0:T(8,128)(2,1)S(1)}, bf16[1,16,1280]{2,1,0:T(8,128)(2,1)S(1)}, u32[]{:S(2)}, u32[]{:S(2)}) collective-permute-start(bf16[1,16,1280]{2,1,0:T(8,128)(2,1)S(1)} %bitcast.16), channel_id=1, source_target_pairs={{0,16},{1,17},{2,18},{3,19},{4,20},{5,21},{6,22},{7,23},{8,24},{9,... | collective-permute-start | bytes 122888 | tf_op jit(solution)/shard_map/ppermute | solution.py:432
  98.1 9.0 %collective-permute-start.11 = (bf16[4,16,1280]{2,1,0:T(8,128)(2,1)S(1)}, bf16[4,16,1280]{2,1,0:T(8,128)(2,1)S(1)}, u32[]{:S(2)}, u32[]{:S(2)}) collective-permute-start(bf16[4,16,1280]{2,1,0:T(8,128)(2,1)S(1)} %pad_maximum_fusion), channel_id=1, source_target_pairs={{0,6},{1,7},{2,4},{3,5},{4,2},{5,3},{6,0},{7,1},{8,14},{9,15},{10,... | collective-permute-start | bytes 491528 | tf_op jit(solution)/shard_map/ppermute | solution.py:432
  99.4 7.8 %collective-permute-start.10 = (bf16[4,16,1280]{2,1,0:T(8,128)(2,1)S(1)}, bf16[4,16,1280]{2,1,0:T(8,128)(2,1)S(1)}, u32[]{:S(2)}, u32[]{:S(2)}) collective-permute-start(bf16[4,16,1280]{2,1,0:T(8,128)(2,1)S(1)} %pad_maximum_fusion), channel_id=1, source_target_pairs={{0,2},{1,3},{2,0},{3,1},{4,6},{5,7},{6,4},{7,5},{8,10},{9,11},{10,... | collective-permute-start | bytes 491528 | tf_op jit(solution)/shard_map/ppermute | solution.py:432
  100.5 6.6 %collective-permute-start.9 = (bf16[4,16,1280]{2,1,0:T(8,128)(2,1)S(1)}, bf16[4,16,1280]{2,1,0:T(8,128)(2,1)S(1)}, u32[]{:S(2)}, u32[]{:S(2)}) collective-permute-start(bf16[4,16,1280]{2,1,0:T(8,128)(2,1)S(1)} %pad_maximum_fusion), channel_id=1, source_target_pairs={{0,4},{1,5},{2,6},{3,7},{4,0},{5,1},{6,2},{7,3},{8,12},{9,13},{10,... | collective-permute-start | bytes 491528 | tf_op jit(solution)/shard_map/ppermute | solution.py:432
  126.3 4.5 %collective-permute-start.14 = (bf16[128,128]{1,0:T(8,128)(2,1)S(1)}, bf16[128,128]{1,0:T(8,128)(2,1)S(1)}, u32[]{:S(2)}, u32[]{:S(2)}) collective-permute-start(bf16[128,128]{1,0:T(8,128)(2,1)S(1)} %get-tuple-element.35), channel_id=1, source_target_pairs={{1,2},{2,1},{3,4},{4,3},{5,6},{6,5},{7,8},{8,7},{9,10},{10,9},{11,... | collective-permute-start | bytes 98312 | tf_op jit(solution)/shard_map/ppermute | solution.py:552
  126.9 4.0 %collective-permute-start.13 = (bf16[128,128]{1,0:T(8,128)(2,1)S(1)}, bf16[128,128]{1,0:T(8,128)(2,1)S(1)}, u32[]{:S(2)}, u32[]{:S(2)}) collective-permute-start(bf16[128,128]{1,0:T(8,128)(2,1)S(1)} %get-tuple-element.35), channel_id=1, source_target_pairs={{0,1},{1,0},{2,3},{3,2},{4,5},{5,4},{6,7},{7,6},{8,9},{9,8},{10,11... | collective-permute-start | bytes 98312 | tf_op jit(solution)/shard_map/ppermute | solution.py:552
  137.2 4.5 %collective-permute-start.16 = (bf16[128,128]{1,0:T(8,128)(2,1)S(1)}, bf16[128,128]{1,0:T(8,128)(2,1)S(1)}, u32[]{:S(2)}, u32[]{:S(2)}) collective-permute-start(bf16[128,128]{1,0:T(8,128)(2,1)S(1)} %get-tuple-element.38), channel_id=1, source_target_pairs={{1,2},{2,1},{3,4},{4,3},{5,6},{6,5},{7,8},{8,7},{9,10},{10,9},{11,... | collective-permute-start | bytes 98312 | tf_op jit(solution)/shard_map/ppermute | solution.py:552
  137.8 4.6 %collective-permute-start.15 = (bf16[128,128]{1,0:T(8,128)(2,1)S(1)}, bf16[128,128]{1,0:T(8,128)(2,1)S(1)}, u32[]{:S(2)}, u32[]{:S(2)}) collective-permute-start(bf16[128,128]{1,0:T(8,128)(2,1)S(1)} %get-tuple-element.38), channel_id=1, source_target_pairs={{0,1},{1,0},{2,3},{3,2},{4,5},{5,4},{6,7},{7,6},{8,9},{9,8},{10,11... | collective-permute-start | bytes 98312 | tf_op jit(solution)/shard_map/ppermute | solution.py:552
  148.1 17.9 %all-to-all-start.1 = ((bf16[32,32,128]{2,1,0:T(8,128)(2,1)}), bf16[32,32,128]{2,1,0:T(8,128)(2,1)S(1)}, u32[]{:S(2)}, u32[]{:S(2)}) async-start(bf16[32,32,128]{2,1,0:T(8,128)(2,1)} %get-tuple-element.39), calls=%async_computation.1 | async-start | bytes 524288 | tf_op jit(solution)/shard_map/all_to_all | solution.py:573
  175.3 6.2 %collective-permute-start.19 = (bf16[1,16,1280]{2,1,0:T(8,128)(2,1)S(1)}, bf16[1,16,1280]{2,1,0:T(8,128)(2,1)S(1)}, u32[]{:S(2)}, u32[]{:S(2)}) collective-permute-start(bf16[1,16,1280]{2,1,0:T(8,128)(2,1)S(1)} %bitcast.10), channel_id=1, source_target_pairs={{0,24},{1,25},{2,26},{3,27},{4,28},{5,29},{6,30},{7,31},{8,16},{9,... | collective-permute-start | bytes 122888 | tf_op jit(solution)/shard_map/ppermute | solution.py:432
  176.7 4.8 %collective-permute-start.18 = (bf16[1,16,1280]{2,1,0:T(8,128)(2,1)S(1)}, bf16[1,16,1280]{2,1,0:T(8,128)(2,1)S(1)}, u32[]{:S(2)}, u32[]{:S(2)}) collective-permute-start(bf16[1,16,1280]{2,1,0:T(8,128)(2,1)S(1)} %bitcast.11), channel_id=1, source_target_pairs={{0,8},{1,9},{2,10},{3,11},{4,12},{5,13},{6,14},{7,15},{8,0},{9,1},... | collective-permute-start | bytes 122888 | tf_op jit(solution)/shard_map/ppermute | solution.py:432
  176.8 5.3 %collective-permute-start.17 = (bf16[1,16,1280]{2,1,0:T(8,128)(2,1)S(1)}, bf16[1,16,1280]{2,1,0:T(8,128)(2,1)S(1)}, u32[]{:S(2)}, u32[]{:S(2)}) collective-permute-start(bf16[1,16,1280]{2,1,0:T(8,128)(2,1)S(1)} %bitcast.12), channel_id=1, source_target_pairs={{0,16},{1,17},{2,18},{3,19},{4,20},{5,21},{6,22},{7,23},{8,24},{9,... | collective-permute-start | bytes 122888 | tf_op jit(solution)/shard_map/ppermute | solution.py:432
  182.1 9.0 %collective-permute-start.22 = (bf16[4,16,1280]{2,1,0:T(8,128)(2,1)S(1)}, bf16[4,16,1280]{2,1,0:T(8,128)(2,1)S(1)}, u32[]{:S(2)}, u32[]{:S(2)}) collective-permute-start(bf16[4,16,1280]{2,1,0:T(8,128)(2,1)S(1)} %pad_maximum_fusion.1), channel_id=1, source_target_pairs={{0,6},{1,7},{2,4},{3,5},{4,2},{5,3},{6,0},{7,1},{8,14},{9,15},{10,... | collective-permute-start | bytes 491528 | tf_op jit(solution)/shard_map/ppermute | solution.py:432
  183.4 7.8 %collective-permute-start.21 = (bf16[4,16,1280]{2,1,0:T(8,128)(2,1)S(1)}, bf16[4,16,1280]{2,1,0:T(8,128)(2,1)S(1)}, u32[]{:S(2)}, u32[]{:S(2)}) collective-permute-start(bf16[4,16,1280]{2,1,0:T(8,128)(2,1)S(1)} %pad_maximum_fusion.1), channel_id=1, source_target_pairs={{0,2},{1,3},{2,0},{3,1},{4,6},{5,7},{6,4},{7,5},{8,10},{9,11},{10,... | collective-permute-start | bytes 491528 | tf_op jit(solution)/shard_map/ppermute | solution.py:432
  184.5 6.6 %collective-permute-start.20 = (bf16[4,16,1280]{2,1,0:T(8,128)(2,1)S(1)}, bf16[4,16,1280]{2,1,0:T(8,128)(2,1)S(1)}, u32[]{:S(2)}, u32[]{:S(2)}) collective-permute-start(bf16[4,16,1280]{2,1,0:T(8,128)(2,1)S(1)} %pad_maximum_fusion.1), channel_id=1, source_target_pairs={{0,4},{1,5},{2,6},{3,7},{4,0},{5,1},{6,2},{7,3},{8,12},{9,13},{10,... | collective-permute-start | bytes 491528 | tf_op jit(solution)/shard_map/ppermute | solution.py:432
  (14 other events, 102.4 us)

commit v5 on v4

--- a/solution.py
+++ b/solution.py
@@ -37,6 +37,22 @@
 
 def resident(value):
     return pltpu.with_memory_space_constraint(value, pltpu.VMEM)
+
+
+def far(value):
+    return pltpu.with_memory_space_constraint(value, pltpu.HBM)
+
+
+def hbm():
+    return pl.BlockSpec(memory_space=pltpu.HBM)
+
+
+def scalars():
+    return pl.BlockSpec(memory_space=pltpu.SMEM)
+
+
+def first_row_of(plan_ref, step):
+    return pl.multiple_of(plan_ref[step] * BLOCK_ATOMS, BLOCK_ATOMS)
 
 
 def vmem():
@@ -92,10 +108,10 @@
         layout_kernel,
         grid=(channels // block,),
         in_specs=[pl.BlockSpec((K, block * L), lambda i: (0, i))],
-        out_specs=[vmem(), pl.BlockSpec(memory_space=pl.ANY)],
+        out_specs=[vmem(), hbm()],
         out_shape=[
             pltpu.VMEM((COARSE, ROWS, channels, K), jnp.bfloat16),
-            jax.ShapeDtypeStruct(dictionary.shape, jnp.float32),
+            pltpu.HBM(dictionary.shape, jnp.float32),
         ],
         scratch_shapes=[
             pltpu.VMEM((ROWS * STRIDE, K), jnp.float32),
@@ -104,7 +120,7 @@
         ],
         compiler_params=pltpu.CompilerParams(vmem_limit_bytes=VMEM_BYTES),
         name="layout",
-    )(dictionary)
+    )(far(dictionary))
 
 
 def convolve(zb, begin, count, taps, zz, fine, acc):
@@ -164,34 +180,35 @@
         acc[0, :count, :] = total
 
 
-def patch_taps(row, atoms_ref, taps, columns, even, odd):
+def patch_taps(row, atoms_ref, taps, columns, turned):
     channels = taps.shape[2]
     lane = lax.broadcasted_iota(jnp.int32, (ROWS, K), 1)
     renewed = (lane >= row) & (lane < row + BLOCK_ATOMS)
-    columns[...] = jnp.zeros_like(columns)
+    groups = K // BLOCK_ATOMS
+    width = ROWS * L
 
     def patch(step, carry):
-        width = 2 * ROWS * L
-        part = pl.ds(pl.multiple_of(step * width, LANES), width)
-        columns[pl.ds(row, BLOCK_ATOMS), :] = atoms_ref[:, part]
-        turn(columns, 0, even)
-        turn(columns, ROWS * L, odd)
-        for half, turned in ((0, even), (1, odd)):
-            own = pl.ds(pl.multiple_of((2 * step + half) * ROWS, ROWS), ROWS)
-            for tap in range(L):
-                fresh = turned[pl.ds(tap, ROWS, stride=STRIDE), :]
+        for group in range(groups):
+            part = pl.ds(pl.multiple_of((step * groups + group) * width, LANES), width)
+            columns[group * BLOCK_ATOMS : (group + 1) * BLOCK_ATOMS, :] = atoms_ref[:, part]
+        turn(columns, 0, turned)
+        for tap in range(L):
+            fresh = turned[pl.ds(tap, ROWS, stride=STRIDE), :]
+            for group in range(groups):
+                placed = pltpu.roll(fresh, (row + K - group * BLOCK_ATOMS) % K, 1)
+                own = pl.ds(pl.multiple_of((step * groups + group) * ROWS, ROWS), ROWS)
                 kept = taps[tap // ROWS, tap % ROWS, own, :].astype(jnp.float32)
-                taps[tap // ROWS, tap % ROWS, own, :] = jnp.where(renewed, fresh, kept).astype(
+                taps[tap // ROWS, tap % ROWS, own, :] = jnp.where(renewed, placed, kept).astype(
                     jnp.bfloat16
                 )
         return carry
 
-    lax.fori_loop(0, channels // (2 * ROWS), patch, 0)
+    lax.fori_loop(0, channels // (groups * ROWS), patch, 0)
 
 
 def put_codes(zb, own, first_ref, second_ref, even):
     segment = own.shape[1]
-    zb[L : L + segment, :] = own[...].T.astype(jnp.bfloat16)
+    zb[L : L + segment, :] = own[...].astype(jnp.float32).T.astype(jnp.bfloat16)
 
     def put(left, right):
         zb[:L, :] = left[:K, :].astype(jnp.float32).T[segment - L :].astype(jnp.bfloat16)
@@ -202,7 +219,7 @@
     pl.when(jnp.logical_not(even))(lambda: put(first_ref, second_ref))
 
 
-def iterate_kernel(total_time, patching, place_ref, limit_ref, *refs):
+def iterate_kernel(total_time, patching, plan_ref, limit_ref, *refs):
     code_ref, first_ref, second_ref, signal_ref, next_first, next_second = refs[:6]
     refs = refs[6:]
     if patching:
@@ -215,7 +232,8 @@
     channels, segment = signal_ref.shape
     tiles = channels // LANES
     scale = (C * L) ** (-0.5)
-    even = place_ref[2] == 0
+    me = lax.axis_index("tm")
+    even = me % 2 == 0
     put_codes(zb, code_ref, first_ref, second_ref, even)
 
     def put(following):
@@ -227,11 +245,11 @@
     pl.when(even)(lambda: put(next_first))
     pl.when(jnp.logical_not(even))(lambda: put(next_second))
     if patching:
-        columns, even_ref, odd_ref = refs[7:]
-        patch_taps(pl.multiple_of(place_ref[1], BLOCK_ATOMS), atoms_ref, taps, columns, even_ref, odd_ref)
+        columns, turned = refs[7:]
+        patch_taps(first_row_of(plan_ref, patching - 1), atoms_ref, taps, columns, turned)
     reach = segment + L
     convolve(zb, L, reach, taps, zz, fine, acc)
-    moment = place_ref[0] + lax.broadcasted_iota(jnp.int32, (reach, LANES), 0)
+    moment = me * segment + lax.broadcasted_iota(jnp.int32, (reach, LANES), 0)
     inside = moment < total_time
     for tile in range(tiles):
         column = slice(tile * LANES, (tile + 1) * LANES)
@@ -246,13 +264,13 @@
     low_out[...] = state.astype(jnp.bfloat16)
 
 
-def iterate(place, limit, code, swapped, signal, following, taps, atoms, peers):
+def iterate(plan, step, limit, code, swapped, signal, following, taps, atoms, peers):
     channels, segment = signal.shape
     patching = atoms is not None
     reach = segment + L
     return pl.pallas_call(
-        functools.partial(iterate_kernel, peers * segment, patching),
-        in_specs=[pl.BlockSpec(memory_space=pltpu.SMEM)] + [vmem()] * (8 + patching),
+        functools.partial(iterate_kernel, peers * segment, step if patching else 0),
+        in_specs=[scalars()] + [vmem()] * (8 + patching),
         out_specs=[vmem()] * (2 + patching),
         out_shape=[
             jax.ShapeDtypeStruct((K, segment), jnp.float32),
@@ -269,31 +287,29 @@
             pltpu.VMEM((L, channels), jnp.float32),
         ]
         + [
-            pltpu.VMEM((K, 2 * ROWS * L), jnp.float32),
-            pltpu.VMEM((ROWS * STRIDE, K), jnp.float32),
+            pltpu.VMEM((K, ROWS * L), jnp.float32),
             pltpu.VMEM((ROWS * STRIDE, K), jnp.float32),
         ]
         * patching,
         input_output_aliases={9: 2} if patching else {},
         compiler_params=pltpu.CompilerParams(vmem_limit_bytes=VMEM_BYTES),
         name="iterate",
-    )(place, limit, code, *swapped, signal, *following, *([resident(atoms)] if patching else []), resident(taps))
+    )(plan, limit, code, *swapped, signal, *following, *([resident(atoms)] if patching else []), resident(taps))
 
 
 def finish_kernel(
-    peers, place_ref, code_ref, first_ref, second_ref, signal_ref, taps, resid_out, payload_out, zb, zz, fine, acc, tall
+    peers, step, plan_ref, low_ref, first_ref, second_ref, signal_ref, taps, resid_out, payload_out, zb, zz, fine, acc, tall
 ):
     channels, segment = signal_ref.shape
     scale = (C * L) ** (-0.5)
-    put_codes(zb, code_ref, first_ref, second_ref, place_ref[1] == 0)
+    put_codes(zb, low_ref, first_ref, second_ref, lax.axis_index("tm") % 2 == 0)
     convolve(zb, L, segment, taps, zz, fine, acc)
     for tile in range(channels // LANES):
         column = slice(tile * LANES, (tile + 1) * LANES)
         value = signal_ref[column, :].astype(jnp.float32) - scale * acc[tile, :segment, :].T
         resid_out[column, :] = value
         tall[column, :] = value
-    row = pl.multiple_of(place_ref[0], BLOCK_ATOMS)
-    block = code_ref[pl.ds(row, BLOCK_ATOMS), :].astype(jnp.bfloat16)
+    block = low_ref[pl.ds(first_row_of(plan_ref, step), BLOCK_ATOMS), :]
     share = channels // peers
     share_rows = payload_out.shape[1] - BLOCK_ATOMS
     tall[channels:, :] = jnp.zeros((tall.shape[0] - channels, segment), jnp.float32)
@@ -303,13 +319,13 @@
         payload_out[peer, share_rows:, :] = block
 
 
-def finish(place, code, swapped, signal, taps, peers):
+def finish(plan, step, low, swapped, signal, taps, peers):
     channels, segment = signal.shape
     share = channels // peers
     share_rows = -(-share // ROWS) * ROWS
     return pl.pallas_call(
-        functools.partial(finish_kernel, peers),
-        in_specs=[pl.BlockSpec(memory_space=pltpu.SMEM)] + [vmem()] * 5,
+        functools.partial(finish_kernel, peers, step),
+        in_specs=[scalars()] + [vmem()] * 5,
         out_specs=[vmem(), vmem()],
         out_shape=[
             jax.ShapeDtypeStruct((channels, segment), jnp.float32),
@@ -324,16 +340,16 @@
         ],
         compiler_params=pltpu.CompilerParams(vmem_limit_bytes=VMEM_BYTES),
         name="finish",
-    )(place, code, *swapped, signal, resident(taps))
-
-
-def gradient_kernel(share, place_ref, source_ref, blocks_ref, dict_hbm, out_ref, rf, zf, rr, zz, old, sem):
+    )(plan, low, *swapped, signal, resident(taps))
+
+
+def gradient_kernel(share, step, plan_ref, source_ref, blocks_ref, dict_hbm, out_ref, rf, zf, rr, zz, old, sem):
     peers, rows, segment = blocks_ref.shape
     share_rows = rows - BLOCK_ATOMS
     span = peers * segment
     entries = share * L
-    rows_of = pl.ds(pl.multiple_of(place_ref[1], BLOCK_ATOMS), BLOCK_ATOMS)
-    columns_of = pl.ds(pl.multiple_of(place_ref[0] * entries, LANES), entries)
+    rows_of = pl.ds(first_row_of(plan_ref, step), BLOCK_ATOMS)
+    columns_of = pl.ds(pl.multiple_of(lax.axis_index("tm") * entries, LANES), entries)
     fetch = pltpu.make_async_copy(dict_hbm.at[rows_of, columns_of], old, sem)
     fetch.start()
     rf[:, span:] = jnp.zeros((share_rows, LANES), jnp.float32)
@@ -385,7 +401,7 @@
     out_ref[:, entries:] = terms.astype(jnp.bfloat16)
 
 
-def share_gradient(place, blocks, dictionary, share):
+def share_gradient(plan, step, blocks, dictionary, share):
     peers, rows, segment = blocks.shape
     share_rows = rows - BLOCK_ATOMS
     span = peers * segment
@@ -393,8 +409,8 @@
     channel, tap = entry // L, entry % L
     source = (tap // ROWS) * (ROWS * share_rows) + (tap % ROWS) * share_rows + channel
     return pl.pallas_call(
-        functools.partial(gradient_kernel, share),
-        in_specs=[pl.BlockSpec(memory_space=pltpu.SMEM), vmem(), vmem(), pl.BlockSpec(memory_space=pl.ANY)],
+        functools.partial(gradient_kernel, share, step),
+        in_specs=[scalars(), vmem(), vmem(), hbm()],
         out_shape=jax.ShapeDtypeStruct((BLOCK_ATOMS, share * L + LANES), jnp.bfloat16),
         scratch_shapes=[
             pltpu.VMEM((share_rows, span + LANES), jnp.float32),
@@ -406,7 +422,7 @@
         ],
         compiler_params=pltpu.CompilerParams(vmem_limit_bytes=VMEM_BYTES),
         name="gradient",
-    )(place, source[None, :], blocks, dictionary)
+    )(plan, source[None, :], blocks, far(dictionary))
 
 
 def gather_steps(peers):
@@ -437,9 +453,9 @@
     return held, exchanged(held, 1)
 
 
-def recall_kernel(place_ref, dict_hbm, piece_ref, old_ref, mean_ref, sem):
+def recall_kernel(step, plan_ref, dict_hbm, piece_ref, old_ref, mean_ref, sem):
     del piece_ref
-    first_row = pl.multiple_of(place_ref[1], BLOCK_ATOMS)
+    first_row = first_row_of(plan_ref, step)
     fetch = pltpu.make_async_copy(dict_hbm.at[pl.ds(first_row, BLOCK_ATOMS)], old_ref, sem)
     fetch.start()
     fetch.wait()
@@ -456,11 +472,10 @@
     mean_ref[...] = jnp.broadcast_to(mean_sq, mean_ref.shape)
 
 
-def recall(place, dictionary, piece):
-    remote = pl.BlockSpec(memory_space=pl.ANY)
+def recall(plan, step, dictionary, piece):
     return pl.pallas_call(
-        recall_kernel,
-        in_specs=[pl.BlockSpec(memory_space=pltpu.SMEM), remote, remote],
+        functools.partial(recall_kernel, step),
+        in_specs=[scalars(), hbm(), pl.BlockSpec(memory_space=pl.ANY)],
         out_specs=[vmem(), vmem()],
         out_shape=[
             pltpu.VMEM((BLOCK_ATOMS, dictionary.shape[1]), jnp.float32),
@@ -469,13 +484,13 @@
         scratch_shapes=[pltpu.SemaphoreType.DMA],
         compiler_params=pltpu.CompilerParams(vmem_limit_bytes=VMEM_BYTES),
         name="recall",
-    )(place, dictionary, piece)
-
-
-def renew_kernel(place_ref, held_ref, came_ref, old, mean_ref, dict_hbm, out_hbm, atoms_ref, grad, sems):
+    )(plan, far(dictionary), piece)
+
+
+def renew_kernel(plan_step, plan_ref, held_ref, came_ref, old, mean_ref, dict_hbm, out_hbm, atoms_ref, grad, sems):
     del dict_hbm
-    me = place_ref[0]
-    first_row = pl.multiple_of(place_ref[1], BLOCK_ATOMS)
+    me = lax.axis_index("tm")
+    first_row = first_row_of(plan_ref, plan_step)
     half, _, wide = held_ref.shape
     width = wide - LANES
     entries = C * L
@@ -517,15 +532,14 @@
         store.wait()
 
 
-def renew(place, held, came, old, mean_sq, dictionary):
+def renew(plan, step, held, came, old, mean_sq, dictionary):
     entries = dictionary.shape[1]
-    remote = pl.BlockSpec(memory_space=pl.ANY)
     return pl.pallas_call(
-        renew_kernel,
-        in_specs=[pl.BlockSpec(memory_space=pltpu.SMEM)] + [vmem()] * 4 + [remote],
-        out_specs=[remote, vmem()],
+        functools.partial(renew_kernel, step),
+        in_specs=[scalars()] + [vmem()] * 4 + [hbm()],
+        out_specs=[hbm(), vmem()],
         out_shape=[
-            jax.ShapeDtypeStruct(dictionary.shape, jnp.float32),
+            pltpu.HBM(dictionary.shape, jnp.float32),
             pltpu.VMEM((BLOCK_ATOMS, entries), jnp.float32),
         ],
         scratch_shapes=[
@@ -535,17 +549,13 @@
         input_output_aliases={5: 0},
         compiler_params=pltpu.CompilerParams(vmem_limit_bytes=VMEM_BYTES),
         name="renew",
-    )(place, held, came, resident(old), mean_sq, dictionary)
+    )(plan, held, came, resident(old), mean_sq, far(dictionary))
 
 
 def whole_channels(signal, codes_init, dictionary_init, threshold, plan):
     channels, segment = signal.shape
     peers = lax.axis_size("tm")
     limit = threshold[None, :]
-    index = lax.axis_index("tm").astype(jnp.int32)
-    first_rows = [plan[step].astype(jnp.int32) * BLOCK_ATOMS for step in range(OUTER)]
-    even = index % 2
-
     def swaps(shard):
         ends = [range(first, peers - 1, 2) for first in (0, 1)]
         pairs = [[p for i in end for p in ((i, i + 1), (i + 1, i))] for end in ends]
@@ -557,25 +567,21 @@
     taps, dictionary = layout(dictionary_init, channels)
     code_state, atoms = codes_init, None
     for step in range(OUTER):
-        previous = first_rows[step - 1] if step else first_rows[0]
-        place = jnp.stack([index * segment, previous, even])
         for inner in range(INNER):
             fresh = atoms if inner == 0 else None
             results = iterate(
-                place, limit, code_state, swapped, signal, following, taps, fresh, peers
+                plan, step, limit, code_state, swapped, signal, following, taps, fresh, peers
             )
             code_state, low = results[:2]
             if fresh is not None:
                 taps = results[2]
             swapped = swaps(low)
-        place = jnp.stack([first_rows[step], even])
-        residual, payload = finish(place, code_state, swapped, signal, taps, peers)
+        residual, payload = finish(plan, step, low, swapped, signal, taps, peers)
         blocks = lax.all_to_all(payload, "tm", 0, 0, tiled=True)
-        place = jnp.stack([index, first_rows[step]])
-        piece = share_gradient(place, blocks, dictionary, channels // peers)
+        piece = share_gradient(plan, step, blocks, dictionary, channels // peers)
         held, came = gather_pieces(piece)
-        old, mean_sq = recall(place, dictionary, piece)
-        dictionary, atoms = renew(place, held, came, old, mean_sq, dictionary)
+        old, mean_sq = recall(plan, step, dictionary, piece)
+        dictionary, atoms = renew(plan, step, held, came, old, mean_sq, dictionary)
     return code_state, dictionary, residual
 
 

time: 199 us -> 178 us (0.89)
  local copies, waits for them, and re-layouts: 28.7 us -> 0.15 us
  blocking collectives: 0 us -> 18 us
  waiting for transfers between devices: 40.7 us -> 29.2 us
  Pallas kernels: 70.6 us -> 80.8 us
  starting transfers between devices: 53.8 us -> 46.6 us
    unnamed x36 -> x28, local copies, waits for them, and re-layouts: 27.4 us -> 0.13 us
    all_to_all x0 -> x1, blocking collectives: none -> 18 us  [whole_channels(): blocks = lax.all_to_all(payload, 'tm', 0, 0, tiled=True)]
    all_to_all x2 -> x1, waiting for transfers between devices: 20.8 us -> 10.4 us  [whole_channels(): blocks = lax.all_to_all(payload, 'tm', 0, 0, tiled=True)]
    pallas_call x12, Pallas kernels: 56.3 us -> 64.3 us  [the longest x4 33.4 us: iterate(): pl.pallas_call(functools.partial(iterate_kernel, peers * segment, step if...]
    all_to_all x2 -> x1, starting transfers between devices: 16.5 us -> 9.22 us  [whole_channels(): blocks = lax.all_to_all(payload, 'tm', 0, 0, tiled=True)]
    pallas_call x1, Pallas kernels: 14.3 us -> 16.4 us  [layout(): pl.pallas_call(layout_kernel, grid=(channels // block,), in_specs=[pl.Blo...]
  transfers between devices with their start and end apart: 26 -> 25, of which waited for: 14 -> 11; matrix products, arithmetic and copies ran while one was open for 1% -> 0% of each run, Pallas kernels for 8% -> 12%
where the time goes in v5:
time: 178 us
  Pallas kernels  80.8 us (45%)
  starting transfers between devices  46.6 us (26%)
  waiting for transfers between devices  29.2 us (16%)
  blocking collectives  18 us (10%)
  other arithmetic  1.86 us (1%)
    pallas_call x4, Pallas kernels, iterate(): pl.pallas_call(functools.partial(iterate_kernel, peers * segment, step if...  33.4 us
    ppermute x10, starting transfers between devices, swaps(): return [lax.ppermute(shard, 'tm', pair) for pair in pairs]  21.3 us
    all_to_all x1, blocking collectives, whole_channels(): blocks = lax.all_to_all(payload, 'tm', 0, 0, tiled=True)  18 us
    pallas_call x1, Pallas kernels, layout(): pl.pallas_call(layout_kernel, grid=(channels // block,), in_specs=[pl.Blo...  16.4 us
    ppermute x14, starting transfers between devices, exchanged(): return lax.ppermute(shard, 'tm', [(i, i ^ mask) for i in range(peers)])  16.2 us
    ppermute x14, waiting for transfers between devices, exchanged(): return lax.ppermute(shard, 'tm', [(i, i ^ mask) for i in range(peers)])  15.4 us
    all_to_all x1, waiting for transfers between devices, whole_channels(): blocks = lax.all_to_all(payload, 'tm', 0, 0, tiled=True)  10.4 us
    pallas_call x2, Pallas kernels, finish(): pl.pallas_call(functools.partial(finish_kernel, peers, step), in_specs=[s...  9.58 us
  transfers between devices with their start and end apart: 25, of which 11 were waited for; matrix products, arithmetic and copies ran while one was open for 0% of the time, Pallas kernels for 12%

profile of v5, /device:TPU:0, one launch (start us, length us, event | category | flops | bytes accessed | tf_op | source)
XLA Modules:
  0.0 177.9 jit_solution(10612033671537065493)
XLA Ops:
  3.2 4.4 %collective-permute-start = (bf16[512,128]{1,0:T(8,128)(2,1)S(1)}, bf16[512,128]{1,0:T(8,128)(2,1)S(1)}, u32[]{:S(2)}, u32[]{:S(2)}) collective-permute-start(bf16[512,128]{1,0:T(8,128)(2,1)S(1)} %pad_maximum_fusion.2), channel_id=1, source_target_pairs={{0,1},{1,0},{2,3},{3,2},{4,5},{5,4},{6,7},{7,6},{8,9},{9,8},{10,11... | collective-permute-start | bytes 393224 | tf_op jit(solution)/shard_map/ppermute | solution.py:562
  7.6 16.4 %layout.1 = (bf16[6,16,384,128]{3,2,1,0:T(8,128)(2,1)S(1)}, f32[128,36864]{1,0:T(8,128)}) custom-call(f32[128,36864]{1,0:T(8,128)} %dict_ref.1), custom_call_target="tpu_custom_call" | custom-call | tf_op jit(solution)/shard_map/layout/pallas_call | solution.py:107
  24.1 5.4 %iterate.4 = (f32[128,128]{1,0:T(8,128)S(1)}, bf16[128,128]{1,0:T(8,128)(2,1)S(1)}) custom-call(s32[8]{0:T(128)S(1)} %copy-done.3, f32[1,128]{1,0:T(1,128)S(1)} %bitcast.15, f32[128,128]{1,0:T(8,128)S(1)} %copy-done.2, bf16[512,128]{1,0:T(8,128)(2,1)S(1)} %collective-permute-done.refs_1_.refs_4_, ...), custom_call_target="tpu_custom_call" | custom-call | tf_op jit(solution)/shard_map/iterate/pallas_call | solution.py:271
  30.2 2.9 %collective-permute-start.2 = (bf16[128,128]{1,0:T(8,128)(2,1)S(1)}, bf16[128,128]{1,0:T(8,128)(2,1)S(1)}, u32[]{:S(2)}, u32[]{:S(2)}) collective-permute-start(bf16[128,128]{1,0:T(8,128)(2,1)S(1)} %get-tuple-element.26), channel_id=1, source_target_pairs={{0,1},{1,0},{2,3},{3,2},{4,5},{5,4},{6,7},{7,6},{8,9},{9,8},{10,11... | collective-permute-start | bytes 98312 | tf_op jit(solution)/shard_map/ppermute | solution.py:562
  34.0 5.4 %iterate.5 = (f32[128,128]{1,0:T(8,128)S(1)}, bf16[128,128]{1,0:T(8,128)(2,1)S(1)}) custom-call(s32[8]{0:T(128)S(1)} %copy-done.3, f32[1,128]{1,0:T(1,128)S(1)} %bitcast.16, f32[128,128]{1,0:T(8,128)S(1)} %get-tuple-element.25.refs_0_, bf16[128,128]{1,0:T(8,128)(2,1)S(1)} %collective-permute-done.2.refs_1_, ...), custom_call_target="tpu_custom_call" | custom-call | tf_op jit(solution)/shard_map/iterate/pallas_call | solution.py:271
  40.0 3.7 %collective-permute-start.4 = (bf16[128,128]{1,0:T(8,128)(2,1)S(1)}, bf16[128,128]{1,0:T(8,128)(2,1)S(1)}, u32[]{:S(2)}, u32[]{:S(2)}) collective-permute-start(bf16[128,128]{1,0:T(8,128)(2,1)S(1)} %get-tuple-element.28.low_ref), channel_id=1, source_target_pairs={{0,1},{1,0},{2,3},{3,2},{4,5},{5,4},{6,7},{7,6},{8,9},{9,8},{10,11... | collective-permute-start | bytes 98312 | tf_op jit(solution)/shard_map/ppermute | solution.py:562
  44.6 4.8 %finish.2 = (f32[384,128]{1,0:T(8,128)}, bf16[32,32,128]{2,1,0:T(8,128)(2,1)}) custom-call(s32[8]{0:T(128)S(1)} %copy-done.3, bf16[128,128]{1,0:T(8,128)(2,1)S(1)} %get-tuple-element.28.low_ref, bf16[128,128]{1,0:T(8,128)(2,1)S(1)} %collective-permute-done.4.first_ref.refs_1_, bf16[128,128]{1,0:T(8,128)(2,1)S(1)} %collective-permute-done.5.second_ref.refs_2_, ...), custom_call_target="tpu_custom_call" | custom-call | tf_op jit(solution)/shard_map/finish/pallas_call | solution.py:326
  49.4 9.2 %all-to-all-start = ((bf16[32,32,128]{2,1,0:T(8,128)(2,1)}), bf16[32,32,128]{2,1,0:T(8,128)(2,1)S(1)}, u32[]{:S(2)}, u32[]{:S(2)}) async-start(bf16[32,32,128]{2,1,0:T(8,128)(2,1)} %get-tuple-element.29), calls=%async_computation | async-start | bytes 524288 | tf_op jit(solution)/shard_map/all_to_all | solution.py:580
  58.7 10.4 %all-to-all-done.blocks_ref = bf16[32,32,128]{2,1,0:T(8,128)(2,1)S(1)} async-done(((bf16[32,32,128]{2,1,0:T(8,128)(2,1)}), bf16[32,32,128]{2,1,0:T(8,128)(2,1)S(1)}, u32[]{:S(2)}, u32[]{:S(2)}) %all-to-all-start) | async-done | bytes 262176 | tf_op jit(solution)/shard_map/all_to_all | solution.py:580
  69.1 3.7 %gradient.2.piece_ref = bf16[16,1280]{1,0:T(8,128)(2,1)S(1)} custom-call(s32[8]{0:T(128)S(1)} %copy-done.3, s32[1,1152]{1,0:T(1,128)S(1)} %fusion.source_ref, bf16[32,32,128]{2,1,0:T(8,128)(2,1)S(1)} %all-to-all-done.blocks_ref, f32[128,36864]{1,0:T(8,128)} %get-tuple-element.30.dict_hbm), custom_call_target="tpu_custom_call" | custom-call | tf_op jit(solution)/shard_map/gradient/pallas_call | solution.py:411
  74.2 3.1 %collective-permute-start.6 = (bf16[1,16,1280]{2,1,0:T(8,128)(2,1)S(1)}, bf16[1,16,1280]{2,1,0:T(8,128)(2,1)S(1)}, u32[]{:S(2)}, u32[]{:S(2)}) collective-permute-start(bf16[1,16,1280]{2,1,0:T(8,128)(2,1)S(1)} %bitcast.13), channel_id=1, source_target_pairs={{0,16},{1,17},{2,18},{3,19},{4,20},{5,21},{6,22},{7,23},{8,24},{9,... | collective-permute-start | bytes 122888 | tf_op jit(solution)/shard_map/ppermute | solution.py:448
  83.1 5.4 %collective-permute-done.9 = bf16[4,16,1280]{2,1,0:T(8,128)(2,1)S(1)} collective-permute-done((bf16[4,16,1280]{2,1,0:T(8,128)(2,1)S(1)}, bf16[4,16,1280]{2,1,0:T(8,128)(2,1)S(1)}, u32[]{:S(2)}, u32[]{:S(2)}) %collective-permute-start.9) | collective-permute-done | bytes 163872 | tf_op jit(solution)/shard_map/ppermute | solution.py:448
  88.7 2.9 %recall.2 = (f32[16,36864]{1,0:T(8,128)S(1)}, f32[16,128]{1,0:T(8,128)S(1)}) custom-call(s32[8]{0:T(128)S(1)} %copy-done.3, f32[128,36864]{1,0:T(8,128)} %get-tuple-element.30.dict_hbm, bf16[16,1280]{1,0:T(8,128)(2,1)S(1)} %gradient.2.piece_ref), custom_call_target="tpu_custom_call" | custom-call | tf_op jit(solution)/shard_map/recall/pallas_call | solution.py:476
  91.6 3.5 %renew.2 = (f32[128,36864]{1,0:T(8,128)}, f32[16,36864]{1,0:T(8,128)S(1)}) custom-call(s32[8]{0:T(128)S(1)} %copy-done.3, bf16[16,16,1280]{2,1,0:T(8,128)(2,1)S(1)} %constant_dynamic-update-slice_fusion.held_ref, bf16[16,16,1280]{2,1,0:T(8,128)(2,1)S(1)} %collective-permute-done.12.came_ref, ...), custom_call_target="tpu_custom_call", output_to_operand_aliasing={{0}: (5, {})} | custom-call | tf_op jit(solution)/shard_map/renew/pallas_call | solution.py:537
  95.2 16.2 %iterate.6 = (f32[128,128]{1,0:T(8,128)S(1)}, bf16[128,128]{1,0:T(8,128)(2,1)S(1)}, bf16[6,16,384,128]{3,2,1,0:T(8,128)(2,1)S(1)}) custom-call(s32[8]{0:T(128)S(1)} %copy-done.3, f32[1,128]{1,0:T(1,128)S(1)} %bitcast.17, f32[128,128]{1,0:T(8,128)S(1)} %get-tuple-element.27.refs_0_, ...), custom_call_target="tpu_custom_call", output_to_operand_aliasing={{2}: (9, {})} | custom-call | tf_op jit(solution)/shard_map/iterate/pallas_call | solution.py:271
  112.1 3.1 %collective-permute-start.13 = (bf16[128,128]{1,0:T(8,128)(2,1)S(1)}, bf16[128,128]{1,0:T(8,128)(2,1)S(1)}, u32[]{:S(2)}, u32[]{:S(2)}) collective-permute-start(bf16[128,128]{1,0:T(8,128)(2,1)S(1)} %get-tuple-element.35), channel_id=1, source_target_pairs={{0,1},{1,0},{2,3},{3,2},{4,5},{5,4},{6,7},{7,6},{8,9},{9,8},{10,11... | collective-permute-start | bytes 98312 | tf_op jit(solution)/shard_map/ppermute | solution.py:562
  116.1 6.4 %iterate.7 = (f32[128,128]{1,0:T(8,128)}, bf16[128,128]{1,0:T(8,128)(2,1)S(1)}) custom-call(s32[8]{0:T(128)S(1)} %copy-done.3, f32[1,128]{1,0:T(1,128)S(1)} %bitcast.18, f32[128,128]{1,0:T(8,128)S(1)} %get-tuple-element.34.refs_0_, bf16[128,128]{1,0:T(8,128)(2,1)S(1)} %collective-permute-done.13.refs_1_, ...), custom_call_target="tpu_custom_call" | custom-call | tf_op jit(solution)/shard_map/iterate/pallas_call | solution.py:271
  123.1 3.7 %collective-permute-start.15 = (bf16[128,128]{1,0:T(8,128)(2,1)S(1)}, bf16[128,128]{1,0:T(8,128)(2,1)S(1)}, u32[]{:S(2)}, u32[]{:S(2)}) collective-permute-start(bf16[128,128]{1,0:T(8,128)(2,1)S(1)} %get-tuple-element.38.low_ref), channel_id=1, source_target_pairs={{0,1},{1,0},{2,3},{3,2},{4,5},{5,4},{6,7},{7,6},{8,9},{9,8},{10,11... | collective-permute-start | bytes 98312 | tf_op jit(solution)/shard_map/ppermute | solution.py:562
  127.7 4.8 %finish.3 = (f32[384,128]{1,0:T(8,128)}, bf16[32,32,128]{2,1,0:T(8,128)(2,1)S(1)}) custom-call(s32[8]{0:T(128)S(1)} %copy-done.3, bf16[128,128]{1,0:T(8,128)(2,1)S(1)} %get-tuple-element.38.low_ref, bf16[128,128]{1,0:T(8,128)(2,1)S(1)} %collective-permute-done.15.first_ref, bf16[128,128]{1,0:T(8,128)(2,1)S(1)} %collective-permute-done.16.second_ref, ...), custom_call_target="tpu_custom_call" | custom-call | tf_op jit(solution)/shard_map/finish/pallas_call | solution.py:326
  132.5 18.0 %all_to_all.10.blocks_ref = bf16[32,32,128]{2,1,0:T(8,128)(2,1)S(1)} all-to-all(bf16[32,32,128]{2,1,0:T(8,128)(2,1)S(1)} %get-tuple-element.39), channel_id=1, replica_groups=mesh['tm'=32,'chan'=1] {'tm'}, dimensions={0} | all-to-all | bytes 524288 | tf_op jit(solution)/shard_map/all_to_all | solution.py:580
  150.5 3.7 %gradient.3.piece_ref = bf16[16,1280]{1,0:T(8,128)(2,1)S(1)} custom-call(s32[8]{0:T(128)S(1)} %copy-done.3, s32[1,1152]{1,0:T(1,128)S(1)} %fusion.source_ref, bf16[32,32,128]{2,1,0:T(8,128)(2,1)S(1)} %all_to_all.10.blocks_ref, f32[128,36864]{1,0:T(8,128)} %get-tuple-element.40.dict_hbm), custom_call_target="tpu_custom_call" | custom-call | tf_op jit(solution)/shard_map/gradient/pallas_call | solution.py:411
  155.6 3.1 %collective-permute-start.17 = (bf16[1,16,1280]{2,1,0:T(8,128)(2,1)S(1)}, bf16[1,16,1280]{2,1,0:T(8,128)(2,1)S(1)}, u32[]{:S(2)}, u32[]{:S(2)}) collective-permute-start(bf16[1,16,1280]{2,1,0:T(8,128)(2,1)S(1)} %bitcast.9), channel_id=1, source_target_pairs={{0,16},{1,17},{2,18},{3,19},{4,20},{5,21},{6,22},{7,23},{8,24},{9,... | collective-permute-start | bytes 122888 | tf_op jit(solution)/shard_map/ppermute | solution.py:448
  164.5 5.4 %collective-permute-done.20 = bf16[4,16,1280]{2,1,0:T(8,128)(2,1)S(1)} collective-permute-done((bf16[4,16,1280]{2,1,0:T(8,128)(2,1)S(1)}, bf16[4,16,1280]{2,1,0:T(8,128)(2,1)S(1)}, u32[]{:S(2)}, u32[]{:S(2)}) %collective-permute-start.20) | collective-permute-done | bytes 163872 | tf_op jit(solution)/shard_map/ppermute | solution.py:448
  172.7 4.9 %renew.3 = (f32[128,36864]{1,0:T(8,128)}, f32[16,36864]{1,0:T(8,128)}) custom-call(s32[8]{0:T(128)S(1)} %copy-done.3, bf16[16,16,1280]{2,1,0:T(8,128)(2,1)S(1)} %constant_dynamic-update-slice_fusion.7.held_ref, bf16[16,16,1280]{2,1,0:T(8,128)(2,1)S(1)} %collective-permute-done.23.came_ref, ...), custom_call_target="tpu_custom_call", output_to_operand_aliasing={{0}: (5, {})} | custom-call | tf_op jit(solution)/shard_map/renew/pallas_call | solution.py:537
  (76 shorter events, 26.2 us)
Async XLA Ops:
  2.4 21.6 %collective-permute-start.1 = (bf16[512,128]{1,0:T(8,128)(2,1)S(1)}, bf16[512,128]{1,0:T(8,128)(2,1)S(1)}, u32[]{:S(2)}, u32[]{:S(2)}) collective-permute-start(bf16[512,128]{1,0:T(8,128)(2,1)S(1)} %pad_maximum_fusion.2), channel_id=1, source_target_pairs={{1,2},{2,1},{3,4},{4,3},{5,6},{6,5},{7,8},{8,7},{9,10},{10,9},{11,... | collective-permute-start | bytes 393224 | tf_op jit(solution)/shard_map/ppermute | solution.py:562
  3.2 20.8 %collective-permute-start = (bf16[512,128]{1,0:T(8,128)(2,1)S(1)}, bf16[512,128]{1,0:T(8,128)(2,1)S(1)}, u32[]{:S(2)}, u32[]{:S(2)}) collective-permute-start(bf16[512,128]{1,0:T(8,128)(2,1)S(1)} %pad_maximum_fusion.2), channel_id=1, source_target_pairs={{0,1},{1,0},{2,3},{3,2},{4,5},{5,4},{6,7},{7,6},{8,9},{9,8},{10,11... | collective-permute-start | bytes 393224 | tf_op jit(solution)/shard_map/ppermute | solution.py:562
  29.5 3.6 %collective-permute-start.3 = (bf16[128,128]{1,0:T(8,128)(2,1)S(1)}, bf16[128,128]{1,0:T(8,128)(2,1)S(1)}, u32[]{:S(2)}, u32[]{:S(2)}) collective-permute-start(bf16[128,128]{1,0:T(8,128)(2,1)S(1)} %get-tuple-element.26), channel_id=1, source_target_pairs={{1,2},{2,1},{3,4},{4,3},{5,6},{6,5},{7,8},{8,7},{9,10},{10,9},{11,... | collective-permute-start | bytes 98312 | tf_op jit(solution)/shard_map/ppermute | solution.py:562
  30.2 3.8 %collective-permute-start.2 = (bf16[128,128]{1,0:T(8,128)(2,1)S(1)}, bf16[128,128]{1,0:T(8,128)(2,1)S(1)}, u32[]{:S(2)}, u32[]{:S(2)}) collective-permute-start(bf16[128,128]{1,0:T(8,128)(2,1)S(1)} %get-tuple-element.26), channel_id=1, source_target_pairs={{0,1},{1,0},{2,3},{3,2},{4,5},{5,4},{6,7},{7,6},{8,9},{9,8},{10,11... | collective-permute-start | bytes 98312 | tf_op jit(solution)/shard_map/ppermute | solution.py:562
  39.4 4.4 %collective-permute-start.5 = (bf16[128,128]{1,0:T(8,128)(2,1)S(1)}, bf16[128,128]{1,0:T(8,128)(2,1)S(1)}, u32[]{:S(2)}, u32[]{:S(2)}) collective-permute-start(bf16[128,128]{1,0:T(8,128)(2,1)S(1)} %get-tuple-element.28.low_ref), channel_id=1, source_target_pairs={{1,2},{2,1},{3,4},{4,3},{5,6},{6,5},{7,8},{8,7},{9,10},{10,9},{11,... | collective-permute-start | bytes 98312 | tf_op jit(solution)/shard_map/ppermute | solution.py:562
  40.0 4.6 %collective-permute-start.4 = (bf16[128,128]{1,0:T(8,128)(2,1)S(1)}, bf16[128,128]{1,0:T(8,128)(2,1)S(1)}, u32[]{:S(2)}, u32[]{:S(2)}) collective-permute-start(bf16[128,128]{1,0:T(8,128)(2,1)S(1)} %get-tuple-element.28.low_ref), channel_id=1, source_target_pairs={{0,1},{1,0},{2,3},{3,2},{4,5},{5,4},{6,7},{7,6},{8,9},{9,8},{10,11... | collective-permute-start | bytes 98312 | tf_op jit(solution)/shard_map/ppermute | solution.py:562
  49.4 19.6 %all-to-all-start = ((bf16[32,32,128]{2,1,0:T(8,128)(2,1)}), bf16[32,32,128]{2,1,0:T(8,128)(2,1)S(1)}, u32[]{:S(2)}, u32[]{:S(2)}) async-start(bf16[32,32,128]{2,1,0:T(8,128)(2,1)} %get-tuple-element.29), calls=%async_computation | async-start | bytes 524288 | tf_op jit(solution)/shard_map/all_to_all | solution.py:580
  72.8 6.2 %collective-permute-start.8 = (bf16[1,16,1280]{2,1,0:T(8,128)(2,1)S(1)}, bf16[1,16,1280]{2,1,0:T(8,128)(2,1)S(1)}, u32[]{:S(2)}, u32[]{:S(2)}) collective-permute-start(bf16[1,16,1280]{2,1,0:T(8,128)(2,1)S(1)} %bitcast.11), channel_id=1, source_target_pairs={{0,24},{1,25},{2,26},{3,27},{4,28},{5,29},{6,30},{7,31},{8,16},{9,... | collective-permute-start | bytes 122888 | tf_op jit(solution)/shard_map/ppermute | solution.py:448
  74.2 4.8 %collective-permute-start.7 = (bf16[1,16,1280]{2,1,0:T(8,128)(2,1)S(1)}, bf16[1,16,1280]{2,1,0:T(8,128)(2,1)S(1)}, u32[]{:S(2)}, u32[]{:S(2)}) collective-permute-start(bf16[1,16,1280]{2,1,0:T(8,128)(2,1)S(1)} %bitcast.12), channel_id=1, source_target_pairs={{0,8},{1,9},{2,10},{3,11},{4,12},{5,13},{6,14},{7,15},{8,0},{9,1},... | collective-permute-start | bytes 122888 | tf_op jit(solution)/shard_map/ppermute | solution.py:448
  74.2 5.3 %collective-permute-start.6 = (bf16[1,16,1280]{2,1,0:T(8,128)(2,1)S(1)}, bf16[1,16,1280]{2,1,0:T(8,128)(2,1)S(1)}, u32[]{:S(2)}, u32[]{:S(2)}) collective-permute-start(bf16[1,16,1280]{2,1,0:T(8,128)(2,1)S(1)} %bitcast.13), channel_id=1, source_target_pairs={{0,16},{1,17},{2,18},{3,19},{4,20},{5,21},{6,22},{7,23},{8,24},{9,... | collective-permute-start | bytes 122888 | tf_op jit(solution)/shard_map/ppermute | solution.py:448
  79.5 9.0 %collective-permute-start.11 = (bf16[4,16,1280]{2,1,0:T(8,128)(2,1)S(1)}, bf16[4,16,1280]{2,1,0:T(8,128)(2,1)S(1)}, u32[]{:S(2)}, u32[]{:S(2)}) collective-permute-start(bf16[4,16,1280]{2,1,0:T(8,128)(2,1)S(1)} %pad_maximum_fusion), channel_id=1, source_target_pairs={{0,6},{1,7},{2,4},{3,5},{4,2},{5,3},{6,0},{7,1},{8,14},{9,15},{10,... | collective-permute-start | bytes 491528 | tf_op jit(solution)/shard_map/ppermute | solution.py:448
  80.8 7.8 %collective-permute-start.10 = (bf16[4,16,1280]{2,1,0:T(8,128)(2,1)S(1)}, bf16[4,16,1280]{2,1,0:T(8,128)(2,1)S(1)}, u32[]{:S(2)}, u32[]{:S(2)}) collective-permute-start(bf16[4,16,1280]{2,1,0:T(8,128)(2,1)S(1)} %pad_maximum_fusion), channel_id=1, source_target_pairs={{0,2},{1,3},{2,0},{3,1},{4,6},{5,7},{6,4},{7,5},{8,10},{9,11},{10,... | collective-permute-start | bytes 491528 | tf_op jit(solution)/shard_map/ppermute | solution.py:448
  81.9 6.6 %collective-permute-start.9 = (bf16[4,16,1280]{2,1,0:T(8,128)(2,1)S(1)}, bf16[4,16,1280]{2,1,0:T(8,128)(2,1)S(1)}, u32[]{:S(2)}, u32[]{:S(2)}) collective-permute-start(bf16[4,16,1280]{2,1,0:T(8,128)(2,1)S(1)} %pad_maximum_fusion), channel_id=1, source_target_pairs={{0,4},{1,5},{2,6},{3,7},{4,0},{5,1},{6,2},{7,3},{8,12},{9,13},{10,... | collective-permute-start | bytes 491528 | tf_op jit(solution)/shard_map/ppermute | solution.py:448
  88.6 3.0 %collective-permute-start.12 = (bf16[16,16,1280]{2,1,0:T(8,128)(2,1)S(1)}, bf16[16,16,1280]{2,1,0:T(8,128)(2,1)S(1)}, u32[]{:S(2)}, u32[]{:S(2)}) collective-permute-start(bf16[16,16,1280]{2,1,0:T(8,128)(2,1)S(1)} %constant_dynamic-update-slice_fusion.held_ref), channel_id=1, source_target_pairs={{0,1},{1,0},{2,3},{3,2},{4,5},{5,4},{6,7},{7,6},{8,9},{9,8},{10,11... | collective-permute-start | bytes 1966088 | tf_op jit(solution)/shard_map/ppermute | solution.py:448
  111.4 3.8 %collective-permute-start.14 = (bf16[128,128]{1,0:T(8,128)(2,1)S(1)}, bf16[128,128]{1,0:T(8,128)(2,1)S(1)}, u32[]{:S(2)}, u32[]{:S(2)}) collective-permute-start(bf16[128,128]{1,0:T(8,128)(2,1)S(1)} %get-tuple-element.35), channel_id=1, source_target_pairs={{1,2},{2,1},{3,4},{4,3},{5,6},{6,5},{7,8},{8,7},{9,10},{10,9},{11,... | collective-permute-start | bytes 98312 | tf_op jit(solution)/shard_map/ppermute | solution.py:562
  112.1 4.0 %collective-permute-start.13 = (bf16[128,128]{1,0:T(8,128)(2,1)S(1)}, bf16[128,128]{1,0:T(8,128)(2,1)S(1)}, u32[]{:S(2)}, u32[]{:S(2)}) collective-permute-start(bf16[128,128]{1,0:T(8,128)(2,1)S(1)} %get-tuple-element.35), channel_id=1, source_target_pairs={{0,1},{1,0},{2,3},{3,2},{4,5},{5,4},{6,7},{7,6},{8,9},{9,8},{10,11... | collective-permute-start | bytes 98312 | tf_op jit(solution)/shard_map/ppermute | solution.py:562
  122.5 4.4 %collective-permute-start.16 = (bf16[128,128]{1,0:T(8,128)(2,1)S(1)}, bf16[128,128]{1,0:T(8,128)(2,1)S(1)}, u32[]{:S(2)}, u32[]{:S(2)}) collective-permute-start(bf16[128,128]{1,0:T(8,128)(2,1)S(1)} %get-tuple-element.38.low_ref), channel_id=1, source_target_pairs={{1,2},{2,1},{3,4},{4,3},{5,6},{6,5},{7,8},{8,7},{9,10},{10,9},{11,... | collective-permute-start | bytes 98312 | tf_op jit(solution)/shard_map/ppermute | solution.py:562
  123.1 4.6 %collective-permute-start.15 = (bf16[128,128]{1,0:T(8,128)(2,1)S(1)}, bf16[128,128]{1,0:T(8,128)(2,1)S(1)}, u32[]{:S(2)}, u32[]{:S(2)}) collective-permute-start(bf16[128,128]{1,0:T(8,128)(2,1)S(1)} %get-tuple-element.38.low_ref), channel_id=1, source_target_pairs={{0,1},{1,0},{2,3},{3,2},{4,5},{5,4},{6,7},{7,6},{8,9},{9,8},{10,11... | collective-permute-start | bytes 98312 | tf_op jit(solution)/shard_map/ppermute | solution.py:562
  154.2 6.2 %collective-permute-start.19 = (bf16[1,16,1280]{2,1,0:T(8,128)(2,1)S(1)}, bf16[1,16,1280]{2,1,0:T(8,128)(2,1)S(1)}, u32[]{:S(2)}, u32[]{:S(2)}) collective-permute-start(bf16[1,16,1280]{2,1,0:T(8,128)(2,1)S(1)} %bitcast.7), channel_id=1, source_target_pairs={{0,24},{1,25},{2,26},{3,27},{4,28},{5,29},{6,30},{7,31},{8,16},{9,... | collective-permute-start | bytes 122888 | tf_op jit(solution)/shard_map/ppermute | solution.py:448
  155.6 4.8 %collective-permute-start.18 = (bf16[1,16,1280]{2,1,0:T(8,128)(2,1)S(1)}, bf16[1,16,1280]{2,1,0:T(8,128)(2,1)S(1)}, u32[]{:S(2)}, u32[]{:S(2)}) collective-permute-start(bf16[1,16,1280]{2,1,0:T(8,128)(2,1)S(1)} %bitcast.8), channel_id=1, source_target_pairs={{0,8},{1,9},{2,10},{3,11},{4,12},{5,13},{6,14},{7,15},{8,0},{9,1},... | collective-permute-start | bytes 122888 | tf_op jit(solution)/shard_map/ppermute | solution.py:448
  155.6 5.3 %collective-permute-start.17 = (bf16[1,16,1280]{2,1,0:T(8,128)(2,1)S(1)}, bf16[1,16,1280]{2,1,0:T(8,128)(2,1)S(1)}, u32[]{:S(2)}, u32[]{:S(2)}) collective-permute-start(bf16[1,16,1280]{2,1,0:T(8,128)(2,1)S(1)} %bitcast.9), channel_id=1, source_target_pairs={{0,16},{1,17},{2,18},{3,19},{4,20},{5,21},{6,22},{7,23},{8,24},{9,... | collective-permute-start | bytes 122888 | tf_op jit(solution)/shard_map/ppermute | solution.py:448
  160.9 9.0 %collective-permute-start.22 = (bf16[4,16,1280]{2,1,0:T(8,128)(2,1)S(1)}, bf16[4,16,1280]{2,1,0:T(8,128)(2,1)S(1)}, u32[]{:S(2)}, u32[]{:S(2)}) collective-permute-start(bf16[4,16,1280]{2,1,0:T(8,128)(2,1)S(1)} %pad_maximum_fusion.1), channel_id=1, source_target_pairs={{0,6},{1,7},{2,4},{3,5},{4,2},{5,3},{6,0},{7,1},{8,14},{9,15},{10,... | collective-permute-start | bytes 491528 | tf_op jit(solution)/shard_map/ppermute | solution.py:448
  162.2 7.8 %collective-permute-start.21 = (bf16[4,16,1280]{2,1,0:T(8,128)(2,1)S(1)}, bf16[4,16,1280]{2,1,0:T(8,128)(2,1)S(1)}, u32[]{:S(2)}, u32[]{:S(2)}) collective-permute-start(bf16[4,16,1280]{2,1,0:T(8,128)(2,1)S(1)} %pad_maximum_fusion.1), channel_id=1, source_target_pairs={{0,2},{1,3},{2,0},{3,1},{4,6},{5,7},{6,4},{7,5},{8,10},{9,11},{10,... | collective-permute-start | bytes 491528 | tf_op jit(solution)/shard_map/ppermute | solution.py:448
  163.3 6.6 %collective-permute-start.20 = (bf16[4,16,1280]{2,1,0:T(8,128)(2,1)S(1)}, bf16[4,16,1280]{2,1,0:T(8,128)(2,1)S(1)}, u32[]{:S(2)}, u32[]{:S(2)}) collective-permute-start(bf16[4,16,1280]{2,1,0:T(8,128)(2,1)S(1)} %pad_maximum_fusion.1), channel_id=1, source_target_pairs={{0,4},{1,5},{2,6},{3,7},{4,0},{5,1},{6,2},{7,3},{8,12},{9,13},{10,... | collective-permute-start | bytes 491528 | tf_op jit(solution)/shard_map/ppermute | solution.py:448
  (9 other events, 126.6 us)

commit v6 on v5

--- a/solution.py
+++ b/solution.py
@@ -2,6 +2,7 @@
 
 import jax
 import jax.numpy as jnp
+import numpy as np
 from jax import lax
 from jax.experimental import pallas as pl
 from jax.experimental.pallas import tpu as pltpu
@@ -20,7 +21,6 @@
 
 ROWS = 16
 COARSE = L // ROWS
-STRIDE = L + 1
 FINE = 4
 LANES = 128
 VMEM_BYTES = 24 * 1024 * 1024
@@ -59,68 +59,52 @@
     return pl.BlockSpec(memory_space=pltpu.VMEM)
 
 
-def turn(columns_ref, start, turned_ref):
-    side = 2 * LANES
-    row = lax.broadcasted_iota(jnp.int32, (side, side), 0)
-    column = lax.broadcasted_iota(jnp.int32, (side, side), 1)
-    identity = (row == column).astype(jnp.float32).astype(jnp.bfloat16)
-    for first in range(0, ROWS * L, 2 * side):
-        pair = jnp.concatenate(
-            [columns_ref[:, pl.ds(start + first + half * side, side)] for half in range(2)], axis=0
-        ).astype(jnp.bfloat16)
-        turned = lax.dot_general(identity, pair, NT, preferred_element_type=jnp.float32)
-        for half in range(2):
-            entry = first + half * side
-            end = entry + side
-            begin = entry
-            while begin < end:
-                channel, tap = begin // L, begin % L
-                count = min(end - begin, L - tap)
-                target = channel * STRIDE + tap
-                turned_ref[target : target + count, :] = turned[
-                    begin - entry : begin - entry + count, half * K : (half + 1) * K
-                ]
-                begin += count
-
-
-def layout_kernel(dict_ref, taps_ref, copy_hbm, even, odd, sem):
+def reorder_matrix():
+    target = np.arange(8 * L)
+    source = target % 8 * L + target // 8
+    return jnp.asarray(source[:, None] == np.arange(8 * L)[None, :], jnp.bfloat16)
+
+
+def by_tap(columns, reorder_ref):
+    pair = jnp.concatenate([columns[:, : 8 * L], columns[:, 8 * L :]], axis=0)
+    return lax.dot_general(reorder_ref[...], pair, NT, preferred_element_type=jnp.float32)
+
+
+def tap_of(turned, tap):
+    rows = turned[tap * 8 : (tap + 1) * 8]
+    return jnp.concatenate([rows[:, :K], rows[:, K:]], axis=0).astype(jnp.bfloat16)
+
+
+def layout_kernel(reorder_ref, dict_ref, taps_ref, copy_hbm, sem):
     width = dict_ref.shape[1]
     column = pl.multiple_of(pl.program_id(0) * width, LANES)
     copy = pltpu.make_async_copy(dict_ref, copy_hbm.at[:, pl.ds(column, width)], sem)
     copy.start()
     groups = width // (ROWS * L)
-    turn(dict_ref, 0, even)
     for group in range(groups):
-        now, later = (even, odd) if group % 2 == 0 else (odd, even)
-        if group + 1 < groups:
-            turn(dict_ref, (group + 1) * ROWS * L, later)
+        columns = dict_ref[:, group * ROWS * L : (group + 1) * ROWS * L].astype(jnp.bfloat16)
+        turned = by_tap(columns, reorder_ref)
         own = pl.ds(pl.multiple_of((pl.program_id(0) * groups + group) * ROWS, ROWS), ROWS)
         for tap in range(L):
-            taps_ref[tap // ROWS, tap % ROWS, own, :] = now[
-                pl.ds(tap, ROWS, stride=STRIDE), :
-            ].astype(jnp.bfloat16)
+            taps_ref[tap // ROWS, tap % ROWS, own, :] = tap_of(turned, tap)
     copy.wait()
 
 
-def layout(dictionary, channels):
-    block = 4 * ROWS
+def layout(reorder, dictionary, channels):
+    block = 2 * ROWS
     return pl.pallas_call(
         layout_kernel,
         grid=(channels // block,),
-        in_specs=[pl.BlockSpec((K, block * L), lambda i: (0, i))],
+        in_specs=[vmem(), pl.BlockSpec((K, block * L), lambda i: (0, i))],
         out_specs=[vmem(), hbm()],
         out_shape=[
             pltpu.VMEM((COARSE, ROWS, channels, K), jnp.bfloat16),
             pltpu.HBM(dictionary.shape, jnp.float32),
         ],
-        scratch_shapes=[
-            pltpu.VMEM((ROWS * STRIDE, K), jnp.float32),
-            pltpu.VMEM((ROWS * STRIDE, K), jnp.float32),
-            pltpu.SemaphoreType.DMA,
-        ],
+        scratch_shapes=[pltpu.SemaphoreType.DMA],
         compiler_params=pltpu.CompilerParams(vmem_limit_bytes=VMEM_BYTES),
         name="layout",
-    )(far(dictionary))
+    )(reorder, far(dictionary))
 
 
 def convolve(zb, begin, count, taps, zz, fine, acc):
@@ -180,102 +164,126 @@
         acc[0, :count, :] = total
 
 
-def patch_taps(row, atoms_ref, taps, columns, turned):
+def patch_taps(row, atoms_ref, taps, reorder_ref, columns):
     channels = taps.shape[2]
     lane = lax.broadcasted_iota(jnp.int32, (ROWS, K), 1)
-    renewed = (lane >= row) & (lane < row + BLOCK_ATOMS)
-    groups = K // BLOCK_ATOMS
-    width = ROWS * L
-
-    def patch(step, carry):
-        for group in range(groups):
-            part = pl.ds(pl.multiple_of((step * groups + group) * width, LANES), width)
-            columns[group * BLOCK_ATOMS : (group + 1) * BLOCK_ATOMS, :] = atoms_ref[:, part]
-        turn(columns, 0, turned)
+    kept = (lane < row) | (lane >= row + BLOCK_ATOMS)
+    keep = kept.astype(jnp.float32).astype(jnp.bfloat16)
+    columns[...] = jnp.zeros_like(columns)
+
+    def patch(group, carry):
+        part = pl.ds(pl.multiple_of(group * (ROWS * L), LANES), ROWS * L)
+        columns[pl.ds(row, BLOCK_ATOMS), :] = atoms_ref[:, part].astype(jnp.bfloat16)
+        turned = by_tap(columns[...], reorder_ref)
+        own = pl.ds(pl.multiple_of(group * ROWS, ROWS), ROWS)
         for tap in range(L):
-            fresh = turned[pl.ds(tap, ROWS, stride=STRIDE), :]
-            for group in range(groups):
-                placed = pltpu.roll(fresh, (row + K - group * BLOCK_ATOMS) % K, 1)
-                own = pl.ds(pl.multiple_of((step * groups + group) * ROWS, ROWS), ROWS)
-                kept = taps[tap // ROWS, tap % ROWS, own, :].astype(jnp.float32)
-                taps[tap // ROWS, tap % ROWS, own, :] = jnp.where(renewed, placed, kept).astype(
-                    jnp.bfloat16
-                )
+            before = taps[tap // ROWS, tap % ROWS, own, :]
+            taps[tap // ROWS, tap % ROWS, own, :] = before * keep + tap_of(turned, tap)
         return carry
 
-    lax.fori_loop(0, channels // (groups * ROWS), patch, 0)
-
-
-def put_codes(zb, own, first_ref, second_ref, even):
-    segment = own.shape[1]
-    zb[L : L + segment, :] = own[...].astype(jnp.float32).T.astype(jnp.bfloat16)
+    lax.fori_loop(0, channels // ROWS, patch, 0)
+
+
+def put_edges(edge_refs, values):
+    even = lax.axis_index("tm") % 2 == 0
+
+    def put(first, second):
+        first[...] = values[-L:]
+        second[...] = values[:L]
+
+    pl.when(even)(lambda: put(*edge_refs))
+    pl.when(jnp.logical_not(even))(lambda: put(*edge_refs[::-1]))
+
+
+def begin_kernel(code_ref, signal_ref, state_out, signal_out, first_out, second_out):
+    state = code_ref[...].T
+    signal = signal_ref[...].astype(jnp.float32).T.astype(jnp.bfloat16)
+    state_out[...] = state
+    signal_out[...] = signal
+    put_edges((first_out, second_out), jnp.concatenate([state.astype(jnp.bfloat16), signal], axis=1))
+
+
+def begin(code, signal):
+    channels, segment = signal.shape
+    return pl.pallas_call(
+        begin_kernel,
+        in_specs=[vmem()] * 2,
+        out_specs=[vmem()] * 4,
+        out_shape=[
+            pltpu.VMEM((segment, K), jnp.float32),
+            pltpu.VMEM((segment, channels), jnp.bfloat16),
+        ]
+        + [jax.ShapeDtypeStruct((L, K + channels), jnp.bfloat16)] * 2,
+        compiler_params=pltpu.CompilerParams(vmem_limit_bytes=VMEM_BYTES),
+        name="begin",
+    )(code, signal)
+
+
+def put_codes(zb, state_ref, first_ref, second_ref):
+    segment = state_ref.shape[0]
+    even = lax.axis_index("tm") % 2 == 0
+    zb[L : L + segment, :] = state_ref[...].astype(jnp.bfloat16)
 
     def put(left, right):
-        zb[:L, :] = left[:K, :].astype(jnp.float32).T[segment - L :].astype(jnp.bfloat16)
+        zb[:L, :] = left[:, :K]
         if zb.shape[0] > L + segment:
-            zb[L + segment :, :] = right[:K, :].astype(jnp.float32).T[:L].astype(jnp.bfloat16)
+            zb[L + segment :, :] = right[:, :K]
 
     pl.when(even)(lambda: put(second_ref, first_ref))
     pl.when(jnp.logical_not(even))(lambda: put(first_ref, second_ref))
 
 
 def iterate_kernel(total_time, patching, plan_ref, limit_ref, *refs):
-    code_ref, first_ref, second_ref, signal_ref, next_first, next_second = refs[:6]
+    state_ref, first_ref, second_ref, signal_ref, next_first, next_second = refs[:6]
     refs = refs[6:]
     if patching:
-        atoms_ref, refs = refs[0], refs[1:]
-    taps, state_out, low_out = refs[:3]
-    refs = refs[3:]
+        (atoms_ref, reorder_ref), refs = refs[:2], refs[2:]
+    taps, state_out, *edges = refs[:4]
+    refs = refs[4:]
     if patching:
         taps, refs = refs[0], refs[1:]
     zb, rb, zz, rr, fine, acc, beyond = refs[:7]
-    channels, segment = signal_ref.shape
+    segment, channels = signal_ref.shape
     tiles = channels // LANES
     scale = (C * L) ** (-0.5)
     me = lax.axis_index("tm")
     even = me % 2 == 0
-    put_codes(zb, code_ref, first_ref, second_ref, even)
+    put_codes(zb, state_ref, first_ref, second_ref)
 
     def put(following):
-        for tile in range(tiles):
-            own = slice(K + tile * LANES, K + (tile + 1) * LANES)
-            turned = following[own, :].astype(jnp.float32).T
-            beyond[:, tile * LANES : (tile + 1) * LANES] = turned[:L]
+        beyond[...] = following[:, K:]
 
     pl.when(even)(lambda: put(next_first))
     pl.when(jnp.logical_not(even))(lambda: put(next_second))
     if patching:
-        columns, turned = refs[7:]
-        patch_taps(first_row_of(plan_ref, patching - 1), atoms_ref, taps, columns, turned)
+        patch_taps(first_row_of(plan_ref, patching - 1), atoms_ref, taps, reorder_ref, refs[7])
     reach = segment + L
     convolve(zb, L, reach, taps, zz, fine, acc)
     moment = me * segment + lax.broadcasted_iota(jnp.int32, (reach, LANES), 0)
     inside = moment < total_time
     for tile in range(tiles):
         column = slice(tile * LANES, (tile + 1) * LANES)
-        own = signal_ref[column, :].astype(jnp.float32).T
-        value = jnp.concatenate([own, beyond[:, column]], axis=0) - scale * acc[tile, :reach, :]
+        signal = jnp.concatenate([signal_ref[:, column], beyond[:, column]], axis=0)
+        value = signal.astype(jnp.float32) - scale * acc[tile, :reach, :]
         rb[:, column] = jnp.where(inside, value, 0.0).astype(jnp.bfloat16)
     correlate(rb, segment, taps, rr, fine, acc)
     limit = limit_ref[...]
-    stepped = code_ref[...].T + code_rate * (scale * acc[0, :segment, :])
-    state = (stepped - jnp.clip(stepped, -limit, limit)).T
+    stepped = state_ref[...] + code_rate * (scale * acc[0, :segment, :])
+    state = stepped - jnp.clip(stepped, -limit, limit)
     state_out[...] = state
-    low_out[...] = state.astype(jnp.bfloat16)
-
-
-def iterate(plan, step, limit, code, swapped, signal, following, taps, atoms, peers):
-    channels, segment = signal.shape
+    put_edges(edges, state.astype(jnp.bfloat16))
+
+
+def iterate(plan, step, limit, state, swapped, signal, following, taps, atoms, reorder, peers):
+    segment, channels = signal.shape
     patching = atoms is not None
     reach = segment + L
     return pl.pallas_call(
         functools.partial(iterate_kernel, peers * segment, step if patching else 0),
-        in_specs=[scalars()] + [vmem()] * (8 + patching),
-        out_specs=[vmem()] * (2 + patching),
-        out_shape=[
-            jax.ShapeDtypeStruct((K, segment), jnp.float32),
-            jax.ShapeDtypeStruct((K, segment), jnp.bfloat16),
-        ]
+        in_specs=[scalars()] + [vmem()] * (8 + 2 * patching),
+        out_specs=[vmem()] * (3 + patching),
+        out_shape=[pltpu.VMEM((segment, K), jnp.float32)]
+        + [jax.ShapeDtypeStruct((L, K), jnp.bfloat16)] * 2
         + [pltpu.VMEM(taps.shape, jnp.bfloat16)] * patching,
         scratch_shapes=[
             pltpu.VMEM((L + reach, K), jnp.bfloat16),
@@ -284,32 +292,45 @@
             pltpu.VMEM((segment + ROWS, COARSE * channels), jnp.bfloat16),
             pltpu.VMEM((2 * FINE, channels // LANES, reach + ROWS, LANES), jnp.float32),
             pltpu.VMEM((channels // LANES, reach, LANES), jnp.float32),
-            pltpu.VMEM((L, channels), jnp.float32),
+            pltpu.VMEM((L, channels), jnp.bfloat16),
         ]
-        + [
-            pltpu.VMEM((K, ROWS * L), jnp.float32),
-            pltpu.VMEM((ROWS * STRIDE, K), jnp.float32),
-        ]
-        * patching,
-        input_output_aliases={9: 2} if patching else {},
+        + [pltpu.VMEM((K, ROWS * L), jnp.bfloat16)] * patching,
+        input_output_aliases={10: 3} if patching else {},
         compiler_params=pltpu.CompilerParams(vmem_limit_bytes=VMEM_BYTES),
         name="iterate",
-    )(plan, limit, code, *swapped, signal, *following, *([resident(atoms)] if patching else []), resident(taps))
+    )(
+        plan,
+        limit,
+        resident(state),
+        *swapped,
+        resident(signal),
+        *following,
+        *([resident(atoms), reorder] if patching else []),
+        resident(taps),
+    )
 
 
 def finish_kernel(
-    peers, step, plan_ref, low_ref, first_ref, second_ref, signal_ref, taps, resid_out, payload_out, zb, zz, fine, acc, tall
+    peers, step, plan_ref, state_ref, first_ref, second_ref, signal_ref, taps, payload_out, *refs
 ):
-    channels, segment = signal_ref.shape
+    last = step + 1 == OUTER
+    if last:
+        resid_out, codes_out, zb, zz, fine, acc, tall = refs
+    else:
+        zb, zz, fine, acc, tall, codes_out = refs
+    segment, channels = signal_ref.shape
     scale = (C * L) ** (-0.5)
-    put_codes(zb, low_ref, first_ref, second_ref, lax.axis_index("tm") % 2 == 0)
+    put_codes(zb, state_ref, first_ref, second_ref)
+    codes_out[...] = state_ref[...].T
     convolve(zb, L, segment, taps, zz, fine, acc)
     for tile in range(channels // LANES):
         column = slice(tile * LANES, (tile + 1) * LANES)
-        value = signal_ref[column, :].astype(jnp.float32) - scale * acc[tile, :segment, :].T
-        resid_out[column, :] = value
+        value = signal_ref[:, column].astype(jnp.float32) - scale * acc[tile, :segment, :]
+        value = value.T
         tall[column, :] = value
-    block = low_ref[pl.ds(first_row_of(plan_ref, step), BLOCK_ATOMS), :]
+        if last:
+            resid_out[column, :] = value
+    block = codes_out[pl.ds(first_row_of(plan_ref, step), BLOCK_ATOMS), :].astype(jnp.bfloat16)
     share = channels // peers
     share_rows = payload_out.shape[1] - BLOCK_ATOMS
     tall[channels:, :] = jnp.zeros((tall.shape[0] - channels, segment), jnp.float32)
@@ -319,28 +340,31 @@
         payload_out[peer, share_rows:, :] = block
 
 
-def finish(plan, step, low, swapped, signal, taps, peers):
-    channels, segment = signal.shape
+def finish(plan, step, state, swapped, signal, taps, peers):
+    segment, channels = signal.shape
     share = channels // peers
     share_rows = -(-share // ROWS) * ROWS
+    last = step + 1 == OUTER
     return pl.pallas_call(
         functools.partial(finish_kernel, peers, step),
         in_specs=[scalars()] + [vmem()] * 5,
-        out_specs=[vmem(), vmem()],
+        out_specs=[vmem()] * (3 if last else 1),
         out_shape=[
-            jax.ShapeDtypeStruct((channels, segment), jnp.float32),
             jax.ShapeDtypeStruct((peers, share_rows + BLOCK_ATOMS, segment), jnp.bfloat16),
-        ],
+            pltpu.VMEM((channels, segment), jnp.float32),
+            pltpu.VMEM((K, segment), jnp.float32),
+        ][: 3 if last else 1],
         scratch_shapes=[
             pltpu.VMEM((L + segment, K), jnp.bfloat16),
             pltpu.VMEM((segment + ROWS, COARSE * K), jnp.bfloat16),
             pltpu.VMEM((2 * FINE, channels // LANES, segment + ROWS, LANES), jnp.float32),
             pltpu.VMEM((channels // LANES, segment, LANES), jnp.float32),
             pltpu.VMEM((channels + ROWS, segment), jnp.float32),
-        ],
+        ]
+        + ([] if last else [pltpu.VMEM((K, segment), jnp.float32)]),
         compiler_params=pltpu.CompilerParams(vmem_limit_bytes=VMEM_BYTES),
         name="finish",
-    )(plan, low, *swapped, signal, resident(taps))
+    )(plan, resident(state), *swapped, resident(signal), resident(taps))
 
 
 def gradient_kernel(share, step, plan_ref, source_ref, blocks_ref, dict_hbm, out_ref, rf, zf, rr, zz, old, sem):
@@ -534,16 +558,15 @@
 
 def renew(plan, step, held, came, old, mean_sq, dictionary):
     entries = dictionary.shape[1]
+    last = step + 1 == OUTER
     return pl.pallas_call(
         functools.partial(renew_kernel, step),
         in_specs=[scalars()] + [vmem()] * 4 + [hbm()],
-        out_specs=[hbm(), vmem()],
-        out_shape=[
-            pltpu.HBM(dictionary.shape, jnp.float32),
-            pltpu.VMEM((BLOCK_ATOMS, entries), jnp.float32),
-        ],
-        scratch_shapes=[
-            pltpu.VMEM((BLOCK_ATOMS, entries), jnp.float32),
+        out_specs=[hbm()] + [vmem()] * (1 - last),
+        out_shape=[pltpu.HBM(dictionary.shape, jnp.float32)]
+        + [pltpu.VMEM((BLOCK_ATOMS, entries), jnp.float32)] * (1 - last),
+        scratch_shapes=[pltpu.VMEM((BLOCK_ATOMS, entries), jnp.float32)] * (1 + last)
+        + [
             pltpu.SemaphoreType.DMA((2 * held.shape[0],)),
         ],
         input_output_aliases={5: 0},
@@ -556,33 +579,35 @@
     channels, segment = signal.shape
     peers = lax.axis_size("tm")
     limit = threshold[None, :]
-    def swaps(shard):
+    def swaps(edges):
         ends = [range(first, peers - 1, 2) for first in (0, 1)]
         pairs = [[p for i in end for p in ((i, i + 1), (i + 1, i))] for end in ends]
-        return [lax.ppermute(shard, "tm", pair) for pair in pairs]
-
-    low = codes_init.astype(jnp.bfloat16)
-    following = swaps(jnp.concatenate([low, signal], axis=0))
+        return [lax.ppermute(edge, "tm", pair) for edge, pair in zip(edges, pairs)]
+
+    state, signal, *edges = begin(codes_init, signal)
+    following = swaps(edges)
     swapped = following
-    taps, dictionary = layout(dictionary_init, channels)
-    code_state, atoms = codes_init, None
+    reorder = reorder_matrix()
+    taps, dictionary = layout(reorder, dictionary_init, channels)
+    atoms = None
     for step in range(OUTER):
         for inner in range(INNER):
             fresh = atoms if inner == 0 else None
-            results = iterate(
-                plan, step, limit, code_state, swapped, signal, following, taps, fresh, peers
+            state, *results = iterate(
+                plan, step, limit, state, swapped, signal, following, taps, fresh, reorder, peers
             )
-            code_state, low = results[:2]
+            swapped = swaps(results[:2])
             if fresh is not None:
                 taps = results[2]
-            swapped = swaps(low)
-        residual, payload = finish(plan, step, low, swapped, signal, taps, peers)
+        payload, *finals = finish(plan, step, state, swapped, signal, taps, peers)
         blocks = lax.all_to_all(payload, "tm", 0, 0, tiled=True)
         piece = share_gradient(plan, step, blocks, dictionary, channels // peers)
         held, came = gather_pieces(piece)
         old, mean_sq = recall(plan, step, dictionary, piece)
-        dictionary, atoms = renew(plan, step, held, came, old, mean_sq, dictionary)
-    return code_state, dictionary, residual
+        dictionary, *renewed = renew(plan, step, held, came, old, mean_sq, dictionary)
+        atoms = renewed[0] if renewed else None
+    residual, codes = finals
+    return codes, dictionary, residual
 
 
 def renew_atoms(old_atoms, across, mean_sq, spread):

time: 178 us -> 182 us (1.022)
  local copies, waits for them, and re-layouts: 0.15 us -> 4.44 us
  blocking collectives: 18 us -> 21.1 us
  waiting for transfers between devices: 29.2 us -> 26.5 us
    unnamed x28 -> x34, local copies, waits for them, and re-layouts: 0.13 us -> 4.41 us
    ppermute x10, starting transfers between devices: 21.3 us -> 17 us  [swaps(): return [lax.ppermute(edge, 'tm', pair) for edge, pair in zip(edges, pairs)]]
    all_to_all x1, starting transfers between devices: 9.22 us -> 12.9 us  [whole_channels(): blocks = lax.all_to_all(payload, 'tm', 0, 0, tiled=True)]
    pallas_call x1 -> x2, Pallas kernels: 16.4 us -> 19.7 us  [the longest x1 19.6 us: layout(): pl.pallas_call(layout_kernel, grid=(channels // block,), in_specs=[vmem()...]
    all_to_all x1, blocking collectives: 18 us -> 21.1 us  [whole_channels(): blocks = lax.all_to_all(payload, 'tm', 0, 0, tiled=True)]
    ppermute x10, waiting for transfers between devices: 3.44 us -> 0.78 us  [swaps(): return [lax.ppermute(edge, 'tm', pair) for edge, pair in zip(edges, pairs)]]
  transfers between devices with their start and end apart: 25 -> 25, of which waited for: 11 -> 11; matrix products, arithmetic and copies ran while one was open for 0% -> 1% of each run, Pallas kernels for 12% -> 14%
where the time goes in v6:
time: 182 us
  Pallas kernels  82.2 us (45%)
  starting transfers between devices  46.1 us (25%)
  waiting for transfers between devices  26.5 us (15%)
  blocking collectives  21.1 us (12%)
  local copies, waits for them, and re-layouts  4.44 us (2%)
    pallas_call x4, Pallas kernels, iterate(): pl.pallas_call(functools.partial(iterate_kernel, peers * segment, step if...  33.9 us
    all_to_all x1, blocking collectives, whole_channels(): blocks = lax.all_to_all(payload, 'tm', 0, 0, tiled=True)  21.1 us
    pallas_call x1, Pallas kernels, layout(): pl.pallas_call(layout_kernel, grid=(channels // block,), in_specs=[vmem()...  19.6 us
    ppermute x10, starting transfers between devices, swaps(): return [lax.ppermute(edge, 'tm', pair) for edge, pair in zip(edges, pairs)]  17 us
    ppermute x14, starting transfers between devices, exchanged(): return lax.ppermute(shard, 'tm', [(i, i ^ mask) for i in range(peers)])  16.2 us
    ppermute x14, waiting for transfers between devices, exchanged(): return lax.ppermute(shard, 'tm', [(i, i ^ mask) for i in range(peers)])  15.4 us
    all_to_all x1, starting transfers between devices, whole_channels(): blocks = lax.all_to_all(payload, 'tm', 0, 0, tiled=True)  12.9 us
    all_to_all x1, waiting for transfers between devices, whole_channels(): blocks = lax.all_to_all(payload, 'tm', 0, 0, tiled=True)  10.4 us
  transfers between devices with their start and end apart: 25, of which 11 were waited for; matrix products, arithmetic and copies ran while one was open for 1% of the time, Pallas kernels for 14%

profile of v6, /device:TPU:0, one launch (start us, length us, event | category | flops | bytes accessed | tf_op | source)
XLA Modules:
  0.0 181.7 jit_solution(4343313627095273055)
XLA Ops:
  5.0 19.6 %layout.1 = (bf16[6,16,384,128]{3,2,1,0:T(8,128)(2,1)S(1)}, f32[128,36864]{1,0:T(8,128)}) custom-call(bf16[768,768]{1,0:T(8,128)(2,1)S(1)} %copy-done.1, f32[128,36864]{1,0:T(8,128)} %dict_ref.1), custom_call_target="tpu_custom_call" | custom-call | tf_op jit(solution)/shard_map/layout/pallas_call | solution.py:95
  24.6 5.3 %iterate.4 = (f32[128,128]{1,0:T(8,128)S(1)}, bf16[96,128]{1,0:T(8,128)(2,1)S(1)}, bf16[96,128]{1,0:T(8,128)(2,1)S(1)}) custom-call(s32[8]{0:T(128)S(1)} %copy-done.4, f32[1,128]{1,0:T(1,128)S(1)} %bitcast.15, f32[128,128]{1,0:T(8,128)S(1)} %get-tuple-element.31.refs_0_, bf16[96,512]{1,0:T(8,128)(2,1)S(1)} %collective-permute-done.refs_1_.refs_4_, ...), custom_call_target="tpu_custom_call" | custom-call | tf_op jit(solution)/shard_map/iterate/pallas_call | solution.py:281
  29.9 3.9 %collective-permute-start.2 = (bf16[96,128]{1,0:T(8,128)(2,1)S(1)}, bf16[96,128]{1,0:T(8,128)(2,1)S(1)}, u32[]{:S(2)}, u32[]{:S(2)}) collective-permute-start(bf16[96,128]{1,0:T(8,128)(2,1)S(1)} %get-tuple-element.37), channel_id=1, source_target_pairs={{0,1},{1,0},{2,3},{3,2},{4,5},{5,4},{6,7},{7,6},{8,9},{9,8},{10,11... | collective-permute-start | bytes 73736 | tf_op jit(solution)/shard_map/ppermute | solution.py:585
  34.7 5.2 %iterate.5 = (f32[128,128]{1,0:T(8,128)S(1)}, bf16[96,128]{1,0:T(8,128)(2,1)S(1)}, bf16[96,128]{1,0:T(8,128)(2,1)S(1)}) custom-call(s32[8]{0:T(128)S(1)} %copy-done.4, f32[1,128]{1,0:T(1,128)S(1)} %bitcast.16, f32[128,128]{1,0:T(8,128)S(1)} %get-tuple-element.36.refs_0_, bf16[96,128]{1,0:T(8,128)(2,1)S(1)} %collective-permute-done.2.refs_1_, ...), custom_call_target="tpu_custom_call" | custom-call | tf_op jit(solution)/shard_map/iterate/pallas_call | solution.py:281
  39.9 4.4 %collective-permute-start.4 = (bf16[96,128]{1,0:T(8,128)(2,1)S(1)}, bf16[96,128]{1,0:T(8,128)(2,1)S(1)}, u32[]{:S(2)}, u32[]{:S(2)}) collective-permute-start(bf16[96,128]{1,0:T(8,128)(2,1)S(1)} %get-tuple-element.40), channel_id=1, source_target_pairs={{0,1},{1,0},{2,3},{3,2},{4,5},{5,4},{6,7},{7,6},{8,9},{9,8},{10,11... | collective-permute-start | bytes 73736 | tf_op jit(solution)/shard_map/ppermute | solution.py:585
  45.1 4.7 %finish.2 = bf16[32,32,128]{2,1,0:T(8,128)(2,1)} custom-call(s32[8]{0:T(128)S(1)} %copy-done.4, f32[128,128]{1,0:T(8,128)S(1)} %get-tuple-element.39.state_ref.refs_0_, bf16[96,128]{1,0:T(8,128)(2,1)S(1)} %collective-permute-done.4.first_ref.refs_1_, bf16[96,128]{1,0:T(8,128)(2,1)S(1)} %collective-permute-done.5.second_ref.refs_2_, ...), custom_call_target="tpu_custom_call" | custom-call | tf_op jit(solution)/shard_map/finish/pallas_call | solution.py:348
  49.8 12.9 %all-to-all-start = ((bf16[32,32,128]{2,1,0:T(8,128)(2,1)}), bf16[32,32,128]{2,1,0:T(8,128)(2,1)S(1)}, u32[]{:S(2)}, u32[]{:S(2)}) async-start(bf16[32,32,128]{2,1,0:T(8,128)(2,1)} %finish.2), calls=%async_computation | async-start | bytes 524288 | tf_op jit(solution)/shard_map/all_to_all | solution.py:603
  62.8 10.4 %all-to-all-done.blocks_ref = bf16[32,32,128]{2,1,0:T(8,128)(2,1)S(1)} async-done(((bf16[32,32,128]{2,1,0:T(8,128)(2,1)}), bf16[32,32,128]{2,1,0:T(8,128)(2,1)S(1)}, u32[]{:S(2)}, u32[]{:S(2)}) %all-to-all-start) | async-done | bytes 262176 | tf_op jit(solution)/shard_map/all_to_all | solution.py:603
  73.1 3.7 %gradient.2.piece_ref = bf16[16,1280]{1,0:T(8,128)(2,1)S(1)} custom-call(s32[8]{0:T(128)S(1)} %copy-done.4, s32[1,1152]{1,0:T(1,128)S(1)} %fusion.source_ref, bf16[32,32,128]{2,1,0:T(8,128)(2,1)S(1)} %all-to-all-done.blocks_ref, f32[128,36864]{1,0:T(8,128)} %get-tuple-element.42.dict_hbm), custom_call_target="tpu_custom_call" | custom-call | tf_op jit(solution)/shard_map/gradient/pallas_call | solution.py:435
  78.2 3.1 %collective-permute-start.6 = (bf16[1,16,1280]{2,1,0:T(8,128)(2,1)S(1)}, bf16[1,16,1280]{2,1,0:T(8,128)(2,1)S(1)}, u32[]{:S(2)}, u32[]{:S(2)}) collective-permute-start(bf16[1,16,1280]{2,1,0:T(8,128)(2,1)S(1)} %bitcast.13), channel_id=1, source_target_pairs={{0,16},{1,17},{2,18},{3,19},{4,20},{5,21},{6,22},{7,23},{8,24},{9,... | collective-permute-start | bytes 122888 | tf_op jit(solution)/shard_map/ppermute | solution.py:472
  87.2 5.4 %collective-permute-done.9 = bf16[4,16,1280]{2,1,0:T(8,128)(2,1)S(1)} collective-permute-done((bf16[4,16,1280]{2,1,0:T(8,128)(2,1)S(1)}, bf16[4,16,1280]{2,1,0:T(8,128)(2,1)S(1)}, u32[]{:S(2)}, u32[]{:S(2)}) %collective-permute-start.9) | collective-permute-done | bytes 163872 | tf_op jit(solution)/shard_map/ppermute | solution.py:472
  92.7 2.9 %recall.2 = (f32[16,36864]{1,0:T(8,128)S(1)}, f32[16,128]{1,0:T(8,128)S(1)}) custom-call(s32[8]{0:T(128)S(1)} %copy-done.4, f32[128,36864]{1,0:T(8,128)} %get-tuple-element.42.dict_hbm, bf16[16,1280]{1,0:T(8,128)(2,1)S(1)} %gradient.2.piece_ref), custom_call_target="tpu_custom_call" | custom-call | tf_op jit(solution)/shard_map/recall/pallas_call | solution.py:500
  95.7 3.5 %renew.2 = (f32[128,36864]{1,0:T(8,128)}, f32[16,36864]{1,0:T(8,128)S(1)}) custom-call(s32[8]{0:T(128)S(1)} %copy-done.4, bf16[16,16,1280]{2,1,0:T(8,128)(2,1)S(1)} %constant_dynamic-update-slice_fusion.held_ref, bf16[16,16,1280]{2,1,0:T(8,128)(2,1)S(1)} %collective-permute-done.12.came_ref, ...), custom_call_target="tpu_custom_call", output_to_operand_aliasing={{0}: (5, {})} | custom-call | tf_op jit(solution)/shard_map/renew/pallas_call | solution.py:562
  99.3 17.9 %iterate.6 = (f32[128,128]{1,0:T(8,128)S(1)}, bf16[96,128]{1,0:T(8,128)(2,1)S(1)}, bf16[96,128]{1,0:T(8,128)(2,1)S(1)}, bf16[6,16,384,128]{3,2,1,0:T(8,128)(2,1)S(1)}) custom-call(s32[8]{0:T(128)S(1)} %copy-done.4, f32[1,128]{1,0:T(1,128)S(1)} %bitcast.17, f32[128,128]{1,0:T(8,128)S(1)} %get-tuple-element.39.state_ref.refs_0_, ...), custom_call_target="tpu_custom_call", output_to_operand_aliasing={{3}: (10, {})} | custom-call | tf_op jit(solution)/shard_map/iterate/pallas_call | solution.py:281
  118.7 5.5 %iterate.7 = (f32[128,128]{1,0:T(8,128)S(1)}, bf16[96,128]{1,0:T(8,128)(2,1)S(1)}, bf16[96,128]{1,0:T(8,128)(2,1)S(1)}) custom-call(s32[8]{0:T(128)S(1)} %copy-done.4, f32[1,128]{1,0:T(1,128)S(1)} %bitcast.18, f32[128,128]{1,0:T(8,128)S(1)} %get-tuple-element.46.refs_0_, bf16[96,128]{1,0:T(8,128)(2,1)S(1)} %collective-permute-done.13.refs_1_, ...), custom_call_target="tpu_custom_call" | custom-call | tf_op jit(solution)/shard_map/iterate/pallas_call | solution.py:281
  124.1 4.4 %collective-permute-start.15 = (bf16[96,128]{1,0:T(8,128)(2,1)S(1)}, bf16[96,128]{1,0:T(8,128)(2,1)S(1)}, u32[]{:S(2)}, u32[]{:S(2)}) collective-permute-start(bf16[96,128]{1,0:T(8,128)(2,1)S(1)} %get-tuple-element.51), channel_id=1, source_target_pairs={{0,1},{1,0},{2,3},{3,2},{4,5},{5,4},{6,7},{7,6},{8,9},{9,8},{10,11... | collective-permute-start | bytes 73736 | tf_op jit(solution)/shard_map/ppermute | solution.py:585
  129.4 4.0 %finish.3 = (bf16[32,32,128]{2,1,0:T(8,128)(2,1)S(1)}, f32[384,128]{1,0:T(8,128)S(1)}, f32[128,128]{1,0:T(8,128)S(1)}) custom-call(s32[8]{0:T(128)S(1)} %copy-done.4, f32[128,128]{1,0:T(8,128)S(1)} %get-tuple-element.50.state_ref, bf16[96,128]{1,0:T(8,128)(2,1)S(1)} %collective-permute-done.15.first_ref, ...), custom_call_target="tpu_custom_call" | custom-call | tf_op jit(solution)/shard_map/finish/pallas_call | solution.py:348
  133.3 21.1 %all_to_all.10.blocks_ref = bf16[32,32,128]{2,1,0:T(8,128)(2,1)S(1)} all-to-all(bf16[32,32,128]{2,1,0:T(8,128)(2,1)S(1)} %get-tuple-element.54), channel_id=1, replica_groups=mesh['tm'=32,'chan'=1] {'tm'}, dimensions={0} | all-to-all | bytes 524288 | tf_op jit(solution)/shard_map/all_to_all | solution.py:603
  154.5 3.7 %gradient.3.piece_ref = bf16[16,1280]{1,0:T(8,128)(2,1)S(1)} custom-call(s32[8]{0:T(128)S(1)} %copy-done.4, s32[1,1152]{1,0:T(1,128)S(1)} %fusion.source_ref, bf16[32,32,128]{2,1,0:T(8,128)(2,1)S(1)} %all_to_all.10.blocks_ref, f32[128,36864]{1,0:T(8,128)} %get-tuple-element.55.dict_hbm), custom_call_target="tpu_custom_call" | custom-call | tf_op jit(solution)/shard_map/gradient/pallas_call | solution.py:435
  159.6 3.1 %collective-permute-start.17 = (bf16[1,16,1280]{2,1,0:T(8,128)(2,1)S(1)}, bf16[1,16,1280]{2,1,0:T(8,128)(2,1)S(1)}, u32[]{:S(2)}, u32[]{:S(2)}) collective-permute-start(bf16[1,16,1280]{2,1,0:T(8,128)(2,1)S(1)} %bitcast.9), channel_id=1, source_target_pairs={{0,16},{1,17},{2,18},{3,19},{4,20},{5,21},{6,22},{7,23},{8,24},{9,... | collective-permute-start | bytes 122888 | tf_op jit(solution)/shard_map/ppermute | solution.py:472
  162.6 1.7 collective-permute-done.19
  168.5 5.4 %collective-permute-done.20 = bf16[4,16,1280]{2,1,0:T(8,128)(2,1)S(1)} collective-permute-done((bf16[4,16,1280]{2,1,0:T(8,128)(2,1)S(1)}, bf16[4,16,1280]{2,1,0:T(8,128)(2,1)S(1)}, u32[]{:S(2)}, u32[]{:S(2)}) %collective-permute-start.20) | collective-permute-done | bytes 163872 | tf_op jit(solution)/shard_map/ppermute | solution.py:472
  175.4 2.6 %recall.3 = (f32[16,36864]{1,0:T(8,128)S(1)}, f32[16,128]{1,0:T(8,128)S(1)}) custom-call(s32[8]{0:T(128)S(1)} %copy-done.4, f32[128,36864]{1,0:T(8,128)} %get-tuple-element.55.dict_hbm, bf16[16,1280]{1,0:T(8,128)(2,1)S(1)} %gradient.3.piece_ref), custom_call_target="tpu_custom_call" | custom-call | tf_op jit(solution)/shard_map/recall/pallas_call | solution.py:500
  178.0 3.5 %renew.3 = f32[128,36864]{1,0:T(8,128)} custom-call(s32[8]{0:T(128)S(1)} %copy-done.4, bf16[16,16,1280]{2,1,0:T(8,128)(2,1)S(1)} %constant_dynamic-update-slice_fusion.7.held_ref, bf16[16,16,1280]{2,1,0:T(8,128)(2,1)S(1)} %collective-permute-done.23.came_ref, f32[16,36864]{1,0:T(8,128)S(1)} %get-tuple-element.56.old, ...), custom_call_target="tpu_custom_call", output_to_operand_aliasing={{}: (5, {})} | custom-call | tf_op jit(solution)/shard_map/renew/pallas_call | solution.py:562
  (81 shorter events, 22.7 us)
Async XLA Ops:
  2.5 22.1 %collective-permute-start = (bf16[96,512]{1,0:T(8,128)(2,1)S(1)}, bf16[96,512]{1,0:T(8,128)(2,1)S(1)}, u32[]{:S(2)}, u32[]{:S(2)}) collective-permute-start(bf16[96,512]{1,0:T(8,128)(2,1)S(1)} %get-tuple-element.32), channel_id=1, source_target_pairs={{0,1},{1,0},{2,3},{3,2},{4,5},{5,4},{6,7},{7,6},{8,9},{9,8},{10,11... | collective-permute-start | bytes 294920 | tf_op jit(solution)/shard_map/ppermute | solution.py:585
  3.0 21.6 %collective-permute-start.1 = (bf16[96,512]{1,0:T(8,128)(2,1)S(1)}, bf16[96,512]{1,0:T(8,128)(2,1)S(1)}, u32[]{:S(2)}, u32[]{:S(2)}) collective-permute-start(bf16[96,512]{1,0:T(8,128)(2,1)S(1)} %get-tuple-element.33), channel_id=1, source_target_pairs={{1,2},{2,1},{3,4},{4,3},{5,6},{6,5},{7,8},{8,7},{9,10},{10,9},{11,... | collective-permute-start | bytes 294920 | tf_op jit(solution)/shard_map/ppermute | solution.py:585
  29.9 4.8 %collective-permute-start.2 = (bf16[96,128]{1,0:T(8,128)(2,1)S(1)}, bf16[96,128]{1,0:T(8,128)(2,1)S(1)}, u32[]{:S(2)}, u32[]{:S(2)}) collective-permute-start(bf16[96,128]{1,0:T(8,128)(2,1)S(1)} %get-tuple-element.37), channel_id=1, source_target_pairs={{0,1},{1,0},{2,3},{3,2},{4,5},{5,4},{6,7},{7,6},{8,9},{9,8},{10,11... | collective-permute-start | bytes 73736 | tf_op jit(solution)/shard_map/ppermute | solution.py:585
  33.8 0.9 collective-permute-start.3
  39.9 5.2 %collective-permute-start.4 = (bf16[96,128]{1,0:T(8,128)(2,1)S(1)}, bf16[96,128]{1,0:T(8,128)(2,1)S(1)}, u32[]{:S(2)}, u32[]{:S(2)}) collective-permute-start(bf16[96,128]{1,0:T(8,128)(2,1)S(1)} %get-tuple-element.40), channel_id=1, source_target_pairs={{0,1},{1,0},{2,3},{3,2},{4,5},{5,4},{6,7},{7,6},{8,9},{9,8},{10,11... | collective-permute-start | bytes 73736 | tf_op jit(solution)/shard_map/ppermute | solution.py:585
  44.3 0.9 collective-permute-start.5
  49.8 23.3 %all-to-all-start = ((bf16[32,32,128]{2,1,0:T(8,128)(2,1)}), bf16[32,32,128]{2,1,0:T(8,128)(2,1)S(1)}, u32[]{:S(2)}, u32[]{:S(2)}) async-start(bf16[32,32,128]{2,1,0:T(8,128)(2,1)} %finish.2), calls=%async_computation | async-start | bytes 524288 | tf_op jit(solution)/shard_map/all_to_all | solution.py:603
  76.8 6.2 %collective-permute-start.8 = (bf16[1,16,1280]{2,1,0:T(8,128)(2,1)S(1)}, bf16[1,16,1280]{2,1,0:T(8,128)(2,1)S(1)}, u32[]{:S(2)}, u32[]{:S(2)}) collective-permute-start(bf16[1,16,1280]{2,1,0:T(8,128)(2,1)S(1)} %bitcast.11), channel_id=1, source_target_pairs={{0,24},{1,25},{2,26},{3,27},{4,28},{5,29},{6,30},{7,31},{8,16},{9,... | collective-permute-start | bytes 122888 | tf_op jit(solution)/shard_map/ppermute | solution.py:472
  78.2 4.8 %collective-permute-start.7 = (bf16[1,16,1280]{2,1,0:T(8,128)(2,1)S(1)}, bf16[1,16,1280]{2,1,0:T(8,128)(2,1)S(1)}, u32[]{:S(2)}, u32[]{:S(2)}) collective-permute-start(bf16[1,16,1280]{2,1,0:T(8,128)(2,1)S(1)} %bitcast.12), channel_id=1, source_target_pairs={{0,8},{1,9},{2,10},{3,11},{4,12},{5,13},{6,14},{7,15},{8,0},{9,1},... | collective-permute-start | bytes 122888 | tf_op jit(solution)/shard_map/ppermute | solution.py:472
  78.2 5.3 %collective-permute-start.6 = (bf16[1,16,1280]{2,1,0:T(8,128)(2,1)S(1)}, bf16[1,16,1280]{2,1,0:T(8,128)(2,1)S(1)}, u32[]{:S(2)}, u32[]{:S(2)}) collective-permute-start(bf16[1,16,1280]{2,1,0:T(8,128)(2,1)S(1)} %bitcast.13), channel_id=1, source_target_pairs={{0,16},{1,17},{2,18},{3,19},{4,20},{5,21},{6,22},{7,23},{8,24},{9,... | collective-permute-start | bytes 122888 | tf_op jit(solution)/shard_map/ppermute | solution.py:472
  83.6 9.0 %collective-permute-start.11 = (bf16[4,16,1280]{2,1,0:T(8,128)(2,1)S(1)}, bf16[4,16,1280]{2,1,0:T(8,128)(2,1)S(1)}, u32[]{:S(2)}, u32[]{:S(2)}) collective-permute-start(bf16[4,16,1280]{2,1,0:T(8,128)(2,1)S(1)} %pad_maximum_fusion), channel_id=1, source_target_pairs={{0,6},{1,7},{2,4},{3,5},{4,2},{5,3},{6,0},{7,1},{8,14},{9,15},{10,... | collective-permute-start | bytes 491528 | tf_op jit(solution)/shard_map/ppermute | solution.py:472
  84.8 7.8 %collective-permute-start.10 = (bf16[4,16,1280]{2,1,0:T(8,128)(2,1)S(1)}, bf16[4,16,1280]{2,1,0:T(8,128)(2,1)S(1)}, u32[]{:S(2)}, u32[]{:S(2)}) collective-permute-start(bf16[4,16,1280]{2,1,0:T(8,128)(2,1)S(1)} %pad_maximum_fusion), channel_id=1, source_target_pairs={{0,2},{1,3},{2,0},{3,1},{4,6},{5,7},{6,4},{7,5},{8,10},{9,11},{10,... | collective-permute-start | bytes 491528 | tf_op jit(solution)/shard_map/ppermute | solution.py:472
  86.0 6.6 %collective-permute-start.9 = (bf16[4,16,1280]{2,1,0:T(8,128)(2,1)S(1)}, bf16[4,16,1280]{2,1,0:T(8,128)(2,1)S(1)}, u32[]{:S(2)}, u32[]{:S(2)}) collective-permute-start(bf16[4,16,1280]{2,1,0:T(8,128)(2,1)S(1)} %pad_maximum_fusion), channel_id=1, source_target_pairs={{0,4},{1,5},{2,6},{3,7},{4,0},{5,1},{6,2},{7,3},{8,12},{9,13},{10,... | collective-permute-start | bytes 491528 | tf_op jit(solution)/shard_map/ppermute | solution.py:472
  92.6 3.0 %collective-permute-start.12 = (bf16[16,16,1280]{2,1,0:T(8,128)(2,1)S(1)}, bf16[16,16,1280]{2,1,0:T(8,128)(2,1)S(1)}, u32[]{:S(2)}, u32[]{:S(2)}) collective-permute-start(bf16[16,16,1280]{2,1,0:T(8,128)(2,1)S(1)} %constant_dynamic-update-slice_fusion.held_ref), channel_id=1, source_target_pairs={{0,1},{1,0},{2,3},{3,2},{4,5},{5,4},{6,7},{7,6},{8,9},{9,8},{10,11... | collective-permute-start | bytes 1966088 | tf_op jit(solution)/shard_map/ppermute | solution.py:472
  117.2 1.4 collective-permute-start.13
  117.8 0.9 collective-permute-start.14
  124.1 5.2 %collective-permute-start.15 = (bf16[96,128]{1,0:T(8,128)(2,1)S(1)}, bf16[96,128]{1,0:T(8,128)(2,1)S(1)}, u32[]{:S(2)}, u32[]{:S(2)}) collective-permute-start(bf16[96,128]{1,0:T(8,128)(2,1)S(1)} %get-tuple-element.51), channel_id=1, source_target_pairs={{0,1},{1,0},{2,3},{3,2},{4,5},{5,4},{6,7},{7,6},{8,9},{9,8},{10,11... | collective-permute-start | bytes 73736 | tf_op jit(solution)/shard_map/ppermute | solution.py:585
  158.2 6.2 %collective-permute-start.19 = (bf16[1,16,1280]{2,1,0:T(8,128)(2,1)S(1)}, bf16[1,16,1280]{2,1,0:T(8,128)(2,1)S(1)}, u32[]{:S(2)}, u32[]{:S(2)}) collective-permute-start(bf16[1,16,1280]{2,1,0:T(8,128)(2,1)S(1)} %bitcast.7), channel_id=1, source_target_pairs={{0,24},{1,25},{2,26},{3,27},{4,28},{5,29},{6,30},{7,31},{8,16},{9,... | collective-permute-start | bytes 122888 | tf_op jit(solution)/shard_map/ppermute | solution.py:472
  159.6 4.8 %collective-permute-start.18 = (bf16[1,16,1280]{2,1,0:T(8,128)(2,1)S(1)}, bf16[1,16,1280]{2,1,0:T(8,128)(2,1)S(1)}, u32[]{:S(2)}, u32[]{:S(2)}) collective-permute-start(bf16[1,16,1280]{2,1,0:T(8,128)(2,1)S(1)} %bitcast.8), channel_id=1, source_target_pairs={{0,8},{1,9},{2,10},{3,11},{4,12},{5,13},{6,14},{7,15},{8,0},{9,1},... | collective-permute-start | bytes 122888 | tf_op jit(solution)/shard_map/ppermute | solution.py:472
  159.6 5.3 %collective-permute-start.17 = (bf16[1,16,1280]{2,1,0:T(8,128)(2,1)S(1)}, bf16[1,16,1280]{2,1,0:T(8,128)(2,1)S(1)}, u32[]{:S(2)}, u32[]{:S(2)}) collective-permute-start(bf16[1,16,1280]{2,1,0:T(8,128)(2,1)S(1)} %bitcast.9), channel_id=1, source_target_pairs={{0,16},{1,17},{2,18},{3,19},{4,20},{5,21},{6,22},{7,23},{8,24},{9,... | collective-permute-start | bytes 122888 | tf_op jit(solution)/shard_map/ppermute | solution.py:472
  164.9 9.0 %collective-permute-start.22 = (bf16[4,16,1280]{2,1,0:T(8,128)(2,1)S(1)}, bf16[4,16,1280]{2,1,0:T(8,128)(2,1)S(1)}, u32[]{:S(2)}, u32[]{:S(2)}) collective-permute-start(bf16[4,16,1280]{2,1,0:T(8,128)(2,1)S(1)} %pad_maximum_fusion.1), channel_id=1, source_target_pairs={{0,6},{1,7},{2,4},{3,5},{4,2},{5,3},{6,0},{7,1},{8,14},{9,15},{10,... | collective-permute-start | bytes 491528 | tf_op jit(solution)/shard_map/ppermute | solution.py:472
  166.2 7.8 %collective-permute-start.21 = (bf16[4,16,1280]{2,1,0:T(8,128)(2,1)S(1)}, bf16[4,16,1280]{2,1,0:T(8,128)(2,1)S(1)}, u32[]{:S(2)}, u32[]{:S(2)}) collective-permute-start(bf16[4,16,1280]{2,1,0:T(8,128)(2,1)S(1)} %pad_maximum_fusion.1), channel_id=1, source_target_pairs={{0,2},{1,3},{2,0},{3,1},{4,6},{5,7},{6,4},{7,5},{8,10},{9,11},{10,... | collective-permute-start | bytes 491528 | tf_op jit(solution)/shard_map/ppermute | solution.py:472
  167.3 6.6 %collective-permute-start.20 = (bf16[4,16,1280]{2,1,0:T(8,128)(2,1)S(1)}, bf16[4,16,1280]{2,1,0:T(8,128)(2,1)S(1)}, u32[]{:S(2)}, u32[]{:S(2)}) collective-permute-start(bf16[4,16,1280]{2,1,0:T(8,128)(2,1)S(1)} %pad_maximum_fusion.1), channel_id=1, source_target_pairs={{0,4},{1,5},{2,6},{3,7},{4,0},{5,1},{6,2},{7,3},{8,12},{9,13},{10,... | collective-permute-start | bytes 491528 | tf_op jit(solution)/shard_map/ppermute | solution.py:472
  174.0 4.0 %collective-permute-start.23 = (bf16[16,16,1280]{2,1,0:T(8,128)(2,1)S(1)}, bf16[16,16,1280]{2,1,0:T(8,128)(2,1)S(1)}, u32[]{:S(2)}, u32[]{:S(2)}) collective-permute-start(bf16[16,16,1280]{2,1,0:T(8,128)(2,1)S(1)} %constant_dynamic-update-slice_fusion.7.held_ref), channel_id=1, source_target_pairs={{0,1},{1,0},{2,3},{3,2},{4,5},{5,4},{6,7},{7,6},{8,9},{9,8},{10,11... | collective-permute-start | bytes 1966088 | tf_op jit(solution)/shard_map/ppermute | solution.py:472
  (11 other events, 83.9 us)

commit v7 on v6

--- a/solution.py
+++ b/solution.py
@@ -2,7 +2,6 @@
 
 import jax
 import jax.numpy as jnp
-import numpy as np
 from jax import lax
 from jax.experimental import pallas as pl
 from jax.experimental.pallas import tpu as pltpu
@@ -21,6 +20,10 @@
 
 ROWS = 16
 COARSE = L // ROWS
+STRIDE = L + 1
+GROUPS = 4
+SUBLANES = 8
+COPIED = (56, 48, 24)
 FINE = 4
 LANES = 128
 VMEM_BYTES = 24 * 1024 * 1024
@@ -59,55 +62,96 @@
     return pl.BlockSpec(memory_space=pltpu.VMEM)
 
 
-def reorder_matrix():
-    target = np.arange(8 * L)
-    source = target % 8 * L + target // 8
-    return jnp.asarray(source[:, None] == np.arange(8 * L)[None, :], jnp.bfloat16)
-
-
-def by_tap(columns, reorder_ref):
-    pair = jnp.concatenate([columns[:, : 8 * L], columns[:, 8 * L :]], axis=0)
-    return lax.dot_general(reorder_ref[...], pair, NT, preferred_element_type=jnp.float32)
-
-
-def tap_of(turned, tap):
-    rows = turned[tap * 8 : (tap + 1) * 8]
-    return jnp.concatenate([rows[:, :K], rows[:, K:]], axis=0).astype(jnp.bfloat16)
-
-
-def layout_kernel(reorder_ref, dict_ref, taps_ref, copy_hbm, sem):
-    width = dict_ref.shape[1]
-    column = pl.multiple_of(pl.program_id(0) * width, LANES)
-    copy = pltpu.make_async_copy(dict_ref, copy_hbm.at[:, pl.ds(column, width)], sem)
-    copy.start()
-    groups = width // (ROWS * L)
-    for group in range(groups):
-        columns = dict_ref[:, group * ROWS * L : (group + 1) * ROWS * L].astype(jnp.bfloat16)
-        turned = by_tap(columns, reorder_ref)
-        own = pl.ds(pl.multiple_of((pl.program_id(0) * groups + group) * ROWS, ROWS), ROWS)
+def turn(columns, turned_ref):
+    side = 2 * LANES
+    row = lax.broadcasted_iota(jnp.int32, (side, side), 0)
+    column = lax.broadcasted_iota(jnp.int32, (side, side), 1)
+    identity = (row == column).astype(jnp.float32).astype(jnp.bfloat16)
+    columns = columns.astype(jnp.bfloat16)
+    for first in range(0, ROWS * L, 2 * side):
+        pair = jnp.concatenate(
+            [columns[:, first + half * side : first + (half + 1) * side] for half in range(2)], axis=0
+        )
+        turned = lax.dot_general(identity, pair, NT, preferred_element_type=jnp.float32)
+        for half in range(2):
+            entry = first + half * side
+            end = entry + side
+            begin = entry
+            while begin < end:
+                channel, tap = begin // L, begin % L
+                count = min(end - begin, L - tap)
+                target = channel * STRIDE + tap
+                turned_ref[target : target + count, :] = turned[
+                    begin - entry : begin - entry + count, half * K : (half + 1) * K
+                ]
+                begin += count
+
+
+def tap_of(turned_ref, tap):
+    return turned_ref[pl.ds(tap, ROWS, stride=STRIDE), :].astype(jnp.bfloat16)
+
+
+def layout_kernel(dict_ref, taps_ref, *turned):
+    def part(group):
+        return dict_ref[:, group * ROWS * L : (group + 1) * ROWS * L]
+
+    turn(part(0), turned[0])
+    for group in range(GROUPS):
+        if group + 1 < GROUPS:
+            turn(part(group + 1), turned[group + 1])
+        own = pl.ds(pl.multiple_of((pl.program_id(0) * GROUPS + group) * ROWS, ROWS), ROWS)
         for tap in range(L):
-            taps_ref[tap // ROWS, tap % ROWS, own, :] = tap_of(turned, tap)
-    copy.wait()
-
-
-def layout(reorder, dictionary, channels):
-    block = 2 * ROWS
+            taps_ref[tap // ROWS, tap % ROWS, own, :] = tap_of(turned[group], tap)
+
+
+def layout(dictionary, channels):
+    block = GROUPS * ROWS
     return pl.pallas_call(
         layout_kernel,
         grid=(channels // block,),
-        in_specs=[vmem(), pl.BlockSpec((K, block * L), lambda i: (0, i))],
-        out_specs=[vmem(), hbm()],
-        out_shape=[
-            pltpu.VMEM((COARSE, ROWS, channels, K), jnp.bfloat16),
-            pltpu.HBM(dictionary.shape, jnp.float32),
-        ],
-        scratch_shapes=[pltpu.SemaphoreType.DMA],
+        in_specs=[pl.BlockSpec((K, block * L), lambda i: (0, i))],
+        out_specs=vmem(),
+        out_shape=pltpu.VMEM((COARSE, ROWS, channels, K), jnp.bfloat16),
+        scratch_shapes=[pltpu.VMEM((ROWS * STRIDE, K), jnp.float32)] * GROUPS,
         compiler_params=pltpu.CompilerParams(vmem_limit_bytes=VMEM_BYTES),
         name="layout",
-    )(reorder, far(dictionary))
-
-
-def convolve(zb, begin, count, taps, zz, fine, acc):
+    )(far(dictionary))
+
+
+class Ferry:
+    def __init__(self, source, target, first, buffer, sems):
+        self.steps = []
+        for step in range(buffer.shape[0] // SUBLANES):
+            held = buffer.at[pl.ds(step * SUBLANES, SUBLANES)]
+            rows = pl.ds(first + step * SUBLANES, SUBLANES)
+            fetch = pltpu.make_async_copy(source.at[rows], held, sems.at[0, step])
+            store = pltpu.make_async_copy(held, target.at[rows], sems.at[1, step])
+            fetch.start()
+            self.steps.append((fetch, store))
+        self.stored = 0
+
+    def tick(self):
+        if self.stored < len(self.steps):
+            fetch, store = self.steps[self.stored]
+            fetch.wait()
+            store.start()
+            self.stored += 1
+
+    def close(self):
+        while self.stored < len(self.steps):
+            self.tick()
+        for _, store in self.steps:
+            store.wait()
+
+
+def ferry_scratch(count, entries):
+    return [
+        pltpu.VMEM((count, entries), jnp.float32),
+        pltpu.SemaphoreType.DMA((2, count // SUBLANES)),
+    ]
+
+
+def convolve(zb, begin, count, taps, zz, fine, acc, ferry):
     channels = taps.shape[2]
     tiles = channels // LANES
     rows = count + ROWS
@@ -129,6 +173,8 @@
                 for tile in range(tiles):
                     column = j * channels + tile * LANES
                     fine[slot + pair + j, tile, :rows, :] = product[:, column : column + LANES]
+        if ferry:
+            ferry.tick()
         for tile in range(tiles):
             total = None if lag == 0 else acc[tile, :count, :]
             for j in range(FINE):
@@ -138,7 +184,7 @@
             acc[tile, :count, :] = total
 
 
-def correlate(rb, count, taps, rr, fine, acc):
+def correlate(rb, count, taps, rr, fine, acc, ferry):
     channels = taps.shape[2]
     rows = count + ROWS
     for coarse in range(COARSE):
@@ -157,6 +203,8 @@
             product = lax.dot_general(rr[:rows, :], weights, NN, preferred_element_type=jnp.float32)
             for j in range(2):
                 fine[slot + pair + j, 0, :rows, :] = product[:, j * K : (j + 1) * K]
+        if ferry:
+            ferry.tick()
         total = None if lag == 0 else acc[0, :count, :]
         for j in range(FINE):
             part = fine[slot + j, 0, lag + j : lag + j + count, :]
@@ -164,24 +212,28 @@
         acc[0, :count, :] = total
 
 
-def patch_taps(row, atoms_ref, taps, reorder_ref, columns):
+def patch_taps(row, atoms_ref, taps, columns, turned):
     channels = taps.shape[2]
     lane = lax.broadcasted_iota(jnp.int32, (ROWS, K), 1)
     kept = (lane < row) | (lane >= row + BLOCK_ATOMS)
     keep = kept.astype(jnp.float32).astype(jnp.bfloat16)
     columns[...] = jnp.zeros_like(columns)
-
-    def patch(group, carry):
-        part = pl.ds(pl.multiple_of(group * (ROWS * L), LANES), ROWS * L)
+    width = ROWS * L
+
+    def patch(step, carry):
+        part = pl.ds(pl.multiple_of(step * (GROUPS * width), LANES), GROUPS * width)
         columns[pl.ds(row, BLOCK_ATOMS), :] = atoms_ref[:, part].astype(jnp.bfloat16)
-        turned = by_tap(columns[...], reorder_ref)
-        own = pl.ds(pl.multiple_of(group * ROWS, ROWS), ROWS)
-        for tap in range(L):
-            before = taps[tap // ROWS, tap % ROWS, own, :]
-            taps[tap // ROWS, tap % ROWS, own, :] = before * keep + tap_of(turned, tap)
+        turn(columns[:, :width], turned[0])
+        for group in range(GROUPS):
+            if group + 1 < GROUPS:
+                turn(columns[:, (group + 1) * width : (group + 2) * width], turned[group + 1])
+            own = pl.ds(pl.multiple_of((step * GROUPS + group) * ROWS, ROWS), ROWS)
+            for tap in range(L):
+                before = taps[tap // ROWS, tap % ROWS, own, :]
+                taps[tap // ROWS, tap % ROWS, own, :] = before * keep + tap_of(turned[group], tap)
         return carry
 
-    lax.fori_loop(0, channels // ROWS, patch, 0)
+    lax.fori_loop(0, channels // (GROUPS * ROWS), patch, 0)
 
 
 def put_edges(edge_refs, values):
@@ -195,7 +247,15 @@
     pl.when(jnp.logical_not(even))(lambda: put(*edge_refs[::-1]))
 
 
-def begin_kernel(code_ref, signal_ref, state_out, signal_out, first_out, second_out):
+def begin_kernel(code_hbm, signal_hbm, state_out, signal_out, first_out, second_out, code_ref, signal_ref, sems):
+    fetches = [
+        pltpu.make_async_copy(code_hbm, code_ref, sems.at[0]),
+        pltpu.make_async_copy(signal_hbm, signal_ref, sems.at[1]),
+    ]
+    for fetch in fetches:
+        fetch.start()
+    for fetch in fetches:
+        fetch.wait()
     state = code_ref[...].T
     signal = signal_ref[...].astype(jnp.float32).T.astype(jnp.bfloat16)
     state_out[...] = state
@@ -207,16 +267,21 @@
     channels, segment = signal.shape
     return pl.pallas_call(
         begin_kernel,
-        in_specs=[vmem()] * 2,
+        in_specs=[hbm()] * 2,
         out_specs=[vmem()] * 4,
         out_shape=[
             pltpu.VMEM((segment, K), jnp.float32),
             pltpu.VMEM((segment, channels), jnp.bfloat16),
         ]
         + [jax.ShapeDtypeStruct((L, K + channels), jnp.bfloat16)] * 2,
+        scratch_shapes=[
+            pltpu.VMEM(code.shape, code.dtype),
+            pltpu.VMEM(signal.shape, signal.dtype),
+            pltpu.SemaphoreType.DMA((2,)),
+        ],
         compiler_params=pltpu.CompilerParams(vmem_limit_bytes=VMEM_BYTES),
         name="begin",
-    )(code, signal)
+    )(far(code), far(signal))
 
 
 def put_codes(zb, state_ref, first_ref, second_ref):
@@ -233,16 +298,24 @@
     pl.when(jnp.logical_not(even))(lambda: put(first_ref, second_ref))
 
 
-def iterate_kernel(total_time, patching, plan_ref, limit_ref, *refs):
-    state_ref, first_ref, second_ref, signal_ref, next_first, next_second = refs[:6]
-    refs = refs[6:]
-    if patching:
-        (atoms_ref, reorder_ref), refs = refs[:2], refs[2:]
-    taps, state_out, *edges = refs[:4]
-    refs = refs[4:]
-    if patching:
-        taps, refs = refs[0], refs[1:]
-    zb, rb, zz, rr, fine, acc, beyond = refs[:7]
+def iterate_kernel(total_time, patching, copied, plan_ref, limit_ref, *refs):
+    refs = list(refs)
+
+    def take(count):
+        taken = refs[:count]
+        del refs[:count]
+        return taken
+
+    state_ref, first_ref, second_ref, signal_ref, next_first, next_second = take(6)
+    atoms = take(1 if patching else 0)
+    (taps,) = take(1)
+    source = take(1 if copied else 0)
+    take(1 if copied and copied[0] else 0)
+    state_out, *edges = take(3)
+    taps = (take(1) if patching else [taps])[0]
+    target = take(1 if copied else 0)
+    zb, rb, zz, rr, fine, acc, beyond = take(7)
+    ferry = Ferry(source[0], target[0], copied[0], *take(2)) if copied else None
     segment, channels = signal_ref.shape
     tiles = channels // LANES
     scale = (C * L) ** (-0.5)
@@ -256,9 +329,10 @@
     pl.when(even)(lambda: put(next_first))
     pl.when(jnp.logical_not(even))(lambda: put(next_second))
     if patching:
-        patch_taps(first_row_of(plan_ref, patching - 1), atoms_ref, taps, reorder_ref, refs[7])
+        columns, *turned = refs
+        patch_taps(first_row_of(plan_ref, patching - 1), atoms[0], taps, columns, turned)
     reach = segment + L
-    convolve(zb, L, reach, taps, zz, fine, acc)
+    convolve(zb, L, reach, taps, zz, fine, acc, ferry)
     moment = me * segment + lax.broadcasted_iota(jnp.int32, (reach, LANES), 0)
     inside = moment < total_time
     for tile in range(tiles):
@@ -266,25 +340,34 @@
         signal = jnp.concatenate([signal_ref[:, column], beyond[:, column]], axis=0)
         value = signal.astype(jnp.float32) - scale * acc[tile, :reach, :]
         rb[:, column] = jnp.where(inside, value, 0.0).astype(jnp.bfloat16)
-    correlate(rb, segment, taps, rr, fine, acc)
+    correlate(rb, segment, taps, rr, fine, acc, ferry)
     limit = limit_ref[...]
     stepped = state_ref[...] + code_rate * (scale * acc[0, :segment, :])
     state = stepped - jnp.clip(stepped, -limit, limit)
     state_out[...] = state
     put_edges(edges, state.astype(jnp.bfloat16))
-
-
-def iterate(plan, step, limit, state, swapped, signal, following, taps, atoms, reorder, peers):
+    if ferry:
+        ferry.close()
+
+
+def iterate(plan, step, limit, state, swapped, signal, following, taps, atoms, ferry, peers):
     segment, channels = signal.shape
     patching = atoms is not None
     reach = segment + L
+    carried = [far(value) for value in (ferry or ())[:2] if value is not None]
+    aliases = {9: 3} if patching else {}
+    if len(carried) == 2:
+        aliases[10 + patching] = 3 + patching
     return pl.pallas_call(
-        functools.partial(iterate_kernel, peers * segment, step if patching else 0),
-        in_specs=[scalars()] + [vmem()] * (8 + 2 * patching),
-        out_specs=[vmem()] * (3 + patching),
+        functools.partial(
+            iterate_kernel, peers * segment, step if patching else 0, ferry[2:] if ferry else None
+        ),
+        in_specs=[scalars()] + [vmem()] * (8 + patching) + [hbm()] * len(carried),
+        out_specs=[vmem()] * (3 + patching) + [hbm()] * (ferry is not None),
         out_shape=[pltpu.VMEM((segment, K), jnp.float32)]
         + [jax.ShapeDtypeStruct((L, K), jnp.bfloat16)] * 2
-        + [pltpu.VMEM(taps.shape, jnp.bfloat16)] * patching,
+        + [pltpu.VMEM(taps.shape, jnp.bfloat16)] * patching
+        + ([pltpu.HBM(ferry[0].shape, jnp.float32)] if ferry else []),
         scratch_shapes=[
             pltpu.VMEM((L + reach, K), jnp.bfloat16),
             pltpu.VMEM((reach, channels), jnp.bfloat16),
@@ -294,8 +377,13 @@
             pltpu.VMEM((channels // LANES, reach, LANES), jnp.float32),
             pltpu.VMEM((L, channels), jnp.bfloat16),
         ]
-        + [pltpu.VMEM((K, ROWS * L), jnp.bfloat16)] * patching,
-        input_output_aliases={10: 3} if patching else {},
+        + (ferry_scratch(ferry[3], ferry[0].shape[1]) if ferry else [])
+        + (
+            [pltpu.VMEM((K, GROUPS * ROWS * L), jnp.bfloat16)]
+            + [pltpu.VMEM((ROWS * STRIDE, K), jnp.float32)] * GROUPS
+        )
+        * patching,
+        input_output_aliases=aliases,
         compiler_params=pltpu.CompilerParams(vmem_limit_bytes=VMEM_BYTES),
         name="iterate",
     )(
@@ -305,24 +393,35 @@
         *swapped,
         resident(signal),
         *following,
-        *([resident(atoms), reorder] if patching else []),
+        *([resident(atoms)] if patching else []),
         resident(taps),
+        *carried,
     )
 
 
 def finish_kernel(
-    peers, step, plan_ref, state_ref, first_ref, second_ref, signal_ref, taps, payload_out, *refs
+    peers, step, copied, plan_ref, state_ref, first_ref, second_ref, signal_ref, taps, *refs
 ):
+    refs = list(refs)
+
+    def take(count):
+        taken = refs[:count]
+        del refs[:count]
+        return taken
+
     last = step + 1 == OUTER
-    if last:
-        resid_out, codes_out, zb, zz, fine, acc, tall = refs
-    else:
-        zb, zz, fine, acc, tall, codes_out = refs
+    source = take(2 if copied else 0)
+    (payload_out,) = take(1)
+    outs = take(2 if last else 0)
+    target = take(1 if copied else 0)
+    zb, zz, fine, acc, tall = take(5)
+    ferry = Ferry(source[0], target[0], copied[0], *take(2)) if copied else None
+    resid_out, codes_out = outs if last else (None, *refs)
     segment, channels = signal_ref.shape
     scale = (C * L) ** (-0.5)
     put_codes(zb, state_ref, first_ref, second_ref)
     codes_out[...] = state_ref[...].T
-    convolve(zb, L, segment, taps, zz, fine, acc)
+    convolve(zb, L, segment, taps, zz, fine, acc, ferry)
     for tile in range(channels // LANES):
         column = slice(tile * LANES, (tile + 1) * LANES)
         value = signal_ref[:, column].astype(jnp.float32) - scale * acc[tile, :segment, :]
@@ -338,22 +437,26 @@
         part = tall[peer * share : peer * share + share_rows, :]
         payload_out[peer, :share_rows, :] = part.astype(jnp.bfloat16)
         payload_out[peer, share_rows:, :] = block
-
-
-def finish(plan, step, state, swapped, signal, taps, peers):
+    if ferry:
+        ferry.close()
+
+
+def finish(plan, step, state, swapped, signal, taps, ferry, peers):
     segment, channels = signal.shape
     share = channels // peers
     share_rows = -(-share // ROWS) * ROWS
     last = step + 1 == OUTER
+    carried = [far(value) for value in (ferry or ())[:2]]
     return pl.pallas_call(
-        functools.partial(finish_kernel, peers, step),
-        in_specs=[scalars()] + [vmem()] * 5,
-        out_specs=[vmem()] * (3 if last else 1),
+        functools.partial(finish_kernel, peers, step, ferry[2:] if ferry else None),
+        in_specs=[scalars()] + [vmem()] * 5 + [hbm()] * len(carried),
+        out_specs=[vmem()] * (3 if last else 1) + [hbm()] * (len(carried) // 2),
         out_shape=[
             jax.ShapeDtypeStruct((peers, share_rows + BLOCK_ATOMS, segment), jnp.bfloat16),
             pltpu.VMEM((channels, segment), jnp.float32),
             pltpu.VMEM((K, segment), jnp.float32),
-        ][: 3 if last else 1],
+        ][: 3 if last else 1]
+        + [pltpu.HBM(value.shape, jnp.float32) for value in carried[1:]],
         scratch_shapes=[
             pltpu.VMEM((L + segment, K), jnp.bfloat16),
             pltpu.VMEM((segment + ROWS, COARSE * K), jnp.bfloat16),
@@ -361,10 +464,12 @@
             pltpu.VMEM((channels // LANES, segment, LANES), jnp.float32),
             pltpu.VMEM((channels + ROWS, segment), jnp.float32),
         ]
+        + (ferry_scratch(ferry[3], ferry[0].shape[1]) if ferry else [])
         + ([] if last else [pltpu.VMEM((K, segment), jnp.float32)]),
+        input_output_aliases={7: 3 if last else 1} if carried else {},
         compiler_params=pltpu.CompilerParams(vmem_limit_bytes=VMEM_BYTES),
         name="finish",
-    )(plan, resident(state), *swapped, resident(signal), resident(taps))
+    )(plan, resident(state), *swapped, resident(signal), resident(taps), *carried)
 
 
 def gradient_kernel(share, step, plan_ref, source_ref, blocks_ref, dict_hbm, out_ref, rf, zf, rr, zz, old, sem):
@@ -465,7 +570,7 @@
     return flips
 
 
-def gather_pieces(piece):
+def gather_pieces(piece, before_last):
     peers = lax.axis_size("tm")
 
     def exchanged(shard, mask):
@@ -474,7 +579,8 @@
     held = piece[None]
     for masks in gather_steps(peers):
         held = jnp.concatenate([held] + [exchanged(held, mask) for mask in masks], axis=0)
-    return held, exchanged(held, 1)
+    ready, _ = lax.optimization_barrier((held, before_last))
+    return held, exchanged(ready, 1)
 
 
 def recall_kernel(step, plan_ref, dict_hbm, piece_ref, old_ref, mean_ref, sem):
@@ -587,23 +693,31 @@
     state, signal, *edges = begin(codes_init, signal)
     following = swaps(edges)
     swapped = following
-    reorder = reorder_matrix()
-    taps, dictionary = layout(reorder, dictionary_init, channels)
-    atoms = None
+    taps = layout(dictionary_init, channels)
+    atoms = dictionary = None
     for step in range(OUTER):
-        for inner in range(INNER):
+        for inner in range(INNER + 1):
+            ferry = None
+            if step == 0:
+                ferry = (dictionary_init, dictionary, sum(COPIED[:inner]), COPIED[inner])
+            if inner == INNER:
+                payload, *finals = finish(plan, step, state, swapped, signal, taps, ferry, peers)
+                if ferry:
+                    *finals, dictionary = finals
+                break
             fresh = atoms if inner == 0 else None
             state, *results = iterate(
-                plan, step, limit, state, swapped, signal, following, taps, fresh, reorder, peers
+                plan, step, limit, state, swapped, signal, following, taps, fresh, ferry, peers
             )
             swapped = swaps(results[:2])
             if fresh is not None:
                 taps = results[2]
-        payload, *finals = finish(plan, step, state, swapped, signal, taps, peers)
+            if ferry:
+                dictionary = results[-1]
         blocks = lax.all_to_all(payload, "tm", 0, 0, tiled=True)
         piece = share_gradient(plan, step, blocks, dictionary, channels // peers)
-        held, came = gather_pieces(piece)
         old, mean_sq = recall(plan, step, dictionary, piece)
+        held, came = gather_pieces(piece, old)
         dictionary, *renewed = renew(plan, step, held, came, old, mean_sq, dictionary)
         atoms = renewed[0] if renewed else None
     residual, codes = finals
@@ -683,7 +797,7 @@
     fits = (
         lax.axis_size("chan") == 1
         and segment % LANES == 0
-        and channels % (4 * ROWS) == 0
+        and channels % (GROUPS * ROWS) == 0
         and channels % LANES == 0
         and channels % peers == 0
         and (channels // peers * L) % LANES == 0

time: 182 us -> 170 us (0.934)
  Pallas kernels: 82.2 us -> 75 us
  local copies, waits for them, and re-layouts: 4.44 us -> 1.44 us
    pallas_call x4, Pallas kernels: 28.4 us -> 20.2 us  [the longest x2 9.55 us: finish(): pl.pallas_call(functools.partial(finish_kernel, peers, step, ferry[2:] if...]
    unnamed x34 -> x26, local copies, waits for them, and re-layouts: 4.41 us -> 1.41 us
  transfers between devices with their start and end apart: 25 -> 25, of which waited for: 11 -> 9; matrix products, arithmetic and copies ran while one was open for 1% -> 1% of each run, Pallas kernels for 14% -> 9%
where the time goes in v7:
time: 170 us
  Pallas kernels  75 us (44%)
  starting transfers between devices  45.8 us (27%)
  waiting for transfers between devices  26.4 us (16%)
  blocking collectives  19.8 us (12%)
    pallas_call x4, Pallas kernels, iterate(): pl.pallas_call(functools.partial(iterate_kernel, peers * segment, step if...  34.9 us
    all_to_all x1, blocking collectives, whole_channels(): blocks = lax.all_to_all(payload, 'tm', 0, 0, tiled=True)  19.8 us
    ppermute x10, starting transfers between devices, swaps(): return [lax.ppermute(edge, 'tm', pair) for edge, pair in zip(edges, pairs)]  16.8 us
    ppermute x14, starting transfers between devices, exchanged(): return lax.ppermute(shard, 'tm', [(i, i ^ mask) for i in range(peers)])  16.2 us
    ppermute x14, waiting for transfers between devices, exchanged(): return lax.ppermute(shard, 'tm', [(i, i ^ mask) for i in range(peers)])  15 us
    all_to_all x1, starting transfers between devices, whole_channels(): blocks = lax.all_to_all(payload, 'tm', 0, 0, tiled=True)  12.9 us
    all_to_all x1, waiting for transfers between devices, whole_channels(): blocks = lax.all_to_all(payload, 'tm', 0, 0, tiled=True)  10.4 us
    pallas_call x2, Pallas kernels, finish(): pl.pallas_call(functools.partial(finish_kernel, peers, step, ferry[2:] if...  9.55 us
  transfers between devices with their start and end apart: 25, of which 9 were waited for; matrix products, arithmetic and copies ran while one was open for 1% of the time, Pallas kernels for 9%

profile of v7, /device:TPU:0, one launch (start us, length us, event | category | flops | bytes accessed | tf_op | source)
XLA Modules:
  0.0 169.8 jit_solution(10276073992006329476)
XLA Ops:
  2.9 9.5 %layout.1.refs_6_.taps.refs_7_ = bf16[6,16,384,128]{3,2,1,0:T(8,128)(2,1)S(1)} custom-call(f32[128,36864]{1,0:T(8,128)} %refs_0_.1), custom_call_target="tpu_custom_call" | custom-call | tf_op jit(solution)/shard_map/layout/pallas_call | solution.py:109
  12.5 9.9 %iterate.4 = (f32[128,128]{1,0:T(8,128)S(1)}, bf16[96,128]{1,0:T(8,128)(2,1)S(1)}, bf16[96,128]{1,0:T(8,128)(2,1)S(1)}, f32[128,36864]{1,0:T(8,128)}) custom-call(s32[8]{0:T(128)S(1)} %copy-done.1, f32[1,128]{1,0:T(1,128)S(1)} %bitcast.15, f32[128,128]{1,0:T(8,128)S(1)} %get-tuple-element.35.refs_0_, ...), custom_call_target="tpu_custom_call" | custom-call | tf_op jit(solution)/shard_map/iterate/pallas_call | solution.py:361
  22.4 3.9 %collective-permute-start.2 = (bf16[96,128]{1,0:T(8,128)(2,1)S(1)}, bf16[96,128]{1,0:T(8,128)(2,1)S(1)}, u32[]{:S(2)}, u32[]{:S(2)}) collective-permute-start(bf16[96,128]{1,0:T(8,128)(2,1)S(1)} %get-tuple-element.40), channel_id=1, source_target_pairs={{0,1},{1,0},{2,3},{3,2},{4,5},{5,4},{6,7},{7,6},{8,9},{9,8},{10,11... | collective-permute-start | bytes 73736 | tf_op jit(solution)/shard_map/ppermute | solution.py:691
  27.2 6.9 %iterate.5 = (f32[128,128]{1,0:T(8,128)S(1)}, bf16[96,128]{1,0:T(8,128)(2,1)S(1)}, bf16[96,128]{1,0:T(8,128)(2,1)S(1)}, f32[128,36864]{1,0:T(8,128)}) custom-call(s32[8]{0:T(128)S(1)} %copy-done.1, f32[1,128]{1,0:T(1,128)S(1)} %bitcast.16, f32[128,128]{1,0:T(8,128)S(1)} %get-tuple-element.39.refs_0_, ...), custom_call_target="tpu_custom_call", output_to_operand_aliasing={{3}: (10, {})} | custom-call | tf_op jit(solution)/shard_map/iterate/pallas_call | solution.py:361
  34.1 4.4 %collective-permute-start.4 = (bf16[96,128]{1,0:T(8,128)(2,1)S(1)}, bf16[96,128]{1,0:T(8,128)(2,1)S(1)}, u32[]{:S(2)}, u32[]{:S(2)}) collective-permute-start(bf16[96,128]{1,0:T(8,128)(2,1)S(1)} %get-tuple-element.44), channel_id=1, source_target_pairs={{0,1},{1,0},{2,3},{3,2},{4,5},{5,4},{6,7},{7,6},{8,9},{9,8},{10,11... | collective-permute-start | bytes 73736 | tf_op jit(solution)/shard_map/ppermute | solution.py:691
  39.3 5.6 %finish.2 = (bf16[32,32,128]{2,1,0:T(8,128)(2,1)}, f32[128,36864]{1,0:T(8,128)}) custom-call(s32[8]{0:T(128)S(1)} %copy-done.1, f32[128,128]{1,0:T(8,128)S(1)} %get-tuple-element.43.state_ref.refs_0_, bf16[96,128]{1,0:T(8,128)(2,1)S(1)} %collective-permute-done.4.first_ref.refs_1_, ...), custom_call_target="tpu_custom_call", output_to_operand_aliasing={{1}: (7, {})} | custom-call | tf_op jit(solution)/shard_map/finish/pallas_call | solution.py:450
  44.9 12.9 %all-to-all-start = ((bf16[32,32,128]{2,1,0:T(8,128)(2,1)}), bf16[32,32,128]{2,1,0:T(8,128)(2,1)S(1)}, u32[]{:S(2)}, u32[]{:S(2)}) async-start(bf16[32,32,128]{2,1,0:T(8,128)(2,1)} %get-tuple-element.47), calls=%async_computation | async-start | bytes 524288 | tf_op jit(solution)/shard_map/all_to_all | solution.py:717
  57.9 10.4 %all-to-all-done.blocks_ref = bf16[32,32,128]{2,1,0:T(8,128)(2,1)S(1)} async-done(((bf16[32,32,128]{2,1,0:T(8,128)(2,1)}), bf16[32,32,128]{2,1,0:T(8,128)(2,1)S(1)}, u32[]{:S(2)}, u32[]{:S(2)}) %all-to-all-start) | async-done | bytes 262176 | tf_op jit(solution)/shard_map/all_to_all | solution.py:717
  68.2 3.7 %gradient.2.piece_ref = bf16[16,1280]{1,0:T(8,128)(2,1)S(1)} custom-call(s32[8]{0:T(128)S(1)} %copy-done.1, s32[1,1152]{1,0:T(1,128)S(1)} %fusion.source_ref, bf16[32,32,128]{2,1,0:T(8,128)(2,1)S(1)} %all-to-all-done.blocks_ref, f32[128,36864]{1,0:T(8,128)} %get-tuple-element.48.dict_hbm), custom_call_target="tpu_custom_call" | custom-call | tf_op jit(solution)/shard_map/gradient/pallas_call | solution.py:540
  73.3 3.1 %collective-permute-start.6 = (bf16[1,16,1280]{2,1,0:T(8,128)(2,1)S(1)}, bf16[1,16,1280]{2,1,0:T(8,128)(2,1)S(1)}, u32[]{:S(2)}, u32[]{:S(2)}) collective-permute-start(bf16[1,16,1280]{2,1,0:T(8,128)(2,1)S(1)} %bitcast.13), channel_id=1, source_target_pairs={{0,16},{1,17},{2,18},{3,19},{4,20},{5,21},{6,22},{7,23},{8,24},{9,... | collective-permute-start | bytes 122888 | tf_op jit(solution)/shard_map/ppermute | solution.py:577
  76.4 2.9 %recall.2 = (f32[16,36864]{1,0:T(8,128)S(1)}, f32[16,128]{1,0:T(8,128)S(1)}) custom-call(s32[8]{0:T(128)S(1)} %copy-done.1, f32[128,36864]{1,0:T(8,128)} %get-tuple-element.48.dict_hbm, bf16[16,1280]{1,0:T(8,128)(2,1)S(1)} %gradient.2.piece_ref), custom_call_target="tpu_custom_call" | custom-call | tf_op jit(solution)/shard_map/recall/pallas_call | solution.py:606
  82.9 6.1 %collective-permute-done.9 = bf16[4,16,1280]{2,1,0:T(8,128)(2,1)S(1)} collective-permute-done((bf16[4,16,1280]{2,1,0:T(8,128)(2,1)S(1)}, bf16[4,16,1280]{2,1,0:T(8,128)(2,1)S(1)}, u32[]{:S(2)}, u32[]{:S(2)}) %collective-permute-start.9) | collective-permute-done | bytes 163872 | tf_op jit(solution)/shard_map/ppermute | solution.py:577
  89.2 2.1 %collective-permute-done.12.came_ref = bf16[16,16,1280]{2,1,0:T(8,128)(2,1)S(1)} collective-permute-done((bf16[16,16,1280]{2,1,0:T(8,128)(2,1)S(1)}, bf16[16,16,1280]{2,1,0:T(8,128)(2,1)S(1)}, u32[]{:S(2)}, u32[]{:S(2)}) %collective-permute-start.12) | collective-permute-done | bytes 655392 | tf_op jit(solution)/shard_map/ppermute | solution.py:577
  91.3 3.5 %renew.2 = (f32[128,36864]{1,0:T(8,128)}, f32[16,36864]{1,0:T(8,128)S(1)}) custom-call(s32[8]{0:T(128)S(1)} %copy-done.1, bf16[16,16,1280]{2,1,0:T(8,128)(2,1)S(1)} %constant_dynamic-update-slice_fusion.held_ref, bf16[16,16,1280]{2,1,0:T(8,128)(2,1)S(1)} %collective-permute-done.12.came_ref, ...), custom_call_target="tpu_custom_call", output_to_operand_aliasing={{0}: (5, {})} | custom-call | tf_op jit(solution)/shard_map/renew/pallas_call | solution.py:668
  94.8 12.7 %iterate.6 = (f32[128,128]{1,0:T(8,128)S(1)}, bf16[96,128]{1,0:T(8,128)(2,1)S(1)}, bf16[96,128]{1,0:T(8,128)(2,1)S(1)}, bf16[6,16,384,128]{3,2,1,0:T(8,128)(2,1)S(1)}) custom-call(s32[8]{0:T(128)S(1)} %copy-done.1, f32[1,128]{1,0:T(1,128)S(1)} %bitcast.17, f32[128,128]{1,0:T(8,128)S(1)} %get-tuple-element.43.state_ref.refs_0_, ...), custom_call_target="tpu_custom_call", output_to_operand_aliasing={{3}: (9, {})} | custom-call | tf_op jit(solution)/shard_map/iterate/pallas_call | solution.py:361
  108.7 5.5 %iterate.7 = (f32[128,128]{1,0:T(8,128)S(1)}, bf16[96,128]{1,0:T(8,128)(2,1)S(1)}, bf16[96,128]{1,0:T(8,128)(2,1)S(1)}) custom-call(s32[8]{0:T(128)S(1)} %copy-done.1, f32[1,128]{1,0:T(1,128)S(1)} %bitcast.18, f32[128,128]{1,0:T(8,128)S(1)} %get-tuple-element.53.refs_0_, bf16[96,128]{1,0:T(8,128)(2,1)S(1)} %collective-permute-done.13.refs_1_, ...), custom_call_target="tpu_custom_call" | custom-call | tf_op jit(solution)/shard_map/iterate/pallas_call | solution.py:361
  114.2 4.5 %collective-permute-start.15 = (bf16[96,128]{1,0:T(8,128)(2,1)S(1)}, bf16[96,128]{1,0:T(8,128)(2,1)S(1)}, u32[]{:S(2)}, u32[]{:S(2)}) collective-permute-start(bf16[96,128]{1,0:T(8,128)(2,1)S(1)} %get-tuple-element.58), channel_id=1, source_target_pairs={{0,1},{1,0},{2,3},{3,2},{4,5},{5,4},{6,7},{7,6},{8,9},{9,8},{10,11... | collective-permute-start | bytes 73736 | tf_op jit(solution)/shard_map/ppermute | solution.py:691
  119.6 4.0 %finish.3 = (bf16[32,32,128]{2,1,0:T(8,128)(2,1)S(1)}, f32[384,128]{1,0:T(8,128)S(1)}, f32[128,128]{1,0:T(8,128)S(1)}) custom-call(s32[8]{0:T(128)S(1)} %copy-done.1, f32[128,128]{1,0:T(8,128)S(1)} %get-tuple-element.57.state_ref, bf16[96,128]{1,0:T(8,128)(2,1)S(1)} %collective-permute-done.15.first_ref, ...), custom_call_target="tpu_custom_call" | custom-call | tf_op jit(solution)/shard_map/finish/pallas_call | solution.py:450
  123.6 19.8 %all_to_all.10.blocks_ref = bf16[32,32,128]{2,1,0:T(8,128)(2,1)S(1)} all-to-all(bf16[32,32,128]{2,1,0:T(8,128)(2,1)S(1)} %get-tuple-element.61), channel_id=1, replica_groups=mesh['tm'=32,'chan'=1] {'tm'}, dimensions={0} | all-to-all | bytes 524288 | tf_op jit(solution)/shard_map/all_to_all | solution.py:717
  143.3 3.7 %gradient.3.piece_ref = bf16[16,1280]{1,0:T(8,128)(2,1)S(1)} custom-call(s32[8]{0:T(128)S(1)} %copy-done.1, s32[1,1152]{1,0:T(1,128)S(1)} %fusion.source_ref, bf16[32,32,128]{2,1,0:T(8,128)(2,1)S(1)} %all_to_all.10.blocks_ref, f32[128,36864]{1,0:T(8,128)} %get-tuple-element.62.dict_hbm), custom_call_target="tpu_custom_call" | custom-call | tf_op jit(solution)/shard_map/gradient/pallas_call | solution.py:540
  148.4 3.1 %collective-permute-start.17 = (bf16[1,16,1280]{2,1,0:T(8,128)(2,1)S(1)}, bf16[1,16,1280]{2,1,0:T(8,128)(2,1)S(1)}, u32[]{:S(2)}, u32[]{:S(2)}) collective-permute-start(bf16[1,16,1280]{2,1,0:T(8,128)(2,1)S(1)} %bitcast.9), channel_id=1, source_target_pairs={{0,16},{1,17},{2,18},{3,19},{4,20},{5,21},{6,22},{7,23},{8,24},{9,... | collective-permute-start | bytes 122888 | tf_op jit(solution)/shard_map/ppermute | solution.py:577
  151.5 2.6 %recall.3 = (f32[16,36864]{1,0:T(8,128)S(1)}, f32[16,128]{1,0:T(8,128)S(1)}) custom-call(s32[8]{0:T(128)S(1)} %copy-done.1, f32[128,36864]{1,0:T(8,128)} %get-tuple-element.62.dict_hbm, bf16[16,1280]{1,0:T(8,128)(2,1)S(1)} %gradient.3.piece_ref), custom_call_target="tpu_custom_call" | custom-call | tf_op jit(solution)/shard_map/recall/pallas_call | solution.py:606
  157.8 6.1 %collective-permute-done.20 = bf16[4,16,1280]{2,1,0:T(8,128)(2,1)S(1)} collective-permute-done((bf16[4,16,1280]{2,1,0:T(8,128)(2,1)S(1)}, bf16[4,16,1280]{2,1,0:T(8,128)(2,1)S(1)}, u32[]{:S(2)}, u32[]{:S(2)}) %collective-permute-start.20) | collective-permute-done | bytes 163872 | tf_op jit(solution)/shard_map/ppermute | solution.py:577
  166.1 3.5 %renew.3 = f32[128,36864]{1,0:T(8,128)} custom-call(s32[8]{0:T(128)S(1)} %copy-done.1, bf16[16,16,1280]{2,1,0:T(8,128)(2,1)S(1)} %constant_dynamic-update-slice_fusion.7.held_ref, bf16[16,16,1280]{2,1,0:T(8,128)(2,1)S(1)} %collective-permute-done.23.came_ref, f32[16,36864]{1,0:T(8,128)S(1)} %get-tuple-element.63.old, ...), custom_call_target="tpu_custom_call", output_to_operand_aliasing={{}: (5, {})} | custom-call | tf_op jit(solution)/shard_map/renew/pallas_call | solution.py:668
  (73 shorter events, 18.5 us)
Async XLA Ops:
  1.8 10.7 %collective-permute-start = (bf16[96,512]{1,0:T(8,128)(2,1)S(1)}, bf16[96,512]{1,0:T(8,128)(2,1)S(1)}, u32[]{:S(2)}, u32[]{:S(2)}) collective-permute-start(bf16[96,512]{1,0:T(8,128)(2,1)S(1)} %get-tuple-element.36), channel_id=1, source_target_pairs={{0,1},{1,0},{2,3},{3,2},{4,5},{5,4},{6,7},{7,6},{8,9},{9,8},{10,11... | collective-permute-start | bytes 294920 | tf_op jit(solution)/shard_map/ppermute | solution.py:691
  2.3 10.2 %collective-permute-start.1 = (bf16[96,512]{1,0:T(8,128)(2,1)S(1)}, bf16[96,512]{1,0:T(8,128)(2,1)S(1)}, u32[]{:S(2)}, u32[]{:S(2)}) collective-permute-start(bf16[96,512]{1,0:T(8,128)(2,1)S(1)} %get-tuple-element.37), channel_id=1, source_target_pairs={{1,2},{2,1},{3,4},{4,3},{5,6},{6,5},{7,8},{8,7},{9,10},{10,9},{11,... | collective-permute-start | bytes 294920 | tf_op jit(solution)/shard_map/ppermute | solution.py:691
  22.4 4.8 %collective-permute-start.2 = (bf16[96,128]{1,0:T(8,128)(2,1)S(1)}, bf16[96,128]{1,0:T(8,128)(2,1)S(1)}, u32[]{:S(2)}, u32[]{:S(2)}) collective-permute-start(bf16[96,128]{1,0:T(8,128)(2,1)S(1)} %get-tuple-element.40), channel_id=1, source_target_pairs={{0,1},{1,0},{2,3},{3,2},{4,5},{5,4},{6,7},{7,6},{8,9},{9,8},{10,11... | collective-permute-start | bytes 73736 | tf_op jit(solution)/shard_map/ppermute | solution.py:691
  26.3 0.9 collective-permute-start.3
  34.1 5.2 %collective-permute-start.4 = (bf16[96,128]{1,0:T(8,128)(2,1)S(1)}, bf16[96,128]{1,0:T(8,128)(2,1)S(1)}, u32[]{:S(2)}, u32[]{:S(2)}) collective-permute-start(bf16[96,128]{1,0:T(8,128)(2,1)S(1)} %get-tuple-element.44), channel_id=1, source_target_pairs={{0,1},{1,0},{2,3},{3,2},{4,5},{5,4},{6,7},{7,6},{8,9},{9,8},{10,11... | collective-permute-start | bytes 73736 | tf_op jit(solution)/shard_map/ppermute | solution.py:691
  44.9 23.3 %all-to-all-start = ((bf16[32,32,128]{2,1,0:T(8,128)(2,1)}), bf16[32,32,128]{2,1,0:T(8,128)(2,1)S(1)}, u32[]{:S(2)}, u32[]{:S(2)}) async-start(bf16[32,32,128]{2,1,0:T(8,128)(2,1)} %get-tuple-element.47), calls=%async_computation | async-start | bytes 524288 | tf_op jit(solution)/shard_map/all_to_all | solution.py:717
  71.9 7.4 %collective-permute-start.8 = (bf16[1,16,1280]{2,1,0:T(8,128)(2,1)S(1)}, bf16[1,16,1280]{2,1,0:T(8,128)(2,1)S(1)}, u32[]{:S(2)}, u32[]{:S(2)}) collective-permute-start(bf16[1,16,1280]{2,1,0:T(8,128)(2,1)S(1)} %bitcast.11), channel_id=1, source_target_pairs={{0,24},{1,25},{2,26},{3,27},{4,28},{5,29},{6,30},{7,31},{8,16},{9,... | collective-permute-start | bytes 122888 | tf_op jit(solution)/shard_map/ppermute | solution.py:577
  73.3 6.0 %collective-permute-start.7 = (bf16[1,16,1280]{2,1,0:T(8,128)(2,1)S(1)}, bf16[1,16,1280]{2,1,0:T(8,128)(2,1)S(1)}, u32[]{:S(2)}, u32[]{:S(2)}) collective-permute-start(bf16[1,16,1280]{2,1,0:T(8,128)(2,1)S(1)} %bitcast.12), channel_id=1, source_target_pairs={{0,8},{1,9},{2,10},{3,11},{4,12},{5,13},{6,14},{7,15},{8,0},{9,1},... | collective-permute-start | bytes 122888 | tf_op jit(solution)/shard_map/ppermute | solution.py:577
  73.3 6.0 %collective-permute-start.6 = (bf16[1,16,1280]{2,1,0:T(8,128)(2,1)S(1)}, bf16[1,16,1280]{2,1,0:T(8,128)(2,1)S(1)}, u32[]{:S(2)}, u32[]{:S(2)}) collective-permute-start(bf16[1,16,1280]{2,1,0:T(8,128)(2,1)S(1)} %bitcast.13), channel_id=1, source_target_pairs={{0,16},{1,17},{2,18},{3,19},{4,20},{5,21},{6,22},{7,23},{8,24},{9,... | collective-permute-start | bytes 122888 | tf_op jit(solution)/shard_map/ppermute | solution.py:577
  79.4 9.7 %collective-permute-start.11 = (bf16[4,16,1280]{2,1,0:T(8,128)(2,1)S(1)}, bf16[4,16,1280]{2,1,0:T(8,128)(2,1)S(1)}, u32[]{:S(2)}, u32[]{:S(2)}) collective-permute-start(bf16[4,16,1280]{2,1,0:T(8,128)(2,1)S(1)} %pad_maximum_fusion), channel_id=1, source_target_pairs={{0,6},{1,7},{2,4},{3,5},{4,2},{5,3},{6,0},{7,1},{8,14},{9,15},{10,... | collective-permute-start | bytes 491528 | tf_op jit(solution)/shard_map/ppermute | solution.py:577
  80.6 8.4 %collective-permute-start.10 = (bf16[4,16,1280]{2,1,0:T(8,128)(2,1)S(1)}, bf16[4,16,1280]{2,1,0:T(8,128)(2,1)S(1)}, u32[]{:S(2)}, u32[]{:S(2)}) collective-permute-start(bf16[4,16,1280]{2,1,0:T(8,128)(2,1)S(1)} %pad_maximum_fusion), channel_id=1, source_target_pairs={{0,2},{1,3},{2,0},{3,1},{4,6},{5,7},{6,4},{7,5},{8,10},{9,11},{10,... | collective-permute-start | bytes 491528 | tf_op jit(solution)/shard_map/ppermute | solution.py:577
  81.8 7.2 %collective-permute-start.9 = (bf16[4,16,1280]{2,1,0:T(8,128)(2,1)S(1)}, bf16[4,16,1280]{2,1,0:T(8,128)(2,1)S(1)}, u32[]{:S(2)}, u32[]{:S(2)}) collective-permute-start(bf16[4,16,1280]{2,1,0:T(8,128)(2,1)S(1)} %pad_maximum_fusion), channel_id=1, source_target_pairs={{0,4},{1,5},{2,6},{3,7},{4,0},{5,1},{6,2},{7,3},{8,12},{9,13},{10,... | collective-permute-start | bytes 491528 | tf_op jit(solution)/shard_map/ppermute | solution.py:577
  89.1 2.2 %collective-permute-start.12 = (bf16[16,16,1280]{2,1,0:T(8,128)(2,1)S(1)}, bf16[16,16,1280]{2,1,0:T(8,128)(2,1)S(1)}, u32[]{:S(2)}, u32[]{:S(2)}) collective-permute-start(bf16[16,16,1280]{2,1,0:T(8,128)(2,1)S(1)} %constant_dynamic-update-slice_fusion.held_ref), channel_id=1, source_target_pairs={{0,1},{1,0},{2,3},{3,2},{4,5},{5,4},{6,7},{7,6},{8,9},{9,8},{10,11... | collective-permute-start | bytes 1966088 | tf_op jit(solution)/shard_map/ppermute | solution.py:577
  107.5 1.3 collective-permute-start.13
  107.7 1.1 collective-permute-start.14
  114.2 5.4 %collective-permute-start.15 = (bf16[96,128]{1,0:T(8,128)(2,1)S(1)}, bf16[96,128]{1,0:T(8,128)(2,1)S(1)}, u32[]{:S(2)}, u32[]{:S(2)}) collective-permute-start(bf16[96,128]{1,0:T(8,128)(2,1)S(1)} %get-tuple-element.58), channel_id=1, source_target_pairs={{0,1},{1,0},{2,3},{3,2},{4,5},{5,4},{6,7},{7,6},{8,9},{9,8},{10,11... | collective-permute-start | bytes 73736 | tf_op jit(solution)/shard_map/ppermute | solution.py:691
  118.7 0.9 collective-permute-start.16
  147.0 7.1 %collective-permute-start.19 = (bf16[1,16,1280]{2,1,0:T(8,128)(2,1)S(1)}, bf16[1,16,1280]{2,1,0:T(8,128)(2,1)S(1)}, u32[]{:S(2)}, u32[]{:S(2)}) collective-permute-start(bf16[1,16,1280]{2,1,0:T(8,128)(2,1)S(1)} %bitcast.7), channel_id=1, source_target_pairs={{0,24},{1,25},{2,26},{3,27},{4,28},{5,29},{6,30},{7,31},{8,16},{9,... | collective-permute-start | bytes 122888 | tf_op jit(solution)/shard_map/ppermute | solution.py:577
  148.4 5.7 %collective-permute-start.18 = (bf16[1,16,1280]{2,1,0:T(8,128)(2,1)S(1)}, bf16[1,16,1280]{2,1,0:T(8,128)(2,1)S(1)}, u32[]{:S(2)}, u32[]{:S(2)}) collective-permute-start(bf16[1,16,1280]{2,1,0:T(8,128)(2,1)S(1)} %bitcast.8), channel_id=1, source_target_pairs={{0,8},{1,9},{2,10},{3,11},{4,12},{5,13},{6,14},{7,15},{8,0},{9,1},... | collective-permute-start | bytes 122888 | tf_op jit(solution)/shard_map/ppermute | solution.py:577
  148.4 5.7 %collective-permute-start.17 = (bf16[1,16,1280]{2,1,0:T(8,128)(2,1)S(1)}, bf16[1,16,1280]{2,1,0:T(8,128)(2,1)S(1)}, u32[]{:S(2)}, u32[]{:S(2)}) collective-permute-start(bf16[1,16,1280]{2,1,0:T(8,128)(2,1)S(1)} %bitcast.9), channel_id=1, source_target_pairs={{0,16},{1,17},{2,18},{3,19},{4,20},{5,21},{6,22},{7,23},{8,24},{9,... | collective-permute-start | bytes 122888 | tf_op jit(solution)/shard_map/ppermute | solution.py:577
  154.2 9.7 %collective-permute-start.22 = (bf16[4,16,1280]{2,1,0:T(8,128)(2,1)S(1)}, bf16[4,16,1280]{2,1,0:T(8,128)(2,1)S(1)}, u32[]{:S(2)}, u32[]{:S(2)}) collective-permute-start(bf16[4,16,1280]{2,1,0:T(8,128)(2,1)S(1)} %pad_maximum_fusion.1), channel_id=1, source_target_pairs={{0,6},{1,7},{2,4},{3,5},{4,2},{5,3},{6,0},{7,1},{8,14},{9,15},{10,... | collective-permute-start | bytes 491528 | tf_op jit(solution)/shard_map/ppermute | solution.py:577
  155.4 8.4 %collective-permute-start.21 = (bf16[4,16,1280]{2,1,0:T(8,128)(2,1)S(1)}, bf16[4,16,1280]{2,1,0:T(8,128)(2,1)S(1)}, u32[]{:S(2)}, u32[]{:S(2)}) collective-permute-start(bf16[4,16,1280]{2,1,0:T(8,128)(2,1)S(1)} %pad_maximum_fusion.1), channel_id=1, source_target_pairs={{0,2},{1,3},{2,0},{3,1},{4,6},{5,7},{6,4},{7,5},{8,10},{9,11},{10,... | collective-permute-start | bytes 491528 | tf_op jit(solution)/shard_map/ppermute | solution.py:577
  156.6 7.2 %collective-permute-start.20 = (bf16[4,16,1280]{2,1,0:T(8,128)(2,1)S(1)}, bf16[4,16,1280]{2,1,0:T(8,128)(2,1)S(1)}, u32[]{:S(2)}, u32[]{:S(2)}) collective-permute-start(bf16[4,16,1280]{2,1,0:T(8,128)(2,1)S(1)} %pad_maximum_fusion.1), channel_id=1, source_target_pairs={{0,4},{1,5},{2,6},{3,7},{4,0},{5,1},{6,2},{7,3},{8,12},{9,13},{10,... | collective-permute-start | bytes 491528 | tf_op jit(solution)/shard_map/ppermute | solution.py:577
  163.9 2.2 %collective-permute-start.23 = (bf16[16,16,1280]{2,1,0:T(8,128)(2,1)S(1)}, bf16[16,16,1280]{2,1,0:T(8,128)(2,1)S(1)}, u32[]{:S(2)}, u32[]{:S(2)}) collective-permute-start(bf16[16,16,1280]{2,1,0:T(8,128)(2,1)S(1)} %constant_dynamic-update-slice_fusion.7.held_ref), channel_id=1, source_target_pairs={{0,1},{1,0},{2,3},{3,2},{4,5},{5,4},{6,7},{7,6},{8,9},{9,8},{10,11... | collective-permute-start | bytes 1966088 | tf_op jit(solution)/shard_map/ppermute | solution.py:577
  (7 other events, 91.8 us)

commit v8 on v7

--- a/solution.py
+++ b/solution.py
@@ -23,7 +23,7 @@
 STRIDE = L + 1
 GROUPS = 4
 SUBLANES = 8
-COPIED = (56, 48, 24)
+COPIED = (16, 24, 16, 48, 24, 0)
 FINE = 4
 LANES = 128
 VMEM_BYTES = 24 * 1024 * 1024
@@ -67,24 +67,28 @@
     row = lax.broadcasted_iota(jnp.int32, (side, side), 0)
     column = lax.broadcasted_iota(jnp.int32, (side, side), 1)
     identity = (row == column).astype(jnp.float32).astype(jnp.bfloat16)
-    columns = columns.astype(jnp.bfloat16)
-    for first in range(0, ROWS * L, 2 * side):
+
+    def put(entry, rows):
+        end = entry + rows.shape[0]
+        begin = entry
+        while begin < end:
+            channel, tap = begin // L, begin % L
+            count = min(end - begin, L - tap)
+            target = channel * STRIDE + tap
+            turned_ref[target : target + count, :] = rows[begin - entry : begin - entry + count]
+            begin += count
+
+    low = columns.astype(jnp.bfloat16)
+    through_matrix = ROWS * L // (6 * side) * 4 * side
+    for first in range(0, through_matrix, 2 * side):
         pair = jnp.concatenate(
-            [columns[:, first + half * side : first + (half + 1) * side] for half in range(2)], axis=0
+            [low[:, first + half * side : first + (half + 1) * side] for half in range(2)], axis=0
         )
         turned = lax.dot_general(identity, pair, NT, preferred_element_type=jnp.float32)
         for half in range(2):
-            entry = first + half * side
-            end = entry + side
-            begin = entry
-            while begin < end:
-                channel, tap = begin // L, begin % L
-                count = min(end - begin, L - tap)
-                target = channel * STRIDE + tap
-                turned_ref[target : target + count, :] = turned[
-                    begin - entry : begin - entry + count, half * K : (half + 1) * K
-                ]
-                begin += count
+            put(first + half * side, turned[:, half * K : (half + 1) * K])
+    for first in range(through_matrix, ROWS * L, LANES):
+        put(first, columns[:, first : first + LANES].astype(jnp.float32).T)
 
 
 def tap_of(turned_ref, tap):
@@ -472,7 +476,7 @@
     )(plan, resident(state), *swapped, resident(signal), resident(taps), *carried)
 
 
-def gradient_kernel(share, step, plan_ref, source_ref, blocks_ref, dict_hbm, out_ref, rf, zf, rr, zz, old, sem):
+def gradient_kernel(share, step, plan_ref, blocks_ref, dict_hbm, out_ref, rf, zf, rr, zz, old, sem):
     peers, rows, segment = blocks_ref.shape
     share_rows = rows - BLOCK_ATOMS
     span = peers * segment
@@ -503,25 +507,33 @@
     for _ in range(3):
         parts.append(left.astype(jnp.bfloat16))
         left = left - parts[-1].astype(jnp.float32)
-    total = jnp.zeros((3 * BLOCK_ATOMS, entries), jnp.float32)
-    for coarse in range(COARSE):
-        row = lax.broadcasted_iota(jnp.int32, (wide, entries), 0) + coarse * wide
-        chosen = (row == source_ref[...]).astype(jnp.float32).astype(jnp.bfloat16)
-        total += lax.dot_general(
-            jnp.concatenate(
-                [part[coarse * BLOCK_ATOMS : (coarse + 1) * BLOCK_ATOMS, :] for part in parts], axis=0
-            ),
-            chosen,
-            NN,
-            preferred_element_type=jnp.float32,
-        )
-    gradient = total[:BLOCK_ATOMS] + total[BLOCK_ATOMS : 2 * BLOCK_ATOMS] + total[2 * BLOCK_ATOMS :]
+    row = lax.broadcasted_iota(jnp.int32, (wide, wide), 0)
+    column = lax.broadcasted_iota(jnp.int32, (wide, wide), 1)
+    chosen = (row // share_rows == column % ROWS) & (row % share_rows == column // ROWS)
+    chosen = chosen.astype(jnp.float32).astype(jnp.bfloat16)
+    by_channel = lax.dot_general(
+        jnp.concatenate(parts, axis=0), chosen, NN, preferred_element_type=jnp.float32
+    )
+    count = COARSE * BLOCK_ATOMS
+    by_channel = by_channel[:count] + by_channel[count : 2 * count] + by_channel[2 * count :]
+    lane = lax.broadcasted_iota(jnp.int32, (BLOCK_ATOMS, LANES), 1)
+    tiles = []
+    for tile in range(entries // LANES):
+        total = jnp.zeros((BLOCK_ATOMS, LANES), jnp.float32)
+        for place in range(LANES // ROWS):
+            channel, coarse = divmod(tile * (LANES // ROWS) + place, COARSE)
+            first = channel * ROWS // LANES * LANES
+            source = by_channel[coarse * BLOCK_ATOMS : (coarse + 1) * BLOCK_ATOMS, first : first + LANES]
+            by = (place * ROWS - channel * ROWS) % LANES
+            moved = pltpu.roll(source, by, 1) if by else source
+            total = jnp.where(lane // ROWS == place, moved, total)
+        tiles.append(total)
+    gradient = jnp.concatenate(tiles, axis=1)
     fetch.wait()
     before = old[...]
     square = jnp.sum(before * before, axis=1, keepdims=True)
     along = jnp.sum(gradient * before, axis=1, keepdims=True) / (square + tiny_eps)
     out_ref[:, :entries] = (gradient - along * before).astype(jnp.bfloat16)
-    lane = lax.broadcasted_iota(jnp.int32, (BLOCK_ATOMS, LANES), 1)
     terms = jnp.zeros((BLOCK_ATOMS, LANES), jnp.float32)
     for i in range(3):
         term = along.astype(jnp.bfloat16).astype(jnp.float32)
@@ -534,12 +546,9 @@
     peers, rows, segment = blocks.shape
     share_rows = rows - BLOCK_ATOMS
     span = peers * segment
-    entry = jnp.arange(share * L, dtype=jnp.int32)
-    channel, tap = entry // L, entry % L
-    source = (tap // ROWS) * (ROWS * share_rows) + (tap % ROWS) * share_rows + channel
     return pl.pallas_call(
         functools.partial(gradient_kernel, share, step),
-        in_specs=[scalars(), vmem(), vmem(), hbm()],
+        in_specs=[scalars(), vmem(), hbm()],
         out_shape=jax.ShapeDtypeStruct((BLOCK_ATOMS, share * L + LANES), jnp.bfloat16),
         scratch_shapes=[
             pltpu.VMEM((share_rows, span + LANES), jnp.float32),
@@ -551,7 +560,7 @@
         ],
         compiler_params=pltpu.CompilerParams(vmem_limit_bytes=VMEM_BYTES),
         name="gradient",
-    )(plan, source[None, :], blocks, far(dictionary))
+    )(plan, blocks, far(dictionary))
 
 
 def gather_steps(peers):
@@ -570,16 +579,19 @@
     return flips
 
 
-def gather_pieces(piece, before_last):
+def gather_pieces(piece, meanwhile):
     peers = lax.axis_size("tm")
 
     def exchanged(shard, mask):
         return lax.ppermute(shard, "tm", [(i, i ^ mask) for i in range(peers)])
 
     held = piece[None]
+    beside = None
     for masks in gather_steps(peers):
         held = jnp.concatenate([held] + [exchanged(held, mask) for mask in masks], axis=0)
-    ready, _ = lax.optimization_barrier((held, before_last))
+        if beside is None:
+            beside = meanwhile(held)
+    ready, _ = lax.optimization_barrier((held, beside))
     return held, exchanged(ready, 1)
 
 
@@ -617,13 +629,27 @@
     )(plan, far(dictionary), piece)
 
 
-def renew_kernel(plan_step, plan_ref, held_ref, came_ref, old, mean_ref, dict_hbm, out_hbm, atoms_ref, grad, sems):
-    del dict_hbm
+def renew_kernel(plan_step, earlier, plan_ref, held_ref, came_ref, old, mean_ref, *refs):
     me = lax.axis_index("tm")
-    first_row = first_row_of(plan_ref, plan_step)
     half, _, wide = held_ref.shape
     width = wide - LANES
     entries = C * L
+    before_refs, refs = refs[:earlier], refs[earlier:]
+    last = plan_step + 1 == OUTER
+    if last:
+        _, out_hbm, atoms_ref, grad, sems = refs
+    else:
+        atoms_ref, grad = refs
+
+    def rows_of(step):
+        return pl.ds(first_row_of(plan_ref, step), BLOCK_ATOMS)
+
+    stores = []
+    for step in range(earlier):
+        stores.append(
+            pltpu.make_async_copy(before_refs[step], out_hbm.at[rows_of(step)], sems.at[2 * half + step])
+        )
+        stores[-1].start()
     shares = []
     for slot, flips in enumerate(gather_slots(2 * half)):
         for source, extra in ((held_ref, 0), (came_ref, 1)):
@@ -642,43 +668,49 @@
     square = zeros
     for _, column in shares:
         value = grad[:, column] - along * old[:, column]
-        grad[:, column] = value
         square += value * value
     spread = jnp.sum(square, axis=1, keepdims=True) / entries + tiny_eps
     step = move_rate / jnp.sqrt(spread)
     norm = 1.0 / jnp.sqrt(mean_sq + 0.25)
-    stores = []
     for index, (_, column) in enumerate(shares):
-        atoms_ref[:, column] = (old[:, column] + step * grad[:, column]) * norm
-        stores.append(
-            pltpu.make_async_copy(
-                atoms_ref.at[:, column],
-                out_hbm.at[pl.ds(first_row, BLOCK_ATOMS), column],
-                sems.at[index],
+        before = old[:, column]
+        across = grad[:, column] - along * before
+        atoms_ref[:, column] = (before + step * across) * norm
+        if last:
+            stores.append(
+                pltpu.make_async_copy(
+                    atoms_ref.at[:, column], out_hbm.at[rows_of(plan_step), column], sems.at[index]
+                )
             )
-        )
-        stores[-1].start()
+            stores[-1].start()
     for store in stores:
         store.wait()
 
 
-def renew(plan, step, held, came, old, mean_sq, dictionary):
-    entries = dictionary.shape[1]
+def renew(plan, step, held, came, old, mean_sq, renewed, dictionary):
     last = step + 1 == OUTER
+    atoms = (BLOCK_ATOMS, old.shape[1])
+    earlier = len(renewed) if last else 0
+    scratch = [pltpu.VMEM(atoms, jnp.float32)]
+    if last:
+        scratch = scratch * 2 + [pltpu.SemaphoreType.DMA((2 * held.shape[0] + earlier,))]
     return pl.pallas_call(
-        functools.partial(renew_kernel, step),
-        in_specs=[scalars()] + [vmem()] * 4 + [hbm()],
-        out_specs=[hbm()] + [vmem()] * (1 - last),
-        out_shape=[pltpu.HBM(dictionary.shape, jnp.float32)]
-        + [pltpu.VMEM((BLOCK_ATOMS, entries), jnp.float32)] * (1 - last),
-        scratch_shapes=[pltpu.VMEM((BLOCK_ATOMS, entries), jnp.float32)] * (1 + last)
-        + [
-            pltpu.SemaphoreType.DMA((2 * held.shape[0],)),
-        ],
-        input_output_aliases={5: 0},
+        functools.partial(renew_kernel, step, earlier),
+        in_specs=[scalars()] + [vmem()] * (4 + earlier) + [hbm()] * last,
+        out_specs=hbm() if last else vmem(),
+        out_shape=pltpu.HBM(dictionary.shape, jnp.float32) if last else pltpu.VMEM(atoms, jnp.float32),
+        scratch_shapes=scratch,
+        input_output_aliases={5 + earlier: 0} if last else {},
         compiler_params=pltpu.CompilerParams(vmem_limit_bytes=VMEM_BYTES),
         name="renew",
-    )(plan, held, came, resident(old), mean_sq, far(dictionary))
+    )(
+        plan,
+        held,
+        came,
+        resident(old),
+        mean_sq,
+        *([resident(value) for value in renewed] + [far(dictionary)] if last else []),
+    )
 
 
 def whole_channels(signal, codes_init, dictionary_init, threshold, plan):
@@ -694,18 +726,21 @@
     following = swaps(edges)
     swapped = following
     taps = layout(dictionary_init, channels)
-    atoms = dictionary = None
+    dictionary = None
+    renewed = []
     for step in range(OUTER):
         for inner in range(INNER + 1):
+            turn_index = step * (INNER + 1) + inner
             ferry = None
-            if step == 0:
-                ferry = (dictionary_init, dictionary, sum(COPIED[:inner]), COPIED[inner])
+            if COPIED[turn_index]:
+                first = sum(COPIED[:turn_index])
+                ferry = (dictionary_init, dictionary, first, COPIED[turn_index])
             if inner == INNER:
                 payload, *finals = finish(plan, step, state, swapped, signal, taps, ferry, peers)
                 if ferry:
                     *finals, dictionary = finals
                 break
-            fresh = atoms if inner == 0 else None
+            fresh = renewed[-1] if inner == 0 and step else None
             state, *results = iterate(
                 plan, step, limit, state, swapped, signal, following, taps, fresh, ferry, peers
             )
@@ -715,11 +750,20 @@
             if ferry:
                 dictionary = results[-1]
         blocks = lax.all_to_all(payload, "tm", 0, 0, tiled=True)
-        piece = share_gradient(plan, step, blocks, dictionary, channels // peers)
-        old, mean_sq = recall(plan, step, dictionary, piece)
-        held, came = gather_pieces(piece, old)
-        dictionary, *renewed = renew(plan, step, held, came, old, mean_sq, dictionary)
-        atoms = renewed[0] if renewed else None
+        piece = share_gradient(plan, step, blocks, dictionary_init, channels // peers)
+        recalled = []
+
+        def recall_beside(held):
+            recalled.extend(recall(plan, step, dictionary_init, held))
+            return recalled[0]
+
+        held, came = gather_pieces(piece, recall_beside)
+        last = step + 1 == OUTER
+        result = renew(plan, step, held, came, *recalled, renewed if last else None, dictionary)
+        if last:
+            dictionary = result
+        else:
+            renewed.append(result)
     residual, codes = finals
     return codes, dictionary, residual
 
@@ -801,7 +845,7 @@
         and channels % LANES == 0
         and channels % peers == 0
         and (channels // peers * L) % LANES == 0
-        and peers > 1
+        and peers > 2
         and peers & (peers - 1) == 0
     )
     body = whole_channels if fits else split_channels

time: 170 us -> 162 us (0.953)
  blocking collectives: 19.8 us -> 44.2 us
  starting transfers between devices: 45.8 us -> 32.9 us
  waiting for transfers between devices: 26.4 us -> 13.9 us
  Pallas kernels: 75 us -> 67.4 us
    all_to_all x1 -> x2, blocking collectives: 19.8 us -> 44.2 us  [whole_channels(): blocks = lax.all_to_all(payload, 'tm', 0, 0, tiled=True)]
    all_to_all x1 -> x0, starting transfers between devices: 12.9 us -> none  [whole_channels(): blocks = lax.all_to_all(payload, 'tm', 0, 0, tiled=True)]
    all_to_all x1 -> x0, waiting for transfers between devices: 10.4 us -> none  [whole_channels(): blocks = lax.all_to_all(payload, 'tm', 0, 0, tiled=True)]
    pallas_call x4, Pallas kernels: 34.9 us -> 31.5 us  [iterate(): pl.pallas_call(functools.partial(iterate_kernel, peers * segment, step if...]
    ppermute x14, waiting for transfers between devices: 15 us -> 12.9 us  [exchanged(): return lax.ppermute(shard, 'tm', [(i, i ^ mask) for i in range(peers)])]
    pallas_call x2, Pallas kernels: 7.34 us -> 5.63 us  [share_gradient(): pl.pallas_call(functools.partial(gradient_kernel, share, step), in_specs=...]
  transfers between devices with their start and end apart: 25 -> 24, of which waited for: 9 -> 12; matrix products, arithmetic and copies ran while one was open for 1% -> 1% of each run, Pallas kernels for 9% -> 9%
where the time goes in v8:
time: 162 us; the launch traced here: 161 us
  Pallas kernels  67.4 us (42%)
  blocking collectives  44.2 us (27%)
  starting transfers between devices  32.9 us (20%)
  waiting for transfers between devices  13.9 us (9%)
    all_to_all x2, blocking collectives, whole_channels(): blocks = lax.all_to_all(payload, 'tm', 0, 0, tiled=True)  44.2 us
    pallas_call x4, Pallas kernels, iterate(): pl.pallas_call(functools.partial(iterate_kernel, peers * segment, step if...  31.5 us
    ppermute x10, starting transfers between devices, swaps(): return [lax.ppermute(edge, 'tm', pair) for edge, pair in zip(edges, pairs)]  16.8 us
    ppermute x14, starting transfers between devices, exchanged(): return lax.ppermute(shard, 'tm', [(i, i ^ mask) for i in range(peers)])  16.2 us
    ppermute x14, waiting for transfers between devices, exchanged(): return lax.ppermute(shard, 'tm', [(i, i ^ mask) for i in range(peers)])  12.9 us
    pallas_call x1, Pallas kernels, layout(): pl.pallas_call(layout_kernel, grid=(channels // block,), in_specs=[pl.Blo...  9.22 us
    pallas_call x2, Pallas kernels, finish(): pl.pallas_call(functools.partial(finish_kernel, peers, step, ferry[2:] if...  8.64 us
    pallas_call x2, Pallas kernels, renew(): pl.pallas_call(functools.partial(renew_kernel, step, earlier), in_specs=[...  6.02 us
  transfers between devices with their start and end apart: 24, of which 12 were waited for; matrix products, arithmetic and copies ran while one was open for 1% of the time, Pallas kernels for 9%

profile of v8, /device:TPU:0, one launch (start us, length us, event | category | flops | bytes accessed | tf_op | source)
XLA Modules:
  0.0 161.2 jit_solution(15765596628604631134)
XLA Ops:
  2.9 9.2 %layout.1.refs_6_.taps.refs_7_ = bf16[6,16,384,128]{3,2,1,0:T(8,128)(2,1)S(1)} custom-call(f32[128,36864]{1,0:T(8,128)} %dict_hbm.7), custom_call_target="tpu_custom_call" | custom-call | tf_op jit(solution)/shard_map/layout/pallas_call | solution.py:113
  12.2 6.1 %iterate.4 = (f32[128,128]{1,0:T(8,128)S(1)}, bf16[96,128]{1,0:T(8,128)(2,1)S(1)}, bf16[96,128]{1,0:T(8,128)(2,1)S(1)}, f32[128,36864]{1,0:T(8,128)}) custom-call(s32[8]{0:T(128)S(1)} %copy-done, f32[1,128]{1,0:T(1,128)S(1)} %bitcast.13, f32[128,128]{1,0:T(8,128)S(1)} %get-tuple-element.35.refs_0_, bf16[96,512]{1,0:T(8,128)(2,1)S(1)} %collective-permute-done.refs_1_.refs_4_, ...), custom_call_target="tpu_custom_call" | custom-call | tf_op jit(solution)/shard_map/iterate/pallas_call | solution.py:365
  18.3 3.9 %collective-permute-start.2 = (bf16[96,128]{1,0:T(8,128)(2,1)S(1)}, bf16[96,128]{1,0:T(8,128)(2,1)S(1)}, u32[]{:S(2)}, u32[]{:S(2)}) collective-permute-start(bf16[96,128]{1,0:T(8,128)(2,1)S(1)} %get-tuple-element.40), channel_id=1, source_target_pairs={{0,1},{1,0},{2,3},{3,2},{4,5},{5,4},{6,7},{7,6},{8,9},{9,8},{10,11... | collective-permute-start | bytes 73736 | tf_op jit(solution)/shard_map/ppermute | solution.py:723
  23.1 6.3 %iterate.5 = (f32[128,128]{1,0:T(8,128)S(1)}, bf16[96,128]{1,0:T(8,128)(2,1)S(1)}, bf16[96,128]{1,0:T(8,128)(2,1)S(1)}, f32[128,36864]{1,0:T(8,128)}) custom-call(s32[8]{0:T(128)S(1)} %copy-done, f32[1,128]{1,0:T(1,128)S(1)} %bitcast.14, f32[128,128]{1,0:T(8,128)S(1)} %get-tuple-element.39.refs_0_, ...), custom_call_target="tpu_custom_call", output_to_operand_aliasing={{3}: (10, {})} | custom-call | tf_op jit(solution)/shard_map/iterate/pallas_call | solution.py:365
  29.3 4.4 %collective-permute-start.4 = (bf16[96,128]{1,0:T(8,128)(2,1)S(1)}, bf16[96,128]{1,0:T(8,128)(2,1)S(1)}, u32[]{:S(2)}, u32[]{:S(2)}) collective-permute-start(bf16[96,128]{1,0:T(8,128)(2,1)S(1)} %get-tuple-element.44), channel_id=1, source_target_pairs={{0,1},{1,0},{2,3},{3,2},{4,5},{5,4},{6,7},{7,6},{8,9},{9,8},{10,11... | collective-permute-start | bytes 73736 | tf_op jit(solution)/shard_map/ppermute | solution.py:723
  34.6 4.7 %finish.2 = (bf16[32,32,128]{2,1,0:T(8,128)(2,1)S(1)}, f32[128,36864]{1,0:T(8,128)}) custom-call(s32[8]{0:T(128)S(1)} %copy-done, f32[128,128]{1,0:T(8,128)S(1)} %get-tuple-element.43.state_ref.refs_0_, bf16[96,128]{1,0:T(8,128)(2,1)S(1)} %collective-permute-done.4.first_ref.refs_1_, ...), custom_call_target="tpu_custom_call", output_to_operand_aliasing={{1}: (7, {})} | custom-call | tf_op jit(solution)/shard_map/finish/pallas_call | solution.py:454
  39.2 23.1 %all_to_all.10.blocks_ref = bf16[32,32,128]{2,1,0:T(8,128)(2,1)S(1)} all-to-all(bf16[32,32,128]{2,1,0:T(8,128)(2,1)S(1)} %get-tuple-element.47), channel_id=1, replica_groups=mesh['tm'=32,'chan'=1] {'tm'}, dimensions={0} | all-to-all | bytes 524288 | tf_op jit(solution)/shard_map/all_to_all | solution.py:752
  62.3 2.8 %gradient.2 = bf16[16,1280]{1,0:T(8,128)(2,1)S(1)} custom-call(s32[8]{0:T(128)S(1)} %copy-done, bf16[32,32,128]{2,1,0:T(8,128)(2,1)S(1)} %all_to_all.10.blocks_ref, f32[128,36864]{1,0:T(8,128)} %dict_hbm.7), custom_call_target="tpu_custom_call" | custom-call | tf_op jit(solution)/shard_map/gradient/pallas_call | solution.py:549
  66.5 3.1 %collective-permute-start.6 = (bf16[1,16,1280]{2,1,0:T(8,128)(2,1)S(1)}, bf16[1,16,1280]{2,1,0:T(8,128)(2,1)S(1)}, u32[]{:S(2)}, u32[]{:S(2)}) collective-permute-start(bf16[1,16,1280]{2,1,0:T(8,128)(2,1)S(1)} %bitcast.7), channel_id=1, source_target_pairs={{0,16},{1,17},{2,18},{3,19},{4,20},{5,21},{6,22},{7,23},{8,24},{9,... | collective-permute-start | bytes 122888 | tf_op jit(solution)/shard_map/ppermute | solution.py:586
  69.6 1.7 %collective-permute-done.8 = bf16[1,16,1280]{2,1,0:T(8,128)(2,1)S(1)} collective-permute-done((bf16[1,16,1280]{2,1,0:T(8,128)(2,1)S(1)}, bf16[1,16,1280]{2,1,0:T(8,128)(2,1)S(1)}, u32[]{:S(2)}, u32[]{:S(2)}) %collective-permute-start.8) | collective-permute-done | bytes 40992 | tf_op jit(solution)/shard_map/ppermute | solution.py:586
  75.5 2.6 %recall.2 = (f32[16,36864]{1,0:T(8,128)S(1)}, f32[16,128]{1,0:T(8,128)S(1)}) custom-call(s32[8]{0:T(128)S(1)} %copy-done, f32[128,36864]{1,0:T(8,128)} %dict_hbm.7, bf16[4,16,1280]{2,1,0:T(8,128)(2,1)S(1)} %pad_maximum_fusion.piece_ref), custom_call_target="tpu_custom_call" | custom-call | tf_op jit(solution)/shard_map/recall/pallas_call | solution.py:618
  78.2 2.7 %collective-permute-done.9 = bf16[4,16,1280]{2,1,0:T(8,128)(2,1)S(1)} collective-permute-done((bf16[4,16,1280]{2,1,0:T(8,128)(2,1)S(1)}, bf16[4,16,1280]{2,1,0:T(8,128)(2,1)S(1)}, u32[]{:S(2)}, u32[]{:S(2)}) %collective-permute-start.9) | collective-permute-done | bytes 163872 | tf_op jit(solution)/shard_map/ppermute | solution.py:586
  81.1 2.1 %collective-permute-done.12.came_ref = bf16[16,16,1280]{2,1,0:T(8,128)(2,1)S(1)} collective-permute-done((bf16[16,16,1280]{2,1,0:T(8,128)(2,1)S(1)}, bf16[16,16,1280]{2,1,0:T(8,128)(2,1)S(1)}, u32[]{:S(2)}, u32[]{:S(2)}) %collective-permute-start.12) | collective-permute-done | bytes 655392 | tf_op jit(solution)/shard_map/ppermute | solution.py:586
  83.1 2.1 %renew.2.refs_6_.refs_0_ = f32[16,36864]{1,0:T(8,128)S(1)} custom-call(s32[8]{0:T(128)S(1)} %copy-done, bf16[16,16,1280]{2,1,0:T(8,128)(2,1)S(1)} %constant_dynamic-update-slice_fusion.held_ref, bf16[16,16,1280]{2,1,0:T(8,128)(2,1)S(1)} %collective-permute-done.12.came_ref, f32[16,36864]{1,0:T(8,128)S(1)} %get-tuple-element.48.old, ...), custom_call_target="tpu_custom_call" | custom-call | tf_op jit(solution)/shard_map/renew/pallas_call | solution.py:697
  85.2 13.0 %iterate.6 = (f32[128,128]{1,0:T(8,128)S(1)}, bf16[96,128]{1,0:T(8,128)(2,1)S(1)}, bf16[96,128]{1,0:T(8,128)(2,1)S(1)}, bf16[6,16,384,128]{3,2,1,0:T(8,128)(2,1)S(1)}, f32[128,36864]{1,0:T(8,128)}) custom-call(s32[8]{0:T(128)S(1)} %copy-done, f32[1,128]{1,0:T(1,128)S(1)} %bitcast.15, ...), custom_call_target="tpu_custom_call", output_to_operand_aliasing={{3}: (9, {}), {4}: (11, {})} | custom-call | tf_op jit(solution)/shard_map/iterate/pallas_call | solution.py:365
  99.5 6.3 %iterate.7 = (f32[128,128]{1,0:T(8,128)S(1)}, bf16[96,128]{1,0:T(8,128)(2,1)S(1)}, bf16[96,128]{1,0:T(8,128)(2,1)S(1)}, f32[128,36864]{1,0:T(8,128)}) custom-call(s32[8]{0:T(128)S(1)} %copy-done, f32[1,128]{1,0:T(1,128)S(1)} %bitcast.16, f32[128,128]{1,0:T(8,128)S(1)} %get-tuple-element.52.refs_0_, ...), custom_call_target="tpu_custom_call", output_to_operand_aliasing={{3}: (10, {})} | custom-call | tf_op jit(solution)/shard_map/iterate/pallas_call | solution.py:365
  105.7 4.5 %collective-permute-start.15 = (bf16[96,128]{1,0:T(8,128)(2,1)S(1)}, bf16[96,128]{1,0:T(8,128)(2,1)S(1)}, u32[]{:S(2)}, u32[]{:S(2)}) collective-permute-start(bf16[96,128]{1,0:T(8,128)(2,1)S(1)} %get-tuple-element.58), channel_id=1, source_target_pairs={{0,1},{1,0},{2,3},{3,2},{4,5},{5,4},{6,7},{7,6},{8,9},{9,8},{10,11... | collective-permute-start | bytes 73736 | tf_op jit(solution)/shard_map/ppermute | solution.py:723
  111.1 4.0 %finish.3 = (bf16[32,32,128]{2,1,0:T(8,128)(2,1)S(1)}, f32[384,128]{1,0:T(8,128)S(1)}, f32[128,128]{1,0:T(8,128)S(1)}) custom-call(s32[8]{0:T(128)S(1)} %copy-done, f32[128,128]{1,0:T(8,128)S(1)} %get-tuple-element.57.state_ref, bf16[96,128]{1,0:T(8,128)(2,1)S(1)} %collective-permute-done.15.first_ref, ...), custom_call_target="tpu_custom_call" | custom-call | tf_op jit(solution)/shard_map/finish/pallas_call | solution.py:454
  115.1 21.1 %all_to_all.11.blocks_ref = bf16[32,32,128]{2,1,0:T(8,128)(2,1)S(1)} all-to-all(bf16[32,32,128]{2,1,0:T(8,128)(2,1)S(1)} %get-tuple-element.61), channel_id=1, replica_groups=mesh['tm'=32,'chan'=1] {'tm'}, dimensions={0} | all-to-all | bytes 524288 | tf_op jit(solution)/shard_map/all_to_all | solution.py:752
  136.2 2.8 %gradient.3 = bf16[16,1280]{1,0:T(8,128)(2,1)S(1)} custom-call(s32[8]{0:T(128)S(1)} %copy-done, bf16[32,32,128]{2,1,0:T(8,128)(2,1)S(1)} %all_to_all.11.blocks_ref, f32[128,36864]{1,0:T(8,128)} %dict_hbm.7), custom_call_target="tpu_custom_call" | custom-call | tf_op jit(solution)/shard_map/gradient/pallas_call | solution.py:549
  140.4 3.1 %collective-permute-start.17 = (bf16[1,16,1280]{2,1,0:T(8,128)(2,1)S(1)}, bf16[1,16,1280]{2,1,0:T(8,128)(2,1)S(1)}, u32[]{:S(2)}, u32[]{:S(2)}) collective-permute-start(bf16[1,16,1280]{2,1,0:T(8,128)(2,1)S(1)} %bitcast.11), channel_id=1, source_target_pairs={{0,16},{1,17},{2,18},{3,19},{4,20},{5,21},{6,22},{7,23},{8,24},{9,... | collective-permute-start | bytes 122888 | tf_op jit(solution)/shard_map/ppermute | solution.py:586
  149.4 2.6 %recall.3 = (f32[16,36864]{1,0:T(8,128)S(1)}, f32[16,128]{1,0:T(8,128)S(1)}) custom-call(s32[8]{0:T(128)S(1)} %copy-done, f32[128,36864]{1,0:T(8,128)} %dict_hbm.7, bf16[4,16,1280]{2,1,0:T(8,128)(2,1)S(1)} %pad_maximum_fusion.1.piece_ref), custom_call_target="tpu_custom_call" | custom-call | tf_op jit(solution)/shard_map/recall/pallas_call | solution.py:618
  152.0 2.7 %collective-permute-done.20 = bf16[4,16,1280]{2,1,0:T(8,128)(2,1)S(1)} collective-permute-done((bf16[4,16,1280]{2,1,0:T(8,128)(2,1)S(1)}, bf16[4,16,1280]{2,1,0:T(8,128)(2,1)S(1)}, u32[]{:S(2)}, u32[]{:S(2)}) %collective-permute-start.20) | collective-permute-done | bytes 163872 | tf_op jit(solution)/shard_map/ppermute | solution.py:586
  157.0 4.0 %renew.3 = f32[128,36864]{1,0:T(8,128)} custom-call(s32[8]{0:T(128)S(1)} %copy-done, bf16[16,16,1280]{2,1,0:T(8,128)(2,1)S(1)} %constant_dynamic-update-slice_fusion.7.held_ref, bf16[16,16,1280]{2,1,0:T(8,128)(2,1)S(1)} %collective-permute-done.23.came_ref, f32[16,36864]{1,0:T(8,128)S(1)} %get-tuple-element.62.old, ...), custom_call_target="tpu_custom_call", output_to_operand_aliasing={{}: (6, {})} | custom-call | tf_op jit(solution)/shard_map/renew/pallas_call | solution.py:697
  (62 shorter events, 21.2 us)
Async XLA Ops:
  1.8 10.4 %collective-permute-start = (bf16[96,512]{1,0:T(8,128)(2,1)S(1)}, bf16[96,512]{1,0:T(8,128)(2,1)S(1)}, u32[]{:S(2)}, u32[]{:S(2)}) collective-permute-start(bf16[96,512]{1,0:T(8,128)(2,1)S(1)} %get-tuple-element.36), channel_id=1, source_target_pairs={{0,1},{1,0},{2,3},{3,2},{4,5},{5,4},{6,7},{7,6},{8,9},{9,8},{10,11... | collective-permute-start | bytes 294920 | tf_op jit(solution)/shard_map/ppermute | solution.py:723
  2.3 9.9 %collective-permute-start.1 = (bf16[96,512]{1,0:T(8,128)(2,1)S(1)}, bf16[96,512]{1,0:T(8,128)(2,1)S(1)}, u32[]{:S(2)}, u32[]{:S(2)}) collective-permute-start(bf16[96,512]{1,0:T(8,128)(2,1)S(1)} %get-tuple-element.37), channel_id=1, source_target_pairs={{1,2},{2,1},{3,4},{4,3},{5,6},{6,5},{7,8},{8,7},{9,10},{10,9},{11,... | collective-permute-start | bytes 294920 | tf_op jit(solution)/shard_map/ppermute | solution.py:723
  18.3 4.8 %collective-permute-start.2 = (bf16[96,128]{1,0:T(8,128)(2,1)S(1)}, bf16[96,128]{1,0:T(8,128)(2,1)S(1)}, u32[]{:S(2)}, u32[]{:S(2)}) collective-permute-start(bf16[96,128]{1,0:T(8,128)(2,1)S(1)} %get-tuple-element.40), channel_id=1, source_target_pairs={{0,1},{1,0},{2,3},{3,2},{4,5},{5,4},{6,7},{7,6},{8,9},{9,8},{10,11... | collective-permute-start | bytes 73736 | tf_op jit(solution)/shard_map/ppermute | solution.py:723
  22.2 0.9 collective-permute-start.3
  29.3 5.2 %collective-permute-start.4 = (bf16[96,128]{1,0:T(8,128)(2,1)S(1)}, bf16[96,128]{1,0:T(8,128)(2,1)S(1)}, u32[]{:S(2)}, u32[]{:S(2)}) collective-permute-start(bf16[96,128]{1,0:T(8,128)(2,1)S(1)} %get-tuple-element.44), channel_id=1, source_target_pairs={{0,1},{1,0},{2,3},{3,2},{4,5},{5,4},{6,7},{7,6},{8,9},{9,8},{10,11... | collective-permute-start | bytes 73736 | tf_op jit(solution)/shard_map/ppermute | solution.py:723
  33.7 0.9 collective-permute-start.5
  65.1 6.2 %collective-permute-start.8 = (bf16[1,16,1280]{2,1,0:T(8,128)(2,1)S(1)}, bf16[1,16,1280]{2,1,0:T(8,128)(2,1)S(1)}, u32[]{:S(2)}, u32[]{:S(2)}) collective-permute-start(bf16[1,16,1280]{2,1,0:T(8,128)(2,1)S(1)} %bitcast.5), channel_id=1, source_target_pairs={{0,24},{1,25},{2,26},{3,27},{4,28},{5,29},{6,30},{7,31},{8,16},{9,... | collective-permute-start | bytes 122888 | tf_op jit(solution)/shard_map/ppermute | solution.py:586
  66.5 4.8 %collective-permute-start.7 = (bf16[1,16,1280]{2,1,0:T(8,128)(2,1)S(1)}, bf16[1,16,1280]{2,1,0:T(8,128)(2,1)S(1)}, u32[]{:S(2)}, u32[]{:S(2)}) collective-permute-start(bf16[1,16,1280]{2,1,0:T(8,128)(2,1)S(1)} %bitcast.6), channel_id=1, source_target_pairs={{0,8},{1,9},{2,10},{3,11},{4,12},{5,13},{6,14},{7,15},{8,0},{9,1},... | collective-permute-start | bytes 122888 | tf_op jit(solution)/shard_map/ppermute | solution.py:586
  66.5 5.3 %collective-permute-start.6 = (bf16[1,16,1280]{2,1,0:T(8,128)(2,1)S(1)}, bf16[1,16,1280]{2,1,0:T(8,128)(2,1)S(1)}, u32[]{:S(2)}, u32[]{:S(2)}) collective-permute-start(bf16[1,16,1280]{2,1,0:T(8,128)(2,1)S(1)} %bitcast.7), channel_id=1, source_target_pairs={{0,16},{1,17},{2,18},{3,19},{4,20},{5,21},{6,22},{7,23},{8,24},{9,... | collective-permute-start | bytes 122888 | tf_op jit(solution)/shard_map/ppermute | solution.py:586
  71.9 9.0 %collective-permute-start.11 = (bf16[4,16,1280]{2,1,0:T(8,128)(2,1)S(1)}, bf16[4,16,1280]{2,1,0:T(8,128)(2,1)S(1)}, u32[]{:S(2)}, u32[]{:S(2)}) collective-permute-start(bf16[4,16,1280]{2,1,0:T(8,128)(2,1)S(1)} %pad_maximum_fusion.piece_ref), channel_id=1, source_target_pairs={{0,6},{1,7},{2,4},{3,5},{4,2},{5,3},{6,0},{7,1},{8,14},{9,15},{10,... | collective-permute-start | bytes 491528 | tf_op jit(solution)/shard_map/ppermute | solution.py:586
  73.2 7.8 %collective-permute-start.10 = (bf16[4,16,1280]{2,1,0:T(8,128)(2,1)S(1)}, bf16[4,16,1280]{2,1,0:T(8,128)(2,1)S(1)}, u32[]{:S(2)}, u32[]{:S(2)}) collective-permute-start(bf16[4,16,1280]{2,1,0:T(8,128)(2,1)S(1)} %pad_maximum_fusion.piece_ref), channel_id=1, source_target_pairs={{0,2},{1,3},{2,0},{3,1},{4,6},{5,7},{6,4},{7,5},{8,10},{9,11},{10,... | collective-permute-start | bytes 491528 | tf_op jit(solution)/shard_map/ppermute | solution.py:586
  74.3 6.6 %collective-permute-start.9 = (bf16[4,16,1280]{2,1,0:T(8,128)(2,1)S(1)}, bf16[4,16,1280]{2,1,0:T(8,128)(2,1)S(1)}, u32[]{:S(2)}, u32[]{:S(2)}) collective-permute-start(bf16[4,16,1280]{2,1,0:T(8,128)(2,1)S(1)} %pad_maximum_fusion.piece_ref), channel_id=1, source_target_pairs={{0,4},{1,5},{2,6},{3,7},{4,0},{5,1},{6,2},{7,3},{8,12},{9,13},{10,... | collective-permute-start | bytes 491528 | tf_op jit(solution)/shard_map/ppermute | solution.py:586
  81.0 2.2 %collective-permute-start.12 = (bf16[16,16,1280]{2,1,0:T(8,128)(2,1)S(1)}, bf16[16,16,1280]{2,1,0:T(8,128)(2,1)S(1)}, u32[]{:S(2)}, u32[]{:S(2)}) collective-permute-start(bf16[16,16,1280]{2,1,0:T(8,128)(2,1)S(1)} %constant_dynamic-update-slice_fusion.held_ref), channel_id=1, source_target_pairs={{0,1},{1,0},{2,3},{3,2},{4,5},{5,4},{6,7},{7,6},{8,9},{9,8},{10,11... | collective-permute-start | bytes 1966088 | tf_op jit(solution)/shard_map/ppermute | solution.py:586
  98.2 1.3 collective-permute-start.13
  98.4 1.1 collective-permute-start.14
  105.7 5.4 %collective-permute-start.15 = (bf16[96,128]{1,0:T(8,128)(2,1)S(1)}, bf16[96,128]{1,0:T(8,128)(2,1)S(1)}, u32[]{:S(2)}, u32[]{:S(2)}) collective-permute-start(bf16[96,128]{1,0:T(8,128)(2,1)S(1)} %get-tuple-element.58), channel_id=1, source_target_pairs={{0,1},{1,0},{2,3},{3,2},{4,5},{5,4},{6,7},{7,6},{8,9},{9,8},{10,11... | collective-permute-start | bytes 73736 | tf_op jit(solution)/shard_map/ppermute | solution.py:723
  110.2 0.9 collective-permute-start.16
  139.0 6.2 %collective-permute-start.19 = (bf16[1,16,1280]{2,1,0:T(8,128)(2,1)S(1)}, bf16[1,16,1280]{2,1,0:T(8,128)(2,1)S(1)}, u32[]{:S(2)}, u32[]{:S(2)}) collective-permute-start(bf16[1,16,1280]{2,1,0:T(8,128)(2,1)S(1)} %bitcast.9), channel_id=1, source_target_pairs={{0,24},{1,25},{2,26},{3,27},{4,28},{5,29},{6,30},{7,31},{8,16},{9,... | collective-permute-start | bytes 122888 | tf_op jit(solution)/shard_map/ppermute | solution.py:586
  140.4 4.8 %collective-permute-start.18 = (bf16[1,16,1280]{2,1,0:T(8,128)(2,1)S(1)}, bf16[1,16,1280]{2,1,0:T(8,128)(2,1)S(1)}, u32[]{:S(2)}, u32[]{:S(2)}) collective-permute-start(bf16[1,16,1280]{2,1,0:T(8,128)(2,1)S(1)} %bitcast.10), channel_id=1, source_target_pairs={{0,8},{1,9},{2,10},{3,11},{4,12},{5,13},{6,14},{7,15},{8,0},{9,1},... | collective-permute-start | bytes 122888 | tf_op jit(solution)/shard_map/ppermute | solution.py:586
  140.4 5.3 %collective-permute-start.17 = (bf16[1,16,1280]{2,1,0:T(8,128)(2,1)S(1)}, bf16[1,16,1280]{2,1,0:T(8,128)(2,1)S(1)}, u32[]{:S(2)}, u32[]{:S(2)}) collective-permute-start(bf16[1,16,1280]{2,1,0:T(8,128)(2,1)S(1)} %bitcast.11), channel_id=1, source_target_pairs={{0,16},{1,17},{2,18},{3,19},{4,20},{5,21},{6,22},{7,23},{8,24},{9,... | collective-permute-start | bytes 122888 | tf_op jit(solution)/shard_map/ppermute | solution.py:586
  145.8 9.0 %collective-permute-start.22 = (bf16[4,16,1280]{2,1,0:T(8,128)(2,1)S(1)}, bf16[4,16,1280]{2,1,0:T(8,128)(2,1)S(1)}, u32[]{:S(2)}, u32[]{:S(2)}) collective-permute-start(bf16[4,16,1280]{2,1,0:T(8,128)(2,1)S(1)} %pad_maximum_fusion.1.piece_ref), channel_id=1, source_target_pairs={{0,6},{1,7},{2,4},{3,5},{4,2},{5,3},{6,0},{7,1},{8,14},{9,15},{10,... | collective-permute-start | bytes 491528 | tf_op jit(solution)/shard_map/ppermute | solution.py:586
  147.0 7.8 %collective-permute-start.21 = (bf16[4,16,1280]{2,1,0:T(8,128)(2,1)S(1)}, bf16[4,16,1280]{2,1,0:T(8,128)(2,1)S(1)}, u32[]{:S(2)}, u32[]{:S(2)}) collective-permute-start(bf16[4,16,1280]{2,1,0:T(8,128)(2,1)S(1)} %pad_maximum_fusion.1.piece_ref), channel_id=1, source_target_pairs={{0,2},{1,3},{2,0},{3,1},{4,6},{5,7},{6,4},{7,5},{8,10},{9,11},{10,... | collective-permute-start | bytes 491528 | tf_op jit(solution)/shard_map/ppermute | solution.py:586
  148.2 6.6 %collective-permute-start.20 = (bf16[4,16,1280]{2,1,0:T(8,128)(2,1)S(1)}, bf16[4,16,1280]{2,1,0:T(8,128)(2,1)S(1)}, u32[]{:S(2)}, u32[]{:S(2)}) collective-permute-start(bf16[4,16,1280]{2,1,0:T(8,128)(2,1)S(1)} %pad_maximum_fusion.1.piece_ref), channel_id=1, source_target_pairs={{0,4},{1,5},{2,6},{3,7},{4,0},{5,1},{6,2},{7,3},{8,12},{9,13},{10,... | collective-permute-start | bytes 491528 | tf_op jit(solution)/shard_map/ppermute | solution.py:586
  154.9 2.2 %collective-permute-start.23 = (bf16[16,16,1280]{2,1,0:T(8,128)(2,1)S(1)}, bf16[16,16,1280]{2,1,0:T(8,128)(2,1)S(1)}, u32[]{:S(2)}, u32[]{:S(2)}) collective-permute-start(bf16[16,16,1280]{2,1,0:T(8,128)(2,1)S(1)} %constant_dynamic-update-slice_fusion.7.held_ref), channel_id=1, source_target_pairs={{0,1},{1,0},{2,3},{3,2},{4,5},{5,4},{6,7},{7,6},{8,9},{9,8},{10,11... | collective-permute-start | bytes 1966088 | tf_op jit(solution)/shard_map/ppermute | solution.py:586
  (2 other events, 23.1 us)

commit v9 on v8

--- a/solution.py
+++ b/solution.py
@@ -23,7 +23,7 @@
 STRIDE = L + 1
 GROUPS = 4
 SUBLANES = 8
-COPIED = (16, 24, 16, 48, 24, 0)
+COPIED = (32, 40, 32, 24)
 FINE = 4
 LANES = 128
 VMEM_BYTES = 24 * 1024 * 1024
@@ -132,18 +132,13 @@
             store = pltpu.make_async_copy(held, target.at[rows], sems.at[1, step])
             fetch.start()
             self.steps.append((fetch, store))
-        self.stored = 0
-
-    def tick(self):
-        if self.stored < len(self.steps):
-            fetch, store = self.steps[self.stored]
+
+    def turn_round(self):
+        for fetch, store in self.steps:
             fetch.wait()
             store.start()
-            self.stored += 1
 
     def close(self):
-        while self.stored < len(self.steps):
-            self.tick()
         for _, store in self.steps:
             store.wait()
 
@@ -155,7 +150,7 @@
     ]
 
 
-def convolve(zb, begin, count, taps, zz, fine, acc, ferry):
+def convolve(zb, begin, count, taps, zz, fine, acc):
     channels = taps.shape[2]
     tiles = channels // LANES
     rows = count + ROWS
@@ -177,8 +172,6 @@
                 for tile in range(tiles):
                     column = j * channels + tile * LANES
                     fine[slot + pair + j, tile, :rows, :] = product[:, column : column + LANES]
-        if ferry:
-            ferry.tick()
         for tile in range(tiles):
             total = None if lag == 0 else acc[tile, :count, :]
             for j in range(FINE):
@@ -188,7 +181,7 @@
             acc[tile, :count, :] = total
 
 
-def correlate(rb, count, taps, rr, fine, acc, ferry):
+def correlate(rb, count, taps, rr, fine, acc):
     channels = taps.shape[2]
     rows = count + ROWS
     for coarse in range(COARSE):
@@ -207,8 +200,6 @@
             product = lax.dot_general(rr[:rows, :], weights, NN, preferred_element_type=jnp.float32)
             for j in range(2):
                 fine[slot + pair + j, 0, :rows, :] = product[:, j * K : (j + 1) * K]
-        if ferry:
-            ferry.tick()
         total = None if lag == 0 else acc[0, :count, :]
         for j in range(FINE):
             part = fine[slot + j, 0, lag + j : lag + j + count, :]
@@ -240,15 +231,24 @@
     lax.fori_loop(0, channels // (GROUPS * ROWS), patch, 0)
 
 
-def put_edges(edge_refs, values):
+def put_edges(edge_refs, rightward, leftward):
     even = lax.axis_index("tm") % 2 == 0
 
     def put(first, second):
-        first[...] = values[-L:]
-        second[...] = values[:L]
+        first[: rightward.shape[0]] = rightward
+        second[: leftward.shape[0]] = leftward
+        unused = second.shape[0] - leftward.shape[0]
+        if unused:
+            second[leftward.shape[0] :] = jnp.zeros((unused, second.shape[1]), second.dtype)
 
     pl.when(even)(lambda: put(*edge_refs))
     pl.when(jnp.logical_not(even))(lambda: put(*edge_refs[::-1]))
+
+
+def by_side(put, first_ref, second_ref):
+    even = lax.axis_index("tm") % 2 == 0
+    pl.when(even)(lambda: put(second_ref, first_ref))
+    pl.when(jnp.logical_not(even))(lambda: put(first_ref, second_ref))
 
 
 def begin_kernel(code_hbm, signal_hbm, state_out, signal_out, first_out, second_out, code_ref, signal_ref, sems):
@@ -264,7 +264,8 @@
     signal = signal_ref[...].astype(jnp.float32).T.astype(jnp.bfloat16)
     state_out[...] = state
     signal_out[...] = signal
-    put_edges((first_out, second_out), jnp.concatenate([state.astype(jnp.bfloat16), signal], axis=1))
+    both = jnp.concatenate([state.astype(jnp.bfloat16), signal], axis=1)
+    put_edges((first_out, second_out), both[-L:], both[:L])
 
 
 def begin(code, signal):
@@ -288,21 +289,7 @@
     )(far(code), far(signal))
 
 
-def put_codes(zb, state_ref, first_ref, second_ref):
-    segment = state_ref.shape[0]
-    even = lax.axis_index("tm") % 2 == 0
-    zb[L : L + segment, :] = state_ref[...].astype(jnp.bfloat16)
-
-    def put(left, right):
-        zb[:L, :] = left[:, :K]
-        if zb.shape[0] > L + segment:
-            zb[L + segment :, :] = right[:, :K]
-
-    pl.when(even)(lambda: put(second_ref, first_ref))
-    pl.when(jnp.logical_not(even))(lambda: put(first_ref, second_ref))
-
-
-def iterate_kernel(total_time, patching, copied, plan_ref, limit_ref, *refs):
+def taker(refs):
     refs = list(refs)
 
     def take(count):
@@ -310,46 +297,74 @@
         del refs[:count]
         return taken
 
+    return take
+
+
+def reaches(segment):
+    near = min(2 * L, segment)
+    return near, 2 * L - near
+
+
+def residual_rows(rb, pieces, start, acc, total_time):
+    rows = rb.shape[0]
+    moment = start + lax.broadcasted_iota(jnp.int32, (rows, LANES), 0)
+    scale = (C * L) ** (-0.5)
+    for tile in range(acc.shape[0]):
+        column = slice(tile * LANES, (tile + 1) * LANES)
+        signal = jnp.concatenate([piece[:, column] for piece in pieces], axis=0)
+        value = signal.astype(jnp.float32) - scale * acc[tile, :rows, :]
+        rb[:, column] = jnp.where(moment < total_time, value, 0.0).astype(jnp.bfloat16)
+
+
+def stepped_codes(state, acc, limit):
+    scale = (C * L) ** (-0.5)
+    stepped = state + code_rate * (scale * acc[0, : state.shape[0], :])
+    return stepped - jnp.clip(stepped, -limit, limit)
+
+
+def iterate_kernel(total_time, patching, copied, plan_ref, limit_ref, *refs):
+    take = taker(refs)
     state_ref, first_ref, second_ref, signal_ref, next_first, next_second = take(6)
     atoms = take(1 if patching else 0)
     (taps,) = take(1)
     source = take(1 if copied else 0)
     take(1 if copied and copied[0] else 0)
-    state_out, *edges = take(3)
+    state_out, first_out, second_out, far_out = take(4)
     taps = (take(1) if patching else [taps])[0]
     target = take(1 if copied else 0)
     zb, rb, zz, rr, fine, acc, beyond = take(7)
     ferry = Ferry(source[0], target[0], copied[0], *take(2)) if copied else None
     segment, channels = signal_ref.shape
-    tiles = channels // LANES
-    scale = (C * L) ** (-0.5)
-    me = lax.axis_index("tm")
-    even = me % 2 == 0
-    put_codes(zb, state_ref, first_ref, second_ref)
-
-    def put(following):
-        beyond[...] = following[:, K:]
-
-    pl.when(even)(lambda: put(next_first))
-    pl.when(jnp.logical_not(even))(lambda: put(next_second))
+    zb[L : L + segment, :] = state_ref[...].astype(jnp.bfloat16)
+
+    def put(left, right):
+        zb[:L, :] = left[:, :K]
+        zb[L + segment :, :] = right[:, :K]
+
+    def put_signal(left, right):
+        beyond[...] = right[:, K:]
+
+    by_side(put, first_ref, second_ref)
+    by_side(put_signal, next_first, next_second)
     if patching:
-        columns, *turned = refs
+        columns, *turned = take(1 + GROUPS)
         patch_taps(first_row_of(plan_ref, patching - 1), atoms[0], taps, columns, turned)
-    reach = segment + L
-    convolve(zb, L, reach, taps, zz, fine, acc, ferry)
-    moment = me * segment + lax.broadcasted_iota(jnp.int32, (reach, LANES), 0)
-    inside = moment < total_time
-    for tile in range(tiles):
-        column = slice(tile * LANES, (tile + 1) * LANES)
-        signal = jnp.concatenate([signal_ref[:, column], beyond[:, column]], axis=0)
-        value = signal.astype(jnp.float32) - scale * acc[tile, :reach, :]
-        rb[:, column] = jnp.where(inside, value, 0.0).astype(jnp.bfloat16)
-    correlate(rb, segment, taps, rr, fine, acc, ferry)
-    limit = limit_ref[...]
-    stepped = state_ref[...] + code_rate * (scale * acc[0, :segment, :])
-    state = stepped - jnp.clip(stepped, -limit, limit)
+    convolve(zb, L, segment + L, taps, zz, fine, acc)
+    if ferry:
+        ferry.turn_round()
+    start = lax.axis_index("tm") * segment
+    residual_rows(rb, (signal_ref, beyond), start, acc, total_time)
+    correlate(rb, segment, taps, rr, fine, acc)
+    state = stepped_codes(state_ref[...], acc, limit_ref[...])
     state_out[...] = state
-    put_edges(edges, state.astype(jnp.bfloat16))
+    low = state.astype(jnp.bfloat16)
+    rest = (state - low.astype(jnp.float32)).astype(jnp.bfloat16)
+    near, beyond_near = reaches(segment)
+    put_edges((first_out, second_out), jnp.concatenate([low[-near:], rest[-L:]], axis=0), low[:L])
+    if beyond_near:
+        far_out[...] = low[-beyond_near:]
+    else:
+        far_out[...] = jnp.zeros_like(far_out)
     if ferry:
         ferry.close()
 
@@ -358,20 +373,20 @@
     segment, channels = signal.shape
     patching = atoms is not None
     reach = segment + L
-    carried = [far(value) for value in (ferry or ())[:2] if value is not None]
-    aliases = {9: 3} if patching else {}
+    near, beyond_near = reaches(segment)
+    carried = [far(value) for value in ferry[:2] if value is not None]
+    aliases = {9: 4} if patching else {}
     if len(carried) == 2:
-        aliases[10 + patching] = 3 + patching
+        aliases[10 + patching] = 4 + patching
     return pl.pallas_call(
-        functools.partial(
-            iterate_kernel, peers * segment, step if patching else 0, ferry[2:] if ferry else None
-        ),
+        functools.partial(iterate_kernel, peers * segment, step if patching else 0, ferry[2:]),
         in_specs=[scalars()] + [vmem()] * (8 + patching) + [hbm()] * len(carried),
-        out_specs=[vmem()] * (3 + patching) + [hbm()] * (ferry is not None),
+        out_specs=[vmem()] * (4 + patching) + [hbm()],
         out_shape=[pltpu.VMEM((segment, K), jnp.float32)]
-        + [jax.ShapeDtypeStruct((L, K), jnp.bfloat16)] * 2
+        + [jax.ShapeDtypeStruct((near + L, K), jnp.bfloat16)] * 2
+        + [jax.ShapeDtypeStruct((max(beyond_near, ROWS), K), jnp.bfloat16)]
         + [pltpu.VMEM(taps.shape, jnp.bfloat16)] * patching
-        + ([pltpu.HBM(ferry[0].shape, jnp.float32)] if ferry else []),
+        + [pltpu.HBM(ferry[0].shape, jnp.float32)],
         scratch_shapes=[
             pltpu.VMEM((L + reach, K), jnp.bfloat16),
             pltpu.VMEM((reach, channels), jnp.bfloat16),
@@ -381,7 +396,7 @@
             pltpu.VMEM((channels // LANES, reach, LANES), jnp.float32),
             pltpu.VMEM((L, channels), jnp.bfloat16),
         ]
-        + (ferry_scratch(ferry[3], ferry[0].shape[1]) if ferry else [])
+        + ferry_scratch(ferry[3], ferry[0].shape[1])
         + (
             [pltpu.VMEM((K, GROUPS * ROWS * L), jnp.bfloat16)]
             + [pltpu.VMEM((ROWS * STRIDE, K), jnp.float32)] * GROUPS
@@ -403,29 +418,54 @@
     )
 
 
-def finish_kernel(
-    peers, step, copied, plan_ref, state_ref, first_ref, second_ref, signal_ref, taps, *refs
-):
-    refs = list(refs)
-
-    def take(count):
-        taken = refs[:count]
-        del refs[:count]
-        return taken
-
+def conclude_kernel(peers, step, copied, plan_ref, limit_ref, *refs):
     last = step + 1 == OUTER
-    source = take(2 if copied else 0)
-    (payload_out,) = take(1)
-    outs = take(2 if last else 0)
-    target = take(1 if copied else 0)
-    zb, zz, fine, acc, tall = take(5)
-    ferry = Ferry(source[0], target[0], copied[0], *take(2)) if copied else None
-    resid_out, codes_out = outs if last else (None, *refs)
+    take = taker(refs)
+    state_ref, first_ref, second_ref, far_ref, signal_ref, next_first, next_second, taps = take(8)
+    source, _, payload_out = take(3)
+    outs = take(2 if last else 3)
+    (target,) = take(1)
+    zb, rb, zz, rr, fine, acc, before, beyond, earlier, tall = take(10)
+    ferry = Ferry(source, target, copied[0], *take(2))
     segment, channels = signal_ref.shape
+    near, beyond_near = reaches(segment)
+    zb[2 * L : 2 * L + segment, :] = state_ref[...].astype(jnp.bfloat16)
+    if beyond_near:
+        zb[:beyond_near, :] = far_ref[...]
+
+    def put(left, right):
+        zb[beyond_near : 2 * L, :] = left[:near]
+        earlier[...] = left[near - L : near].astype(jnp.float32) + left[near:].astype(jnp.float32)
+        zb[2 * L + segment :, :] = right[:L]
+
+    def put_signal(left, right):
+        before[...] = left[:, K:]
+        beyond[...] = right[:, K:]
+
+    by_side(put, first_ref, second_ref)
+    by_side(put_signal, next_first, next_second)
+    convolve(zb, L, 2 * L + segment, taps, zz, fine, acc)
+    ferry.turn_round()
+    start = lax.axis_index("tm") * segment - L
+    residual_rows(rb, (before, signal_ref, beyond), start, acc, peers * segment)
+    correlate(rb, L + segment, taps, rr, fine, acc)
+    state = jnp.concatenate([earlier[...], state_ref[...]], axis=0)
+    state = stepped_codes(state, acc, limit_ref[...])
+    moment = start + lax.broadcasted_iota(jnp.int32, state.shape, 0)
+    state = jnp.where(moment >= 0, state, 0.0)
+    low = state.astype(jnp.bfloat16)
+    zb[: L + segment, :] = low
+    own = state[L:]
+    if last:
+        resid_out, codes_out = outs
+    else:
+        state_out, *edges = outs
+        (codes_out,) = take(1)
+        state_out[...] = own
+        put_edges(edges, low[-L:], low[L : 2 * L])
+    codes_out[...] = own.T
+    convolve(zb, L, segment, taps, zz, fine, acc)
     scale = (C * L) ** (-0.5)
-    put_codes(zb, state_ref, first_ref, second_ref)
-    codes_out[...] = state_ref[...].T
-    convolve(zb, L, segment, taps, zz, fine, acc, ferry)
     for tile in range(channels // LANES):
         column = slice(tile * LANES, (tile + 1) * LANES)
         value = signal_ref[:, column].astype(jnp.float32) - scale * acc[tile, :segment, :]
@@ -441,39 +481,58 @@
         part = tall[peer * share : peer * share + share_rows, :]
         payload_out[peer, :share_rows, :] = part.astype(jnp.bfloat16)
         payload_out[peer, share_rows:, :] = block
-    if ferry:
-        ferry.close()
-
-
-def finish(plan, step, state, swapped, signal, taps, ferry, peers):
+    ferry.close()
+
+
+def conclude(plan, step, limit, state, swapped, far_edge, signal, following, taps, ferry, peers):
     segment, channels = signal.shape
     share = channels // peers
     share_rows = -(-share // ROWS) * ROWS
     last = step + 1 == OUTER
-    carried = [far(value) for value in (ferry or ())[:2]]
+    carried = [far(value) for value in ferry[:2]]
+    rows = 2 * L + segment
+    outs = [
+        pltpu.VMEM((channels, segment), jnp.float32),
+        pltpu.VMEM((K, segment), jnp.float32),
+    ]
+    if not last:
+        outs = [pltpu.VMEM((segment, K), jnp.float32)]
+        outs += [jax.ShapeDtypeStruct((L, K), jnp.bfloat16)] * 2
     return pl.pallas_call(
-        functools.partial(finish_kernel, peers, step, ferry[2:] if ferry else None),
-        in_specs=[scalars()] + [vmem()] * 5 + [hbm()] * len(carried),
-        out_specs=[vmem()] * (3 if last else 1) + [hbm()] * (len(carried) // 2),
-        out_shape=[
-            jax.ShapeDtypeStruct((peers, share_rows + BLOCK_ATOMS, segment), jnp.bfloat16),
-            pltpu.VMEM((channels, segment), jnp.float32),
-            pltpu.VMEM((K, segment), jnp.float32),
-        ][: 3 if last else 1]
-        + [pltpu.HBM(value.shape, jnp.float32) for value in carried[1:]],
+        functools.partial(conclude_kernel, peers, step, ferry[2:]),
+        in_specs=[scalars()] + [vmem()] * 9 + [hbm()] * 2,
+        out_specs=[vmem()] * (1 + len(outs)) + [hbm()],
+        out_shape=[jax.ShapeDtypeStruct((peers, share_rows + BLOCK_ATOMS, segment), jnp.bfloat16)]
+        + outs
+        + [pltpu.HBM(ferry[0].shape, jnp.float32)],
         scratch_shapes=[
-            pltpu.VMEM((L + segment, K), jnp.bfloat16),
-            pltpu.VMEM((segment + ROWS, COARSE * K), jnp.bfloat16),
-            pltpu.VMEM((2 * FINE, channels // LANES, segment + ROWS, LANES), jnp.float32),
-            pltpu.VMEM((channels // LANES, segment, LANES), jnp.float32),
+            pltpu.VMEM((rows + L, K), jnp.bfloat16),
+            pltpu.VMEM((rows, channels), jnp.bfloat16),
+            pltpu.VMEM((rows + ROWS, COARSE * K), jnp.bfloat16),
+            pltpu.VMEM((L + segment + ROWS, COARSE * channels), jnp.bfloat16),
+            pltpu.VMEM((2 * FINE, channels // LANES, rows + ROWS, LANES), jnp.float32),
+            pltpu.VMEM((channels // LANES, rows, LANES), jnp.float32),
+            pltpu.VMEM((L, channels), jnp.bfloat16),
+            pltpu.VMEM((L, channels), jnp.bfloat16),
+            pltpu.VMEM((L, K), jnp.float32),
             pltpu.VMEM((channels + ROWS, segment), jnp.float32),
         ]
-        + (ferry_scratch(ferry[3], ferry[0].shape[1]) if ferry else [])
+        + ferry_scratch(ferry[3], ferry[0].shape[1])
         + ([] if last else [pltpu.VMEM((K, segment), jnp.float32)]),
-        input_output_aliases={7: 3 if last else 1} if carried else {},
+        input_output_aliases={11: 1 + len(outs)},
         compiler_params=pltpu.CompilerParams(vmem_limit_bytes=VMEM_BYTES),
-        name="finish",
-    )(plan, resident(state), *swapped, resident(signal), resident(taps), *carried)
+        name="conclude",
+    )(
+        plan,
+        limit,
+        resident(state),
+        *swapped,
+        far_edge,
+        resident(signal),
+        *following,
+        resident(taps),
+        *carried,
+    )
 
 
 def gradient_kernel(share, step, plan_ref, blocks_ref, dict_hbm, out_ref, rf, zf, rr, zz, old, sem):
@@ -586,13 +645,12 @@
         return lax.ppermute(shard, "tm", [(i, i ^ mask) for i in range(peers)])
 
     held = piece[None]
-    beside = None
-    for masks in gather_steps(peers):
+    for index, masks in enumerate(gather_steps(peers)):
         held = jnp.concatenate([held] + [exchanged(held, mask) for mask in masks], axis=0)
-        if beside is None:
-            beside = meanwhile(held)
-    ready, _ = lax.optimization_barrier((held, beside))
-    return held, exchanged(ready, 1)
+        if index == 0:
+            needed, extra = meanwhile(held)
+    ready, _ = lax.optimization_barrier((held, needed))
+    return held, exchanged(ready, 1), extra
 
 
 def recall_kernel(step, plan_ref, dict_hbm, piece_ref, old_ref, mean_ref, sem):
@@ -729,42 +787,51 @@
     dictionary = None
     renewed = []
     for step in range(OUTER):
-        for inner in range(INNER + 1):
-            turn_index = step * (INNER + 1) + inner
-            ferry = None
-            if COPIED[turn_index]:
-                first = sum(COPIED[:turn_index])
-                ferry = (dictionary_init, dictionary, first, COPIED[turn_index])
-            if inner == INNER:
-                payload, *finals = finish(plan, step, state, swapped, signal, taps, ferry, peers)
-                if ferry:
-                    *finals, dictionary = finals
-                break
-            fresh = renewed[-1] if inner == 0 and step else None
-            state, *results = iterate(
-                plan, step, limit, state, swapped, signal, following, taps, fresh, ferry, peers
-            )
-            swapped = swaps(results[:2])
-            if fresh is not None:
-                taps = results[2]
-            if ferry:
-                dictionary = results[-1]
+        last = step + 1 == OUTER
+        rows = COPIED[2 * step : 2 * step + 2]
+        first = sum(COPIED[: 2 * step])
+        ferry = (dictionary_init, dictionary, first, rows[0])
+        atoms = renewed[-1] if renewed else None
+        state, *results = iterate(
+            plan, step, limit, state, swapped, signal, following, taps, atoms, ferry, peers
+        )
+        if renewed:
+            taps = results[3]
+        edges, far_edge, dictionary = results[:2], results[2], results[-1]
+        ferry = (dictionary_init, dictionary, first + rows[0], rows[1])
+        payload, *results, dictionary = conclude(
+            plan,
+            step,
+            limit,
+            state,
+            swaps(edges),
+            shifted(far_edge, "tm", 2),
+            signal,
+            following,
+            taps,
+            ferry,
+            peers,
+        )
         blocks = lax.all_to_all(payload, "tm", 0, 0, tiled=True)
         piece = share_gradient(plan, step, blocks, dictionary_init, channels // peers)
-        recalled = []
-
-        def recall_beside(held):
-            recalled.extend(recall(plan, step, dictionary_init, held))
-            return recalled[0]
-
-        held, came = gather_pieces(piece, recall_beside)
-        last = step + 1 == OUTER
+        recalled = [] if last else list(recall(plan, step, dictionary_init, piece))
+
+        def beside(held):
+            if last:
+                recalled.extend(recall(plan, step, dictionary_init, held))
+                return recalled[0], None
+            state, *edges = results
+            edges, _ = lax.optimization_barrier((edges, held))
+            return recalled[0], swaps(edges)
+
+        held, came, extra = gather_pieces(piece, beside)
         result = renew(plan, step, held, came, *recalled, renewed if last else None, dictionary)
         if last:
             dictionary = result
         else:
             renewed.append(result)
-    residual, codes = finals
+            state, swapped = results[0], extra
+    residual, codes = results
     return codes, dictionary, residual
 
 
@@ -841,6 +908,7 @@
     fits = (
         lax.axis_size("chan") == 1
         and segment % LANES == 0
+        and INNER == 2
         and channels % (GROUPS * ROWS) == 0
         and channels % LANES == 0
         and channels % peers == 0

time: 162 us -> 157 us (0.969)
  blocking collectives: 44.2 us -> 36.5 us
  starting transfers between devices: 32.9 us -> 35.1 us
  waiting for transfers between devices: 13.9 us -> 15.7 us
    pallas_call x4 -> x2, Pallas kernels: 31.5 us -> 18 us  [iterate(): pl.pallas_call(functools.partial(iterate_kernel, peers * segment, step if...]
    pallas_call x2, Pallas kernels: 8.64 us -> 21.3 us  [conclude(): pl.pallas_call(functools.partial(conclude_kernel, peers, step, ferry[2:])...]
    ppermute x0 -> x2, starting transfers between devices: none -> 9.77 us  [shifted(): return lax.ppermute(shard, axis, pairs)]
    all_to_all x2, blocking collectives: 44.2 us -> 36.5 us  [whole_channels(): blocks = lax.all_to_all(payload, 'tm', 0, 0, tiled=True)]
    ppermute x10 -> x8, starting transfers between devices: 16.8 us -> 9.15 us  [swaps(): return [lax.ppermute(edge, 'tm', pair) for edge, pair in zip(edges, pairs)]]
    ppermute x0 -> x2, waiting for transfers between devices: none -> 2.85 us  [shifted(): return lax.ppermute(shard, axis, pairs)]
  transfers between devices with their start and end apart: 24 -> 24, of which waited for: 12 -> 8; matrix products, arithmetic and copies ran while one was open for 1% -> 1% of each run, Pallas kernels for 9% -> 11%
where the time goes in v9:
time: 157 us; the launch traced here: 156 us
  Pallas kernels  66.5 us (42%)
  blocking collectives  36.5 us (23%)
  starting transfers between devices  35.1 us (22%)
  waiting for transfers between devices  15.7 us (10%)
    all_to_all x2, blocking collectives, whole_channels(): blocks = lax.all_to_all(payload, 'tm', 0, 0, tiled=True)  36.5 us
    pallas_call x2, Pallas kernels, conclude(): pl.pallas_call(functools.partial(conclude_kernel, peers, step, ferry[2:])...  21.3 us
    pallas_call x2, Pallas kernels, iterate(): pl.pallas_call(functools.partial(iterate_kernel, peers * segment, step if...  18 us
    ppermute x14, starting transfers between devices, exchanged(): return lax.ppermute(shard, 'tm', [(i, i ^ mask) for i in range(peers)])  16.2 us
    ppermute x14, waiting for transfers between devices, exchanged(): return lax.ppermute(shard, 'tm', [(i, i ^ mask) for i in range(peers)])  12.8 us
    ppermute x2, starting transfers between devices, shifted(): return lax.ppermute(shard, axis, pairs)  9.77 us
    pallas_call x1, Pallas kernels, layout(): pl.pallas_call(layout_kernel, grid=(channels // block,), in_specs=[pl.Blo...  9.19 us
    ppermute x8, starting transfers between devices, swaps(): return [lax.ppermute(edge, 'tm', pair) for edge, pair in zip(edges, pairs)]  9.15 us
  transfers between devices with their start and end apart: 24, of which 8 were waited for; matrix products, arithmetic and copies ran while one was open for 1% of the time, Pallas kernels for 11%

profile of v9, /device:TPU:0, one launch (start us, length us, event | category | flops | bytes accessed | tf_op | source)
XLA Modules:
  0.0 156.5 jit_solution(2734883512003050510)
XLA Ops:
  2.9 9.2 %layout.1.refs_6_.refs_7_ = bf16[6,16,384,128]{3,2,1,0:T(8,128)(2,1)S(1)} custom-call(f32[128,36864]{1,0:T(8,128)} %dict_hbm.7), custom_call_target="tpu_custom_call" | custom-call | tf_op jit(solution)/shard_map/layout/pallas_call | solution.py:113
  12.2 5.8 %iterate.2 = (f32[128,128]{1,0:T(8,128)S(1)}, bf16[224,128]{1,0:T(8,128)(2,1)S(1)}, bf16[224,128]{1,0:T(8,128)(2,1)S(1)}, bf16[64,128]{1,0:T(8,128)(2,1)S(1)}, f32[128,36864]{1,0:T(8,128)}) custom-call(s32[8]{0:T(128)S(1)} %copy-done, f32[1,128]{1,0:T(1,128)S(1)} %bitcast.13, f32[128,128]{1,0:T(8,128)S(1)} %get-tuple-element.35.refs_0_, ...), custom_call_target="tpu_custom_call" | custom-call | tf_op jit(solution)/shard_map/iterate/pallas_call | solution.py:381
  18.0 3.9 %collective-permute-start.2 = (bf16[224,128]{1,0:T(8,128)(2,1)S(1)}, bf16[224,128]{1,0:T(8,128)(2,1)S(1)}, u32[]{:S(2)}, u32[]{:S(2)}) collective-permute-start(bf16[224,128]{1,0:T(8,128)(2,1)S(1)} %get-tuple-element.40), channel_id=1, source_target_pairs={{0,1},{1,0},{2,3},{3,2},{4,5},{5,4},{6,7},{7,6},{8,9},{9,8},{10,11... | collective-permute-start | bytes 172040 | tf_op jit(solution)/shard_map/ppermute | solution.py:781
  22.6 4.8 %collective-permute-start.4 = (bf16[64,128]{1,0:T(8,128)(2,1)S(1)}, bf16[64,128]{1,0:T(8,128)(2,1)S(1)}, u32[]{:S(2)}, u32[]{:S(2)}) collective-permute-start(bf16[64,128]{1,0:T(8,128)(2,1)S(1)} %get-tuple-element.42), channel_id=1, source_target_pairs={{0,2},{1,3},{2,4},{3,5},{4,6},{5,7},{6,8},{7,9},{8,10},{9,11},{10,... | collective-permute-start | bytes 49160 | tf_op jit(solution)/shard_map/ppermute | solution.py:38
  27.4 1.4 collective-permute-done.4.refs_3_
  28.8 10.6 %conclude.2 = (bf16[32,32,128]{2,1,0:T(8,128)(2,1)S(1)}, f32[128,128]{1,0:T(8,128)S(1)}, bf16[96,128]{1,0:T(8,128)(2,1)S(1)}, bf16[96,128]{1,0:T(8,128)(2,1)S(1)}, f32[128,36864]{1,0:T(8,128)}) custom-call(s32[8]{0:T(128)S(1)} %copy-done, f32[1,128]{1,0:T(1,128)S(1)} %bitcast.14, ...), custom_call_target="tpu_custom_call", output_to_operand_aliasing={{4}: (11, {})} | custom-call | tf_op jit(solution)/shard_map/conclude/pallas_call | solution.py:501
  39.4 18.8 %all_to_all.10.blocks_ref = bf16[32,32,128]{2,1,0:T(8,128)(2,1)S(1)} all-to-all(bf16[32,32,128]{2,1,0:T(8,128)(2,1)S(1)} %get-tuple-element.47), channel_id=1, replica_groups=mesh['tm'=32,'chan'=1] {'tm'}, dimensions={0} | all-to-all | bytes 524288 | tf_op jit(solution)/shard_map/all_to_all | solution.py:815
  58.2 2.8 %gradient.2.piece_ref = bf16[16,1280]{1,0:T(8,128)(2,1)S(1)} custom-call(s32[8]{0:T(128)S(1)} %copy-done, bf16[32,32,128]{2,1,0:T(8,128)(2,1)S(1)} %all_to_all.10.blocks_ref, f32[128,36864]{1,0:T(8,128)} %dict_hbm.7), custom_call_target="tpu_custom_call" | custom-call | tf_op jit(solution)/shard_map/gradient/pallas_call | solution.py:608
  62.4 3.1 %collective-permute-start.5 = (bf16[1,16,1280]{2,1,0:T(8,128)(2,1)S(1)}, bf16[1,16,1280]{2,1,0:T(8,128)(2,1)S(1)}, u32[]{:S(2)}, u32[]{:S(2)}) collective-permute-start(bf16[1,16,1280]{2,1,0:T(8,128)(2,1)S(1)} %bitcast.7), channel_id=1, source_target_pairs={{0,16},{1,17},{2,18},{3,19},{4,20},{5,21},{6,22},{7,23},{8,24},{9,... | collective-permute-start | bytes 122888 | tf_op jit(solution)/shard_map/ppermute | solution.py:645
  65.4 2.6 %recall.2 = (f32[16,36864]{1,0:T(8,128)S(1)}, f32[16,128]{1,0:T(8,128)S(1)}) custom-call(s32[8]{0:T(128)S(1)} %copy-done, f32[128,36864]{1,0:T(8,128)} %dict_hbm.7, bf16[16,1280]{1,0:T(8,128)(2,1)S(1)} %gradient.2.piece_ref), custom_call_target="tpu_custom_call" | custom-call | tf_op jit(solution)/shard_map/recall/pallas_call | solution.py:676
  71.7 6.1 %collective-permute-done.10 = bf16[4,16,1280]{2,1,0:T(8,128)(2,1)S(1)} collective-permute-done((bf16[4,16,1280]{2,1,0:T(8,128)(2,1)S(1)}, bf16[4,16,1280]{2,1,0:T(8,128)(2,1)S(1)}, u32[]{:S(2)}, u32[]{:S(2)}) %collective-permute-start.10) | collective-permute-done | bytes 163872 | tf_op jit(solution)/shard_map/ppermute | solution.py:645
  80.0 2.1 %renew.2.refs_6_.refs_0_ = f32[16,36864]{1,0:T(8,128)S(1)} custom-call(s32[8]{0:T(128)S(1)} %copy-done, bf16[16,16,1280]{2,1,0:T(8,128)(2,1)S(1)} %constant_dynamic-update-slice_fusion.held_ref, bf16[16,16,1280]{2,1,0:T(8,128)(2,1)S(1)} %collective-permute-done.13.came_ref, f32[16,36864]{1,0:T(8,128)S(1)} %get-tuple-element.50.old, ...), custom_call_target="tpu_custom_call" | custom-call | tf_op jit(solution)/shard_map/renew/pallas_call | solution.py:755
  82.1 12.2 %iterate.3 = (f32[128,128]{1,0:T(8,128)S(1)}, bf16[224,128]{1,0:T(8,128)(2,1)S(1)}, bf16[224,128]{1,0:T(8,128)(2,1)S(1)}, bf16[64,128]{1,0:T(8,128)(2,1)S(1)}, b...) custom-call(s32[8]{0:T(128)S(1)} %copy-done, ...), custom_call_target="tpu_custom_call", output_to_operand_aliasing={{4}: (9, {}), {5}: (11, {})} | custom-call | tf_op jit(solution)/shard_map/iterate/pallas_call | solution.py:381
  94.4 1.6 %collective-permute-start.14 = (bf16[224,128]{1,0:T(8,128)(2,1)S(1)}, bf16[224,128]{1,0:T(8,128)(2,1)S(1)}, u32[]{:S(2)}, u32[]{:S(2)}) collective-permute-start(bf16[224,128]{1,0:T(8,128)(2,1)S(1)} %get-tuple-element.55), channel_id=1, source_target_pairs={{0,1},{1,0},{2,3},{3,2},{4,5},{5,4},{6,7},{7,6},{8,9},{9,8},{10,11... | collective-permute-start | bytes 172040 | tf_op jit(solution)/shard_map/ppermute | solution.py:781
  96.6 5.0 %collective-permute-start.16 = (bf16[64,128]{1,0:T(8,128)(2,1)S(1)}, bf16[64,128]{1,0:T(8,128)(2,1)S(1)}, u32[]{:S(2)}, u32[]{:S(2)}) collective-permute-start(bf16[64,128]{1,0:T(8,128)(2,1)S(1)} %get-tuple-element.57), channel_id=1, source_target_pairs={{0,2},{1,3},{2,4},{3,5},{4,6},{5,7},{6,8},{7,9},{8,10},{9,11},{10,... | collective-permute-start | bytes 49160 | tf_op jit(solution)/shard_map/ppermute | solution.py:38
  101.6 1.4 collective-permute-done.16.refs_3_
  103.0 10.7 %conclude.3 = (bf16[32,32,128]{2,1,0:T(8,128)(2,1)S(1)}, f32[384,128]{1,0:T(8,128)S(1)}, f32[128,128]{1,0:T(8,128)S(1)}, f32[128,36864]{1,0:T(8,128)}) custom-call(s32[8]{0:T(128)S(1)} %copy-done, f32[1,128]{1,0:T(1,128)S(1)} %bitcast.16, f32[128,128]{1,0:T(8,128)S(1)} %get-tuple-element.54.refs_0_, ...), custom_call_target="tpu_custom_call", output_to_operand_aliasing={{3}: (11, {})} | custom-call | tf_op jit(solution)/shard_map/conclude/pallas_call | solution.py:501
  113.7 17.7 %all_to_all.11.blocks_ref = bf16[32,32,128]{2,1,0:T(8,128)(2,1)S(1)} all-to-all(bf16[32,32,128]{2,1,0:T(8,128)(2,1)S(1)} %get-tuple-element.61), channel_id=1, replica_groups=mesh['tm'=32,'chan'=1] {'tm'}, dimensions={0} | all-to-all | bytes 524288 | tf_op jit(solution)/shard_map/all_to_all | solution.py:815
  131.5 2.8 %gradient.3 = bf16[16,1280]{1,0:T(8,128)(2,1)S(1)} custom-call(s32[8]{0:T(128)S(1)} %copy-done, bf16[32,32,128]{2,1,0:T(8,128)(2,1)S(1)} %all_to_all.11.blocks_ref, f32[128,36864]{1,0:T(8,128)} %dict_hbm.7), custom_call_target="tpu_custom_call" | custom-call | tf_op jit(solution)/shard_map/gradient/pallas_call | solution.py:608
  135.7 3.1 %collective-permute-start.17 = (bf16[1,16,1280]{2,1,0:T(8,128)(2,1)S(1)}, bf16[1,16,1280]{2,1,0:T(8,128)(2,1)S(1)}, u32[]{:S(2)}, u32[]{:S(2)}) collective-permute-start(bf16[1,16,1280]{2,1,0:T(8,128)(2,1)S(1)} %bitcast.11), channel_id=1, source_target_pairs={{0,16},{1,17},{2,18},{3,19},{4,20},{5,21},{6,22},{7,23},{8,24},{9,... | collective-permute-start | bytes 122888 | tf_op jit(solution)/shard_map/ppermute | solution.py:645
  138.8 1.7 %collective-permute-done.19 = bf16[1,16,1280]{2,1,0:T(8,128)(2,1)S(1)} collective-permute-done((bf16[1,16,1280]{2,1,0:T(8,128)(2,1)S(1)}, bf16[1,16,1280]{2,1,0:T(8,128)(2,1)S(1)}, u32[]{:S(2)}, u32[]{:S(2)}) %collective-permute-start.19) | collective-permute-done | bytes 40992 | tf_op jit(solution)/shard_map/ppermute | solution.py:645
  144.6 2.6 %recall.3 = (f32[16,36864]{1,0:T(8,128)S(1)}, f32[16,128]{1,0:T(8,128)S(1)}) custom-call(s32[8]{0:T(128)S(1)} %copy-done, f32[128,36864]{1,0:T(8,128)} %dict_hbm.7, bf16[4,16,1280]{2,1,0:T(8,128)(2,1)S(1)} %pad_maximum_fusion.1.piece_ref), custom_call_target="tpu_custom_call" | custom-call | tf_op jit(solution)/shard_map/recall/pallas_call | solution.py:676
  147.3 2.7 %collective-permute-done.20 = bf16[4,16,1280]{2,1,0:T(8,128)(2,1)S(1)} collective-permute-done((bf16[4,16,1280]{2,1,0:T(8,128)(2,1)S(1)}, bf16[4,16,1280]{2,1,0:T(8,128)(2,1)S(1)}, u32[]{:S(2)}, u32[]{:S(2)}) %collective-permute-start.20) | collective-permute-done | bytes 163872 | tf_op jit(solution)/shard_map/ppermute | solution.py:645
  152.3 4.0 %renew.3 = f32[128,36864]{1,0:T(8,128)} custom-call(s32[8]{0:T(128)S(1)} %copy-done, bf16[16,16,1280]{2,1,0:T(8,128)(2,1)S(1)} %constant_dynamic-update-slice_fusion.7.held_ref, bf16[16,16,1280]{2,1,0:T(8,128)(2,1)S(1)} %collective-permute-done.23.came_ref, f32[16,36864]{1,0:T(8,128)S(1)} %get-tuple-element.62.old, ...), custom_call_target="tpu_custom_call", output_to_operand_aliasing={{}: (6, {})} | custom-call | tf_op jit(solution)/shard_map/renew/pallas_call | solution.py:755
  (60 shorter events, 18.5 us)
Async XLA Ops:
  1.8 10.4 %collective-permute-start = (bf16[96,512]{1,0:T(8,128)(2,1)S(1)}, bf16[96,512]{1,0:T(8,128)(2,1)S(1)}, u32[]{:S(2)}, u32[]{:S(2)}) collective-permute-start(bf16[96,512]{1,0:T(8,128)(2,1)S(1)} %get-tuple-element.36), channel_id=1, source_target_pairs={{0,1},{1,0},{2,3},{3,2},{4,5},{5,4},{6,7},{7,6},{8,9},{9,8},{10,11... | collective-permute-start | bytes 294920 | tf_op jit(solution)/shard_map/ppermute | solution.py:781
  2.3 9.9 %collective-permute-start.1 = (bf16[96,512]{1,0:T(8,128)(2,1)S(1)}, bf16[96,512]{1,0:T(8,128)(2,1)S(1)}, u32[]{:S(2)}, u32[]{:S(2)}) collective-permute-start(bf16[96,512]{1,0:T(8,128)(2,1)S(1)} %get-tuple-element.37), channel_id=1, source_target_pairs={{1,2},{2,1},{3,4},{4,3},{5,6},{6,5},{7,8},{8,7},{9,10},{10,9},{11,... | collective-permute-start | bytes 294920 | tf_op jit(solution)/shard_map/ppermute | solution.py:781
  18.0 10.8 %collective-permute-start.2 = (bf16[224,128]{1,0:T(8,128)(2,1)S(1)}, bf16[224,128]{1,0:T(8,128)(2,1)S(1)}, u32[]{:S(2)}, u32[]{:S(2)}) collective-permute-start(bf16[224,128]{1,0:T(8,128)(2,1)S(1)} %get-tuple-element.40), channel_id=1, source_target_pairs={{0,1},{1,0},{2,3},{3,2},{4,5},{5,4},{6,7},{7,6},{8,9},{9,8},{10,11... | collective-permute-start | bytes 172040 | tf_op jit(solution)/shard_map/ppermute | solution.py:781
  21.9 6.9 %collective-permute-start.3 = (bf16[224,128]{1,0:T(8,128)(2,1)S(1)}, bf16[224,128]{1,0:T(8,128)(2,1)S(1)}, u32[]{:S(2)}, u32[]{:S(2)}) collective-permute-start(bf16[224,128]{1,0:T(8,128)(2,1)S(1)} %get-tuple-element.41), channel_id=1, source_target_pairs={{1,2},{2,1},{3,4},{4,3},{5,6},{6,5},{7,8},{8,7},{9,10},{10,9},{11,... | collective-permute-start | bytes 172040 | tf_op jit(solution)/shard_map/ppermute | solution.py:781
  22.6 6.2 %collective-permute-start.4 = (bf16[64,128]{1,0:T(8,128)(2,1)S(1)}, bf16[64,128]{1,0:T(8,128)(2,1)S(1)}, u32[]{:S(2)}, u32[]{:S(2)}) collective-permute-start(bf16[64,128]{1,0:T(8,128)(2,1)S(1)} %get-tuple-element.42), channel_id=1, source_target_pairs={{0,2},{1,3},{2,4},{3,5},{4,6},{5,7},{6,8},{7,9},{8,10},{9,11},{10,... | collective-permute-start | bytes 49160 | tf_op jit(solution)/shard_map/ppermute | solution.py:38
  61.0 7.1 %collective-permute-start.7 = (bf16[1,16,1280]{2,1,0:T(8,128)(2,1)S(1)}, bf16[1,16,1280]{2,1,0:T(8,128)(2,1)S(1)}, u32[]{:S(2)}, u32[]{:S(2)}) collective-permute-start(bf16[1,16,1280]{2,1,0:T(8,128)(2,1)S(1)} %bitcast.5), channel_id=1, source_target_pairs={{0,24},{1,25},{2,26},{3,27},{4,28},{5,29},{6,30},{7,31},{8,16},{9,... | collective-permute-start | bytes 122888 | tf_op jit(solution)/shard_map/ppermute | solution.py:645
  62.4 5.7 %collective-permute-start.6 = (bf16[1,16,1280]{2,1,0:T(8,128)(2,1)S(1)}, bf16[1,16,1280]{2,1,0:T(8,128)(2,1)S(1)}, u32[]{:S(2)}, u32[]{:S(2)}) collective-permute-start(bf16[1,16,1280]{2,1,0:T(8,128)(2,1)S(1)} %bitcast.6), channel_id=1, source_target_pairs={{0,8},{1,9},{2,10},{3,11},{4,12},{5,13},{6,14},{7,15},{8,0},{9,1},... | collective-permute-start | bytes 122888 | tf_op jit(solution)/shard_map/ppermute | solution.py:645
  62.4 5.7 %collective-permute-start.5 = (bf16[1,16,1280]{2,1,0:T(8,128)(2,1)S(1)}, bf16[1,16,1280]{2,1,0:T(8,128)(2,1)S(1)}, u32[]{:S(2)}, u32[]{:S(2)}) collective-permute-start(bf16[1,16,1280]{2,1,0:T(8,128)(2,1)S(1)} %bitcast.7), channel_id=1, source_target_pairs={{0,16},{1,17},{2,18},{3,19},{4,20},{5,21},{6,22},{7,23},{8,24},{9,... | collective-permute-start | bytes 122888 | tf_op jit(solution)/shard_map/ppermute | solution.py:645
  68.1 9.7 %collective-permute-start.12 = (bf16[4,16,1280]{2,1,0:T(8,128)(2,1)S(1)}, bf16[4,16,1280]{2,1,0:T(8,128)(2,1)S(1)}, u32[]{:S(2)}, u32[]{:S(2)}) collective-permute-start(bf16[4,16,1280]{2,1,0:T(8,128)(2,1)S(1)} %pad_maximum_fusion), channel_id=1, source_target_pairs={{0,6},{1,7},{2,4},{3,5},{4,2},{5,3},{6,0},{7,1},{8,14},{9,15},{10,... | collective-permute-start | bytes 491528 | tf_op jit(solution)/shard_map/ppermute | solution.py:645
  69.4 8.4 %collective-permute-start.11 = (bf16[4,16,1280]{2,1,0:T(8,128)(2,1)S(1)}, bf16[4,16,1280]{2,1,0:T(8,128)(2,1)S(1)}, u32[]{:S(2)}, u32[]{:S(2)}) collective-permute-start(bf16[4,16,1280]{2,1,0:T(8,128)(2,1)S(1)} %pad_maximum_fusion), channel_id=1, source_target_pairs={{0,2},{1,3},{2,0},{3,1},{4,6},{5,7},{6,4},{7,5},{8,10},{9,11},{10,... | collective-permute-start | bytes 491528 | tf_op jit(solution)/shard_map/ppermute | solution.py:645
  70.6 7.2 %collective-permute-start.10 = (bf16[4,16,1280]{2,1,0:T(8,128)(2,1)S(1)}, bf16[4,16,1280]{2,1,0:T(8,128)(2,1)S(1)}, u32[]{:S(2)}, u32[]{:S(2)}) collective-permute-start(bf16[4,16,1280]{2,1,0:T(8,128)(2,1)S(1)} %pad_maximum_fusion), channel_id=1, source_target_pairs={{0,4},{1,5},{2,6},{3,7},{4,0},{5,1},{6,2},{7,3},{8,12},{9,13},{10,... | collective-permute-start | bytes 491528 | tf_op jit(solution)/shard_map/ppermute | solution.py:645
  77.9 2.2 %collective-permute-start.13 = (bf16[16,16,1280]{2,1,0:T(8,128)(2,1)S(1)}, bf16[16,16,1280]{2,1,0:T(8,128)(2,1)S(1)}, u32[]{:S(2)}, u32[]{:S(2)}) collective-permute-start(bf16[16,16,1280]{2,1,0:T(8,128)(2,1)S(1)} %constant_dynamic-update-slice_fusion.held_ref), channel_id=1, source_target_pairs={{0,1},{1,0},{2,3},{3,2},{4,5},{5,4},{6,7},{7,6},{8,9},{9,8},{10,11... | collective-permute-start | bytes 1966088 | tf_op jit(solution)/shard_map/ppermute | solution.py:645
  78.0 4.2 %collective-permute-start.8 = (bf16[96,128]{1,0:T(8,128)(2,1)S(1)}, bf16[96,128]{1,0:T(8,128)(2,1)S(1)}, u32[]{:S(2)}, u32[]{:S(2)}) collective-permute-start(bf16[96,128]{1,0:T(8,128)(2,1)S(1)} %get-tuple-element.48), channel_id=1, source_target_pairs={{0,1},{1,0},{2,3},{3,2},{4,5},{5,4},{6,7},{7,6},{8,9},{9,8},{10,11... | collective-permute-start | bytes 73736 | tf_op jit(solution)/shard_map/ppermute | solution.py:781
  78.5 3.7 %collective-permute-start.9 = (bf16[96,128]{1,0:T(8,128)(2,1)S(1)}, bf16[96,128]{1,0:T(8,128)(2,1)S(1)}, u32[]{:S(2)}, u32[]{:S(2)}) collective-permute-start(bf16[96,128]{1,0:T(8,128)(2,1)S(1)} %get-tuple-element.49), channel_id=1, source_target_pairs={{1,2},{2,1},{3,4},{4,3},{5,6},{6,5},{7,8},{8,7},{9,10},{10,9},{11,... | collective-permute-start | bytes 73736 | tf_op jit(solution)/shard_map/ppermute | solution.py:781
  94.4 8.7 %collective-permute-start.14 = (bf16[224,128]{1,0:T(8,128)(2,1)S(1)}, bf16[224,128]{1,0:T(8,128)(2,1)S(1)}, u32[]{:S(2)}, u32[]{:S(2)}) collective-permute-start(bf16[224,128]{1,0:T(8,128)(2,1)S(1)} %get-tuple-element.55), channel_id=1, source_target_pairs={{0,1},{1,0},{2,3},{3,2},{4,5},{5,4},{6,7},{7,6},{8,9},{9,8},{10,11... | collective-permute-start | bytes 172040 | tf_op jit(solution)/shard_map/ppermute | solution.py:781
  95.9 7.1 %collective-permute-start.15 = (bf16[224,128]{1,0:T(8,128)(2,1)S(1)}, bf16[224,128]{1,0:T(8,128)(2,1)S(1)}, u32[]{:S(2)}, u32[]{:S(2)}) collective-permute-start(bf16[224,128]{1,0:T(8,128)(2,1)S(1)} %get-tuple-element.56), channel_id=1, source_target_pairs={{1,2},{2,1},{3,4},{4,3},{5,6},{6,5},{7,8},{8,7},{9,10},{10,9},{11,... | collective-permute-start | bytes 172040 | tf_op jit(solution)/shard_map/ppermute | solution.py:781
  96.6 6.4 %collective-permute-start.16 = (bf16[64,128]{1,0:T(8,128)(2,1)S(1)}, bf16[64,128]{1,0:T(8,128)(2,1)S(1)}, u32[]{:S(2)}, u32[]{:S(2)}) collective-permute-start(bf16[64,128]{1,0:T(8,128)(2,1)S(1)} %get-tuple-element.57), channel_id=1, source_target_pairs={{0,2},{1,3},{2,4},{3,5},{4,6},{5,7},{6,8},{7,9},{8,10},{9,11},{10,... | collective-permute-start | bytes 49160 | tf_op jit(solution)/shard_map/ppermute | solution.py:38
  134.3 6.2 %collective-permute-start.19 = (bf16[1,16,1280]{2,1,0:T(8,128)(2,1)S(1)}, bf16[1,16,1280]{2,1,0:T(8,128)(2,1)S(1)}, u32[]{:S(2)}, u32[]{:S(2)}) collective-permute-start(bf16[1,16,1280]{2,1,0:T(8,128)(2,1)S(1)} %bitcast.9), channel_id=1, source_target_pairs={{0,24},{1,25},{2,26},{3,27},{4,28},{5,29},{6,30},{7,31},{8,16},{9,... | collective-permute-start | bytes 122888 | tf_op jit(solution)/shard_map/ppermute | solution.py:645
  135.7 4.8 %collective-permute-start.18 = (bf16[1,16,1280]{2,1,0:T(8,128)(2,1)S(1)}, bf16[1,16,1280]{2,1,0:T(8,128)(2,1)S(1)}, u32[]{:S(2)}, u32[]{:S(2)}) collective-permute-start(bf16[1,16,1280]{2,1,0:T(8,128)(2,1)S(1)} %bitcast.10), channel_id=1, source_target_pairs={{0,8},{1,9},{2,10},{3,11},{4,12},{5,13},{6,14},{7,15},{8,0},{9,1},... | collective-permute-start | bytes 122888 | tf_op jit(solution)/shard_map/ppermute | solution.py:645
  135.7 5.3 %collective-permute-start.17 = (bf16[1,16,1280]{2,1,0:T(8,128)(2,1)S(1)}, bf16[1,16,1280]{2,1,0:T(8,128)(2,1)S(1)}, u32[]{:S(2)}, u32[]{:S(2)}) collective-permute-start(bf16[1,16,1280]{2,1,0:T(8,128)(2,1)S(1)} %bitcast.11), channel_id=1, source_target_pairs={{0,16},{1,17},{2,18},{3,19},{4,20},{5,21},{6,22},{7,23},{8,24},{9,... | collective-permute-start | bytes 122888 | tf_op jit(solution)/shard_map/ppermute | solution.py:645
  141.1 9.0 %collective-permute-start.22 = (bf16[4,16,1280]{2,1,0:T(8,128)(2,1)S(1)}, bf16[4,16,1280]{2,1,0:T(8,128)(2,1)S(1)}, u32[]{:S(2)}, u32[]{:S(2)}) collective-permute-start(bf16[4,16,1280]{2,1,0:T(8,128)(2,1)S(1)} %pad_maximum_fusion.1.piece_ref), channel_id=1, source_target_pairs={{0,6},{1,7},{2,4},{3,5},{4,2},{5,3},{6,0},{7,1},{8,14},{9,15},{10,... | collective-permute-start | bytes 491528 | tf_op jit(solution)/shard_map/ppermute | solution.py:645
  142.3 7.8 %collective-permute-start.21 = (bf16[4,16,1280]{2,1,0:T(8,128)(2,1)S(1)}, bf16[4,16,1280]{2,1,0:T(8,128)(2,1)S(1)}, u32[]{:S(2)}, u32[]{:S(2)}) collective-permute-start(bf16[4,16,1280]{2,1,0:T(8,128)(2,1)S(1)} %pad_maximum_fusion.1.piece_ref), channel_id=1, source_target_pairs={{0,2},{1,3},{2,0},{3,1},{4,6},{5,7},{6,4},{7,5},{8,10},{9,11},{10,... | collective-permute-start | bytes 491528 | tf_op jit(solution)/shard_map/ppermute | solution.py:645
  143.5 6.6 %collective-permute-start.20 = (bf16[4,16,1280]{2,1,0:T(8,128)(2,1)S(1)}, bf16[4,16,1280]{2,1,0:T(8,128)(2,1)S(1)}, u32[]{:S(2)}, u32[]{:S(2)}) collective-permute-start(bf16[4,16,1280]{2,1,0:T(8,128)(2,1)S(1)} %pad_maximum_fusion.1.piece_ref), channel_id=1, source_target_pairs={{0,4},{1,5},{2,6},{3,7},{4,0},{5,1},{6,2},{7,3},{8,12},{9,13},{10,... | collective-permute-start | bytes 491528 | tf_op jit(solution)/shard_map/ppermute | solution.py:645
  150.1 2.2 %collective-permute-start.23 = (bf16[16,16,1280]{2,1,0:T(8,128)(2,1)S(1)}, bf16[16,16,1280]{2,1,0:T(8,128)(2,1)S(1)}, u32[]{:S(2)}, u32[]{:S(2)}) collective-permute-start(bf16[16,16,1280]{2,1,0:T(8,128)(2,1)S(1)} %constant_dynamic-update-slice_fusion.7.held_ref), channel_id=1, source_target_pairs={{0,1},{1,0},{2,3},{3,2},{4,5},{5,4},{6,7},{7,6},{8,9},{9,8},{10,11... | collective-permute-start | bytes 1966088 | tf_op jit(solution)/shard_map/ppermute | solution.py:645
  (2 other events, 23.1 us)

commit v10 on v9

--- a/solution.py
+++ b/solution.py
@@ -23,7 +23,7 @@
 STRIDE = L + 1
 GROUPS = 4
 SUBLANES = 8
-COPIED = (32, 40, 32, 24)
+COPIED = (32, 72, 24)
 FINE = 4
 LANES = 128
 VMEM_BYTES = 24 * 1024 * 1024
@@ -95,7 +95,13 @@
     return turned_ref[pl.ds(tap, ROWS, stride=STRIDE), :].astype(jnp.bfloat16)
 
 
-def layout_kernel(dict_ref, taps_ref, *turned):
+def layout_kernel(dict_ref, taps_ref, copy_hbm, sem, *turned):
+    width = dict_ref.shape[1]
+    column = pl.ds(pl.multiple_of(pl.program_id(0) * width, LANES), width)
+    rows = pl.ds(0, COPIED[0])
+    copy = pltpu.make_async_copy(dict_ref.at[rows], copy_hbm.at[rows, column], sem)
+    copy.start()
+
     def part(group):
         return dict_ref[:, group * ROWS * L : (group + 1) * ROWS * L]
 
@@ -106,6 +112,7 @@
         own = pl.ds(pl.multiple_of((pl.program_id(0) * GROUPS + group) * ROWS, ROWS), ROWS)
         for tap in range(L):
             taps_ref[tap // ROWS, tap % ROWS, own, :] = tap_of(turned[group], tap)
+    copy.wait()
 
 
 def layout(dictionary, channels):
@@ -114,9 +121,13 @@
         layout_kernel,
         grid=(channels // block,),
         in_specs=[pl.BlockSpec((K, block * L), lambda i: (0, i))],
-        out_specs=vmem(),
-        out_shape=pltpu.VMEM((COARSE, ROWS, channels, K), jnp.bfloat16),
-        scratch_shapes=[pltpu.VMEM((ROWS * STRIDE, K), jnp.float32)] * GROUPS,
+        out_specs=[vmem(), hbm()],
+        out_shape=[
+            pltpu.VMEM((COARSE, ROWS, channels, K), jnp.bfloat16),
+            pltpu.HBM(dictionary.shape, jnp.float32),
+        ],
+        scratch_shapes=[pltpu.SemaphoreType.DMA]
+        + [pltpu.VMEM((ROWS * STRIDE, K), jnp.float32)] * GROUPS,
         compiler_params=pltpu.CompilerParams(vmem_limit_bytes=VMEM_BYTES),
         name="layout",
     )(far(dictionary))
@@ -322,18 +333,17 @@
     return stepped - jnp.clip(stepped, -limit, limit)
 
 
-def iterate_kernel(total_time, patching, copied, plan_ref, limit_ref, *refs):
+def iterate_kernel(total_time, patching, first_copied, plan_ref, limit_ref, *refs):
     take = taker(refs)
     state_ref, first_ref, second_ref, signal_ref, next_first, next_second = take(6)
     atoms = take(1 if patching else 0)
     (taps,) = take(1)
-    source = take(1 if copied else 0)
-    take(1 if copied and copied[0] else 0)
+    source = take(2 if patching else 0)
     state_out, first_out, second_out, far_out = take(4)
     taps = (take(1) if patching else [taps])[0]
-    target = take(1 if copied else 0)
+    target = take(1 if patching else 0)
     zb, rb, zz, rr, fine, acc, beyond = take(7)
-    ferry = Ferry(source[0], target[0], copied[0], *take(2)) if copied else None
+    ferry = Ferry(source[0], target[0], first_copied, *take(2)) if patching else None
     segment, channels = signal_ref.shape
     zb[L : L + segment, :] = state_ref[...].astype(jnp.bfloat16)
 
@@ -349,9 +359,8 @@
     if patching:
         columns, *turned = take(1 + GROUPS)
         patch_taps(first_row_of(plan_ref, patching - 1), atoms[0], taps, columns, turned)
+        ferry.turn_round()
     convolve(zb, L, segment + L, taps, zz, fine, acc)
-    if ferry:
-        ferry.turn_round()
     start = lax.axis_index("tm") * segment
     residual_rows(rb, (signal_ref, beyond), start, acc, total_time)
     correlate(rb, segment, taps, rr, fine, acc)
@@ -374,19 +383,16 @@
     patching = atoms is not None
     reach = segment + L
     near, beyond_near = reaches(segment)
-    carried = [far(value) for value in ferry[:2] if value is not None]
-    aliases = {9: 4} if patching else {}
-    if len(carried) == 2:
-        aliases[10 + patching] = 4 + patching
+    carried = [far(value) for value in ferry[:2]] if patching else []
     return pl.pallas_call(
-        functools.partial(iterate_kernel, peers * segment, step if patching else 0, ferry[2:]),
+        functools.partial(iterate_kernel, peers * segment, step if patching else 0, ferry[2]),
         in_specs=[scalars()] + [vmem()] * (8 + patching) + [hbm()] * len(carried),
-        out_specs=[vmem()] * (4 + patching) + [hbm()],
+        out_specs=[vmem()] * (4 + patching) + [hbm()] * patching,
         out_shape=[pltpu.VMEM((segment, K), jnp.float32)]
         + [jax.ShapeDtypeStruct((near + L, K), jnp.bfloat16)] * 2
         + [jax.ShapeDtypeStruct((max(beyond_near, ROWS), K), jnp.bfloat16)]
         + [pltpu.VMEM(taps.shape, jnp.bfloat16)] * patching
-        + [pltpu.HBM(ferry[0].shape, jnp.float32)],
+        + [pltpu.HBM(ferry[0].shape, jnp.float32)] * patching,
         scratch_shapes=[
             pltpu.VMEM((L + reach, K), jnp.bfloat16),
             pltpu.VMEM((reach, channels), jnp.bfloat16),
@@ -396,13 +402,13 @@
             pltpu.VMEM((channels // LANES, reach, LANES), jnp.float32),
             pltpu.VMEM((L, channels), jnp.bfloat16),
         ]
-        + ferry_scratch(ferry[3], ferry[0].shape[1])
         + (
-            [pltpu.VMEM((K, GROUPS * ROWS * L), jnp.bfloat16)]
+            ferry_scratch(ferry[3], ferry[0].shape[1])
+            + [pltpu.VMEM((K, GROUPS * ROWS * L), jnp.bfloat16)]
             + [pltpu.VMEM((ROWS * STRIDE, K), jnp.float32)] * GROUPS
         )
         * patching,
-        input_output_aliases=aliases,
+        input_output_aliases={9: 4, 11: 5} if patching else {},
         compiler_params=pltpu.CompilerParams(vmem_limit_bytes=VMEM_BYTES),
         name="iterate",
     )(
@@ -418,15 +424,13 @@
     )
 
 
-def conclude_kernel(peers, step, copied, plan_ref, limit_ref, *refs):
+def conclude_kernel(peers, step, plan_ref, limit_ref, *refs):
     last = step + 1 == OUTER
     take = taker(refs)
     state_ref, first_ref, second_ref, far_ref, signal_ref, next_first, next_second, taps = take(8)
-    source, _, payload_out = take(3)
+    (payload_out,) = take(1)
     outs = take(2 if last else 3)
-    (target,) = take(1)
     zb, rb, zz, rr, fine, acc, before, beyond, earlier, tall = take(10)
-    ferry = Ferry(source, target, copied[0], *take(2))
     segment, channels = signal_ref.shape
     near, beyond_near = reaches(segment)
     zb[2 * L : 2 * L + segment, :] = state_ref[...].astype(jnp.bfloat16)
@@ -445,7 +449,6 @@
     by_side(put, first_ref, second_ref)
     by_side(put_signal, next_first, next_second)
     convolve(zb, L, 2 * L + segment, taps, zz, fine, acc)
-    ferry.turn_round()
     start = lax.axis_index("tm") * segment - L
     residual_rows(rb, (before, signal_ref, beyond), start, acc, peers * segment)
     correlate(rb, L + segment, taps, rr, fine, acc)
@@ -481,15 +484,13 @@
         part = tall[peer * share : peer * share + share_rows, :]
         payload_out[peer, :share_rows, :] = part.astype(jnp.bfloat16)
         payload_out[peer, share_rows:, :] = block
-    ferry.close()
-
-
-def conclude(plan, step, limit, state, swapped, far_edge, signal, following, taps, ferry, peers):
+
+
+def conclude(plan, step, limit, state, swapped, far_edge, signal, following, taps, peers):
     segment, channels = signal.shape
     share = channels // peers
     share_rows = -(-share // ROWS) * ROWS
     last = step + 1 == OUTER
-    carried = [far(value) for value in ferry[:2]]
     rows = 2 * L + segment
     outs = [
         pltpu.VMEM((channels, segment), jnp.float32),
@@ -499,12 +500,11 @@
         outs = [pltpu.VMEM((segment, K), jnp.float32)]
         outs += [jax.ShapeDtypeStruct((L, K), jnp.bfloat16)] * 2
     return pl.pallas_call(
-        functools.partial(conclude_kernel, peers, step, ferry[2:]),
-        in_specs=[scalars()] + [vmem()] * 9 + [hbm()] * 2,
-        out_specs=[vmem()] * (1 + len(outs)) + [hbm()],
+        functools.partial(conclude_kernel, peers, step),
+        in_specs=[scalars()] + [vmem()] * 9,
+        out_specs=[vmem()] * (1 + len(outs)),
         out_shape=[jax.ShapeDtypeStruct((peers, share_rows + BLOCK_ATOMS, segment), jnp.bfloat16)]
-        + outs
-        + [pltpu.HBM(ferry[0].shape, jnp.float32)],
+        + outs,
         scratch_shapes=[
             pltpu.VMEM((rows + L, K), jnp.bfloat16),
             pltpu.VMEM((rows, channels), jnp.bfloat16),
@@ -517,9 +517,7 @@
             pltpu.VMEM((L, K), jnp.float32),
             pltpu.VMEM((channels + ROWS, segment), jnp.float32),
         ]
-        + ferry_scratch(ferry[3], ferry[0].shape[1])
         + ([] if last else [pltpu.VMEM((K, segment), jnp.float32)]),
-        input_output_aliases={11: 1 + len(outs)},
         compiler_params=pltpu.CompilerParams(vmem_limit_bytes=VMEM_BYTES),
         name="conclude",
     )(
@@ -531,7 +529,6 @@
         resident(signal),
         *following,
         resident(taps),
-        *carried,
     )
 
 
@@ -544,21 +541,17 @@
     columns_of = pl.ds(pl.multiple_of(lax.axis_index("tm") * entries, LANES), entries)
     fetch = pltpu.make_async_copy(dict_hbm.at[rows_of, columns_of], old, sem)
     fetch.start()
-    rf[:, span:] = jnp.zeros((share_rows, LANES), jnp.float32)
-    zf[:, :LANES] = jnp.zeros((BLOCK_ATOMS, LANES), jnp.float32)
+    rf[:, span:] = jnp.zeros((share_rows, LANES), jnp.bfloat16)
+    zf[:, :LANES] = jnp.zeros((BLOCK_ATOMS, LANES), jnp.bfloat16)
     for peer in range(peers):
         column = peer * segment
-        rf[:, column : column + segment] = blocks_ref[peer, :share_rows, :].astype(jnp.float32)
-        zf[:, LANES + column : LANES + column + segment] = blocks_ref[peer, share_rows:, :].astype(
-            jnp.float32
-        )
+        rf[:, column : column + segment] = blocks_ref[peer, :share_rows, :]
+        zf[:, LANES + column : LANES + column + segment] = blocks_ref[peer, share_rows:, :]
     for lag in range(ROWS):
-        rr[lag * share_rows : (lag + 1) * share_rows, :] = rf[:, lag : lag + span].astype(jnp.bfloat16)
+        rr[lag * share_rows : (lag + 1) * share_rows, :] = rf[:, lag : lag + span]
     for coarse in range(COARSE):
         begin = LANES - ROWS * coarse
-        zz[coarse * BLOCK_ATOMS : (coarse + 1) * BLOCK_ATOMS, :] = zf[:, begin : begin + span].astype(
-            jnp.bfloat16
-        )
+        zz[coarse * BLOCK_ATOMS : (coarse + 1) * BLOCK_ATOMS, :] = zf[:, begin : begin + span]
     lagged = lax.dot_general(zz[...], rr[...], NT, preferred_element_type=jnp.float32)
     wide = ROWS * share_rows
     parts = []
@@ -610,8 +603,8 @@
         in_specs=[scalars(), vmem(), hbm()],
         out_shape=jax.ShapeDtypeStruct((BLOCK_ATOMS, share * L + LANES), jnp.bfloat16),
         scratch_shapes=[
-            pltpu.VMEM((share_rows, span + LANES), jnp.float32),
-            pltpu.VMEM((BLOCK_ATOMS, LANES + span), jnp.float32),
+            pltpu.VMEM((share_rows, span + LANES), jnp.bfloat16),
+            pltpu.VMEM((BLOCK_ATOMS, LANES + span), jnp.bfloat16),
             pltpu.VMEM((ROWS * share_rows, span), jnp.bfloat16),
             pltpu.VMEM((COARSE * BLOCK_ATOMS, span), jnp.bfloat16),
             pltpu.VMEM((BLOCK_ATOMS, share * L), jnp.float32),
@@ -653,12 +646,23 @@
     return held, exchanged(ready, 1), extra
 
 
-def recall_kernel(step, plan_ref, dict_hbm, piece_ref, old_ref, mean_ref, sem):
-    del piece_ref
-    first_row = first_row_of(plan_ref, step)
-    fetch = pltpu.make_async_copy(dict_hbm.at[pl.ds(first_row, BLOCK_ATOMS)], old_ref, sem)
+def recall_kernel(step, earlier, plan_ref, dict_hbm, when_ref, *refs):
+    del when_ref
+    take = taker(refs)
+    earlier_refs = take(earlier)
+    take(1 if earlier else 0)
+    old_ref, mean_ref = take(2)
+    target = take(1 if earlier else 0)
+    (sem,) = take(1)
+    fetch = pltpu.make_async_copy(
+        dict_hbm.at[pl.ds(first_row_of(plan_ref, step), BLOCK_ATOMS)], old_ref, sem
+    )
     fetch.start()
+    if earlier:
+        ferry = Ferry(dict_hbm, target[0], sum(COPIED[:-1]), *take(2))
     fetch.wait()
+    if earlier:
+        ferry.turn_round()
     width = 9 * LANES if old_ref.shape[1] % (9 * LANES) == 0 else LANES
 
     def add(step, square):
@@ -670,44 +674,61 @@
     )
     mean_sq = jnp.sum(square, axis=1, keepdims=True) / (C * L) + tiny_eps
     mean_ref[...] = jnp.broadcast_to(mean_sq, mean_ref.shape)
-
-
-def recall(plan, step, dictionary, piece):
+    if earlier:
+        ferry.close()
+        stores = [
+            pltpu.make_async_copy(
+                earlier_refs[index],
+                target[0].at[pl.ds(first_row_of(plan_ref, index), BLOCK_ATOMS)],
+                sem,
+            )
+            for index in range(earlier)
+        ]
+        for store in stores:
+            store.start()
+            store.wait()
+
+
+def recall(plan, step, dictionary, when, renewed, copied):
+    entries = dictionary.shape[1]
+    earlier = len(renewed)
     return pl.pallas_call(
-        functools.partial(recall_kernel, step),
-        in_specs=[scalars(), hbm(), pl.BlockSpec(memory_space=pl.ANY)],
-        out_specs=[vmem(), vmem()],
+        functools.partial(recall_kernel, step, earlier),
+        in_specs=[scalars(), hbm(), pl.BlockSpec(memory_space=pl.ANY)]
+        + [vmem()] * earlier
+        + [hbm()] * (earlier > 0),
+        out_specs=[vmem(), vmem()] + [hbm()] * (earlier > 0),
         out_shape=[
-            pltpu.VMEM((BLOCK_ATOMS, dictionary.shape[1]), jnp.float32),
+            pltpu.VMEM((BLOCK_ATOMS, entries), jnp.float32),
             jax.ShapeDtypeStruct((BLOCK_ATOMS, LANES), jnp.float32),
-        ],
-        scratch_shapes=[pltpu.SemaphoreType.DMA],
+        ]
+        + [pltpu.HBM(dictionary.shape, jnp.float32)] * (earlier > 0),
+        scratch_shapes=[pltpu.SemaphoreType.DMA]
+        + (ferry_scratch(COPIED[-1], entries) if earlier else []),
+        input_output_aliases={3 + earlier: 2} if earlier else {},
         compiler_params=pltpu.CompilerParams(vmem_limit_bytes=VMEM_BYTES),
         name="recall",
-    )(plan, far(dictionary), piece)
-
-
-def renew_kernel(plan_step, earlier, plan_ref, held_ref, came_ref, old, mean_ref, *refs):
+    )(
+        plan,
+        far(dictionary),
+        when,
+        *[resident(value) for value in renewed],
+        *([far(copied)] if earlier else []),
+    )
+
+
+def renew_kernel(plan_step, plan_ref, held_ref, came_ref, old, mean_ref, *refs):
     me = lax.axis_index("tm")
     half, _, wide = held_ref.shape
     width = wide - LANES
     entries = C * L
-    before_refs, refs = refs[:earlier], refs[earlier:]
     last = plan_step + 1 == OUTER
     if last:
         _, out_hbm, atoms_ref, grad, sems = refs
     else:
         atoms_ref, grad = refs
 
-    def rows_of(step):
-        return pl.ds(first_row_of(plan_ref, step), BLOCK_ATOMS)
-
     stores = []
-    for step in range(earlier):
-        stores.append(
-            pltpu.make_async_copy(before_refs[step], out_hbm.at[rows_of(step)], sems.at[2 * half + step])
-        )
-        stores[-1].start()
     shares = []
     for slot, flips in enumerate(gather_slots(2 * half)):
         for source, extra in ((held_ref, 0), (came_ref, 1)):
@@ -730,6 +751,7 @@
     spread = jnp.sum(square, axis=1, keepdims=True) / entries + tiny_eps
     step = move_rate / jnp.sqrt(spread)
     norm = 1.0 / jnp.sqrt(mean_sq + 0.25)
+    rows = pl.ds(first_row_of(plan_ref, plan_step), BLOCK_ATOMS)
     for index, (_, column) in enumerate(shares):
         before = old[:, column]
         across = grad[:, column] - along * before
@@ -737,7 +759,7 @@
         if last:
             stores.append(
                 pltpu.make_async_copy(
-                    atoms_ref.at[:, column], out_hbm.at[rows_of(plan_step), column], sems.at[index]
+                    atoms_ref.at[:, column], out_hbm.at[rows, column], sems.at[index]
                 )
             )
             stores[-1].start()
@@ -745,30 +767,22 @@
         store.wait()
 
 
-def renew(plan, step, held, came, old, mean_sq, renewed, dictionary):
-    last = step + 1 == OUTER
+def renew(plan, step, held, came, old, mean_sq, dictionary):
+    last = dictionary is not None
     atoms = (BLOCK_ATOMS, old.shape[1])
-    earlier = len(renewed) if last else 0
     scratch = [pltpu.VMEM(atoms, jnp.float32)]
     if last:
-        scratch = scratch * 2 + [pltpu.SemaphoreType.DMA((2 * held.shape[0] + earlier,))]
+        scratch = scratch * 2 + [pltpu.SemaphoreType.DMA((2 * held.shape[0],))]
     return pl.pallas_call(
-        functools.partial(renew_kernel, step, earlier),
-        in_specs=[scalars()] + [vmem()] * (4 + earlier) + [hbm()] * last,
+        functools.partial(renew_kernel, step),
+        in_specs=[scalars()] + [vmem()] * 4 + [hbm()] * last,
         out_specs=hbm() if last else vmem(),
         out_shape=pltpu.HBM(dictionary.shape, jnp.float32) if last else pltpu.VMEM(atoms, jnp.float32),
         scratch_shapes=scratch,
-        input_output_aliases={5 + earlier: 0} if last else {},
+        input_output_aliases={5: 0} if last else {},
         compiler_params=pltpu.CompilerParams(vmem_limit_bytes=VMEM_BYTES),
         name="renew",
-    )(
-        plan,
-        held,
-        came,
-        resident(old),
-        mean_sq,
-        *([resident(value) for value in renewed] + [far(dictionary)] if last else []),
-    )
+    )(plan, held, came, resident(old), mean_sq, *([far(dictionary)] if last else []))
 
 
 def whole_channels(signal, codes_init, dictionary_init, threshold, plan):
@@ -778,54 +792,45 @@
     def swaps(edges):
         ends = [range(first, peers - 1, 2) for first in (0, 1)]
         pairs = [[p for i in end for p in ((i, i + 1), (i + 1, i))] for end in ends]
-        return [lax.ppermute(edge, "tm", pair) for edge, pair in zip(edges, pairs)]
+        far_first = [lax.ppermute(edge, "tm", pair) for edge, pair in zip(edges[::-1], pairs[::-1])]
+        return far_first[::-1]
 
     state, signal, *edges = begin(codes_init, signal)
     following = swaps(edges)
     swapped = following
-    taps = layout(dictionary_init, channels)
-    dictionary = None
+    taps, dictionary = layout(dictionary_init, channels)
     renewed = []
     for step in range(OUTER):
         last = step + 1 == OUTER
-        rows = COPIED[2 * step : 2 * step + 2]
-        first = sum(COPIED[: 2 * step])
-        ferry = (dictionary_init, dictionary, first, rows[0])
+        ferry = (dictionary_init, dictionary, COPIED[0], COPIED[1])
         atoms = renewed[-1] if renewed else None
         state, *results = iterate(
             plan, step, limit, state, swapped, signal, following, taps, atoms, ferry, peers
         )
+        edges, far_edge = results[:2], results[2]
         if renewed:
-            taps = results[3]
-        edges, far_edge, dictionary = results[:2], results[2], results[-1]
-        ferry = (dictionary_init, dictionary, first + rows[0], rows[1])
-        payload, *results, dictionary = conclude(
-            plan,
-            step,
-            limit,
-            state,
-            swaps(edges),
-            shifted(far_edge, "tm", 2),
-            signal,
-            following,
-            taps,
-            ferry,
-            peers,
+            taps, dictionary = results[3:]
+        beyond = shifted(far_edge, "tm", 2)
+        payload, *results = conclude(
+            plan, step, limit, state, swaps(edges), beyond, signal, following, taps, peers
         )
         blocks = lax.all_to_all(payload, "tm", 0, 0, tiled=True)
         piece = share_gradient(plan, step, blocks, dictionary_init, channels // peers)
-        recalled = [] if last else list(recall(plan, step, dictionary_init, piece))
+        recalled = []
+        if not last:
+            recalled.extend(recall(plan, step, dictionary_init, piece, [], None))
 
         def beside(held):
             if last:
-                recalled.extend(recall(plan, step, dictionary_init, held))
+                recalled.extend(recall(plan, step, dictionary_init, held, renewed, dictionary))
                 return recalled[0], None
             state, *edges = results
             edges, _ = lax.optimization_barrier((edges, held))
             return recalled[0], swaps(edges)
 
         held, came, extra = gather_pieces(piece, beside)
-        result = renew(plan, step, held, came, *recalled, renewed if last else None, dictionary)
+        old, mean_sq, *copied = recalled
+        result = renew(plan, step, held, came, old, mean_sq, copied[0] if last else None)
         if last:
             dictionary = result
         else:
@@ -909,6 +914,7 @@
         lax.axis_size("chan") == 1
         and segment % LANES == 0
         and INNER == 2
+        and OUTER == 2
         and channels % (GROUPS * ROWS) == 0
         and channels % LANES == 0
         and channels % peers == 0

time: 157 us -> 159 us (1.013)
  Pallas kernels: 66.5 us -> 71.4 us
  waiting for transfers between devices: 15.7 us -> 13 us
    pallas_call x6, Pallas kernels: 32.6 us -> 35.8 us  [the longest x2 21.2 us: conclude(): pl.pallas_call(functools.partial(conclude_kernel, peers, step), in_specs=...]
    ppermute x14, waiting for transfers between devices: 12.8 us -> 10.1 us  [exchanged(): return lax.ppermute(shard, 'tm', [(i, i ^ mask) for i in range(peers)])]
    pallas_call x1, Pallas kernels: 9.19 us -> 11.8 us  [layout(): pl.pallas_call(layout_kernel, grid=(channels // block,), in_specs=[pl.Blo...]
  transfers between devices with their start and end apart: 24 -> 24, of which waited for: 8 -> 7; matrix products, arithmetic and copies ran while one was open for 1% -> 1% of each run, Pallas kernels for 11% -> 15%
where the time goes in v10:
time: 159 us
  Pallas kernels  71.4 us (45%)
  blocking collectives  36.5 us (23%)
  starting transfers between devices  35.1 us (22%)
  waiting for transfers between devices  13 us (8%)
    all_to_all x2, blocking collectives, whole_channels(): blocks = lax.all_to_all(payload, 'tm', 0, 0, tiled=True)  36.5 us
    pallas_call x2, Pallas kernels, conclude(): pl.pallas_call(functools.partial(conclude_kernel, peers, step), in_specs=...  21.2 us
    pallas_call x2, Pallas kernels, iterate(): pl.pallas_call(functools.partial(iterate_kernel, peers * segment, step if...  17.1 us
    ppermute x14, starting transfers between devices, exchanged(): return lax.ppermute(shard, 'tm', [(i, i ^ mask) for i in range(peers)])  16.2 us
    pallas_call x1, Pallas kernels, layout(): pl.pallas_call(layout_kernel, grid=(channels // block,), in_specs=[pl.Blo...  11.8 us
    ppermute x14, waiting for transfers between devices, exchanged(): return lax.ppermute(shard, 'tm', [(i, i ^ mask) for i in range(peers)])  10.1 us
    ppermute x2, starting transfers between devices, shifted(): return lax.ppermute(shard, axis, pairs)  9.77 us
    pallas_call x2, Pallas kernels, recall(): pl.pallas_call(functools.partial(recall_kernel, step, earlier), in_specs=...  9.18 us
  transfers between devices with their start and end apart: 24, of which 7 were waited for; matrix products, arithmetic and copies ran while one was open for 1% of the time, Pallas kernels for 15%

profile of v10, /device:TPU:0, one launch (start us, length us, event | category | flops | bytes accessed | tf_op | source)
XLA Modules:
  0.0 158.7 jit_solution(7666299038358984250)
XLA Ops:
  2.9 11.8 %layout.1 = (bf16[6,16,384,128]{3,2,1,0:T(8,128)(2,1)S(1)}, f32[128,36864]{1,0:T(8,128)}) custom-call(f32[128,36864]{1,0:T(8,128)} %dict_hbm.7), custom_call_target="tpu_custom_call" | custom-call | tf_op jit(solution)/shard_map/layout/pallas_call | solution.py:120
  14.8 5.3 %iterate.2 = (f32[128,128]{1,0:T(8,128)S(1)}, bf16[224,128]{1,0:T(8,128)(2,1)S(1)}, bf16[224,128]{1,0:T(8,128)(2,1)S(1)}, bf16[64,128]{1,0:T(8,128)(2,1)S(1)}) custom-call(s32[8]{0:T(128)S(1)} %copy-done, f32[1,128]{1,0:T(1,128)S(1)} %bitcast.13, f32[128,128]{1,0:T(8,128)S(1)} %get-tuple-element.35.refs_0_, ...), custom_call_target="tpu_custom_call" | custom-call | tf_op jit(solution)/shard_map/iterate/pallas_call | solution.py:387
  20.0 3.9 %collective-permute-start.2 = (bf16[224,128]{1,0:T(8,128)(2,1)S(1)}, bf16[224,128]{1,0:T(8,128)(2,1)S(1)}, u32[]{:S(2)}, u32[]{:S(2)}) collective-permute-start(bf16[224,128]{1,0:T(8,128)(2,1)S(1)} %get-tuple-element.41), channel_id=1, source_target_pairs={{0,1},{1,0},{2,3},{3,2},{4,5},{5,4},{6,7},{7,6},{8,9},{9,8},{10,11... | collective-permute-start | bytes 172040 | tf_op jit(solution)/shard_map/ppermute | solution.py:795
  24.6 4.8 %collective-permute-start.4 = (bf16[64,128]{1,0:T(8,128)(2,1)S(1)}, bf16[64,128]{1,0:T(8,128)(2,1)S(1)}, u32[]{:S(2)}, u32[]{:S(2)}) collective-permute-start(bf16[64,128]{1,0:T(8,128)(2,1)S(1)} %get-tuple-element.43), channel_id=1, source_target_pairs={{0,2},{1,3},{2,4},{3,5},{4,6},{5,7},{6,8},{7,9},{8,10},{9,11},{10,... | collective-permute-start | bytes 49160 | tf_op jit(solution)/shard_map/ppermute | solution.py:38
  29.5 1.4 collective-permute-done.4.refs_3_
  30.9 10.5 %conclude.2 = (bf16[32,32,128]{2,1,0:T(8,128)(2,1)S(1)}, f32[128,128]{1,0:T(8,128)S(1)}, bf16[96,128]{1,0:T(8,128)(2,1)S(1)}, bf16[96,128]{1,0:T(8,128)(2,1)S(1)}) custom-call(s32[8]{0:T(128)S(1)} %copy-done, f32[1,128]{1,0:T(1,128)S(1)} %bitcast.14, f32[128,128]{1,0:T(8,128)S(1)} %get-tuple-element.40.refs_0_, ...), custom_call_target="tpu_custom_call" | custom-call | tf_op jit(solution)/shard_map/conclude/pallas_call | solution.py:502
  41.4 18.8 %all_to_all.10.blocks_ref = bf16[32,32,128]{2,1,0:T(8,128)(2,1)S(1)} all-to-all(bf16[32,32,128]{2,1,0:T(8,128)(2,1)S(1)} %get-tuple-element.47), channel_id=1, replica_groups=mesh['tm'=32,'chan'=1] {'tm'}, dimensions={0} | all-to-all | bytes 524288 | tf_op jit(solution)/shard_map/all_to_all | solution.py:817
  60.2 2.8 %gradient.2.when_ref = bf16[16,1280]{1,0:T(8,128)(2,1)S(1)} custom-call(s32[8]{0:T(128)S(1)} %copy-done, bf16[32,32,128]{2,1,0:T(8,128)(2,1)S(1)} %all_to_all.10.blocks_ref, f32[128,36864]{1,0:T(8,128)} %dict_hbm.7), custom_call_target="tpu_custom_call" | custom-call | tf_op jit(solution)/shard_map/gradient/pallas_call | solution.py:601
  64.4 3.1 %collective-permute-start.5 = (bf16[1,16,1280]{2,1,0:T(8,128)(2,1)S(1)}, bf16[1,16,1280]{2,1,0:T(8,128)(2,1)S(1)}, u32[]{:S(2)}, u32[]{:S(2)}) collective-permute-start(bf16[1,16,1280]{2,1,0:T(8,128)(2,1)S(1)} %bitcast.7), channel_id=1, source_target_pairs={{0,16},{1,17},{2,18},{3,19},{4,20},{5,21},{6,22},{7,23},{8,24},{9,... | collective-permute-start | bytes 122888 | tf_op jit(solution)/shard_map/ppermute | solution.py:638
  67.5 2.6 %recall.2 = (f32[16,36864]{1,0:T(8,128)S(1)}, f32[16,128]{1,0:T(8,128)S(1)}) custom-call(s32[8]{0:T(128)S(1)} %copy-done, f32[128,36864]{1,0:T(8,128)} %dict_hbm.7, bf16[16,1280]{1,0:T(8,128)(2,1)S(1)} %gradient.2.when_ref), custom_call_target="tpu_custom_call" | custom-call | tf_op jit(solution)/shard_map/recall/pallas_call | solution.py:695
  73.8 6.1 %collective-permute-done.10 = bf16[4,16,1280]{2,1,0:T(8,128)(2,1)S(1)} collective-permute-done((bf16[4,16,1280]{2,1,0:T(8,128)(2,1)S(1)}, bf16[4,16,1280]{2,1,0:T(8,128)(2,1)S(1)}, u32[]{:S(2)}, u32[]{:S(2)}) %collective-permute-start.10) | collective-permute-done | bytes 163872 | tf_op jit(solution)/shard_map/ppermute | solution.py:638
  82.1 2.1 %renew.2.refs_6_.refs_0_ = f32[16,36864]{1,0:T(8,128)S(1)} custom-call(s32[8]{0:T(128)S(1)} %copy-done, bf16[16,16,1280]{2,1,0:T(8,128)(2,1)S(1)} %constant_dynamic-update-slice_fusion.held_ref, bf16[16,16,1280]{2,1,0:T(8,128)(2,1)S(1)} %collective-permute-done.13.came_ref, f32[16,36864]{1,0:T(8,128)S(1)} %get-tuple-element.50.old, ...), custom_call_target="tpu_custom_call" | custom-call | tf_op jit(solution)/shard_map/renew/pallas_call | solution.py:776
  84.2 11.9 %iterate.3 = (f32[128,128]{1,0:T(8,128)S(1)}, bf16[224,128]{1,0:T(8,128)(2,1)S(1)}, bf16[224,128]{1,0:T(8,128)(2,1)S(1)}, bf16[64,128]{1,0:T(8,128)(2,1)S(1)}, b...) custom-call(s32[8]{0:T(128)S(1)} %copy-done, ...), custom_call_target="tpu_custom_call", output_to_operand_aliasing={{4}: (9, {}), {5}: (11, {})} | custom-call | tf_op jit(solution)/shard_map/iterate/pallas_call | solution.py:387
  96.1 1.6 %collective-permute-start.14 = (bf16[224,128]{1,0:T(8,128)(2,1)S(1)}, bf16[224,128]{1,0:T(8,128)(2,1)S(1)}, u32[]{:S(2)}, u32[]{:S(2)}) collective-permute-start(bf16[224,128]{1,0:T(8,128)(2,1)S(1)} %get-tuple-element.55), channel_id=1, source_target_pairs={{0,1},{1,0},{2,3},{3,2},{4,5},{5,4},{6,7},{7,6},{8,9},{9,8},{10,11... | collective-permute-start | bytes 172040 | tf_op jit(solution)/shard_map/ppermute | solution.py:795
  98.3 5.0 %collective-permute-start.16 = (bf16[64,128]{1,0:T(8,128)(2,1)S(1)}, bf16[64,128]{1,0:T(8,128)(2,1)S(1)}, u32[]{:S(2)}, u32[]{:S(2)}) collective-permute-start(bf16[64,128]{1,0:T(8,128)(2,1)S(1)} %get-tuple-element.57), channel_id=1, source_target_pairs={{0,2},{1,3},{2,4},{3,5},{4,6},{5,7},{6,8},{7,9},{8,10},{9,11},{10,... | collective-permute-start | bytes 49160 | tf_op jit(solution)/shard_map/ppermute | solution.py:38
  103.3 1.4 collective-permute-done.16.refs_3_
  104.7 10.7 %conclude.3 = (bf16[32,32,128]{2,1,0:T(8,128)(2,1)S(1)}, f32[384,128]{1,0:T(8,128)S(1)}, f32[128,128]{1,0:T(8,128)S(1)}) custom-call(s32[8]{0:T(128)S(1)} %copy-done, f32[1,128]{1,0:T(1,128)S(1)} %bitcast.16, f32[128,128]{1,0:T(8,128)S(1)} %get-tuple-element.54.refs_0_, bf16[224,128]{1,0:T(8,128)(2,1)S(1)} %collective-permute-done.14.refs_1_, ...), custom_call_target="tpu_custom_call" | custom-call | tf_op jit(solution)/shard_map/conclude/pallas_call | solution.py:502
  115.4 17.7 %all_to_all.11.blocks_ref = bf16[32,32,128]{2,1,0:T(8,128)(2,1)S(1)} all-to-all(bf16[32,32,128]{2,1,0:T(8,128)(2,1)S(1)} %get-tuple-element.60), channel_id=1, replica_groups=mesh['tm'=32,'chan'=1] {'tm'}, dimensions={0} | all-to-all | bytes 524288 | tf_op jit(solution)/shard_map/all_to_all | solution.py:817
  133.2 2.8 %gradient.3 = bf16[16,1280]{1,0:T(8,128)(2,1)S(1)} custom-call(s32[8]{0:T(128)S(1)} %copy-done, bf16[32,32,128]{2,1,0:T(8,128)(2,1)S(1)} %all_to_all.11.blocks_ref, f32[128,36864]{1,0:T(8,128)} %dict_hbm.7), custom_call_target="tpu_custom_call" | custom-call | tf_op jit(solution)/shard_map/gradient/pallas_call | solution.py:601
  136.0 1.4 collective-permute-start.19
  137.4 3.1 %collective-permute-start.17 = (bf16[1,16,1280]{2,1,0:T(8,128)(2,1)S(1)}, bf16[1,16,1280]{2,1,0:T(8,128)(2,1)S(1)}, u32[]{:S(2)}, u32[]{:S(2)}) collective-permute-start(bf16[1,16,1280]{2,1,0:T(8,128)(2,1)S(1)} %bitcast.11), channel_id=1, source_target_pairs={{0,16},{1,17},{2,18},{3,19},{4,20},{5,21},{6,22},{7,23},{8,24},{9,... | collective-permute-start | bytes 122888 | tf_op jit(solution)/shard_map/ppermute | solution.py:638
  140.4 1.7 %collective-permute-done.19 = bf16[1,16,1280]{2,1,0:T(8,128)(2,1)S(1)} collective-permute-done((bf16[1,16,1280]{2,1,0:T(8,128)(2,1)S(1)}, bf16[1,16,1280]{2,1,0:T(8,128)(2,1)S(1)}, u32[]{:S(2)}, u32[]{:S(2)}) %collective-permute-start.19) | collective-permute-done | bytes 40992 | tf_op jit(solution)/shard_map/ppermute | solution.py:638
  146.3 6.5 %recall.3 = (f32[16,36864]{1,0:T(8,128)S(1)}, f32[16,128]{1,0:T(8,128)S(1)}, f32[128,36864]{1,0:T(8,128)}) custom-call(s32[8]{0:T(128)S(1)} %copy-done, f32[128,36864]{1,0:T(8,128)} %dict_hbm.7, bf16[4,16,1280]{2,1,0:T(8,128)(2,1)S(1)} %pad_maximum_fusion.1.when_ref, f32[16,36864]{1,0:T(8,128)S(1)} %renew.2.refs_6_.refs_0_, ...), custom_call_target="tpu_custom_call", output_to_operand_aliasing={{2}: (4, {})} | custom-call | tf_op jit(solution)/shard_map/recall/pallas_call | solution.py:695
  155.2 3.3 %renew.3 = f32[128,36864]{1,0:T(8,128)} custom-call(s32[8]{0:T(128)S(1)} %copy-done, bf16[16,16,1280]{2,1,0:T(8,128)(2,1)S(1)} %constant_dynamic-update-slice_fusion.7.held_ref, bf16[16,16,1280]{2,1,0:T(8,128)(2,1)S(1)} %collective-permute-done.23.came_ref, f32[16,36864]{1,0:T(8,128)S(1)} %get-tuple-element.62.old, ...), custom_call_target="tpu_custom_call", output_to_operand_aliasing={{}: (5, {})} | custom-call | tf_op jit(solution)/shard_map/renew/pallas_call | solution.py:776
  (60 shorter events, 17.2 us)
Async XLA Ops:
  1.8 13.0 %collective-permute-start = (bf16[96,512]{1,0:T(8,128)(2,1)S(1)}, bf16[96,512]{1,0:T(8,128)(2,1)S(1)}, u32[]{:S(2)}, u32[]{:S(2)}) collective-permute-start(bf16[96,512]{1,0:T(8,128)(2,1)S(1)} %get-tuple-element.36), channel_id=1, source_target_pairs={{0,1},{1,0},{2,3},{3,2},{4,5},{5,4},{6,7},{7,6},{8,9},{9,8},{10,11... | collective-permute-start | bytes 294920 | tf_op jit(solution)/shard_map/ppermute | solution.py:795
  2.3 12.5 %collective-permute-start.1 = (bf16[96,512]{1,0:T(8,128)(2,1)S(1)}, bf16[96,512]{1,0:T(8,128)(2,1)S(1)}, u32[]{:S(2)}, u32[]{:S(2)}) collective-permute-start(bf16[96,512]{1,0:T(8,128)(2,1)S(1)} %get-tuple-element.37), channel_id=1, source_target_pairs={{1,2},{2,1},{3,4},{4,3},{5,6},{6,5},{7,8},{8,7},{9,10},{10,9},{11,... | collective-permute-start | bytes 294920 | tf_op jit(solution)/shard_map/ppermute | solution.py:795
  20.0 10.8 %collective-permute-start.2 = (bf16[224,128]{1,0:T(8,128)(2,1)S(1)}, bf16[224,128]{1,0:T(8,128)(2,1)S(1)}, u32[]{:S(2)}, u32[]{:S(2)}) collective-permute-start(bf16[224,128]{1,0:T(8,128)(2,1)S(1)} %get-tuple-element.41), channel_id=1, source_target_pairs={{0,1},{1,0},{2,3},{3,2},{4,5},{5,4},{6,7},{7,6},{8,9},{9,8},{10,11... | collective-permute-start | bytes 172040 | tf_op jit(solution)/shard_map/ppermute | solution.py:795
  24.0 6.9 %collective-permute-start.3 = (bf16[224,128]{1,0:T(8,128)(2,1)S(1)}, bf16[224,128]{1,0:T(8,128)(2,1)S(1)}, u32[]{:S(2)}, u32[]{:S(2)}) collective-permute-start(bf16[224,128]{1,0:T(8,128)(2,1)S(1)} %get-tuple-element.42), channel_id=1, source_target_pairs={{1,2},{2,1},{3,4},{4,3},{5,6},{6,5},{7,8},{8,7},{9,10},{10,9},{11,... | collective-permute-start | bytes 172040 | tf_op jit(solution)/shard_map/ppermute | solution.py:795
  24.6 6.2 %collective-permute-start.4 = (bf16[64,128]{1,0:T(8,128)(2,1)S(1)}, bf16[64,128]{1,0:T(8,128)(2,1)S(1)}, u32[]{:S(2)}, u32[]{:S(2)}) collective-permute-start(bf16[64,128]{1,0:T(8,128)(2,1)S(1)} %get-tuple-element.43), channel_id=1, source_target_pairs={{0,2},{1,3},{2,4},{3,5},{4,6},{5,7},{6,8},{7,9},{8,10},{9,11},{10,... | collective-permute-start | bytes 49160 | tf_op jit(solution)/shard_map/ppermute | solution.py:38
  63.0 7.1 %collective-permute-start.7 = (bf16[1,16,1280]{2,1,0:T(8,128)(2,1)S(1)}, bf16[1,16,1280]{2,1,0:T(8,128)(2,1)S(1)}, u32[]{:S(2)}, u32[]{:S(2)}) collective-permute-start(bf16[1,16,1280]{2,1,0:T(8,128)(2,1)S(1)} %bitcast.5), channel_id=1, source_target_pairs={{0,24},{1,25},{2,26},{3,27},{4,28},{5,29},{6,30},{7,31},{8,16},{9,... | collective-permute-start | bytes 122888 | tf_op jit(solution)/shard_map/ppermute | solution.py:638
  64.4 5.7 %collective-permute-start.6 = (bf16[1,16,1280]{2,1,0:T(8,128)(2,1)S(1)}, bf16[1,16,1280]{2,1,0:T(8,128)(2,1)S(1)}, u32[]{:S(2)}, u32[]{:S(2)}) collective-permute-start(bf16[1,16,1280]{2,1,0:T(8,128)(2,1)S(1)} %bitcast.6), channel_id=1, source_target_pairs={{0,8},{1,9},{2,10},{3,11},{4,12},{5,13},{6,14},{7,15},{8,0},{9,1},... | collective-permute-start | bytes 122888 | tf_op jit(solution)/shard_map/ppermute | solution.py:638
  64.4 5.7 %collective-permute-start.5 = (bf16[1,16,1280]{2,1,0:T(8,128)(2,1)S(1)}, bf16[1,16,1280]{2,1,0:T(8,128)(2,1)S(1)}, u32[]{:S(2)}, u32[]{:S(2)}) collective-permute-start(bf16[1,16,1280]{2,1,0:T(8,128)(2,1)S(1)} %bitcast.7), channel_id=1, source_target_pairs={{0,16},{1,17},{2,18},{3,19},{4,20},{5,21},{6,22},{7,23},{8,24},{9,... | collective-permute-start | bytes 122888 | tf_op jit(solution)/shard_map/ppermute | solution.py:638
  70.2 9.7 %collective-permute-start.12 = (bf16[4,16,1280]{2,1,0:T(8,128)(2,1)S(1)}, bf16[4,16,1280]{2,1,0:T(8,128)(2,1)S(1)}, u32[]{:S(2)}, u32[]{:S(2)}) collective-permute-start(bf16[4,16,1280]{2,1,0:T(8,128)(2,1)S(1)} %pad_maximum_fusion), channel_id=1, source_target_pairs={{0,6},{1,7},{2,4},{3,5},{4,2},{5,3},{6,0},{7,1},{8,14},{9,15},{10,... | collective-permute-start | bytes 491528 | tf_op jit(solution)/shard_map/ppermute | solution.py:638
  71.4 8.4 %collective-permute-start.11 = (bf16[4,16,1280]{2,1,0:T(8,128)(2,1)S(1)}, bf16[4,16,1280]{2,1,0:T(8,128)(2,1)S(1)}, u32[]{:S(2)}, u32[]{:S(2)}) collective-permute-start(bf16[4,16,1280]{2,1,0:T(8,128)(2,1)S(1)} %pad_maximum_fusion), channel_id=1, source_target_pairs={{0,2},{1,3},{2,0},{3,1},{4,6},{5,7},{6,4},{7,5},{8,10},{9,11},{10,... | collective-permute-start | bytes 491528 | tf_op jit(solution)/shard_map/ppermute | solution.py:638
  72.6 7.2 %collective-permute-start.10 = (bf16[4,16,1280]{2,1,0:T(8,128)(2,1)S(1)}, bf16[4,16,1280]{2,1,0:T(8,128)(2,1)S(1)}, u32[]{:S(2)}, u32[]{:S(2)}) collective-permute-start(bf16[4,16,1280]{2,1,0:T(8,128)(2,1)S(1)} %pad_maximum_fusion), channel_id=1, source_target_pairs={{0,4},{1,5},{2,6},{3,7},{4,0},{5,1},{6,2},{7,3},{8,12},{9,13},{10,... | collective-permute-start | bytes 491528 | tf_op jit(solution)/shard_map/ppermute | solution.py:638
  79.9 2.2 %collective-permute-start.13 = (bf16[16,16,1280]{2,1,0:T(8,128)(2,1)S(1)}, bf16[16,16,1280]{2,1,0:T(8,128)(2,1)S(1)}, u32[]{:S(2)}, u32[]{:S(2)}) collective-permute-start(bf16[16,16,1280]{2,1,0:T(8,128)(2,1)S(1)} %constant_dynamic-update-slice_fusion.held_ref), channel_id=1, source_target_pairs={{0,1},{1,0},{2,3},{3,2},{4,5},{5,4},{6,7},{7,6},{8,9},{9,8},{10,11... | collective-permute-start | bytes 1966088 | tf_op jit(solution)/shard_map/ppermute | solution.py:638
  80.0 4.2 %collective-permute-start.8 = (bf16[96,128]{1,0:T(8,128)(2,1)S(1)}, bf16[96,128]{1,0:T(8,128)(2,1)S(1)}, u32[]{:S(2)}, u32[]{:S(2)}) collective-permute-start(bf16[96,128]{1,0:T(8,128)(2,1)S(1)} %get-tuple-element.48), channel_id=1, source_target_pairs={{0,1},{1,0},{2,3},{3,2},{4,5},{5,4},{6,7},{7,6},{8,9},{9,8},{10,11... | collective-permute-start | bytes 73736 | tf_op jit(solution)/shard_map/ppermute | solution.py:795
  80.5 3.7 %collective-permute-start.9 = (bf16[96,128]{1,0:T(8,128)(2,1)S(1)}, bf16[96,128]{1,0:T(8,128)(2,1)S(1)}, u32[]{:S(2)}, u32[]{:S(2)}) collective-permute-start(bf16[96,128]{1,0:T(8,128)(2,1)S(1)} %get-tuple-element.49), channel_id=1, source_target_pairs={{1,2},{2,1},{3,4},{4,3},{5,6},{6,5},{7,8},{8,7},{9,10},{10,9},{11,... | collective-permute-start | bytes 73736 | tf_op jit(solution)/shard_map/ppermute | solution.py:795
  96.1 8.7 %collective-permute-start.14 = (bf16[224,128]{1,0:T(8,128)(2,1)S(1)}, bf16[224,128]{1,0:T(8,128)(2,1)S(1)}, u32[]{:S(2)}, u32[]{:S(2)}) collective-permute-start(bf16[224,128]{1,0:T(8,128)(2,1)S(1)} %get-tuple-element.55), channel_id=1, source_target_pairs={{0,1},{1,0},{2,3},{3,2},{4,5},{5,4},{6,7},{7,6},{8,9},{9,8},{10,11... | collective-permute-start | bytes 172040 | tf_op jit(solution)/shard_map/ppermute | solution.py:795
  97.7 7.1 %collective-permute-start.15 = (bf16[224,128]{1,0:T(8,128)(2,1)S(1)}, bf16[224,128]{1,0:T(8,128)(2,1)S(1)}, u32[]{:S(2)}, u32[]{:S(2)}) collective-permute-start(bf16[224,128]{1,0:T(8,128)(2,1)S(1)} %get-tuple-element.56), channel_id=1, source_target_pairs={{1,2},{2,1},{3,4},{4,3},{5,6},{6,5},{7,8},{8,7},{9,10},{10,9},{11,... | collective-permute-start | bytes 172040 | tf_op jit(solution)/shard_map/ppermute | solution.py:795
  98.3 6.4 %collective-permute-start.16 = (bf16[64,128]{1,0:T(8,128)(2,1)S(1)}, bf16[64,128]{1,0:T(8,128)(2,1)S(1)}, u32[]{:S(2)}, u32[]{:S(2)}) collective-permute-start(bf16[64,128]{1,0:T(8,128)(2,1)S(1)} %get-tuple-element.57), channel_id=1, source_target_pairs={{0,2},{1,3},{2,4},{3,5},{4,6},{5,7},{6,8},{7,9},{8,10},{9,11},{10,... | collective-permute-start | bytes 49160 | tf_op jit(solution)/shard_map/ppermute | solution.py:38
  136.0 6.2 %collective-permute-start.19 = (bf16[1,16,1280]{2,1,0:T(8,128)(2,1)S(1)}, bf16[1,16,1280]{2,1,0:T(8,128)(2,1)S(1)}, u32[]{:S(2)}, u32[]{:S(2)}) collective-permute-start(bf16[1,16,1280]{2,1,0:T(8,128)(2,1)S(1)} %bitcast.9), channel_id=1, source_target_pairs={{0,24},{1,25},{2,26},{3,27},{4,28},{5,29},{6,30},{7,31},{8,16},{9,... | collective-permute-start | bytes 122888 | tf_op jit(solution)/shard_map/ppermute | solution.py:638
  137.4 4.8 %collective-permute-start.18 = (bf16[1,16,1280]{2,1,0:T(8,128)(2,1)S(1)}, bf16[1,16,1280]{2,1,0:T(8,128)(2,1)S(1)}, u32[]{:S(2)}, u32[]{:S(2)}) collective-permute-start(bf16[1,16,1280]{2,1,0:T(8,128)(2,1)S(1)} %bitcast.10), channel_id=1, source_target_pairs={{0,8},{1,9},{2,10},{3,11},{4,12},{5,13},{6,14},{7,15},{8,0},{9,1},... | collective-permute-start | bytes 122888 | tf_op jit(solution)/shard_map/ppermute | solution.py:638
  137.4 5.3 %collective-permute-start.17 = (bf16[1,16,1280]{2,1,0:T(8,128)(2,1)S(1)}, bf16[1,16,1280]{2,1,0:T(8,128)(2,1)S(1)}, u32[]{:S(2)}, u32[]{:S(2)}) collective-permute-start(bf16[1,16,1280]{2,1,0:T(8,128)(2,1)S(1)} %bitcast.11), channel_id=1, source_target_pairs={{0,16},{1,17},{2,18},{3,19},{4,20},{5,21},{6,22},{7,23},{8,24},{9,... | collective-permute-start | bytes 122888 | tf_op jit(solution)/shard_map/ppermute | solution.py:638
  142.8 10.2 %collective-permute-start.22 = (bf16[4,16,1280]{2,1,0:T(8,128)(2,1)S(1)}, bf16[4,16,1280]{2,1,0:T(8,128)(2,1)S(1)}, u32[]{:S(2)}, u32[]{:S(2)}) collective-permute-start(bf16[4,16,1280]{2,1,0:T(8,128)(2,1)S(1)} %pad_maximum_fusion.1.when_ref), channel_id=1, source_target_pairs={{0,6},{1,7},{2,4},{3,5},{4,2},{5,3},{6,0},{7,1},{8,14},{9,15},{10,... | collective-permute-start | bytes 491528 | tf_op jit(solution)/shard_map/ppermute | solution.py:638
  144.0 8.9 %collective-permute-start.21 = (bf16[4,16,1280]{2,1,0:T(8,128)(2,1)S(1)}, bf16[4,16,1280]{2,1,0:T(8,128)(2,1)S(1)}, u32[]{:S(2)}, u32[]{:S(2)}) collective-permute-start(bf16[4,16,1280]{2,1,0:T(8,128)(2,1)S(1)} %pad_maximum_fusion.1.when_ref), channel_id=1, source_target_pairs={{0,2},{1,3},{2,0},{3,1},{4,6},{5,7},{6,4},{7,5},{8,10},{9,11},{10,... | collective-permute-start | bytes 491528 | tf_op jit(solution)/shard_map/ppermute | solution.py:638
  145.2 7.7 %collective-permute-start.20 = (bf16[4,16,1280]{2,1,0:T(8,128)(2,1)S(1)}, bf16[4,16,1280]{2,1,0:T(8,128)(2,1)S(1)}, u32[]{:S(2)}, u32[]{:S(2)}) collective-permute-start(bf16[4,16,1280]{2,1,0:T(8,128)(2,1)S(1)} %pad_maximum_fusion.1.when_ref), channel_id=1, source_target_pairs={{0,4},{1,5},{2,6},{3,7},{4,0},{5,1},{6,2},{7,3},{8,12},{9,13},{10,... | collective-permute-start | bytes 491528 | tf_op jit(solution)/shard_map/ppermute | solution.py:638
  153.0 2.2 %collective-permute-start.23 = (bf16[16,16,1280]{2,1,0:T(8,128)(2,1)S(1)}, bf16[16,16,1280]{2,1,0:T(8,128)(2,1)S(1)}, u32[]{:S(2)}, u32[]{:S(2)}) collective-permute-start(bf16[16,16,1280]{2,1,0:T(8,128)(2,1)S(1)} %constant_dynamic-update-slice_fusion.7.held_ref), channel_id=1, source_target_pairs={{0,1},{1,0},{2,3},{3,2},{4,5},{5,4},{6,7},{7,6},{8,9},{9,8},{10,11... | collective-permute-start | bytes 1966088 | tf_op jit(solution)/shard_map/ppermute | solution.py:638
  (2 other events, 28.3 us)

commit v11 on v10

--- a/solution.py
+++ b/solution.py
@@ -23,7 +23,7 @@
 STRIDE = L + 1
 GROUPS = 4
 SUBLANES = 8
-COPIED = (32, 72, 24)
+COPIED = (48, 40, 40)
 FINE = 4
 LANES = 128
 VMEM_BYTES = 24 * 1024 * 1024
@@ -95,13 +95,7 @@
     return turned_ref[pl.ds(tap, ROWS, stride=STRIDE), :].astype(jnp.bfloat16)
 
 
-def layout_kernel(dict_ref, taps_ref, copy_hbm, sem, *turned):
-    width = dict_ref.shape[1]
-    column = pl.ds(pl.multiple_of(pl.program_id(0) * width, LANES), width)
-    rows = pl.ds(0, COPIED[0])
-    copy = pltpu.make_async_copy(dict_ref.at[rows], copy_hbm.at[rows, column], sem)
-    copy.start()
-
+def layout_kernel(dict_ref, taps_ref, *turned):
     def part(group):
         return dict_ref[:, group * ROWS * L : (group + 1) * ROWS * L]
 
@@ -112,7 +106,6 @@
         own = pl.ds(pl.multiple_of((pl.program_id(0) * GROUPS + group) * ROWS, ROWS), ROWS)
         for tap in range(L):
             taps_ref[tap // ROWS, tap % ROWS, own, :] = tap_of(turned[group], tap)
-    copy.wait()
 
 
 def layout(dictionary, channels):
@@ -121,13 +114,9 @@
         layout_kernel,
         grid=(channels // block,),
         in_specs=[pl.BlockSpec((K, block * L), lambda i: (0, i))],
-        out_specs=[vmem(), hbm()],
-        out_shape=[
-            pltpu.VMEM((COARSE, ROWS, channels, K), jnp.bfloat16),
-            pltpu.HBM(dictionary.shape, jnp.float32),
-        ],
-        scratch_shapes=[pltpu.SemaphoreType.DMA]
-        + [pltpu.VMEM((ROWS * STRIDE, K), jnp.float32)] * GROUPS,
+        out_specs=vmem(),
+        out_shape=pltpu.VMEM((COARSE, ROWS, channels, K), jnp.bfloat16),
+        scratch_shapes=[pltpu.VMEM((ROWS * STRIDE, K), jnp.float32)] * GROUPS,
         compiler_params=pltpu.CompilerParams(vmem_limit_bytes=VMEM_BYTES),
         name="layout",
     )(far(dictionary))
@@ -246,11 +235,8 @@
     even = lax.axis_index("tm") % 2 == 0
 
     def put(first, second):
-        first[: rightward.shape[0]] = rightward
-        second[: leftward.shape[0]] = leftward
-        unused = second.shape[0] - leftward.shape[0]
-        if unused:
-            second[leftward.shape[0] :] = jnp.zeros((unused, second.shape[1]), second.dtype)
+        first[...] = rightward
+        second[...] = leftward
 
     pl.when(even)(lambda: put(*edge_refs))
     pl.when(jnp.logical_not(even))(lambda: put(*edge_refs[::-1]))
@@ -311,11 +297,6 @@
     return take
 
 
-def reaches(segment):
-    near = min(2 * L, segment)
-    return near, 2 * L - near
-
-
 def residual_rows(rb, pieces, start, acc, total_time):
     rows = rb.shape[0]
     moment = start + lax.broadcasted_iota(jnp.int32, (rows, LANES), 0)
@@ -339,7 +320,7 @@
     atoms = take(1 if patching else 0)
     (taps,) = take(1)
     source = take(2 if patching else 0)
-    state_out, first_out, second_out, far_out = take(4)
+    state_out, *edges = take(3)
     taps = (take(1) if patching else [taps])[0]
     target = take(1 if patching else 0)
     zb, rb, zz, rr, fine, acc, beyond = take(7)
@@ -367,13 +348,7 @@
     state = stepped_codes(state_ref[...], acc, limit_ref[...])
     state_out[...] = state
     low = state.astype(jnp.bfloat16)
-    rest = (state - low.astype(jnp.float32)).astype(jnp.bfloat16)
-    near, beyond_near = reaches(segment)
-    put_edges((first_out, second_out), jnp.concatenate([low[-near:], rest[-L:]], axis=0), low[:L])
-    if beyond_near:
-        far_out[...] = low[-beyond_near:]
-    else:
-        far_out[...] = jnp.zeros_like(far_out)
+    put_edges(edges, low[-L:], low[:L])
     if ferry:
         ferry.close()
 
@@ -382,15 +357,13 @@
     segment, channels = signal.shape
     patching = atoms is not None
     reach = segment + L
-    near, beyond_near = reaches(segment)
     carried = [far(value) for value in ferry[:2]] if patching else []
     return pl.pallas_call(
         functools.partial(iterate_kernel, peers * segment, step if patching else 0, ferry[2]),
         in_specs=[scalars()] + [vmem()] * (8 + patching) + [hbm()] * len(carried),
-        out_specs=[vmem()] * (4 + patching) + [hbm()] * patching,
+        out_specs=[vmem()] * (3 + patching) + [hbm()] * patching,
         out_shape=[pltpu.VMEM((segment, K), jnp.float32)]
-        + [jax.ShapeDtypeStruct((near + L, K), jnp.bfloat16)] * 2
-        + [jax.ShapeDtypeStruct((max(beyond_near, ROWS), K), jnp.bfloat16)]
+        + [jax.ShapeDtypeStruct((L, K), jnp.bfloat16)] * 2
         + [pltpu.VMEM(taps.shape, jnp.bfloat16)] * patching
         + [pltpu.HBM(ferry[0].shape, jnp.float32)] * patching,
         scratch_shapes=[
@@ -408,7 +381,7 @@
             + [pltpu.VMEM((ROWS * STRIDE, K), jnp.float32)] * GROUPS
         )
         * patching,
-        input_output_aliases={9: 4, 11: 5} if patching else {},
+        input_output_aliases={9: 3, 11: 4} if patching else {},
         compiler_params=pltpu.CompilerParams(vmem_limit_bytes=VMEM_BYTES),
         name="iterate",
     )(
@@ -424,100 +397,102 @@
     )
 
 
-def conclude_kernel(peers, step, plan_ref, limit_ref, *refs):
+def conclude_kernel(peers, step, copied, plan_ref, limit_ref, *refs):
     last = step + 1 == OUTER
     take = taker(refs)
-    state_ref, first_ref, second_ref, far_ref, signal_ref, next_first, next_second, taps = take(8)
+    state_ref, first_ref, second_ref, signal_ref, next_first, next_second, taps = take(7)
+    source = take(2 if copied else 1)[0]
     (payload_out,) = take(1)
-    outs = take(2 if last else 3)
-    zb, rb, zz, rr, fine, acc, before, beyond, earlier, tall = take(10)
+    state_out, partial_out, codes_out = (None, *take(2)) if last else (*take(1), None, None)
+    *edges, target = take(3)
+    zb, rb, zz, rr, fine, acc, beyond, tall = take(8)
+    ferry = Ferry(source, target, copied, *take(2))
+    if not last:
+        (codes_out,) = take(1)
     segment, channels = signal_ref.shape
-    near, beyond_near = reaches(segment)
-    zb[2 * L : 2 * L + segment, :] = state_ref[...].astype(jnp.bfloat16)
-    if beyond_near:
-        zb[:beyond_near, :] = far_ref[...]
+    reach = segment + L
+    zb[L:reach, :] = state_ref[...].astype(jnp.bfloat16)
 
     def put(left, right):
-        zb[beyond_near : 2 * L, :] = left[:near]
-        earlier[...] = left[near - L : near].astype(jnp.float32) + left[near:].astype(jnp.float32)
-        zb[2 * L + segment :, :] = right[:L]
+        zb[:L, :] = left[...]
+        zb[reach:, :] = right[...]
 
     def put_signal(left, right):
-        before[...] = left[:, K:]
         beyond[...] = right[:, K:]
 
     by_side(put, first_ref, second_ref)
     by_side(put_signal, next_first, next_second)
-    convolve(zb, L, 2 * L + segment, taps, zz, fine, acc)
-    start = lax.axis_index("tm") * segment - L
-    residual_rows(rb, (before, signal_ref, beyond), start, acc, peers * segment)
-    correlate(rb, L + segment, taps, rr, fine, acc)
-    state = jnp.concatenate([earlier[...], state_ref[...]], axis=0)
-    state = stepped_codes(state, acc, limit_ref[...])
-    moment = start + lax.broadcasted_iota(jnp.int32, state.shape, 0)
-    state = jnp.where(moment >= 0, state, 0.0)
+    convolve(zb, L, reach, taps, zz, fine, acc)
+    ferry.turn_round()
+    start = lax.axis_index("tm") * segment
+    residual_rows(rb, (signal_ref, beyond), start, acc, peers * segment)
+    correlate(rb, segment, taps, rr, fine, acc)
+    state = stepped_codes(state_ref[...], acc, limit_ref[...])
     low = state.astype(jnp.bfloat16)
-    zb[: L + segment, :] = low
-    own = state[L:]
-    if last:
-        resid_out, codes_out = outs
-    else:
-        state_out, *edges = outs
-        (codes_out,) = take(1)
-        state_out[...] = own
-        put_edges(edges, low[-L:], low[L : 2 * L])
-    codes_out[...] = own.T
-    convolve(zb, L, segment, taps, zz, fine, acc)
+    if not last:
+        state_out[...] = state
+    put_edges(edges, low[-L:], low[:L])
+    codes_out[...] = state.T
+    zb[:L, :] = jnp.zeros((L, K), jnp.bfloat16)
+    zb[L:reach, :] = low
+    zb[reach:, :] = jnp.zeros((L, K), jnp.bfloat16)
+    convolve(zb, L, reach, taps, zz, fine, acc)
     scale = (C * L) ** (-0.5)
+    block = codes_out[pl.ds(first_row_of(plan_ref, step), BLOCK_ATOMS), :].astype(jnp.bfloat16)
+    share = channels // peers
+    share_rows = (payload_out.shape[1] - BLOCK_ATOMS) // 2
+    unused = jnp.zeros((tall.shape[1] - channels, segment), jnp.float32)
     for tile in range(channels // LANES):
         column = slice(tile * LANES, (tile + 1) * LANES)
         value = signal_ref[:, column].astype(jnp.float32) - scale * acc[tile, :segment, :]
-        value = value.T
-        tall[column, :] = value
         if last:
-            resid_out[column, :] = value
-    block = codes_out[pl.ds(first_row_of(plan_ref, step), BLOCK_ATOMS), :].astype(jnp.bfloat16)
-    share = channels // peers
-    share_rows = payload_out.shape[1] - BLOCK_ATOMS
-    tall[channels:, :] = jnp.zeros((tall.shape[0] - channels, segment), jnp.float32)
+            partial_out[:, column] = value
+        tall[0, column, :] = value.T
+        spill = jnp.concatenate(
+            [-scale * acc[tile, segment:reach, :], jnp.zeros((segment - L, LANES), jnp.float32)], axis=0
+        )
+        tall[1, column, :] = spill.T
+    for part in range(2):
+        tall[part, channels:, :] = unused
     for peer in range(peers):
-        part = tall[peer * share : peer * share + share_rows, :]
-        payload_out[peer, :share_rows, :] = part.astype(jnp.bfloat16)
-        payload_out[peer, share_rows:, :] = block
-
-
-def conclude(plan, step, limit, state, swapped, far_edge, signal, following, taps, peers):
+        for part in range(2):
+            rows = tall[part, peer * share : peer * share + share_rows, :]
+            payload_out[peer, part * share_rows : (part + 1) * share_rows, :] = rows.astype(jnp.bfloat16)
+        payload_out[peer, 2 * share_rows :, :] = block
+    ferry.close()
+
+
+def conclude(plan, step, limit, state, swapped, signal, following, taps, ferry, peers):
     segment, channels = signal.shape
     share = channels // peers
     share_rows = -(-share // ROWS) * ROWS
     last = step + 1 == OUTER
-    rows = 2 * L + segment
-    outs = [
-        pltpu.VMEM((channels, segment), jnp.float32),
-        pltpu.VMEM((K, segment), jnp.float32),
-    ]
-    if not last:
-        outs = [pltpu.VMEM((segment, K), jnp.float32)]
-        outs += [jax.ShapeDtypeStruct((L, K), jnp.bfloat16)] * 2
+    carried = [far(value) for value in ferry[:2] if value is not None]
+    reach = segment + L
+    outs = [pltpu.VMEM((segment, K), jnp.float32)]
+    if last:
+        outs = [pltpu.VMEM((segment, channels), jnp.float32), pltpu.VMEM((K, segment), jnp.float32)]
+    outs += [jax.ShapeDtypeStruct((L, K), jnp.bfloat16)] * 2
     return pl.pallas_call(
-        functools.partial(conclude_kernel, peers, step),
-        in_specs=[scalars()] + [vmem()] * 9,
-        out_specs=[vmem()] * (1 + len(outs)),
-        out_shape=[jax.ShapeDtypeStruct((peers, share_rows + BLOCK_ATOMS, segment), jnp.bfloat16)]
-        + outs,
+        functools.partial(conclude_kernel, peers, step, ferry[2]),
+        in_specs=[scalars()] + [vmem()] * 8 + [hbm()] * len(carried),
+        out_specs=[vmem()] * (1 + len(outs)) + [hbm()],
+        out_shape=[jax.ShapeDtypeStruct((peers, 2 * share_rows + BLOCK_ATOMS, segment), jnp.bfloat16)]
+        + outs
+        + [pltpu.HBM(ferry[0].shape, jnp.float32)],
         scratch_shapes=[
-            pltpu.VMEM((rows + L, K), jnp.bfloat16),
-            pltpu.VMEM((rows, channels), jnp.bfloat16),
-            pltpu.VMEM((rows + ROWS, COARSE * K), jnp.bfloat16),
-            pltpu.VMEM((L + segment + ROWS, COARSE * channels), jnp.bfloat16),
-            pltpu.VMEM((2 * FINE, channels // LANES, rows + ROWS, LANES), jnp.float32),
-            pltpu.VMEM((channels // LANES, rows, LANES), jnp.float32),
+            pltpu.VMEM((L + reach, K), jnp.bfloat16),
+            pltpu.VMEM((reach, channels), jnp.bfloat16),
+            pltpu.VMEM((reach + ROWS, COARSE * K), jnp.bfloat16),
+            pltpu.VMEM((segment + ROWS, COARSE * channels), jnp.bfloat16),
+            pltpu.VMEM((2 * FINE, channels // LANES, reach + ROWS, LANES), jnp.float32),
+            pltpu.VMEM((channels // LANES, reach, LANES), jnp.float32),
             pltpu.VMEM((L, channels), jnp.bfloat16),
-            pltpu.VMEM((L, channels), jnp.bfloat16),
-            pltpu.VMEM((L, K), jnp.float32),
-            pltpu.VMEM((channels + ROWS, segment), jnp.float32),
+            pltpu.VMEM((2, channels + ROWS, segment), jnp.float32),
         ]
+        + ferry_scratch(ferry[3], ferry[0].shape[1])
         + ([] if last else [pltpu.VMEM((K, segment), jnp.float32)]),
+        input_output_aliases={10: 1 + len(outs)} if len(carried) == 2 else {},
         compiler_params=pltpu.CompilerParams(vmem_limit_bytes=VMEM_BYTES),
         name="conclude",
     )(
@@ -525,16 +500,52 @@
         limit,
         resident(state),
         *swapped,
-        far_edge,
         resident(signal),
         *following,
         resident(taps),
+        *carried,
     )
+
+
+def settle_kernel(partial_ref, first_ref, second_ref, taps, resid_out, zb, zz, fine, acc):
+    segment, channels = partial_ref.shape
+
+    def put(left, right):
+        zb[:L, :] = left[...]
+
+    zb[L:, :] = jnp.zeros((L, K), jnp.bfloat16)
+    by_side(put, first_ref, second_ref)
+    convolve(zb, L, L, taps, zz, fine, acc)
+    scale = (C * L) ** (-0.5)
+    for tile in range(channels // LANES):
+        column = slice(tile * LANES, (tile + 1) * LANES)
+        value = jnp.concatenate(
+            [partial_ref[:L, column] - scale * acc[tile], partial_ref[L:, column]], axis=0
+        )
+        resid_out[column, :] = value.T
+
+
+def settle(partial, swapped, taps):
+    segment, channels = partial.shape
+    return pl.pallas_call(
+        settle_kernel,
+        in_specs=[vmem()] * 4,
+        out_specs=vmem(),
+        out_shape=pltpu.VMEM((channels, segment), jnp.float32),
+        scratch_shapes=[
+            pltpu.VMEM((2 * L, K), jnp.bfloat16),
+            pltpu.VMEM((L + ROWS, COARSE * K), jnp.bfloat16),
+            pltpu.VMEM((2 * FINE, channels // LANES, L + ROWS, LANES), jnp.float32),
+            pltpu.VMEM((channels // LANES, L, LANES), jnp.float32),
+        ],
+        compiler_params=pltpu.CompilerParams(vmem_limit_bytes=VMEM_BYTES),
+        name="settle",
+    )(resident(partial), *swapped, resident(taps))
 
 
 def gradient_kernel(share, step, plan_ref, blocks_ref, dict_hbm, out_ref, rf, zf, rr, zz, old, sem):
     peers, rows, segment = blocks_ref.shape
-    share_rows = rows - BLOCK_ATOMS
+    share_rows = (rows - BLOCK_ATOMS) // 2
     span = peers * segment
     entries = share * L
     rows_of = pl.ds(first_row_of(plan_ref, step), BLOCK_ATOMS)
@@ -545,8 +556,12 @@
     zf[:, :LANES] = jnp.zeros((BLOCK_ATOMS, LANES), jnp.bfloat16)
     for peer in range(peers):
         column = peer * segment
-        rf[:, column : column + segment] = blocks_ref[peer, :share_rows, :]
-        zf[:, LANES + column : LANES + column + segment] = blocks_ref[peer, share_rows:, :]
+        own = blocks_ref[peer, :share_rows, :]
+        if peer:
+            spill = blocks_ref[peer - 1, share_rows : 2 * share_rows, :]
+            own = (own.astype(jnp.float32) + spill.astype(jnp.float32)).astype(jnp.bfloat16)
+        rf[:, column : column + segment] = own
+        zf[:, LANES + column : LANES + column + segment] = blocks_ref[peer, 2 * share_rows :, :]
     for lag in range(ROWS):
         rr[lag * share_rows : (lag + 1) * share_rows, :] = rf[:, lag : lag + span]
     for coarse in range(COARSE):
@@ -596,7 +611,7 @@
 
 def share_gradient(plan, step, blocks, dictionary, share):
     peers, rows, segment = blocks.shape
-    share_rows = rows - BLOCK_ATOMS
+    share_rows = (rows - BLOCK_ATOMS) // 2
     span = peers * segment
     return pl.pallas_call(
         functools.partial(gradient_kernel, share, step),
@@ -653,16 +668,22 @@
     take(1 if earlier else 0)
     old_ref, mean_ref = take(2)
     target = take(1 if earlier else 0)
-    (sem,) = take(1)
+    (sems,) = take(1)
     fetch = pltpu.make_async_copy(
-        dict_hbm.at[pl.ds(first_row_of(plan_ref, step), BLOCK_ATOMS)], old_ref, sem
+        dict_hbm.at[pl.ds(first_row_of(plan_ref, step), BLOCK_ATOMS)], old_ref, sems.at[0]
     )
     fetch.start()
-    if earlier:
-        ferry = Ferry(dict_hbm, target[0], sum(COPIED[:-1]), *take(2))
     fetch.wait()
-    if earlier:
-        ferry.turn_round()
+    stores = [
+        pltpu.make_async_copy(
+            earlier_refs[index],
+            target[0].at[pl.ds(first_row_of(plan_ref, index), BLOCK_ATOMS)],
+            sems.at[1 + index],
+        )
+        for index in range(earlier)
+    ]
+    for store in stores:
+        store.start()
     width = 9 * LANES if old_ref.shape[1] % (9 * LANES) == 0 else LANES
 
     def add(step, square):
@@ -674,19 +695,8 @@
     )
     mean_sq = jnp.sum(square, axis=1, keepdims=True) / (C * L) + tiny_eps
     mean_ref[...] = jnp.broadcast_to(mean_sq, mean_ref.shape)
-    if earlier:
-        ferry.close()
-        stores = [
-            pltpu.make_async_copy(
-                earlier_refs[index],
-                target[0].at[pl.ds(first_row_of(plan_ref, index), BLOCK_ATOMS)],
-                sem,
-            )
-            for index in range(earlier)
-        ]
-        for store in stores:
-            store.start()
-            store.wait()
+    for store in stores:
+        store.wait()
 
 
 def recall(plan, step, dictionary, when, renewed, copied):
@@ -703,8 +713,7 @@
             jax.ShapeDtypeStruct((BLOCK_ATOMS, LANES), jnp.float32),
         ]
         + [pltpu.HBM(dictionary.shape, jnp.float32)] * (earlier > 0),
-        scratch_shapes=[pltpu.SemaphoreType.DMA]
-        + (ferry_scratch(COPIED[-1], entries) if earlier else []),
+        scratch_shapes=[pltpu.SemaphoreType.DMA((1 + earlier,))],
         input_output_aliases={3 + earlier: 2} if earlier else {},
         compiler_params=pltpu.CompilerParams(vmem_limit_bytes=VMEM_BYTES),
         name="recall",
@@ -798,7 +807,8 @@
     state, signal, *edges = begin(codes_init, signal)
     following = swaps(edges)
     swapped = following
-    taps, dictionary = layout(dictionary_init, channels)
+    taps = layout(dictionary_init, channels)
+    dictionary = None
     renewed = []
     for step in range(OUTER):
         last = step + 1 == OUTER
@@ -807,26 +817,31 @@
         state, *results = iterate(
             plan, step, limit, state, swapped, signal, following, taps, atoms, ferry, peers
         )
-        edges, far_edge = results[:2], results[2]
+        edges = results[:2]
         if renewed:
-            taps, dictionary = results[3:]
-        beyond = shifted(far_edge, "tm", 2)
-        payload, *results = conclude(
-            plan, step, limit, state, swaps(edges), beyond, signal, following, taps, peers
-        )
+            taps, dictionary = results[2:]
+        ferry = (dictionary_init, dictionary, sum(COPIED[: 2 * step]), COPIED[2 * step])
+        payload, *results, first_edge, second_edge, dictionary = conclude(
+            plan, step, limit, state, swaps(edges), signal, following, taps, ferry, peers
+        )
+        edges = [first_edge, second_edge]
         blocks = lax.all_to_all(payload, "tm", 0, 0, tiled=True)
         piece = share_gradient(plan, step, blocks, dictionary_init, channels // peers)
         recalled = []
-        if not last:
+        if last:
+            edges, _ = lax.optimization_barrier((edges, piece))
+            swapped = swaps(edges)
+        else:
             recalled.extend(recall(plan, step, dictionary_init, piece, [], None))
 
         def beside(held):
             if last:
                 recalled.extend(recall(plan, step, dictionary_init, held, renewed, dictionary))
-                return recalled[0], None
-            state, *edges = results
-            edges, _ = lax.optimization_barrier((edges, held))
-            return recalled[0], swaps(edges)
+                partial, _ = lax.optimization_barrier((results[0], held))
+                residual = settle(partial, swapped, taps)
+                return (recalled[0], residual), residual
+            later, _ = lax.optimization_barrier((edges, held))
+            return recalled[0], swaps(later)
 
         held, came, extra = gather_pieces(piece, beside)
         old, mean_sq, *copied = recalled
@@ -836,8 +851,7 @@
         else:
             renewed.append(result)
             state, swapped = results[0], extra
-    residual, codes = results
-    return codes, dictionary, residual
+    return results[1], dictionary, extra
 
 
 def renew_atoms(old_atoms, across, mean_sq, spread):

time: 159 us -> 151 us (0.950)
  blocking collectives: 36.5 us -> 46.7 us
  starting transfers between devices: 35.1 us -> 26.4 us
  Pallas kernels: 71.4 us -> 65.2 us
  waiting for transfers between devices: 13 us -> 9.88 us
    all_to_all x2, blocking collectives: 36.5 us -> 46.7 us  [whole_channels(): blocks = lax.all_to_all(payload, 'tm', 0, 0, tiled=True)]
    ppermute x2 -> x0, starting transfers between devices: 9.77 us -> none  [shifted(): return lax.ppermute(shard, axis, pairs)]
    pallas_call x2, Pallas kernels: 9.18 us -> 6.28 us  [recall(): pl.pallas_call(functools.partial(recall_kernel, step, earlier), in_specs=...]
    ppermute x2 -> x0, waiting for transfers between devices: 2.85 us -> none  [shifted(): return lax.ppermute(shard, axis, pairs)]
    pallas_call x1, Pallas kernels: 11.8 us -> 9.22 us  [layout(): pl.pallas_call(layout_kernel, grid=(channels // block,), in_specs=[pl.Blo...]
    ppermute x8 -> x10, starting transfers between devices: 9.18 us -> 10.2 us  [swaps(): lax.ppermute(edge, 'tm', pair)]
    pallas_call x2 -> x3, Pallas kernels: 21.2 us -> 20.6 us  [the longest x2 17.4 us: conclude(): pl.pallas_call(functools.partial(conclude_kernel, peers, step, ferry[2]),...]
  transfers between devices with their start and end apart: 24 -> 24, of which waited for: 7 -> 8; matrix products, arithmetic and copies ran while one was open for 1% -> 1% of each run, Pallas kernels for 15% -> 14%
where the time goes in v11:
time: 151 us
  Pallas kernels  65.2 us (43%)
  blocking collectives  46.7 us (31%)
  starting transfers between devices  26.4 us (17%)
  waiting for transfers between devices  9.88 us (7%)
    all_to_all x2, blocking collectives, whole_channels(): blocks = lax.all_to_all(payload, 'tm', 0, 0, tiled=True)  46.7 us
    pallas_call x2, Pallas kernels, conclude(): pl.pallas_call(functools.partial(conclude_kernel, peers, step, ferry[2]),...  17.4 us
    pallas_call x2, Pallas kernels, iterate(): pl.pallas_call(functools.partial(iterate_kernel, peers * segment, step if...  17 us
    ppermute x14, starting transfers between devices, exchanged(): return lax.ppermute(shard, 'tm', [(i, i ^ mask) for i in range(peers)])  16.2 us
    ppermute x10, starting transfers between devices, swaps(): lax.ppermute(edge, 'tm', pair)  10.2 us
    ppermute x14, waiting for transfers between devices, exchanged(): return lax.ppermute(shard, 'tm', [(i, i ^ mask) for i in range(peers)])  9.47 us
    pallas_call x1, Pallas kernels, layout(): pl.pallas_call(layout_kernel, grid=(channels // block,), in_specs=[pl.Blo...  9.22 us
    pallas_call x2, Pallas kernels, recall(): pl.pallas_call(functools.partial(recall_kernel, step, earlier), in_specs=...  6.28 us
  transfers between devices with their start and end apart: 24, of which 8 were waited for; matrix products, arithmetic and copies ran while one was open for 1% of the time, Pallas kernels for 14%

profile of v11, /device:TPU:0, one launch (start us, length us, event | category | flops | bytes accessed | tf_op | source)
XLA Modules:
  0.0 150.9 jit_solution(14827761434504259285)
XLA Ops:
  0.7 1.1 begin.1
  2.9 9.2 %layout.1.refs_6_.refs_7_ = bf16[6,16,384,128]{3,2,1,0:T(8,128)(2,1)S(1)} custom-call(f32[128,36864]{1,0:T(8,128)} %dict_hbm.7), custom_call_target="tpu_custom_call" | custom-call | tf_op jit(solution)/shard_map/layout/pallas_call | solution.py:113
  12.2 5.3 %iterate.2 = (f32[128,128]{1,0:T(8,128)S(1)}, bf16[96,128]{1,0:T(8,128)(2,1)S(1)}, bf16[96,128]{1,0:T(8,128)(2,1)S(1)}) custom-call(s32[8]{0:T(128)S(1)} %copy-done, f32[1,128]{1,0:T(1,128)S(1)} %bitcast.13, f32[128,128]{1,0:T(8,128)S(1)} %get-tuple-element.38.refs_0_, bf16[96,512]{1,0:T(8,128)(2,1)S(1)} %collective-permute-done.refs_1_.refs_4_, ...), custom_call_target="tpu_custom_call" | custom-call | tf_op jit(solution)/shard_map/iterate/pallas_call | solution.py:361
  17.5 3.9 %collective-permute-start.2 = (bf16[96,128]{1,0:T(8,128)(2,1)S(1)}, bf16[96,128]{1,0:T(8,128)(2,1)S(1)}, u32[]{:S(2)}, u32[]{:S(2)}) collective-permute-start(bf16[96,128]{1,0:T(8,128)(2,1)S(1)} %get-tuple-element.43), channel_id=1, source_target_pairs={{0,1},{1,0},{2,3},{3,2},{4,5},{5,4},{6,7},{7,6},{8,9},{9,8},{10,11... | collective-permute-start | bytes 73736 | tf_op jit(solution)/shard_map/ppermute | solution.py:804
  22.3 8.6 %conclude.2 = (bf16[32,48,128]{2,1,0:T(8,128)(2,1)S(1)}, f32[128,128]{1,0:T(8,128)S(1)}, bf16[96,128]{1,0:T(8,128)(2,1)S(1)}, bf16[96,128]{1,0:T(8,128)(2,1)S(1)}, f32[128,36864]{1,0:T(8,128)}) custom-call(s32[8]{0:T(128)S(1)} %copy-done, f32[1,128]{1,0:T(1,128)S(1)} %bitcast.14, f32[128,128]{1,0:T(8,128)S(1)} %get-tuple-element.42.refs_0_, ...), custom_call_target="tpu_custom_call" | custom-call | tf_op jit(solution)/shard_map/conclude/pallas_call | solution.py:476
  30.9 23.9 %all_to_all.10.blocks_ref = bf16[32,48,128]{2,1,0:T(8,128)(2,1)S(1)} all-to-all(bf16[32,48,128]{2,1,0:T(8,128)(2,1)S(1)} %get-tuple-element.48), channel_id=1, replica_groups=mesh['tm'=32,'chan'=1] {'tm'}, dimensions={0} | all-to-all | bytes 786432 | tf_op jit(solution)/shard_map/all_to_all | solution.py:828
  54.8 2.8 %gradient.2.when_ref = bf16[16,1280]{1,0:T(8,128)(2,1)S(1)} custom-call(s32[8]{0:T(128)S(1)} %copy-done, bf16[32,48,128]{2,1,0:T(8,128)(2,1)S(1)} %all_to_all.10.blocks_ref, f32[128,36864]{1,0:T(8,128)} %dict_hbm.7), custom_call_target="tpu_custom_call" | custom-call | tf_op jit(solution)/shard_map/gradient/pallas_call | solution.py:616
  57.6 1.2 collective-permute-start.6
  58.8 3.3 %collective-permute-start.4 = (bf16[1,16,1280]{2,1,0:T(8,128)(2,1)S(1)}, bf16[1,16,1280]{2,1,0:T(8,128)(2,1)S(1)}, u32[]{:S(2)}, u32[]{:S(2)}) collective-permute-start(bf16[1,16,1280]{2,1,0:T(8,128)(2,1)S(1)} %bitcast.7), channel_id=1, source_target_pairs={{0,16},{1,17},{2,18},{3,19},{4,20},{5,21},{6,22},{7,23},{8,24},{9,... | collective-permute-start | bytes 122888 | tf_op jit(solution)/shard_map/ppermute | solution.py:653
  62.1 2.6 %recall.2 = (f32[16,36864]{1,0:T(8,128)S(1)}, f32[16,128]{1,0:T(8,128)S(1)}) custom-call(s32[8]{0:T(128)S(1)} %copy-done, f32[128,36864]{1,0:T(8,128)} %dict_hbm.7, bf16[16,1280]{1,0:T(8,128)(2,1)S(1)} %gradient.2.when_ref), custom_call_target="tpu_custom_call" | custom-call | tf_op jit(solution)/shard_map/recall/pallas_call | solution.py:705
  64.8 1.5 collective-permute-start.11
  68.3 5.6 %collective-permute-done.9 = bf16[4,16,1280]{2,1,0:T(8,128)(2,1)S(1)} collective-permute-done((bf16[4,16,1280]{2,1,0:T(8,128)(2,1)S(1)}, bf16[4,16,1280]{2,1,0:T(8,128)(2,1)S(1)}, u32[]{:S(2)}, u32[]{:S(2)}) %collective-permute-start.9) | collective-permute-done | bytes 163872 | tf_op jit(solution)/shard_map/ppermute | solution.py:653
  76.2 2.1 %renew.2.refs_6_.refs_0_ = f32[16,36864]{1,0:T(8,128)S(1)} custom-call(s32[8]{0:T(128)S(1)} %copy-done, bf16[16,16,1280]{2,1,0:T(8,128)(2,1)S(1)} %constant_dynamic-update-slice_fusion.held_ref, bf16[16,16,1280]{2,1,0:T(8,128)(2,1)S(1)} %collective-permute-done.12.came_ref, f32[16,36864]{1,0:T(8,128)S(1)} %get-tuple-element.51.old, ...), custom_call_target="tpu_custom_call" | custom-call | tf_op jit(solution)/shard_map/renew/pallas_call | solution.py:785
  78.3 11.8 %iterate.3 = (f32[128,128]{1,0:T(8,128)S(1)}, bf16[96,128]{1,0:T(8,128)(2,1)S(1)}, bf16[96,128]{1,0:T(8,128)(2,1)S(1)}, bf16[6,16,384,128]{3,2,1,0:T(8,128)(2,1)S(1)}, f32[128,36864]{1,0:T(8,128)}) custom-call(s32[8]{0:T(128)S(1)} %copy-done, f32[1,128]{1,0:T(1,128)S(1)} %bitcast.15, ...), custom_call_target="tpu_custom_call", output_to_operand_aliasing={{3}: (9, {}), {4}: (11, {})} | custom-call | tf_op jit(solution)/shard_map/iterate/pallas_call | solution.py:361
  90.1 2.0 %collective-permute-start.13 = (bf16[96,128]{1,0:T(8,128)(2,1)S(1)}, bf16[96,128]{1,0:T(8,128)(2,1)S(1)}, u32[]{:S(2)}, u32[]{:S(2)}) collective-permute-start(bf16[96,128]{1,0:T(8,128)(2,1)S(1)} %get-tuple-element.56), channel_id=1, source_target_pairs={{0,1},{1,0},{2,3},{3,2},{4,5},{5,4},{6,7},{7,6},{8,9},{9,8},{10,11... | collective-permute-start | bytes 73736 | tf_op jit(solution)/shard_map/ppermute | solution.py:804
  92.9 8.7 %conclude.3 = (bf16[32,48,128]{2,1,0:T(8,128)(2,1)S(1)}, f32[128,384]{1,0:T(8,128)S(1)}, f32[128,128]{1,0:T(8,128)S(1)}, bf16[96,128]{1,0:T(8,128)(2,1)S(1)}, bf...) custom-call(s32[8]{0:T(128)S(1)} %copy-done, f32[1,128]{1,0:T(1,128)S(1)} %bitcast.16, ...), custom_call_target="tpu_custom_call", output_to_operand_aliasing={{5}: (10, {})} | custom-call | tf_op jit(solution)/shard_map/conclude/pallas_call | solution.py:476
  101.7 22.9 %all_to_all.11.blocks_ref = bf16[32,48,128]{2,1,0:T(8,128)(2,1)S(1)} all-to-all(bf16[32,48,128]{2,1,0:T(8,128)(2,1)S(1)} %get-tuple-element.61), channel_id=1, replica_groups=mesh['tm'=32,'chan'=1] {'tm'}, dimensions={0} | all-to-all | bytes 786432 | tf_op jit(solution)/shard_map/all_to_all | solution.py:828
  124.6 2.8 %gradient.3 = bf16[16,1280]{1,0:T(8,128)(2,1)S(1)} custom-call(s32[8]{0:T(128)S(1)} %copy-done, bf16[32,48,128]{2,1,0:T(8,128)(2,1)S(1)} %all_to_all.11.blocks_ref, f32[128,36864]{1,0:T(8,128)} %dict_hbm.7), custom_call_target="tpu_custom_call" | custom-call | tf_op jit(solution)/shard_map/gradient/pallas_call | solution.py:616
  127.4 1.2 collective-permute-start.17
  128.6 3.3 %collective-permute-start.15 = (bf16[1,16,1280]{2,1,0:T(8,128)(2,1)S(1)}, bf16[1,16,1280]{2,1,0:T(8,128)(2,1)S(1)}, u32[]{:S(2)}, u32[]{:S(2)}) collective-permute-start(bf16[1,16,1280]{2,1,0:T(8,128)(2,1)S(1)} %bitcast.11), channel_id=1, source_target_pairs={{0,16},{1,17},{2,18},{3,19},{4,20},{5,21},{6,22},{7,23},{8,24},{9,... | collective-permute-start | bytes 122888 | tf_op jit(solution)/shard_map/ppermute | solution.py:653
  134.2 2.3 %collective-permute-start.20 = (bf16[4,16,1280]{2,1,0:T(8,128)(2,1)S(1)}, bf16[4,16,1280]{2,1,0:T(8,128)(2,1)S(1)}, u32[]{:S(2)}, u32[]{:S(2)}) collective-permute-start(bf16[4,16,1280]{2,1,0:T(8,128)(2,1)S(1)} %pad_maximum_fusion.1.when_ref), channel_id=1, source_target_pairs={{0,6},{1,7},{2,4},{3,5},{4,2},{5,3},{6,0},{7,1},{8,14},{9,15},{10,... | collective-permute-start | bytes 491528 | tf_op jit(solution)/shard_map/ppermute | solution.py:653
  137.7 3.6 %recall.3 = (f32[16,36864]{1,0:T(8,128)S(1)}, f32[16,128]{1,0:T(8,128)S(1)}, f32[128,36864]{1,0:T(8,128)}) custom-call(s32[8]{0:T(128)S(1)} %copy-done, f32[128,36864]{1,0:T(8,128)} %dict_hbm.7, bf16[4,16,1280]{2,1,0:T(8,128)(2,1)S(1)} %pad_maximum_fusion.1.when_ref, f32[16,36864]{1,0:T(8,128)S(1)} %renew.2.refs_6_.refs_0_, ...), custom_call_target="tpu_custom_call", output_to_operand_aliasing={{2}: (4, {})} | custom-call | tf_op jit(solution)/shard_map/recall/pallas_call | solution.py:705
  141.4 3.2 %settle.1 = f32[384,128]{1,0:T(8,128)S(1)} custom-call(f32[128,384]{1,0:T(8,128)S(1)} %get-tuple-element.65.partial_ref, bf16[96,128]{1,0:T(8,128)(2,1)S(1)} %collective-permute-done.21.first_ref, bf16[96,128]{1,0:T(8,128)(2,1)S(1)} %collective-permute-done.22.second_ref, bf16[6,16,384,128]{3,2,1,0:T(8,128)(2,1)S(1)} %get-tuple-element.58.refs_6_.taps), custom_call_target="tpu_custom_call" | custom-call | tf_op jit(solution)/shard_map/settle/pallas_call | solution.py:530
  147.4 3.3 %renew.3 = f32[128,36864]{1,0:T(8,128)} custom-call(s32[8]{0:T(128)S(1)} %copy-done, bf16[16,16,1280]{2,1,0:T(8,128)(2,1)S(1)} %constant_dynamic-update-slice_fusion.7.held_ref, bf16[16,16,1280]{2,1,0:T(8,128)(2,1)S(1)} %collective-permute-done.23.came_ref, f32[16,36864]{1,0:T(8,128)S(1)} %get-tuple-element.63.old, ...), custom_call_target="tpu_custom_call", output_to_operand_aliasing={{}: (5, {})} | custom-call | tf_op jit(solution)/shard_map/renew/pallas_call | solution.py:785
  (61 shorter events, 13.5 us)
Async XLA Ops:
  1.8 10.4 %collective-permute-start = (bf16[96,512]{1,0:T(8,128)(2,1)S(1)}, bf16[96,512]{1,0:T(8,128)(2,1)S(1)}, u32[]{:S(2)}, u32[]{:S(2)}) collective-permute-start(bf16[96,512]{1,0:T(8,128)(2,1)S(1)} %get-tuple-element.39), channel_id=1, source_target_pairs={{0,1},{1,0},{2,3},{3,2},{4,5},{5,4},{6,7},{7,6},{8,9},{9,8},{10,11... | collective-permute-start | bytes 294920 | tf_op jit(solution)/shard_map/ppermute | solution.py:804
  2.3 9.9 %collective-permute-start.1 = (bf16[96,512]{1,0:T(8,128)(2,1)S(1)}, bf16[96,512]{1,0:T(8,128)(2,1)S(1)}, u32[]{:S(2)}, u32[]{:S(2)}) collective-permute-start(bf16[96,512]{1,0:T(8,128)(2,1)S(1)} %get-tuple-element.40), channel_id=1, source_target_pairs={{1,2},{2,1},{3,4},{4,3},{5,6},{6,5},{7,8},{8,7},{9,10},{10,9},{11,... | collective-permute-start | bytes 294920 | tf_op jit(solution)/shard_map/ppermute | solution.py:804
  17.5 4.8 %collective-permute-start.2 = (bf16[96,128]{1,0:T(8,128)(2,1)S(1)}, bf16[96,128]{1,0:T(8,128)(2,1)S(1)}, u32[]{:S(2)}, u32[]{:S(2)}) collective-permute-start(bf16[96,128]{1,0:T(8,128)(2,1)S(1)} %get-tuple-element.43), channel_id=1, source_target_pairs={{0,1},{1,0},{2,3},{3,2},{4,5},{5,4},{6,7},{7,6},{8,9},{9,8},{10,11... | collective-permute-start | bytes 73736 | tf_op jit(solution)/shard_map/ppermute | solution.py:804
  21.4 0.9 collective-permute-start.3
  57.6 7.1 %collective-permute-start.6 = (bf16[1,16,1280]{2,1,0:T(8,128)(2,1)S(1)}, bf16[1,16,1280]{2,1,0:T(8,128)(2,1)S(1)}, u32[]{:S(2)}, u32[]{:S(2)}) collective-permute-start(bf16[1,16,1280]{2,1,0:T(8,128)(2,1)S(1)} %bitcast.5), channel_id=1, source_target_pairs={{0,24},{1,25},{2,26},{3,27},{4,28},{5,29},{6,30},{7,31},{8,16},{9,... | collective-permute-start | bytes 122888 | tf_op jit(solution)/shard_map/ppermute | solution.py:653
  58.8 6.0 %collective-permute-start.5 = (bf16[1,16,1280]{2,1,0:T(8,128)(2,1)S(1)}, bf16[1,16,1280]{2,1,0:T(8,128)(2,1)S(1)}, u32[]{:S(2)}, u32[]{:S(2)}) collective-permute-start(bf16[1,16,1280]{2,1,0:T(8,128)(2,1)S(1)} %bitcast.6), channel_id=1, source_target_pairs={{0,8},{1,9},{2,10},{3,11},{4,12},{5,13},{6,14},{7,15},{8,0},{9,1},... | collective-permute-start | bytes 122888 | tf_op jit(solution)/shard_map/ppermute | solution.py:653
  58.8 6.0 %collective-permute-start.4 = (bf16[1,16,1280]{2,1,0:T(8,128)(2,1)S(1)}, bf16[1,16,1280]{2,1,0:T(8,128)(2,1)S(1)}, u32[]{:S(2)}, u32[]{:S(2)}) collective-permute-start(bf16[1,16,1280]{2,1,0:T(8,128)(2,1)S(1)} %bitcast.7), channel_id=1, source_target_pairs={{0,16},{1,17},{2,18},{3,19},{4,20},{5,21},{6,22},{7,23},{8,24},{9,... | collective-permute-start | bytes 122888 | tf_op jit(solution)/shard_map/ppermute | solution.py:653
  64.8 9.3 %collective-permute-start.11 = (bf16[4,16,1280]{2,1,0:T(8,128)(2,1)S(1)}, bf16[4,16,1280]{2,1,0:T(8,128)(2,1)S(1)}, u32[]{:S(2)}, u32[]{:S(2)}) collective-permute-start(bf16[4,16,1280]{2,1,0:T(8,128)(2,1)S(1)} %pad_maximum_fusion), channel_id=1, source_target_pairs={{0,6},{1,7},{2,4},{3,5},{4,2},{5,3},{6,0},{7,1},{8,14},{9,15},{10,... | collective-permute-start | bytes 491528 | tf_op jit(solution)/shard_map/ppermute | solution.py:653
  66.2 7.8 %collective-permute-start.10 = (bf16[4,16,1280]{2,1,0:T(8,128)(2,1)S(1)}, bf16[4,16,1280]{2,1,0:T(8,128)(2,1)S(1)}, u32[]{:S(2)}, u32[]{:S(2)}) collective-permute-start(bf16[4,16,1280]{2,1,0:T(8,128)(2,1)S(1)} %pad_maximum_fusion), channel_id=1, source_target_pairs={{0,2},{1,3},{2,0},{3,1},{4,6},{5,7},{6,4},{7,5},{8,10},{9,11},{10,... | collective-permute-start | bytes 491528 | tf_op jit(solution)/shard_map/ppermute | solution.py:653
  67.3 6.7 %collective-permute-start.9 = (bf16[4,16,1280]{2,1,0:T(8,128)(2,1)S(1)}, bf16[4,16,1280]{2,1,0:T(8,128)(2,1)S(1)}, u32[]{:S(2)}, u32[]{:S(2)}) collective-permute-start(bf16[4,16,1280]{2,1,0:T(8,128)(2,1)S(1)} %pad_maximum_fusion), channel_id=1, source_target_pairs={{0,4},{1,5},{2,6},{3,7},{4,0},{5,1},{6,2},{7,3},{8,12},{9,13},{10,... | collective-permute-start | bytes 491528 | tf_op jit(solution)/shard_map/ppermute | solution.py:653
  74.1 2.2 %collective-permute-start.12 = (bf16[16,16,1280]{2,1,0:T(8,128)(2,1)S(1)}, bf16[16,16,1280]{2,1,0:T(8,128)(2,1)S(1)}, u32[]{:S(2)}, u32[]{:S(2)}) collective-permute-start(bf16[16,16,1280]{2,1,0:T(8,128)(2,1)S(1)} %constant_dynamic-update-slice_fusion.held_ref), channel_id=1, source_target_pairs={{0,1},{1,0},{2,3},{3,2},{4,5},{5,4},{6,7},{7,6},{8,9},{9,8},{10,11... | collective-permute-start | bytes 1966088 | tf_op jit(solution)/shard_map/ppermute | solution.py:653
  74.1 4.2 %collective-permute-start.7 = (bf16[96,128]{1,0:T(8,128)(2,1)S(1)}, bf16[96,128]{1,0:T(8,128)(2,1)S(1)}, u32[]{:S(2)}, u32[]{:S(2)}) collective-permute-start(bf16[96,128]{1,0:T(8,128)(2,1)S(1)} %get-tuple-element.49), channel_id=1, source_target_pairs={{0,1},{1,0},{2,3},{3,2},{4,5},{5,4},{6,7},{7,6},{8,9},{9,8},{10,11... | collective-permute-start | bytes 73736 | tf_op jit(solution)/shard_map/ppermute | solution.py:804
  74.6 3.7 %collective-permute-start.8 = (bf16[96,128]{1,0:T(8,128)(2,1)S(1)}, bf16[96,128]{1,0:T(8,128)(2,1)S(1)}, u32[]{:S(2)}, u32[]{:S(2)}) collective-permute-start(bf16[96,128]{1,0:T(8,128)(2,1)S(1)} %get-tuple-element.50), channel_id=1, source_target_pairs={{1,2},{2,1},{3,4},{4,3},{5,6},{6,5},{7,8},{8,7},{9,10},{10,9},{11,... | collective-permute-start | bytes 73736 | tf_op jit(solution)/shard_map/ppermute | solution.py:804
  90.1 2.8 %collective-permute-start.13 = (bf16[96,128]{1,0:T(8,128)(2,1)S(1)}, bf16[96,128]{1,0:T(8,128)(2,1)S(1)}, u32[]{:S(2)}, u32[]{:S(2)}) collective-permute-start(bf16[96,128]{1,0:T(8,128)(2,1)S(1)} %get-tuple-element.56), channel_id=1, source_target_pairs={{0,1},{1,0},{2,3},{3,2},{4,5},{5,4},{6,7},{7,6},{8,9},{9,8},{10,11... | collective-permute-start | bytes 73736 | tf_op jit(solution)/shard_map/ppermute | solution.py:804
  92.1 0.9 collective-permute-start.14
  127.4 6.2 %collective-permute-start.17 = (bf16[1,16,1280]{2,1,0:T(8,128)(2,1)S(1)}, bf16[1,16,1280]{2,1,0:T(8,128)(2,1)S(1)}, u32[]{:S(2)}, u32[]{:S(2)}) collective-permute-start(bf16[1,16,1280]{2,1,0:T(8,128)(2,1)S(1)} %bitcast.9), channel_id=1, source_target_pairs={{0,24},{1,25},{2,26},{3,27},{4,28},{5,29},{6,30},{7,31},{8,16},{9,... | collective-permute-start | bytes 122888 | tf_op jit(solution)/shard_map/ppermute | solution.py:653
  128.6 5.0 %collective-permute-start.16 = (bf16[1,16,1280]{2,1,0:T(8,128)(2,1)S(1)}, bf16[1,16,1280]{2,1,0:T(8,128)(2,1)S(1)}, u32[]{:S(2)}, u32[]{:S(2)}) collective-permute-start(bf16[1,16,1280]{2,1,0:T(8,128)(2,1)S(1)} %bitcast.10), channel_id=1, source_target_pairs={{0,8},{1,9},{2,10},{3,11},{4,12},{5,13},{6,14},{7,15},{8,0},{9,1},... | collective-permute-start | bytes 122888 | tf_op jit(solution)/shard_map/ppermute | solution.py:653
  128.6 5.6 %collective-permute-start.15 = (bf16[1,16,1280]{2,1,0:T(8,128)(2,1)S(1)}, bf16[1,16,1280]{2,1,0:T(8,128)(2,1)S(1)}, u32[]{:S(2)}, u32[]{:S(2)}) collective-permute-start(bf16[1,16,1280]{2,1,0:T(8,128)(2,1)S(1)} %bitcast.11), channel_id=1, source_target_pairs={{0,16},{1,17},{2,18},{3,19},{4,20},{5,21},{6,22},{7,23},{8,24},{9,... | collective-permute-start | bytes 122888 | tf_op jit(solution)/shard_map/ppermute | solution.py:653
  131.9 9.5 %collective-permute-start.21 = (bf16[96,128]{1,0:T(8,128)(2,1)S(1)}, bf16[96,128]{1,0:T(8,128)(2,1)S(1)}, u32[]{:S(2)}, u32[]{:S(2)}) collective-permute-start(bf16[96,128]{1,0:T(8,128)(2,1)S(1)} %get-tuple-element.68), channel_id=1, source_target_pairs={{0,1},{1,0},{2,3},{3,2},{4,5},{5,4},{6,7},{7,6},{8,9},{9,8},{10,11... | collective-permute-start | bytes 73736 | tf_op jit(solution)/shard_map/ppermute | solution.py:804
  131.9 9.5 %collective-permute-start.22 = (bf16[96,128]{1,0:T(8,128)(2,1)S(1)}, bf16[96,128]{1,0:T(8,128)(2,1)S(1)}, u32[]{:S(2)}, u32[]{:S(2)}) collective-permute-start(bf16[96,128]{1,0:T(8,128)(2,1)S(1)} %get-tuple-element.69), channel_id=1, source_target_pairs={{1,2},{2,1},{3,4},{4,3},{5,6},{6,5},{7,8},{8,7},{9,10},{10,9},{11,... | collective-permute-start | bytes 73736 | tf_op jit(solution)/shard_map/ppermute | solution.py:804
  134.2 11.0 %collective-permute-start.20 = (bf16[4,16,1280]{2,1,0:T(8,128)(2,1)S(1)}, bf16[4,16,1280]{2,1,0:T(8,128)(2,1)S(1)}, u32[]{:S(2)}, u32[]{:S(2)}) collective-permute-start(bf16[4,16,1280]{2,1,0:T(8,128)(2,1)S(1)} %pad_maximum_fusion.1.when_ref), channel_id=1, source_target_pairs={{0,6},{1,7},{2,4},{3,5},{4,2},{5,3},{6,0},{7,1},{8,14},{9,15},{10,... | collective-permute-start | bytes 491528 | tf_op jit(solution)/shard_map/ppermute | solution.py:653
  136.5 8.7 %collective-permute-start.19 = (bf16[4,16,1280]{2,1,0:T(8,128)(2,1)S(1)}, bf16[4,16,1280]{2,1,0:T(8,128)(2,1)S(1)}, u32[]{:S(2)}, u32[]{:S(2)}) collective-permute-start(bf16[4,16,1280]{2,1,0:T(8,128)(2,1)S(1)} %pad_maximum_fusion.1.when_ref), channel_id=1, source_target_pairs={{0,2},{1,3},{2,0},{3,1},{4,6},{5,7},{6,4},{7,5},{8,10},{9,11},{10,... | collective-permute-start | bytes 491528 | tf_op jit(solution)/shard_map/ppermute | solution.py:653
  137.4 7.7 %collective-permute-start.18 = (bf16[4,16,1280]{2,1,0:T(8,128)(2,1)S(1)}, bf16[4,16,1280]{2,1,0:T(8,128)(2,1)S(1)}, u32[]{:S(2)}, u32[]{:S(2)}) collective-permute-start(bf16[4,16,1280]{2,1,0:T(8,128)(2,1)S(1)} %pad_maximum_fusion.1.when_ref), channel_id=1, source_target_pairs={{0,4},{1,5},{2,6},{3,7},{4,0},{5,1},{6,2},{7,3},{8,12},{9,13},{10,... | collective-permute-start | bytes 491528 | tf_op jit(solution)/shard_map/ppermute | solution.py:653
  145.2 2.2 %collective-permute-start.23 = (bf16[16,16,1280]{2,1,0:T(8,128)(2,1)S(1)}, bf16[16,16,1280]{2,1,0:T(8,128)(2,1)S(1)}, u32[]{:S(2)}, u32[]{:S(2)}) collective-permute-start(bf16[16,16,1280]{2,1,0:T(8,128)(2,1)S(1)} %constant_dynamic-update-slice_fusion.7.held_ref), channel_id=1, source_target_pairs={{0,1},{1,0},{2,3},{3,2},{4,5},{5,4},{6,7},{7,6},{8,9},{9,8},{10,11... | collective-permute-start | bytes 1966088 | tf_op jit(solution)/shard_map/ppermute | solution.py:653
  (2 other events, 23.1 us)

commit v12 on v11

--- a/solution.py
+++ b/solution.py
@@ -405,7 +405,7 @@
     (payload_out,) = take(1)
     state_out, partial_out, codes_out = (None, *take(2)) if last else (*take(1), None, None)
     *edges, target = take(3)
-    zb, rb, zz, rr, fine, acc, beyond, tall = take(8)
+    zb, rb, zz, rr, fine, acc, beyond, tall, packed = take(9)
     ferry = Ferry(source, target, copied, *take(2))
     if not last:
         (codes_out,) = take(1)
@@ -438,10 +438,8 @@
     zb[reach:, :] = jnp.zeros((L, K), jnp.bfloat16)
     convolve(zb, L, reach, taps, zz, fine, acc)
     scale = (C * L) ** (-0.5)
-    block = codes_out[pl.ds(first_row_of(plan_ref, step), BLOCK_ATOMS), :].astype(jnp.bfloat16)
+    block = codes_out[pl.ds(first_row_of(plan_ref, step), BLOCK_ATOMS), :]
     share = channels // peers
-    share_rows = (payload_out.shape[1] - BLOCK_ATOMS) // 2
-    unused = jnp.zeros((tall.shape[1] - channels, segment), jnp.float32)
     for tile in range(channels // LANES):
         column = slice(tile * LANES, (tile + 1) * LANES)
         value = signal_ref[:, column].astype(jnp.float32) - scale * acc[tile, :segment, :]
@@ -452,20 +450,19 @@
             [-scale * acc[tile, segment:reach, :], jnp.zeros((segment - L, LANES), jnp.float32)], axis=0
         )
         tall[1, column, :] = spill.T
-    for part in range(2):
-        tall[part, channels:, :] = unused
     for peer in range(peers):
         for part in range(2):
-            rows = tall[part, peer * share : peer * share + share_rows, :]
-            payload_out[peer, part * share_rows : (part + 1) * share_rows, :] = rows.astype(jnp.bfloat16)
-        payload_out[peer, 2 * share_rows :, :] = block
+            packed[peer, part * share : (part + 1) * share, :] = tall[
+                part, peer * share : (peer + 1) * share, :
+            ]
+        packed[peer, 2 * share :, :] = block
+    payload_out[...] = packed[...].astype(jnp.bfloat16)
     ferry.close()
 
 
 def conclude(plan, step, limit, state, swapped, signal, following, taps, ferry, peers):
     segment, channels = signal.shape
     share = channels // peers
-    share_rows = -(-share // ROWS) * ROWS
     last = step + 1 == OUTER
     carried = [far(value) for value in ferry[:2] if value is not None]
     reach = segment + L
@@ -477,7 +474,7 @@
         functools.partial(conclude_kernel, peers, step, ferry[2]),
         in_specs=[scalars()] + [vmem()] * 8 + [hbm()] * len(carried),
         out_specs=[vmem()] * (1 + len(outs)) + [hbm()],
-        out_shape=[jax.ShapeDtypeStruct((peers, 2 * share_rows + BLOCK_ATOMS, segment), jnp.bfloat16)]
+        out_shape=[jax.ShapeDtypeStruct((peers, 2 * share + BLOCK_ATOMS, segment), jnp.bfloat16)]
         + outs
         + [pltpu.HBM(ferry[0].shape, jnp.float32)],
         scratch_shapes=[
@@ -488,7 +485,8 @@
             pltpu.VMEM((2 * FINE, channels // LANES, reach + ROWS, LANES), jnp.float32),
             pltpu.VMEM((channels // LANES, reach, LANES), jnp.float32),
             pltpu.VMEM((L, channels), jnp.bfloat16),
-            pltpu.VMEM((2, channels + ROWS, segment), jnp.float32),
+            pltpu.VMEM((2, channels, segment), jnp.float32),
+            pltpu.VMEM((peers, 2 * share + BLOCK_ATOMS, segment), jnp.float32),
         ]
         + ferry_scratch(ferry[3], ferry[0].shape[1])
         + ([] if last else [pltpu.VMEM((K, segment), jnp.float32)]),
@@ -507,8 +505,19 @@
     )
 
 
-def settle_kernel(partial_ref, first_ref, second_ref, taps, resid_out, zb, zz, fine, acc):
+def settle_kernel(earlier, plan_ref, partial_ref, first_ref, second_ref, taps, *refs):
+    take = taker(refs)
+    atoms = take(earlier)
+    _, resid_out, dict_out, zb, zz, fine, acc, sems = refs[earlier:]
     segment, channels = partial_ref.shape
+    stores = [
+        pltpu.make_async_copy(
+            atoms[step], dict_out.at[pl.ds(first_row_of(plan_ref, step), BLOCK_ATOMS)], sems.at[step]
+        )
+        for step in range(earlier)
+    ]
+    for store in stores:
+        store.start()
 
     def put(left, right):
         zb[:L, :] = left[...]
@@ -523,29 +532,44 @@
             [partial_ref[:L, column] - scale * acc[tile], partial_ref[L:, column]], axis=0
         )
         resid_out[column, :] = value.T
-
-
-def settle(partial, swapped, taps):
+    for store in stores:
+        store.wait()
+
+
+def settle(plan, partial, swapped, taps, renewed, dictionary):
     segment, channels = partial.shape
+    earlier = len(renewed)
     return pl.pallas_call(
-        settle_kernel,
-        in_specs=[vmem()] * 4,
-        out_specs=vmem(),
-        out_shape=pltpu.VMEM((channels, segment), jnp.float32),
+        functools.partial(settle_kernel, earlier),
+        in_specs=[scalars()] + [vmem()] * (4 + earlier) + [hbm()],
+        out_specs=[vmem(), hbm()],
+        out_shape=[
+            pltpu.VMEM((channels, segment), jnp.float32),
+            pltpu.HBM(dictionary.shape, jnp.float32),
+        ],
         scratch_shapes=[
             pltpu.VMEM((2 * L, K), jnp.bfloat16),
             pltpu.VMEM((L + ROWS, COARSE * K), jnp.bfloat16),
             pltpu.VMEM((2 * FINE, channels // LANES, L + ROWS, LANES), jnp.float32),
             pltpu.VMEM((channels // LANES, L, LANES), jnp.float32),
+            pltpu.SemaphoreType.DMA((earlier,)),
         ],
+        input_output_aliases={5 + earlier: 1},
         compiler_params=pltpu.CompilerParams(vmem_limit_bytes=VMEM_BYTES),
         name="settle",
-    )(resident(partial), *swapped, resident(taps))
-
-
-def gradient_kernel(share, step, plan_ref, blocks_ref, dict_hbm, out_ref, rf, zf, rr, zz, old, sem):
+    )(
+        plan,
+        resident(partial),
+        *swapped,
+        resident(taps),
+        *[resident(value) for value in renewed],
+        far(dictionary),
+    )
+
+
+def gradient_kernel(share, step, plan_ref, blocks_ref, dict_hbm, out_ref, packed, rf, zf, rr, zz, old, sem):
     peers, rows, segment = blocks_ref.shape
-    share_rows = (rows - BLOCK_ATOMS) // 2
+    share_rows = rf.shape[0]
     span = peers * segment
     entries = share * L
     rows_of = pl.ds(first_row_of(plan_ref, step), BLOCK_ATOMS)
@@ -554,14 +578,16 @@
     fetch.start()
     rf[:, span:] = jnp.zeros((share_rows, LANES), jnp.bfloat16)
     zf[:, :LANES] = jnp.zeros((BLOCK_ATOMS, LANES), jnp.bfloat16)
+    packed[...] = blocks_ref[...].astype(jnp.float32)
     for peer in range(peers):
         column = peer * segment
-        own = blocks_ref[peer, :share_rows, :]
+        own = packed[peer, :share_rows, :]
         if peer:
-            spill = blocks_ref[peer - 1, share_rows : 2 * share_rows, :]
-            own = (own.astype(jnp.float32) + spill.astype(jnp.float32)).astype(jnp.bfloat16)
-        rf[:, column : column + segment] = own
-        zf[:, LANES + column : LANES + column + segment] = blocks_ref[peer, 2 * share_rows :, :]
+            own += packed[peer - 1, share : share + share_rows, :]
+        rf[:, column : column + segment] = own.astype(jnp.bfloat16)
+        zf[:, LANES + column : LANES + column + segment] = packed[peer, 2 * share :, :].astype(
+            jnp.bfloat16
+        )
     for lag in range(ROWS):
         rr[lag * share_rows : (lag + 1) * share_rows, :] = rf[:, lag : lag + span]
     for coarse in range(COARSE):
@@ -611,13 +637,14 @@
 
 def share_gradient(plan, step, blocks, dictionary, share):
     peers, rows, segment = blocks.shape
-    share_rows = (rows - BLOCK_ATOMS) // 2
+    share_rows = -(-share // ROWS) * ROWS
     span = peers * segment
     return pl.pallas_call(
         functools.partial(gradient_kernel, share, step),
         in_specs=[scalars(), vmem(), hbm()],
         out_shape=jax.ShapeDtypeStruct((BLOCK_ATOMS, share * L + LANES), jnp.bfloat16),
         scratch_shapes=[
+            pltpu.VMEM(blocks.shape, jnp.float32),
             pltpu.VMEM((share_rows, span + LANES), jnp.bfloat16),
             pltpu.VMEM((BLOCK_ATOMS, LANES + span), jnp.bfloat16),
             pltpu.VMEM((ROWS * share_rows, span), jnp.bfloat16),
@@ -661,69 +688,47 @@
     return held, exchanged(ready, 1), extra
 
 
-def recall_kernel(step, earlier, plan_ref, dict_hbm, when_ref, *refs):
+def recall_kernel(plan_ref, dict_hbm, when_ref, *refs):
     del when_ref
     take = taker(refs)
-    earlier_refs = take(earlier)
-    take(1 if earlier else 0)
-    old_ref, mean_ref = take(2)
-    target = take(1 if earlier else 0)
+    olds, means = take(OUTER), take(OUTER)
     (sems,) = take(1)
-    fetch = pltpu.make_async_copy(
-        dict_hbm.at[pl.ds(first_row_of(plan_ref, step), BLOCK_ATOMS)], old_ref, sems.at[0]
-    )
-    fetch.start()
-    fetch.wait()
-    stores = [
+    entries = olds[0].shape[1]
+    fetches = [
         pltpu.make_async_copy(
-            earlier_refs[index],
-            target[0].at[pl.ds(first_row_of(plan_ref, index), BLOCK_ATOMS)],
-            sems.at[1 + index],
-        )
-        for index in range(earlier)
+            dict_hbm.at[pl.ds(first_row_of(plan_ref, step), BLOCK_ATOMS)], olds[step], sems.at[step]
+        )
+        for step in range(OUTER)
     ]
-    for store in stores:
-        store.start()
-    width = 9 * LANES if old_ref.shape[1] % (9 * LANES) == 0 else LANES
-
-    def add(step, square):
-        before = old_ref[:, pl.ds(pl.multiple_of(step * width, LANES), width)]
-        return square + before * before
-
-    square = lax.fori_loop(
-        0, old_ref.shape[1] // width, add, jnp.zeros((BLOCK_ATOMS, width), jnp.float32)
-    )
-    mean_sq = jnp.sum(square, axis=1, keepdims=True) / (C * L) + tiny_eps
-    mean_ref[...] = jnp.broadcast_to(mean_sq, mean_ref.shape)
-    for store in stores:
-        store.wait()
-
-
-def recall(plan, step, dictionary, when, renewed, copied):
+    for fetch in fetches:
+        fetch.start()
+    width = 9 * LANES if entries % (9 * LANES) == 0 else LANES
+    for fetch, old_ref, mean_ref in zip(fetches, olds, means):
+        fetch.wait()
+
+        def add(step, square):
+            before = old_ref[:, pl.ds(pl.multiple_of(step * width, LANES), width)]
+            return square + before * before
+
+        zeros = jnp.zeros((BLOCK_ATOMS, width), jnp.float32)
+        square = lax.fori_loop(0, entries // width, add, zeros)
+        mean_sq = jnp.sum(square, axis=1, keepdims=True) / (C * L) + tiny_eps
+        mean_ref[...] = jnp.broadcast_to(mean_sq, mean_ref.shape)
+
+
+def recall(plan, dictionary, when):
     entries = dictionary.shape[1]
-    earlier = len(renewed)
-    return pl.pallas_call(
-        functools.partial(recall_kernel, step, earlier),
-        in_specs=[scalars(), hbm(), pl.BlockSpec(memory_space=pl.ANY)]
-        + [vmem()] * earlier
-        + [hbm()] * (earlier > 0),
-        out_specs=[vmem(), vmem()] + [hbm()] * (earlier > 0),
-        out_shape=[
-            pltpu.VMEM((BLOCK_ATOMS, entries), jnp.float32),
-            jax.ShapeDtypeStruct((BLOCK_ATOMS, LANES), jnp.float32),
-        ]
-        + [pltpu.HBM(dictionary.shape, jnp.float32)] * (earlier > 0),
-        scratch_shapes=[pltpu.SemaphoreType.DMA((1 + earlier,))],
-        input_output_aliases={3 + earlier: 2} if earlier else {},
+    results = pl.pallas_call(
+        recall_kernel,
+        in_specs=[scalars(), hbm(), pl.BlockSpec(memory_space=pl.ANY)],
+        out_specs=[vmem()] * (2 * OUTER),
+        out_shape=[pltpu.VMEM((BLOCK_ATOMS, entries), jnp.float32)] * OUTER
+        + [pltpu.VMEM((BLOCK_ATOMS, LANES), jnp.float32)] * OUTER,
+        scratch_shapes=[pltpu.SemaphoreType.DMA((OUTER,))],
         compiler_params=pltpu.CompilerParams(vmem_limit_bytes=VMEM_BYTES),
         name="recall",
-    )(
-        plan,
-        far(dictionary),
-        when,
-        *[resident(value) for value in renewed],
-        *([far(copied)] if earlier else []),
-    )
+    )(plan, far(dictionary), when)
+    return list(zip(results[:OUTER], results[OUTER:]))
 
 
 def renew_kernel(plan_step, plan_ref, held_ref, came_ref, old, mean_ref, *refs):
@@ -791,7 +796,7 @@
         input_output_aliases={5: 0} if last else {},
         compiler_params=pltpu.CompilerParams(vmem_limit_bytes=VMEM_BYTES),
         name="renew",
-    )(plan, held, came, resident(old), mean_sq, *([far(dictionary)] if last else []))
+    )(plan, held, came, resident(old), resident(mean_sq), *([far(dictionary)] if last else []))
 
 
 def whole_channels(signal, codes_init, dictionary_init, threshold, plan):
@@ -827,31 +832,25 @@
         edges = [first_edge, second_edge]
         blocks = lax.all_to_all(payload, "tm", 0, 0, tiled=True)
         piece = share_gradient(plan, step, blocks, dictionary_init, channels // peers)
-        recalled = []
+        edges, _ = lax.optimization_barrier((edges, piece))
+        swapped = swaps(edges)
+
+        def beside(held):
+            if not last:
+                recalled = recall(plan, dictionary_init, held)
+                return (recalled[0][0], swapped), recalled
+            partial, _ = lax.optimization_barrier((results[0], held))
+            settled = settle(plan, partial, swapped, taps, renewed, dictionary)
+            return settled[0], settled
+
+        held, came, extra = gather_pieces(piece, beside)
         if last:
-            edges, _ = lax.optimization_barrier((edges, piece))
-            swapped = swaps(edges)
+            residual, dictionary = extra
+            dictionary = renew(plan, step, held, came, *recalled[step], dictionary)
         else:
-            recalled.extend(recall(plan, step, dictionary_init, piece, [], None))
-
-        def beside(held):
-            if last:
-                recalled.extend(recall(plan, step, dictionary_init, held, renewed, dictionary))
-                partial, _ = lax.optimization_barrier((results[0], held))
-                residual = settle(partial, swapped, taps)
-                return (recalled[0], residual), residual
-            later, _ = lax.optimization_barrier((edges, held))
-            return recalled[0], swaps(later)
-
-        held, came, extra = gather_pieces(piece, beside)
-        old, mean_sq, *copied = recalled
-        result = renew(plan, step, held, came, old, mean_sq, copied[0] if last else None)
-        if last:
-            dictionary = result
-        else:
-            renewed.append(result)
-            state, swapped = results[0], extra
-    return results[1], dictionary, extra
+            recalled, state = extra, results[0]
+            renewed.append(renew(plan, step, held, came, *recalled[step], None))
+    return results[1], dictionary, residual
 
 
 def renew_atoms(old_atoms, across, mean_sq, spread):

time: 151 us -> 148 us (0.980)
  waiting for transfers between devices: 9.88 us -> 14 us
  blocking collectives: 46.7 us -> 43.8 us
  starting transfers between devices: 26.4 us -> 24.1 us
  Pallas kernels: 65.2 us -> 63 us
    ppermute x14, waiting for transfers between devices: 9.47 us -> 13.4 us  [exchanged(): return lax.ppermute(shard, 'tm', [(i, i ^ mask) for i in range(peers)])]
    all_to_all x2, blocking collectives: 46.7 us -> 43.8 us  [whole_channels(): blocks = lax.all_to_all(payload, 'tm', 0, 0, tiled=True)]
    pallas_call x3 -> x2, Pallas kernels: 9.49 us -> 7.13 us  [the longest x1 3.77 us: settle(): pl.pallas_call(functools.partial(settle_kernel, earlier), in_specs=[scala...]
    ppermute x10, starting transfers between devices: 10.2 us -> 7.94 us  [swaps(): lax.ppermute(edge, 'tm', pair)]
  transfers between devices with their start and end apart: 24 -> 24, of which waited for: 8 -> 10; matrix products, arithmetic and copies ran while one was open for 1% -> 1% of each run, Pallas kernels for 14% -> 11%
where the time goes in v12:
time: 148 us; the launch traced here: 147 us
  Pallas kernels  63 us (43%)
  blocking collectives  43.8 us (30%)
  starting transfers between devices  24.1 us (16%)
  waiting for transfers between devices  14 us (9%)
    all_to_all x2, blocking collectives, whole_channels(): blocks = lax.all_to_all(payload, 'tm', 0, 0, tiled=True)  43.8 us
    pallas_call x2, Pallas kernels, conclude(): pl.pallas_call(functools.partial(conclude_kernel, peers, step, ferry[2]),...  17.4 us
    pallas_call x2, Pallas kernels, iterate(): pl.pallas_call(functools.partial(iterate_kernel, peers * segment, step if...  17 us
    ppermute x14, starting transfers between devices, exchanged(): return lax.ppermute(shard, 'tm', [(i, i ^ mask) for i in range(peers)])  16.2 us
    ppermute x14, waiting for transfers between devices, exchanged(): return lax.ppermute(shard, 'tm', [(i, i ^ mask) for i in range(peers)])  13.4 us
    pallas_call x1, Pallas kernels, layout(): pl.pallas_call(layout_kernel, grid=(channels // block,), in_specs=[pl.Blo...  9.22 us
    ppermute x10, starting transfers between devices, swaps(): lax.ppermute(edge, 'tm', pair)  7.94 us
    pallas_call x2, Pallas kernels, share_gradient(): pl.pallas_call(functools.partial(gradient_kernel, share, step), in_specs=...  5.71 us
  transfers between devices with their start and end apart: 24, of which 10 were waited for; matrix products, arithmetic and copies ran while one was open for 1% of the time, Pallas kernels for 11%

profile of v12, /device:TPU:0, one launch (start us, length us, event | category | flops | bytes accessed | tf_op | source)
XLA Modules:
  0.0 147.4 jit_solution(736897447184904960)
XLA Ops:
  2.9 9.2 %layout.1.refs_6_.refs_7_ = bf16[6,16,384,128]{3,2,1,0:T(8,128)(2,1)S(1)} custom-call(f32[128,36864]{1,0:T(8,128)} %dict_hbm.5), custom_call_target="tpu_custom_call" | custom-call | tf_op jit(solution)/shard_map/layout/pallas_call | solution.py:113
  12.2 5.3 %iterate.2 = (f32[128,128]{1,0:T(8,128)S(1)}, bf16[96,128]{1,0:T(8,128)(2,1)S(1)}, bf16[96,128]{1,0:T(8,128)(2,1)S(1)}) custom-call(s32[8]{0:T(128)S(1)} %copy-done, f32[1,128]{1,0:T(1,128)S(1)} %bitcast.13, f32[128,128]{1,0:T(8,128)S(1)} %get-tuple-element.39.refs_0_, bf16[96,512]{1,0:T(8,128)(2,1)S(1)} %collective-permute-done.refs_1_.refs_4_, ...), custom_call_target="tpu_custom_call" | custom-call | tf_op jit(solution)/shard_map/iterate/pallas_call | solution.py:361
  17.5 3.9 %collective-permute-start.2 = (bf16[96,128]{1,0:T(8,128)(2,1)S(1)}, bf16[96,128]{1,0:T(8,128)(2,1)S(1)}, u32[]{:S(2)}, u32[]{:S(2)}) collective-permute-start(bf16[96,128]{1,0:T(8,128)(2,1)S(1)} %get-tuple-element.44), channel_id=1, source_target_pairs={{0,1},{1,0},{2,3},{3,2},{4,5},{5,4},{6,7},{7,6},{8,9},{9,8},{10,11... | collective-permute-start | bytes 73736 | tf_op jit(solution)/shard_map/ppermute | solution.py:809
  22.3 8.6 %conclude.2 = (bf16[32,40,128]{2,1,0:T(8,128)(2,1)S(1)}, f32[128,128]{1,0:T(8,128)S(1)}, bf16[96,128]{1,0:T(8,128)(2,1)S(1)}, bf16[96,128]{1,0:T(8,128)(2,1)S(1)}, f32[128,36864]{1,0:T(8,128)}) custom-call(s32[8]{0:T(128)S(1)} %copy-done, f32[1,128]{1,0:T(1,128)S(1)} %bitcast.14, f32[128,128]{1,0:T(8,128)S(1)} %get-tuple-element.43.refs_0_, ...), custom_call_target="tpu_custom_call" | custom-call | tf_op jit(solution)/shard_map/conclude/pallas_call | solution.py:473
  30.9 22.7 %all_to_all.10.blocks_ref = bf16[32,40,128]{2,1,0:T(8,128)(2,1)S(1)} all-to-all(bf16[32,40,128]{2,1,0:T(8,128)(2,1)S(1)} %get-tuple-element.49), channel_id=1, replica_groups=mesh['tm'=32,'chan'=1] {'tm'}, dimensions={0} | all-to-all | bytes 655360 | tf_op jit(solution)/shard_map/all_to_all | solution.py:833
  53.6 2.9 %gradient.2 = bf16[16,1280]{1,0:T(8,128)(2,1)S(1)} custom-call(s32[8]{0:T(128)S(1)} %copy-done, bf16[32,40,128]{2,1,0:T(8,128)(2,1)S(1)} %all_to_all.10.blocks_ref, f32[128,36864]{1,0:T(8,128)} %dict_hbm.5), custom_call_target="tpu_custom_call" | custom-call | tf_op jit(solution)/shard_map/gradient/pallas_call | solution.py:642
  56.4 1.2 collective-permute-start.8
  57.7 3.2 %collective-permute-start.6 = (bf16[1,16,1280]{2,1,0:T(8,128)(2,1)S(1)}, bf16[1,16,1280]{2,1,0:T(8,128)(2,1)S(1)}, u32[]{:S(2)}, u32[]{:S(2)}) collective-permute-start(bf16[1,16,1280]{2,1,0:T(8,128)(2,1)S(1)} %bitcast.7), channel_id=1, source_target_pairs={{0,16},{1,17},{2,18},{3,19},{4,20},{5,21},{6,22},{7,23},{8,24},{9,... | collective-permute-start | bytes 122888 | tf_op jit(solution)/shard_map/ppermute | solution.py:680
  61.6 1.2 collective-permute-done.8
  63.2 2.2 %collective-permute-start.11 = (bf16[4,16,1280]{2,1,0:T(8,128)(2,1)S(1)}, bf16[4,16,1280]{2,1,0:T(8,128)(2,1)S(1)}, u32[]{:S(2)}, u32[]{:S(2)}) collective-permute-start(bf16[4,16,1280]{2,1,0:T(8,128)(2,1)S(1)} %pad_maximum_fusion.when_ref), channel_id=1, source_target_pairs={{0,6},{1,7},{2,4},{3,5},{4,2},{5,3},{6,0},{7,1},{8,14},{9,15},{10,... | collective-permute-start | bytes 491528 | tf_op jit(solution)/shard_map/ppermute | solution.py:680
  66.7 3.4 %recall.1 = (f32[16,36864]{1,0:T(8,128)S(1)}, f32[16,36864]{1,0:T(8,128)S(1)}, f32[16,128]{1,0:T(8,128)S(1)}, f32[16,128]{1,0:T(8,128)S(1)}) custom-call(s32[8]{0:T(128)S(1)} %copy-done, f32[128,36864]{1,0:T(8,128)} %dict_hbm.5, bf16[4,16,1280]{2,1,0:T(8,128)(2,1)S(1)} %pad_maximum_fusion.when_ref), custom_call_target="tpu_custom_call" | custom-call | tf_op jit(solution)/shard_map/recall/pallas_call | solution.py:721
  70.2 3.9 %collective-permute-done.9 = bf16[4,16,1280]{2,1,0:T(8,128)(2,1)S(1)} collective-permute-done((bf16[4,16,1280]{2,1,0:T(8,128)(2,1)S(1)}, bf16[4,16,1280]{2,1,0:T(8,128)(2,1)S(1)}, u32[]{:S(2)}, u32[]{:S(2)}) %collective-permute-start.9) | collective-permute-done | bytes 163872 | tf_op jit(solution)/shard_map/ppermute | solution.py:680
  74.2 2.1 %collective-permute-done.12.came_ref = bf16[16,16,1280]{2,1,0:T(8,128)(2,1)S(1)} collective-permute-done((bf16[16,16,1280]{2,1,0:T(8,128)(2,1)S(1)}, bf16[16,16,1280]{2,1,0:T(8,128)(2,1)S(1)}, u32[]{:S(2)}, u32[]{:S(2)}) %collective-permute-start.12) | collective-permute-done | bytes 655392 | tf_op jit(solution)/shard_map/ppermute | solution.py:680
  76.3 2.0 %renew.2.refs_6_.refs_0_ = f32[16,36864]{1,0:T(8,128)S(1)} custom-call(s32[8]{0:T(128)S(1)} %copy-done, bf16[16,16,1280]{2,1,0:T(8,128)(2,1)S(1)} %constant_dynamic-update-slice_fusion.held_ref, bf16[16,16,1280]{2,1,0:T(8,128)(2,1)S(1)} %collective-permute-done.12.came_ref, f32[16,36864]{1,0:T(8,128)S(1)} %get-tuple-element.52.old, ...), custom_call_target="tpu_custom_call" | custom-call | tf_op jit(solution)/shard_map/renew/pallas_call | solution.py:790
  78.3 11.8 %iterate.3 = (f32[128,128]{1,0:T(8,128)S(1)}, bf16[96,128]{1,0:T(8,128)(2,1)S(1)}, bf16[96,128]{1,0:T(8,128)(2,1)S(1)}, bf16[6,16,384,128]{3,2,1,0:T(8,128)(2,1)S(1)}, f32[128,36864]{1,0:T(8,128)}) custom-call(s32[8]{0:T(128)S(1)} %copy-done, f32[1,128]{1,0:T(1,128)S(1)} %bitcast.15, ...), custom_call_target="tpu_custom_call", output_to_operand_aliasing={{3}: (9, {}), {4}: (11, {})} | custom-call | tf_op jit(solution)/shard_map/iterate/pallas_call | solution.py:361
  91.4 8.8 %conclude.3 = (bf16[32,40,128]{2,1,0:T(8,128)(2,1)S(1)}, f32[128,384]{1,0:T(8,128)S(1)}, f32[128,128]{1,0:T(8,128)S(1)}, bf16[96,128]{1,0:T(8,128)(2,1)S(1)}, bf...) custom-call(s32[8]{0:T(128)S(1)} %copy-done, f32[1,128]{1,0:T(1,128)S(1)} %bitcast.16, ...), custom_call_target="tpu_custom_call", output_to_operand_aliasing={{5}: (10, {})} | custom-call | tf_op jit(solution)/shard_map/conclude/pallas_call | solution.py:473
  100.2 21.1 %all_to_all.11.blocks_ref = bf16[32,40,128]{2,1,0:T(8,128)(2,1)S(1)} all-to-all(bf16[32,40,128]{2,1,0:T(8,128)(2,1)S(1)} %get-tuple-element.62), channel_id=1, replica_groups=mesh['tm'=32,'chan'=1] {'tm'}, dimensions={0} | all-to-all | bytes 655360 | tf_op jit(solution)/shard_map/all_to_all | solution.py:833
  121.3 2.9 %gradient.3 = bf16[16,1280]{1,0:T(8,128)(2,1)S(1)} custom-call(s32[8]{0:T(128)S(1)} %copy-done, bf16[32,40,128]{2,1,0:T(8,128)(2,1)S(1)} %all_to_all.11.blocks_ref, f32[128,36864]{1,0:T(8,128)} %dict_hbm.5), custom_call_target="tpu_custom_call" | custom-call | tf_op jit(solution)/shard_map/gradient/pallas_call | solution.py:642
  124.1 1.2 collective-permute-start.17
  125.4 3.2 %collective-permute-start.15 = (bf16[1,16,1280]{2,1,0:T(8,128)(2,1)S(1)}, bf16[1,16,1280]{2,1,0:T(8,128)(2,1)S(1)}, u32[]{:S(2)}, u32[]{:S(2)}) collective-permute-start(bf16[1,16,1280]{2,1,0:T(8,128)(2,1)S(1)} %bitcast.11), channel_id=1, source_target_pairs={{0,16},{1,17},{2,18},{3,19},{4,20},{5,21},{6,22},{7,23},{8,24},{9,... | collective-permute-start | bytes 122888 | tf_op jit(solution)/shard_map/ppermute | solution.py:680
  130.9 2.2 %collective-permute-start.20 = (bf16[4,16,1280]{2,1,0:T(8,128)(2,1)S(1)}, bf16[4,16,1280]{2,1,0:T(8,128)(2,1)S(1)}, u32[]{:S(2)}, u32[]{:S(2)}) collective-permute-start(bf16[4,16,1280]{2,1,0:T(8,128)(2,1)S(1)} %pad_maximum_fusion.1), channel_id=1, source_target_pairs={{0,6},{1,7},{2,4},{3,5},{4,2},{5,3},{6,0},{7,1},{8,14},{9,15},{10,... | collective-permute-start | bytes 491528 | tf_op jit(solution)/shard_map/ppermute | solution.py:680
  134.5 3.8 %settle.1 = (f32[384,128]{1,0:T(8,128)S(1)}, f32[128,36864]{1,0:T(8,128)}) custom-call(s32[8]{0:T(128)S(1)} %copy-done, f32[128,384]{1,0:T(8,128)S(1)} %get-tuple-element.64.partial_ref, bf16[96,128]{1,0:T(8,128)(2,1)S(1)} %collective-permute-done.21.first_ref, ...), custom_call_target="tpu_custom_call", output_to_operand_aliasing={{1}: (6, {})} | custom-call | tf_op jit(solution)/shard_map/settle/pallas_call | solution.py:542
  138.3 3.4 %collective-permute-done.18 = bf16[4,16,1280]{2,1,0:T(8,128)(2,1)S(1)} collective-permute-done((bf16[4,16,1280]{2,1,0:T(8,128)(2,1)S(1)}, bf16[4,16,1280]{2,1,0:T(8,128)(2,1)S(1)}, u32[]{:S(2)}, u32[]{:S(2)}) %collective-permute-start.18) | collective-permute-done | bytes 163872 | tf_op jit(solution)/shard_map/ppermute | solution.py:680
  143.9 3.3 %renew.3 = f32[128,36864]{1,0:T(8,128)} custom-call(s32[8]{0:T(128)S(1)} %copy-done, bf16[16,16,1280]{2,1,0:T(8,128)(2,1)S(1)} %constant_dynamic-update-slice_fusion.7.held_ref, bf16[16,16,1280]{2,1,0:T(8,128)(2,1)S(1)} %collective-permute-done.23.came_ref, f32[16,36864]{1,0:T(8,128)S(1)} %get-tuple-element.72.old, ...), custom_call_target="tpu_custom_call", output_to_operand_aliasing={{}: (5, {})} | custom-call | tf_op jit(solution)/shard_map/renew/pallas_call | solution.py:790
  (60 shorter events, 12.9 us)
Async XLA Ops:
  1.8 10.4 %collective-permute-start = (bf16[96,512]{1,0:T(8,128)(2,1)S(1)}, bf16[96,512]{1,0:T(8,128)(2,1)S(1)}, u32[]{:S(2)}, u32[]{:S(2)}) collective-permute-start(bf16[96,512]{1,0:T(8,128)(2,1)S(1)} %get-tuple-element.40), channel_id=1, source_target_pairs={{0,1},{1,0},{2,3},{3,2},{4,5},{5,4},{6,7},{7,6},{8,9},{9,8},{10,11... | collective-permute-start | bytes 294920 | tf_op jit(solution)/shard_map/ppermute | solution.py:809
  2.3 9.9 %collective-permute-start.1 = (bf16[96,512]{1,0:T(8,128)(2,1)S(1)}, bf16[96,512]{1,0:T(8,128)(2,1)S(1)}, u32[]{:S(2)}, u32[]{:S(2)}) collective-permute-start(bf16[96,512]{1,0:T(8,128)(2,1)S(1)} %get-tuple-element.41), channel_id=1, source_target_pairs={{1,2},{2,1},{3,4},{4,3},{5,6},{6,5},{7,8},{8,7},{9,10},{10,9},{11,... | collective-permute-start | bytes 294920 | tf_op jit(solution)/shard_map/ppermute | solution.py:809
  17.5 4.8 %collective-permute-start.2 = (bf16[96,128]{1,0:T(8,128)(2,1)S(1)}, bf16[96,128]{1,0:T(8,128)(2,1)S(1)}, u32[]{:S(2)}, u32[]{:S(2)}) collective-permute-start(bf16[96,128]{1,0:T(8,128)(2,1)S(1)} %get-tuple-element.44), channel_id=1, source_target_pairs={{0,1},{1,0},{2,3},{3,2},{4,5},{5,4},{6,7},{7,6},{8,9},{9,8},{10,11... | collective-permute-start | bytes 73736 | tf_op jit(solution)/shard_map/ppermute | solution.py:809
  21.4 0.9 collective-permute-start.3
  56.4 6.3 %collective-permute-start.8 = (bf16[1,16,1280]{2,1,0:T(8,128)(2,1)S(1)}, bf16[1,16,1280]{2,1,0:T(8,128)(2,1)S(1)}, u32[]{:S(2)}, u32[]{:S(2)}) collective-permute-start(bf16[1,16,1280]{2,1,0:T(8,128)(2,1)S(1)} %bitcast.5), channel_id=1, source_target_pairs={{0,24},{1,25},{2,26},{3,27},{4,28},{5,29},{6,30},{7,31},{8,16},{9,... | collective-permute-start | bytes 122888 | tf_op jit(solution)/shard_map/ppermute | solution.py:680
  57.7 5.1 %collective-permute-start.7 = (bf16[1,16,1280]{2,1,0:T(8,128)(2,1)S(1)}, bf16[1,16,1280]{2,1,0:T(8,128)(2,1)S(1)}, u32[]{:S(2)}, u32[]{:S(2)}) collective-permute-start(bf16[1,16,1280]{2,1,0:T(8,128)(2,1)S(1)} %bitcast.6), channel_id=1, source_target_pairs={{0,8},{1,9},{2,10},{3,11},{4,12},{5,13},{6,14},{7,15},{8,0},{9,1},... | collective-permute-start | bytes 122888 | tf_op jit(solution)/shard_map/ppermute | solution.py:680
  57.7 5.5 %collective-permute-start.6 = (bf16[1,16,1280]{2,1,0:T(8,128)(2,1)S(1)}, bf16[1,16,1280]{2,1,0:T(8,128)(2,1)S(1)}, u32[]{:S(2)}, u32[]{:S(2)}) collective-permute-start(bf16[1,16,1280]{2,1,0:T(8,128)(2,1)S(1)} %bitcast.7), channel_id=1, source_target_pairs={{0,16},{1,17},{2,18},{3,19},{4,20},{5,21},{6,22},{7,23},{8,24},{9,... | collective-permute-start | bytes 122888 | tf_op jit(solution)/shard_map/ppermute | solution.py:680
  60.9 13.2 %collective-permute-start.4 = (bf16[96,128]{1,0:T(8,128)(2,1)S(1)}, bf16[96,128]{1,0:T(8,128)(2,1)S(1)}, u32[]{:S(2)}, u32[]{:S(2)}) collective-permute-start(bf16[96,128]{1,0:T(8,128)(2,1)S(1)} %get-tuple-element.50), channel_id=1, source_target_pairs={{0,1},{1,0},{2,3},{3,2},{4,5},{5,4},{6,7},{7,6},{8,9},{9,8},{10,11... | collective-permute-start | bytes 73736 | tf_op jit(solution)/shard_map/ppermute | solution.py:809
  60.9 13.2 %collective-permute-start.5 = (bf16[96,128]{1,0:T(8,128)(2,1)S(1)}, bf16[96,128]{1,0:T(8,128)(2,1)S(1)}, u32[]{:S(2)}, u32[]{:S(2)}) collective-permute-start(bf16[96,128]{1,0:T(8,128)(2,1)S(1)} %get-tuple-element.51), channel_id=1, source_target_pairs={{1,2},{2,1},{3,4},{4,3},{5,6},{6,5},{7,8},{8,7},{9,10},{10,9},{11,... | collective-permute-start | bytes 73736 | tf_op jit(solution)/shard_map/ppermute | solution.py:809
  63.2 10.9 %collective-permute-start.11 = (bf16[4,16,1280]{2,1,0:T(8,128)(2,1)S(1)}, bf16[4,16,1280]{2,1,0:T(8,128)(2,1)S(1)}, u32[]{:S(2)}, u32[]{:S(2)}) collective-permute-start(bf16[4,16,1280]{2,1,0:T(8,128)(2,1)S(1)} %pad_maximum_fusion.when_ref), channel_id=1, source_target_pairs={{0,6},{1,7},{2,4},{3,5},{4,2},{5,3},{6,0},{7,1},{8,14},{9,15},{10,... | collective-permute-start | bytes 491528 | tf_op jit(solution)/shard_map/ppermute | solution.py:680
  65.3 8.7 %collective-permute-start.10 = (bf16[4,16,1280]{2,1,0:T(8,128)(2,1)S(1)}, bf16[4,16,1280]{2,1,0:T(8,128)(2,1)S(1)}, u32[]{:S(2)}, u32[]{:S(2)}) collective-permute-start(bf16[4,16,1280]{2,1,0:T(8,128)(2,1)S(1)} %pad_maximum_fusion.when_ref), channel_id=1, source_target_pairs={{0,2},{1,3},{2,0},{3,1},{4,6},{5,7},{6,4},{7,5},{8,10},{9,11},{10,... | collective-permute-start | bytes 491528 | tf_op jit(solution)/shard_map/ppermute | solution.py:680
  66.2 7.8 %collective-permute-start.9 = (bf16[4,16,1280]{2,1,0:T(8,128)(2,1)S(1)}, bf16[4,16,1280]{2,1,0:T(8,128)(2,1)S(1)}, u32[]{:S(2)}, u32[]{:S(2)}) collective-permute-start(bf16[4,16,1280]{2,1,0:T(8,128)(2,1)S(1)} %pad_maximum_fusion.when_ref), channel_id=1, source_target_pairs={{0,4},{1,5},{2,6},{3,7},{4,0},{5,1},{6,2},{7,3},{8,12},{9,13},{10,... | collective-permute-start | bytes 491528 | tf_op jit(solution)/shard_map/ppermute | solution.py:680
  74.1 2.2 %collective-permute-start.12 = (bf16[16,16,1280]{2,1,0:T(8,128)(2,1)S(1)}, bf16[16,16,1280]{2,1,0:T(8,128)(2,1)S(1)}, u32[]{:S(2)}, u32[]{:S(2)}) collective-permute-start(bf16[16,16,1280]{2,1,0:T(8,128)(2,1)S(1)} %constant_dynamic-update-slice_fusion.held_ref), channel_id=1, source_target_pairs={{0,1},{1,0},{2,3},{3,2},{4,5},{5,4},{6,7},{7,6},{8,9},{9,8},{10,11... | collective-permute-start | bytes 1966088 | tf_op jit(solution)/shard_map/ppermute | solution.py:680
  90.1 1.3 collective-permute-start.13
  90.3 1.0 collective-permute-start.14
  124.1 6.3 %collective-permute-start.17 = (bf16[1,16,1280]{2,1,0:T(8,128)(2,1)S(1)}, bf16[1,16,1280]{2,1,0:T(8,128)(2,1)S(1)}, u32[]{:S(2)}, u32[]{:S(2)}) collective-permute-start(bf16[1,16,1280]{2,1,0:T(8,128)(2,1)S(1)} %bitcast.9), channel_id=1, source_target_pairs={{0,24},{1,25},{2,26},{3,27},{4,28},{5,29},{6,30},{7,31},{8,16},{9,... | collective-permute-start | bytes 122888 | tf_op jit(solution)/shard_map/ppermute | solution.py:680
  125.4 5.1 %collective-permute-start.16 = (bf16[1,16,1280]{2,1,0:T(8,128)(2,1)S(1)}, bf16[1,16,1280]{2,1,0:T(8,128)(2,1)S(1)}, u32[]{:S(2)}, u32[]{:S(2)}) collective-permute-start(bf16[1,16,1280]{2,1,0:T(8,128)(2,1)S(1)} %bitcast.10), channel_id=1, source_target_pairs={{0,8},{1,9},{2,10},{3,11},{4,12},{5,13},{6,14},{7,15},{8,0},{9,1},... | collective-permute-start | bytes 122888 | tf_op jit(solution)/shard_map/ppermute | solution.py:680
  125.4 5.5 %collective-permute-start.15 = (bf16[1,16,1280]{2,1,0:T(8,128)(2,1)S(1)}, bf16[1,16,1280]{2,1,0:T(8,128)(2,1)S(1)}, u32[]{:S(2)}, u32[]{:S(2)}) collective-permute-start(bf16[1,16,1280]{2,1,0:T(8,128)(2,1)S(1)} %bitcast.11), channel_id=1, source_target_pairs={{0,16},{1,17},{2,18},{3,19},{4,20},{5,21},{6,22},{7,23},{8,24},{9,... | collective-permute-start | bytes 122888 | tf_op jit(solution)/shard_map/ppermute | solution.py:680
  128.6 5.9 %collective-permute-start.21 = (bf16[96,128]{1,0:T(8,128)(2,1)S(1)}, bf16[96,128]{1,0:T(8,128)(2,1)S(1)}, u32[]{:S(2)}, u32[]{:S(2)}) collective-permute-start(bf16[96,128]{1,0:T(8,128)(2,1)S(1)} %get-tuple-element.67), channel_id=1, source_target_pairs={{0,1},{1,0},{2,3},{3,2},{4,5},{5,4},{6,7},{7,6},{8,9},{9,8},{10,11... | collective-permute-start | bytes 73736 | tf_op jit(solution)/shard_map/ppermute | solution.py:809
  128.6 5.9 %collective-permute-start.22 = (bf16[96,128]{1,0:T(8,128)(2,1)S(1)}, bf16[96,128]{1,0:T(8,128)(2,1)S(1)}, u32[]{:S(2)}, u32[]{:S(2)}) collective-permute-start(bf16[96,128]{1,0:T(8,128)(2,1)S(1)} %get-tuple-element.68), channel_id=1, source_target_pairs={{1,2},{2,1},{3,4},{4,3},{5,6},{6,5},{7,8},{8,7},{9,10},{10,9},{11,... | collective-permute-start | bytes 73736 | tf_op jit(solution)/shard_map/ppermute | solution.py:809
  130.9 10.9 %collective-permute-start.20 = (bf16[4,16,1280]{2,1,0:T(8,128)(2,1)S(1)}, bf16[4,16,1280]{2,1,0:T(8,128)(2,1)S(1)}, u32[]{:S(2)}, u32[]{:S(2)}) collective-permute-start(bf16[4,16,1280]{2,1,0:T(8,128)(2,1)S(1)} %pad_maximum_fusion.1), channel_id=1, source_target_pairs={{0,6},{1,7},{2,4},{3,5},{4,2},{5,3},{6,0},{7,1},{8,14},{9,15},{10,... | collective-permute-start | bytes 491528 | tf_op jit(solution)/shard_map/ppermute | solution.py:680
  133.0 8.7 %collective-permute-start.19 = (bf16[4,16,1280]{2,1,0:T(8,128)(2,1)S(1)}, bf16[4,16,1280]{2,1,0:T(8,128)(2,1)S(1)}, u32[]{:S(2)}, u32[]{:S(2)}) collective-permute-start(bf16[4,16,1280]{2,1,0:T(8,128)(2,1)S(1)} %pad_maximum_fusion.1), channel_id=1, source_target_pairs={{0,2},{1,3},{2,0},{3,1},{4,6},{5,7},{6,4},{7,5},{8,10},{9,11},{10,... | collective-permute-start | bytes 491528 | tf_op jit(solution)/shard_map/ppermute | solution.py:680
  133.9 7.8 %collective-permute-start.18 = (bf16[4,16,1280]{2,1,0:T(8,128)(2,1)S(1)}, bf16[4,16,1280]{2,1,0:T(8,128)(2,1)S(1)}, u32[]{:S(2)}, u32[]{:S(2)}) collective-permute-start(bf16[4,16,1280]{2,1,0:T(8,128)(2,1)S(1)} %pad_maximum_fusion.1), channel_id=1, source_target_pairs={{0,4},{1,5},{2,6},{3,7},{4,0},{5,1},{6,2},{7,3},{8,12},{9,13},{10,... | collective-permute-start | bytes 491528 | tf_op jit(solution)/shard_map/ppermute | solution.py:680
  141.8 2.2 %collective-permute-start.23 = (bf16[16,16,1280]{2,1,0:T(8,128)(2,1)S(1)}, bf16[16,16,1280]{2,1,0:T(8,128)(2,1)S(1)}, u32[]{:S(2)}, u32[]{:S(2)}) collective-permute-start(bf16[16,16,1280]{2,1,0:T(8,128)(2,1)S(1)} %constant_dynamic-update-slice_fusion.7.held_ref), channel_id=1, source_target_pairs={{0,1},{1,0},{2,3},{3,2},{4,5},{5,4},{6,7},{7,6},{8,9},{9,8},{10,11... | collective-permute-start | bytes 1966088 | tf_op jit(solution)/shard_map/ppermute | solution.py:680
  (2 other events, 23.1 us)

commit v13 on v12

--- a/solution.py
+++ b/solution.py
@@ -150,35 +150,45 @@
     ]
 
 
-def convolve(zb, begin, count, taps, zz, fine, acc):
-    channels = taps.shape[2]
-    tiles = channels // LANES
+def lag_rows(zb, begin, count, zz):
     rows = count + ROWS
     for coarse in range(COARSE):
         first = begin - ROWS - ROWS * coarse
         zz[:rows, coarse * K : (coarse + 1) * K] = zb[first : first + rows, :]
+
+
+def convolve_lags(lag, columns, count, taps, zz, fine, acc):
+    channels = len(columns) * LANES
+    own = slice(columns[0] * LANES, columns[0] * LANES + channels)
+    rows = count + ROWS
+    slot = lag // FINE % 2 * FINE
+    for pair in range(0, FINE, 2):
+        weights = jnp.concatenate(
+            [
+                jnp.concatenate([taps[m, lag + pair + j, own, :] for m in range(COARSE)], axis=1)
+                for j in range(2)
+            ],
+            axis=0,
+        )
+        product = lax.dot_general(zz[:rows, :], weights, NT, preferred_element_type=jnp.float32)
+        for j in range(2):
+            for index, tile in enumerate(columns):
+                column = j * channels + index * LANES
+                fine[slot + pair + j, tile, :rows, :] = product[:, column : column + LANES]
+    for tile in columns:
+        total = None if lag == 0 else acc[tile, :count, :]
+        for j in range(FINE):
+            first = ROWS - lag - j
+            part = fine[slot + j, tile, first : first + count, :]
+            total = part if total is None else total + part
+        acc[tile, :count, :] = total
+
+
+def convolve(zb, begin, count, taps, zz, fine, acc):
+    lag_rows(zb, begin, count, zz)
+    columns = list(range(taps.shape[2] // LANES))
     for lag in range(0, ROWS, FINE):
-        slot = lag // FINE % 2 * FINE
-        for pair in range(0, FINE, 2):
-            weights = jnp.concatenate(
-                [
-                    jnp.concatenate([taps[m, lag + pair + j] for m in range(COARSE)], axis=1)
-                    for j in range(2)
-                ],
-                axis=0,
-            )
-            product = lax.dot_general(zz[:rows, :], weights, NT, preferred_element_type=jnp.float32)
-            for j in range(2):
-                for tile in range(tiles):
-                    column = j * channels + tile * LANES
-                    fine[slot + pair + j, tile, :rows, :] = product[:, column : column + LANES]
-        for tile in range(tiles):
-            total = None if lag == 0 else acc[tile, :count, :]
-            for j in range(FINE):
-                first = ROWS - lag - j
-                part = fine[slot + j, tile, first : first + count, :]
-                total = part if total is None else total + part
-            acc[tile, :count, :] = total
+        convolve_lags(lag, columns, count, taps, zz, fine, acc)
 
 
 def correlate(rb, count, taps, rr, fine, acc):
@@ -207,15 +217,15 @@
         acc[0, :count, :] = total
 
 
-def patch_taps(row, atoms_ref, taps, columns, turned):
-    channels = taps.shape[2]
+def patch_taps(row, atoms_ref, taps, columns, turned, convolve_after):
     lane = lax.broadcasted_iota(jnp.int32, (ROWS, K), 1)
     kept = (lane < row) | (lane >= row + BLOCK_ATOMS)
     keep = kept.astype(jnp.float32).astype(jnp.bfloat16)
     columns[...] = jnp.zeros_like(columns)
     width = ROWS * L
-
-    def patch(step, carry):
+    steps = LANES // (GROUPS * ROWS)
+
+    def patch(step, after):
         part = pl.ds(pl.multiple_of(step * (GROUPS * width), LANES), GROUPS * width)
         columns[pl.ds(row, BLOCK_ATOMS), :] = atoms_ref[:, part].astype(jnp.bfloat16)
         turn(columns[:, :width], turned[0])
@@ -226,9 +236,27 @@
             for tap in range(L):
                 before = taps[tap // ROWS, tap % ROWS, own, :]
                 taps[tap // ROWS, tap % ROWS, own, :] = before * keep + tap_of(turned[group], tap)
+            after(group)
+
+    def alone(step, carry):
+        patch(step, lambda group: None)
         return carry
 
-    lax.fori_loop(0, channels // (GROUPS * ROWS), patch, 0)
+    lax.fori_loop(0, steps, alone, 0)
+    tiles = taps.shape[2] // LANES
+    lags = list(range(0, ROWS, FINE))
+    for tile in range(1, tiles):
+        for step in range(steps):
+
+            def after(group):
+                done = (step * GROUPS + group + 1) * len(lags) // (steps * GROUPS)
+                past = (step * GROUPS + group) * len(lags) // (steps * GROUPS)
+                for index in range(past, done):
+                    convolve_after(lags[index], tile - 1)
+
+            patch(tile * steps + step, after)
+    for lag in lags:
+        convolve_after(lag, tiles - 1)
 
 
 def put_edges(edge_refs, rightward, leftward):
@@ -339,9 +367,17 @@
     by_side(put_signal, next_first, next_second)
     if patching:
         columns, *turned = take(1 + GROUPS)
-        patch_taps(first_row_of(plan_ref, patching - 1), atoms[0], taps, columns, turned)
+        lag_rows(zb, L, segment + L, zz)
+
+        def convolve_after(lag, tile):
+            convolve_lags(lag, [tile], segment + L, taps, zz, fine, acc)
+
+        patch_taps(
+            first_row_of(plan_ref, patching - 1), atoms[0], taps, columns, turned, convolve_after
+        )
         ferry.turn_round()
-    convolve(zb, L, segment + L, taps, zz, fine, acc)
+    else:
+        convolve(zb, L, segment + L, taps, zz, fine, acc)
     start = lax.axis_index("tm") * segment
     residual_rows(rb, (signal_ref, beyond), start, acc, total_time)
     correlate(rb, segment, taps, rr, fine, acc)
@@ -928,7 +964,6 @@
         and segment % LANES == 0
         and INNER == 2
         and OUTER == 2
-        and channels % (GROUPS * ROWS) == 0
         and channels % LANES == 0
         and channels % peers == 0
         and (channels // peers * L) % LANES == 0

time: 148 us -> 147 us (level)
  no operation moved by 1% of the time
where the time goes in v13:
time: 147 us
  Pallas kernels  62.5 us (43%)
  blocking collectives  43.8 us (30%)
  starting transfers between devices  24.1 us (16%)
  waiting for transfers between devices  14 us (10%)
    all_to_all x2, blocking collectives, whole_channels(): blocks = lax.all_to_all(payload, 'tm', 0, 0, tiled=True)  43.8 us
    pallas_call x2, Pallas kernels, conclude(): pl.pallas_call(functools.partial(conclude_kernel, peers, step, ferry[2]),...  17.4 us
    pallas_call x2, Pallas kernels, iterate(): pl.pallas_call(functools.partial(iterate_kernel, peers * segment, step if...  16.5 us
    ppermute x14, starting transfers between devices, exchanged(): return lax.ppermute(shard, 'tm', [(i, i ^ mask) for i in range(peers)])  16.2 us
    ppermute x14, waiting for transfers between devices, exchanged(): return lax.ppermute(shard, 'tm', [(i, i ^ mask) for i in range(peers)])  13.4 us
    pallas_call x1, Pallas kernels, layout(): pl.pallas_call(layout_kernel, grid=(channels // block,), in_specs=[pl.Blo...  9.22 us
    ppermute x10, starting transfers between devices, swaps(): lax.ppermute(edge, 'tm', pair)  7.95 us
    pallas_call x2, Pallas kernels, share_gradient(): pl.pallas_call(functools.partial(gradient_kernel, share, step), in_specs=...  5.71 us
  transfers between devices with their start and end apart: 24, of which 10 were waited for; matrix products, arithmetic and copies ran while one was open for 1% of the time, Pallas kernels for 11%

profile of v13, /device:TPU:0, one launch (start us, length us, event | category | flops | bytes accessed | tf_op | source)
XLA Modules:
  0.0 146.9 jit_solution(8921112429719065482)
XLA Ops:
  2.9 9.2 %layout.1.refs_6_.refs_7_ = bf16[6,16,384,128]{3,2,1,0:T(8,128)(2,1)S(1)} custom-call(f32[128,36864]{1,0:T(8,128)} %dict_hbm.5), custom_call_target="tpu_custom_call" | custom-call | tf_op jit(solution)/shard_map/layout/pallas_call | solution.py:113
  12.2 5.3 %iterate.2 = (f32[128,128]{1,0:T(8,128)S(1)}, bf16[96,128]{1,0:T(8,128)(2,1)S(1)}, bf16[96,128]{1,0:T(8,128)(2,1)S(1)}) custom-call(s32[8]{0:T(128)S(1)} %copy-done, f32[1,128]{1,0:T(1,128)S(1)} %bitcast.13, f32[128,128]{1,0:T(8,128)S(1)} %get-tuple-element.39.refs_0_, bf16[96,512]{1,0:T(8,128)(2,1)S(1)} %collective-permute-done.refs_1_.refs_4_, ...), custom_call_target="tpu_custom_call" | custom-call | tf_op jit(solution)/shard_map/iterate/pallas_call | solution.py:397
  17.5 3.9 %collective-permute-start.2 = (bf16[96,128]{1,0:T(8,128)(2,1)S(1)}, bf16[96,128]{1,0:T(8,128)(2,1)S(1)}, u32[]{:S(2)}, u32[]{:S(2)}) collective-permute-start(bf16[96,128]{1,0:T(8,128)(2,1)S(1)} %get-tuple-element.44), channel_id=1, source_target_pairs={{0,1},{1,0},{2,3},{3,2},{4,5},{5,4},{6,7},{7,6},{8,9},{9,8},{10,11... | collective-permute-start | bytes 73736 | tf_op jit(solution)/shard_map/ppermute | solution.py:845
  22.3 8.6 %conclude.2 = (bf16[32,40,128]{2,1,0:T(8,128)(2,1)S(1)}, f32[128,128]{1,0:T(8,128)S(1)}, bf16[96,128]{1,0:T(8,128)(2,1)S(1)}, bf16[96,128]{1,0:T(8,128)(2,1)S(1)}, f32[128,36864]{1,0:T(8,128)}) custom-call(s32[8]{0:T(128)S(1)} %copy-done, f32[1,128]{1,0:T(1,128)S(1)} %bitcast.14, f32[128,128]{1,0:T(8,128)S(1)} %get-tuple-element.43.refs_0_, ...), custom_call_target="tpu_custom_call" | custom-call | tf_op jit(solution)/shard_map/conclude/pallas_call | solution.py:509
  30.9 22.7 %all_to_all.10.blocks_ref = bf16[32,40,128]{2,1,0:T(8,128)(2,1)S(1)} all-to-all(bf16[32,40,128]{2,1,0:T(8,128)(2,1)S(1)} %get-tuple-element.49), channel_id=1, replica_groups=mesh['tm'=32,'chan'=1] {'tm'}, dimensions={0} | all-to-all | bytes 655360 | tf_op jit(solution)/shard_map/all_to_all | solution.py:869
  53.6 2.9 %gradient.2 = bf16[16,1280]{1,0:T(8,128)(2,1)S(1)} custom-call(s32[8]{0:T(128)S(1)} %copy-done, bf16[32,40,128]{2,1,0:T(8,128)(2,1)S(1)} %all_to_all.10.blocks_ref, f32[128,36864]{1,0:T(8,128)} %dict_hbm.5), custom_call_target="tpu_custom_call" | custom-call | tf_op jit(solution)/shard_map/gradient/pallas_call | solution.py:678
  56.4 1.2 collective-permute-start.8
  57.7 3.2 %collective-permute-start.6 = (bf16[1,16,1280]{2,1,0:T(8,128)(2,1)S(1)}, bf16[1,16,1280]{2,1,0:T(8,128)(2,1)S(1)}, u32[]{:S(2)}, u32[]{:S(2)}) collective-permute-start(bf16[1,16,1280]{2,1,0:T(8,128)(2,1)S(1)} %bitcast.7), channel_id=1, source_target_pairs={{0,16},{1,17},{2,18},{3,19},{4,20},{5,21},{6,22},{7,23},{8,24},{9,... | collective-permute-start | bytes 122888 | tf_op jit(solution)/shard_map/ppermute | solution.py:716
  61.6 1.2 collective-permute-done.8
  63.2 2.2 %collective-permute-start.11 = (bf16[4,16,1280]{2,1,0:T(8,128)(2,1)S(1)}, bf16[4,16,1280]{2,1,0:T(8,128)(2,1)S(1)}, u32[]{:S(2)}, u32[]{:S(2)}) collective-permute-start(bf16[4,16,1280]{2,1,0:T(8,128)(2,1)S(1)} %pad_maximum_fusion.when_ref), channel_id=1, source_target_pairs={{0,6},{1,7},{2,4},{3,5},{4,2},{5,3},{6,0},{7,1},{8,14},{9,15},{10,... | collective-permute-start | bytes 491528 | tf_op jit(solution)/shard_map/ppermute | solution.py:716
  66.7 3.4 %recall.1 = (f32[16,36864]{1,0:T(8,128)S(1)}, f32[16,36864]{1,0:T(8,128)S(1)}, f32[16,128]{1,0:T(8,128)S(1)}, f32[16,128]{1,0:T(8,128)S(1)}) custom-call(s32[8]{0:T(128)S(1)} %copy-done, f32[128,36864]{1,0:T(8,128)} %dict_hbm.5, bf16[4,16,1280]{2,1,0:T(8,128)(2,1)S(1)} %pad_maximum_fusion.when_ref), custom_call_target="tpu_custom_call" | custom-call | tf_op jit(solution)/shard_map/recall/pallas_call | solution.py:757
  70.2 3.9 %collective-permute-done.9 = bf16[4,16,1280]{2,1,0:T(8,128)(2,1)S(1)} collective-permute-done((bf16[4,16,1280]{2,1,0:T(8,128)(2,1)S(1)}, bf16[4,16,1280]{2,1,0:T(8,128)(2,1)S(1)}, u32[]{:S(2)}, u32[]{:S(2)}) %collective-permute-start.9) | collective-permute-done | bytes 163872 | tf_op jit(solution)/shard_map/ppermute | solution.py:716
  74.2 2.1 %collective-permute-done.12.came_ref = bf16[16,16,1280]{2,1,0:T(8,128)(2,1)S(1)} collective-permute-done((bf16[16,16,1280]{2,1,0:T(8,128)(2,1)S(1)}, bf16[16,16,1280]{2,1,0:T(8,128)(2,1)S(1)}, u32[]{:S(2)}, u32[]{:S(2)}) %collective-permute-start.12) | collective-permute-done | bytes 655392 | tf_op jit(solution)/shard_map/ppermute | solution.py:716
  76.3 2.0 %renew.2.refs_6_.refs_0_ = f32[16,36864]{1,0:T(8,128)S(1)} custom-call(s32[8]{0:T(128)S(1)} %copy-done, bf16[16,16,1280]{2,1,0:T(8,128)(2,1)S(1)} %constant_dynamic-update-slice_fusion.held_ref, bf16[16,16,1280]{2,1,0:T(8,128)(2,1)S(1)} %collective-permute-done.12.came_ref, f32[16,36864]{1,0:T(8,128)S(1)} %get-tuple-element.52.old, ...), custom_call_target="tpu_custom_call" | custom-call | tf_op jit(solution)/shard_map/renew/pallas_call | solution.py:826
  78.3 11.3 %iterate.3 = (f32[128,128]{1,0:T(8,128)S(1)}, bf16[96,128]{1,0:T(8,128)(2,1)S(1)}, bf16[96,128]{1,0:T(8,128)(2,1)S(1)}, bf16[6,16,384,128]{3,2,1,0:T(8,128)(2,1)S(1)}, f32[128,36864]{1,0:T(8,128)}) custom-call(s32[8]{0:T(128)S(1)} %copy-done, f32[1,128]{1,0:T(1,128)S(1)} %bitcast.15, ...), custom_call_target="tpu_custom_call", output_to_operand_aliasing={{3}: (9, {}), {4}: (11, {})} | custom-call | tf_op jit(solution)/shard_map/iterate/pallas_call | solution.py:397
  90.9 8.8 %conclude.3 = (bf16[32,40,128]{2,1,0:T(8,128)(2,1)S(1)}, f32[128,384]{1,0:T(8,128)S(1)}, f32[128,128]{1,0:T(8,128)S(1)}, bf16[96,128]{1,0:T(8,128)(2,1)S(1)}, bf...) custom-call(s32[8]{0:T(128)S(1)} %copy-done, f32[1,128]{1,0:T(1,128)S(1)} %bitcast.16, ...), custom_call_target="tpu_custom_call", output_to_operand_aliasing={{5}: (10, {})} | custom-call | tf_op jit(solution)/shard_map/conclude/pallas_call | solution.py:509
  99.7 21.1 %all_to_all.11.blocks_ref = bf16[32,40,128]{2,1,0:T(8,128)(2,1)S(1)} all-to-all(bf16[32,40,128]{2,1,0:T(8,128)(2,1)S(1)} %get-tuple-element.62), channel_id=1, replica_groups=mesh['tm'=32,'chan'=1] {'tm'}, dimensions={0} | all-to-all | bytes 655360 | tf_op jit(solution)/shard_map/all_to_all | solution.py:869
  120.8 2.9 %gradient.3 = bf16[16,1280]{1,0:T(8,128)(2,1)S(1)} custom-call(s32[8]{0:T(128)S(1)} %copy-done, bf16[32,40,128]{2,1,0:T(8,128)(2,1)S(1)} %all_to_all.11.blocks_ref, f32[128,36864]{1,0:T(8,128)} %dict_hbm.5), custom_call_target="tpu_custom_call" | custom-call | tf_op jit(solution)/shard_map/gradient/pallas_call | solution.py:678
  123.6 1.2 collective-permute-start.17
  124.9 3.2 %collective-permute-start.15 = (bf16[1,16,1280]{2,1,0:T(8,128)(2,1)S(1)}, bf16[1,16,1280]{2,1,0:T(8,128)(2,1)S(1)}, u32[]{:S(2)}, u32[]{:S(2)}) collective-permute-start(bf16[1,16,1280]{2,1,0:T(8,128)(2,1)S(1)} %bitcast.11), channel_id=1, source_target_pairs={{0,16},{1,17},{2,18},{3,19},{4,20},{5,21},{6,22},{7,23},{8,24},{9,... | collective-permute-start | bytes 122888 | tf_op jit(solution)/shard_map/ppermute | solution.py:716
  130.4 2.2 %collective-permute-start.20 = (bf16[4,16,1280]{2,1,0:T(8,128)(2,1)S(1)}, bf16[4,16,1280]{2,1,0:T(8,128)(2,1)S(1)}, u32[]{:S(2)}, u32[]{:S(2)}) collective-permute-start(bf16[4,16,1280]{2,1,0:T(8,128)(2,1)S(1)} %pad_maximum_fusion.1), channel_id=1, source_target_pairs={{0,6},{1,7},{2,4},{3,5},{4,2},{5,3},{6,0},{7,1},{8,14},{9,15},{10,... | collective-permute-start | bytes 491528 | tf_op jit(solution)/shard_map/ppermute | solution.py:716
  134.0 3.8 %settle.1 = (f32[384,128]{1,0:T(8,128)S(1)}, f32[128,36864]{1,0:T(8,128)}) custom-call(s32[8]{0:T(128)S(1)} %copy-done, f32[128,384]{1,0:T(8,128)S(1)} %get-tuple-element.64.partial_ref, bf16[96,128]{1,0:T(8,128)(2,1)S(1)} %collective-permute-done.21.first_ref, ...), custom_call_target="tpu_custom_call", output_to_operand_aliasing={{1}: (6, {})} | custom-call | tf_op jit(solution)/shard_map/settle/pallas_call | solution.py:578
  137.8 3.4 %collective-permute-done.18 = bf16[4,16,1280]{2,1,0:T(8,128)(2,1)S(1)} collective-permute-done((bf16[4,16,1280]{2,1,0:T(8,128)(2,1)S(1)}, bf16[4,16,1280]{2,1,0:T(8,128)(2,1)S(1)}, u32[]{:S(2)}, u32[]{:S(2)}) %collective-permute-start.18) | collective-permute-done | bytes 163872 | tf_op jit(solution)/shard_map/ppermute | solution.py:716
  143.4 3.3 %renew.3 = f32[128,36864]{1,0:T(8,128)} custom-call(s32[8]{0:T(128)S(1)} %copy-done, bf16[16,16,1280]{2,1,0:T(8,128)(2,1)S(1)} %constant_dynamic-update-slice_fusion.7.held_ref, bf16[16,16,1280]{2,1,0:T(8,128)(2,1)S(1)} %collective-permute-done.23.came_ref, f32[16,36864]{1,0:T(8,128)S(1)} %get-tuple-element.72.old, ...), custom_call_target="tpu_custom_call", output_to_operand_aliasing={{}: (5, {})} | custom-call | tf_op jit(solution)/shard_map/renew/pallas_call | solution.py:826
  (60 shorter events, 12.9 us)
Async XLA Ops:
  1.8 10.4 %collective-permute-start = (bf16[96,512]{1,0:T(8,128)(2,1)S(1)}, bf16[96,512]{1,0:T(8,128)(2,1)S(1)}, u32[]{:S(2)}, u32[]{:S(2)}) collective-permute-start(bf16[96,512]{1,0:T(8,128)(2,1)S(1)} %get-tuple-element.40), channel_id=1, source_target_pairs={{0,1},{1,0},{2,3},{3,2},{4,5},{5,4},{6,7},{7,6},{8,9},{9,8},{10,11... | collective-permute-start | bytes 294920 | tf_op jit(solution)/shard_map/ppermute | solution.py:845
  2.3 9.9 %collective-permute-start.1 = (bf16[96,512]{1,0:T(8,128)(2,1)S(1)}, bf16[96,512]{1,0:T(8,128)(2,1)S(1)}, u32[]{:S(2)}, u32[]{:S(2)}) collective-permute-start(bf16[96,512]{1,0:T(8,128)(2,1)S(1)} %get-tuple-element.41), channel_id=1, source_target_pairs={{1,2},{2,1},{3,4},{4,3},{5,6},{6,5},{7,8},{8,7},{9,10},{10,9},{11,... | collective-permute-start | bytes 294920 | tf_op jit(solution)/shard_map/ppermute | solution.py:845
  17.5 4.8 %collective-permute-start.2 = (bf16[96,128]{1,0:T(8,128)(2,1)S(1)}, bf16[96,128]{1,0:T(8,128)(2,1)S(1)}, u32[]{:S(2)}, u32[]{:S(2)}) collective-permute-start(bf16[96,128]{1,0:T(8,128)(2,1)S(1)} %get-tuple-element.44), channel_id=1, source_target_pairs={{0,1},{1,0},{2,3},{3,2},{4,5},{5,4},{6,7},{7,6},{8,9},{9,8},{10,11... | collective-permute-start | bytes 73736 | tf_op jit(solution)/shard_map/ppermute | solution.py:845
  21.4 0.9 collective-permute-start.3
  56.4 6.3 %collective-permute-start.8 = (bf16[1,16,1280]{2,1,0:T(8,128)(2,1)S(1)}, bf16[1,16,1280]{2,1,0:T(8,128)(2,1)S(1)}, u32[]{:S(2)}, u32[]{:S(2)}) collective-permute-start(bf16[1,16,1280]{2,1,0:T(8,128)(2,1)S(1)} %bitcast.5), channel_id=1, source_target_pairs={{0,24},{1,25},{2,26},{3,27},{4,28},{5,29},{6,30},{7,31},{8,16},{9,... | collective-permute-start | bytes 122888 | tf_op jit(solution)/shard_map/ppermute | solution.py:716
  57.7 5.1 %collective-permute-start.7 = (bf16[1,16,1280]{2,1,0:T(8,128)(2,1)S(1)}, bf16[1,16,1280]{2,1,0:T(8,128)(2,1)S(1)}, u32[]{:S(2)}, u32[]{:S(2)}) collective-permute-start(bf16[1,16,1280]{2,1,0:T(8,128)(2,1)S(1)} %bitcast.6), channel_id=1, source_target_pairs={{0,8},{1,9},{2,10},{3,11},{4,12},{5,13},{6,14},{7,15},{8,0},{9,1},... | collective-permute-start | bytes 122888 | tf_op jit(solution)/shard_map/ppermute | solution.py:716
  57.7 5.5 %collective-permute-start.6 = (bf16[1,16,1280]{2,1,0:T(8,128)(2,1)S(1)}, bf16[1,16,1280]{2,1,0:T(8,128)(2,1)S(1)}, u32[]{:S(2)}, u32[]{:S(2)}) collective-permute-start(bf16[1,16,1280]{2,1,0:T(8,128)(2,1)S(1)} %bitcast.7), channel_id=1, source_target_pairs={{0,16},{1,17},{2,18},{3,19},{4,20},{5,21},{6,22},{7,23},{8,24},{9,... | collective-permute-start | bytes 122888 | tf_op jit(solution)/shard_map/ppermute | solution.py:716
  60.9 13.2 %collective-permute-start.4 = (bf16[96,128]{1,0:T(8,128)(2,1)S(1)}, bf16[96,128]{1,0:T(8,128)(2,1)S(1)}, u32[]{:S(2)}, u32[]{:S(2)}) collective-permute-start(bf16[96,128]{1,0:T(8,128)(2,1)S(1)} %get-tuple-element.50), channel_id=1, source_target_pairs={{0,1},{1,0},{2,3},{3,2},{4,5},{5,4},{6,7},{7,6},{8,9},{9,8},{10,11... | collective-permute-start | bytes 73736 | tf_op jit(solution)/shard_map/ppermute | solution.py:845
  60.9 13.2 %collective-permute-start.5 = (bf16[96,128]{1,0:T(8,128)(2,1)S(1)}, bf16[96,128]{1,0:T(8,128)(2,1)S(1)}, u32[]{:S(2)}, u32[]{:S(2)}) collective-permute-start(bf16[96,128]{1,0:T(8,128)(2,1)S(1)} %get-tuple-element.51), channel_id=1, source_target_pairs={{1,2},{2,1},{3,4},{4,3},{5,6},{6,5},{7,8},{8,7},{9,10},{10,9},{11,... | collective-permute-start | bytes 73736 | tf_op jit(solution)/shard_map/ppermute | solution.py:845
  63.2 10.9 %collective-permute-start.11 = (bf16[4,16,1280]{2,1,0:T(8,128)(2,1)S(1)}, bf16[4,16,1280]{2,1,0:T(8,128)(2,1)S(1)}, u32[]{:S(2)}, u32[]{:S(2)}) collective-permute-start(bf16[4,16,1280]{2,1,0:T(8,128)(2,1)S(1)} %pad_maximum_fusion.when_ref), channel_id=1, source_target_pairs={{0,6},{1,7},{2,4},{3,5},{4,2},{5,3},{6,0},{7,1},{8,14},{9,15},{10,... | collective-permute-start | bytes 491528 | tf_op jit(solution)/shard_map/ppermute | solution.py:716
  65.3 8.7 %collective-permute-start.10 = (bf16[4,16,1280]{2,1,0:T(8,128)(2,1)S(1)}, bf16[4,16,1280]{2,1,0:T(8,128)(2,1)S(1)}, u32[]{:S(2)}, u32[]{:S(2)}) collective-permute-start(bf16[4,16,1280]{2,1,0:T(8,128)(2,1)S(1)} %pad_maximum_fusion.when_ref), channel_id=1, source_target_pairs={{0,2},{1,3},{2,0},{3,1},{4,6},{5,7},{6,4},{7,5},{8,10},{9,11},{10,... | collective-permute-start | bytes 491528 | tf_op jit(solution)/shard_map/ppermute | solution.py:716
  66.2 7.8 %collective-permute-start.9 = (bf16[4,16,1280]{2,1,0:T(8,128)(2,1)S(1)}, bf16[4,16,1280]{2,1,0:T(8,128)(2,1)S(1)}, u32[]{:S(2)}, u32[]{:S(2)}) collective-permute-start(bf16[4,16,1280]{2,1,0:T(8,128)(2,1)S(1)} %pad_maximum_fusion.when_ref), channel_id=1, source_target_pairs={{0,4},{1,5},{2,6},{3,7},{4,0},{5,1},{6,2},{7,3},{8,12},{9,13},{10,... | collective-permute-start | bytes 491528 | tf_op jit(solution)/shard_map/ppermute | solution.py:716
  74.1 2.2 %collective-permute-start.12 = (bf16[16,16,1280]{2,1,0:T(8,128)(2,1)S(1)}, bf16[16,16,1280]{2,1,0:T(8,128)(2,1)S(1)}, u32[]{:S(2)}, u32[]{:S(2)}) collective-permute-start(bf16[16,16,1280]{2,1,0:T(8,128)(2,1)S(1)} %constant_dynamic-update-slice_fusion.held_ref), channel_id=1, source_target_pairs={{0,1},{1,0},{2,3},{3,2},{4,5},{5,4},{6,7},{7,6},{8,9},{9,8},{10,11... | collective-permute-start | bytes 1966088 | tf_op jit(solution)/shard_map/ppermute | solution.py:716
  89.6 1.3 collective-permute-start.13
  89.9 1.0 collective-permute-start.14
  123.6 6.3 %collective-permute-start.17 = (bf16[1,16,1280]{2,1,0:T(8,128)(2,1)S(1)}, bf16[1,16,1280]{2,1,0:T(8,128)(2,1)S(1)}, u32[]{:S(2)}, u32[]{:S(2)}) collective-permute-start(bf16[1,16,1280]{2,1,0:T(8,128)(2,1)S(1)} %bitcast.9), channel_id=1, source_target_pairs={{0,24},{1,25},{2,26},{3,27},{4,28},{5,29},{6,30},{7,31},{8,16},{9,... | collective-permute-start | bytes 122888 | tf_op jit(solution)/shard_map/ppermute | solution.py:716
  124.9 5.1 %collective-permute-start.16 = (bf16[1,16,1280]{2,1,0:T(8,128)(2,1)S(1)}, bf16[1,16,1280]{2,1,0:T(8,128)(2,1)S(1)}, u32[]{:S(2)}, u32[]{:S(2)}) collective-permute-start(bf16[1,16,1280]{2,1,0:T(8,128)(2,1)S(1)} %bitcast.10), channel_id=1, source_target_pairs={{0,8},{1,9},{2,10},{3,11},{4,12},{5,13},{6,14},{7,15},{8,0},{9,1},... | collective-permute-start | bytes 122888 | tf_op jit(solution)/shard_map/ppermute | solution.py:716
  124.9 5.5 %collective-permute-start.15 = (bf16[1,16,1280]{2,1,0:T(8,128)(2,1)S(1)}, bf16[1,16,1280]{2,1,0:T(8,128)(2,1)S(1)}, u32[]{:S(2)}, u32[]{:S(2)}) collective-permute-start(bf16[1,16,1280]{2,1,0:T(8,128)(2,1)S(1)} %bitcast.11), channel_id=1, source_target_pairs={{0,16},{1,17},{2,18},{3,19},{4,20},{5,21},{6,22},{7,23},{8,24},{9,... | collective-permute-start | bytes 122888 | tf_op jit(solution)/shard_map/ppermute | solution.py:716
  128.1 5.9 %collective-permute-start.21 = (bf16[96,128]{1,0:T(8,128)(2,1)S(1)}, bf16[96,128]{1,0:T(8,128)(2,1)S(1)}, u32[]{:S(2)}, u32[]{:S(2)}) collective-permute-start(bf16[96,128]{1,0:T(8,128)(2,1)S(1)} %get-tuple-element.67), channel_id=1, source_target_pairs={{0,1},{1,0},{2,3},{3,2},{4,5},{5,4},{6,7},{7,6},{8,9},{9,8},{10,11... | collective-permute-start | bytes 73736 | tf_op jit(solution)/shard_map/ppermute | solution.py:845
  128.1 5.9 %collective-permute-start.22 = (bf16[96,128]{1,0:T(8,128)(2,1)S(1)}, bf16[96,128]{1,0:T(8,128)(2,1)S(1)}, u32[]{:S(2)}, u32[]{:S(2)}) collective-permute-start(bf16[96,128]{1,0:T(8,128)(2,1)S(1)} %get-tuple-element.68), channel_id=1, source_target_pairs={{1,2},{2,1},{3,4},{4,3},{5,6},{6,5},{7,8},{8,7},{9,10},{10,9},{11,... | collective-permute-start | bytes 73736 | tf_op jit(solution)/shard_map/ppermute | solution.py:845
  130.4 10.9 %collective-permute-start.20 = (bf16[4,16,1280]{2,1,0:T(8,128)(2,1)S(1)}, bf16[4,16,1280]{2,1,0:T(8,128)(2,1)S(1)}, u32[]{:S(2)}, u32[]{:S(2)}) collective-permute-start(bf16[4,16,1280]{2,1,0:T(8,128)(2,1)S(1)} %pad_maximum_fusion.1), channel_id=1, source_target_pairs={{0,6},{1,7},{2,4},{3,5},{4,2},{5,3},{6,0},{7,1},{8,14},{9,15},{10,... | collective-permute-start | bytes 491528 | tf_op jit(solution)/shard_map/ppermute | solution.py:716
  132.5 8.7 %collective-permute-start.19 = (bf16[4,16,1280]{2,1,0:T(8,128)(2,1)S(1)}, bf16[4,16,1280]{2,1,0:T(8,128)(2,1)S(1)}, u32[]{:S(2)}, u32[]{:S(2)}) collective-permute-start(bf16[4,16,1280]{2,1,0:T(8,128)(2,1)S(1)} %pad_maximum_fusion.1), channel_id=1, source_target_pairs={{0,2},{1,3},{2,0},{3,1},{4,6},{5,7},{6,4},{7,5},{8,10},{9,11},{10,... | collective-permute-start | bytes 491528 | tf_op jit(solution)/shard_map/ppermute | solution.py:716
  133.4 7.8 %collective-permute-start.18 = (bf16[4,16,1280]{2,1,0:T(8,128)(2,1)S(1)}, bf16[4,16,1280]{2,1,0:T(8,128)(2,1)S(1)}, u32[]{:S(2)}, u32[]{:S(2)}) collective-permute-start(bf16[4,16,1280]{2,1,0:T(8,128)(2,1)S(1)} %pad_maximum_fusion.1), channel_id=1, source_target_pairs={{0,4},{1,5},{2,6},{3,7},{4,0},{5,1},{6,2},{7,3},{8,12},{9,13},{10,... | collective-permute-start | bytes 491528 | tf_op jit(solution)/shard_map/ppermute | solution.py:716
  141.3 2.2 %collective-permute-start.23 = (bf16[16,16,1280]{2,1,0:T(8,128)(2,1)S(1)}, bf16[16,16,1280]{2,1,0:T(8,128)(2,1)S(1)}, u32[]{:S(2)}, u32[]{:S(2)}) collective-permute-start(bf16[16,16,1280]{2,1,0:T(8,128)(2,1)S(1)} %constant_dynamic-update-slice_fusion.7.held_ref), channel_id=1, source_target_pairs={{0,1},{1,0},{2,3},{3,2},{4,5},{5,4},{6,7},{7,6},{8,9},{9,8},{10,11... | collective-permute-start | bytes 1966088 | tf_op jit(solution)/shard_map/ppermute | solution.py:716
  (2 other events, 23.1 us)

commit v14 on v13

--- a/solution.py
+++ b/solution.py
@@ -157,9 +157,8 @@
         zz[:rows, coarse * K : (coarse + 1) * K] = zb[first : first + rows, :]
 
 
-def convolve_lags(lag, columns, count, taps, zz, fine, acc):
-    channels = len(columns) * LANES
-    own = slice(columns[0] * LANES, columns[0] * LANES + channels)
+def convolve_lags(lag, tile, count, taps, zz, fine, acc):
+    own = slice(tile * LANES, (tile + 1) * LANES)
     rows = count + ROWS
     slot = lag // FINE % 2 * FINE
     for pair in range(0, FINE, 2):
@@ -172,31 +171,25 @@
         )
         product = lax.dot_general(zz[:rows, :], weights, NT, preferred_element_type=jnp.float32)
         for j in range(2):
-            for index, tile in enumerate(columns):
-                column = j * channels + index * LANES
-                fine[slot + pair + j, tile, :rows, :] = product[:, column : column + LANES]
-    for tile in columns:
-        total = None if lag == 0 else acc[tile, :count, :]
-        for j in range(FINE):
-            first = ROWS - lag - j
-            part = fine[slot + j, tile, first : first + count, :]
-            total = part if total is None else total + part
-        acc[tile, :count, :] = total
-
-
-def convolve(zb, begin, count, taps, zz, fine, acc):
+            fine[slot + pair + j, tile, :rows, :] = product[:, j * LANES : (j + 1) * LANES]
+    total = None if lag == 0 else acc[tile, :count, :]
+    for j in range(FINE):
+        first = ROWS - lag - j
+        part = fine[slot + j, tile, first : first + count, :]
+        total = part if total is None else total + part
+    acc[tile, :count, :] = total
+
+
+def convolve(zb, begin, count, taps, zz, fine, acc, after):
     lag_rows(zb, begin, count, zz)
-    columns = list(range(taps.shape[2] // LANES))
-    for lag in range(0, ROWS, FINE):
-        convolve_lags(lag, columns, count, taps, zz, fine, acc)
-
-
-def correlate(rb, count, taps, rr, fine, acc):
-    channels = taps.shape[2]
+    for tile in range(taps.shape[2] // LANES):
+        for lag in range(0, ROWS, FINE):
+            convolve_lags(lag, tile, count, taps, zz, fine, acc)
+        after(tile)
+
+
+def correlate(count, taps, rr, fine, acc):
     rows = count + ROWS
-    for coarse in range(COARSE):
-        first = ROWS * coarse
-        rr[:rows, coarse * channels : (coarse + 1) * channels] = rb[first : first + rows, :]
     for lag in range(0, ROWS, FINE):
         slot = lag // FINE % 2 * FINE
         for pair in range(0, FINE, 2):
@@ -325,15 +318,18 @@
     return take
 
 
-def residual_rows(rb, pieces, start, acc, total_time):
-    rows = rb.shape[0]
+def residual_tile(tile, rb, rr, pieces, start, acc, total_time):
+    rows, channels = rb.shape
+    column = slice(tile * LANES, (tile + 1) * LANES)
     moment = start + lax.broadcasted_iota(jnp.int32, (rows, LANES), 0)
     scale = (C * L) ** (-0.5)
-    for tile in range(acc.shape[0]):
-        column = slice(tile * LANES, (tile + 1) * LANES)
-        signal = jnp.concatenate([piece[:, column] for piece in pieces], axis=0)
-        value = signal.astype(jnp.float32) - scale * acc[tile, :rows, :]
-        rb[:, column] = jnp.where(moment < total_time, value, 0.0).astype(jnp.bfloat16)
+    signal = jnp.concatenate([piece[:, column] for piece in pieces], axis=0)
+    value = signal.astype(jnp.float32) - scale * acc[tile, :rows, :]
+    rb[:, column] = jnp.where(moment < total_time, value, 0.0).astype(jnp.bfloat16)
+    for coarse in range(COARSE):
+        first = coarse * channels + tile * LANES
+        part = rb[ROWS * coarse : ROWS * coarse + rr.shape[0], column]
+        rr[:, first : first + LANES] = part
 
 
 def stepped_codes(state, acc, limit):
@@ -365,22 +361,27 @@
 
     by_side(put, first_ref, second_ref)
     by_side(put_signal, next_first, next_second)
+    start = lax.axis_index("tm") * segment
+
+    def settle_tile(tile):
+        residual_tile(tile, rb, rr, (signal_ref, beyond), start, acc, total_time)
+
     if patching:
         columns, *turned = take(1 + GROUPS)
         lag_rows(zb, L, segment + L, zz)
 
         def convolve_after(lag, tile):
-            convolve_lags(lag, [tile], segment + L, taps, zz, fine, acc)
+            convolve_lags(lag, tile, segment + L, taps, zz, fine, acc)
+            if lag + FINE == ROWS:
+                settle_tile(tile)
 
         patch_taps(
             first_row_of(plan_ref, patching - 1), atoms[0], taps, columns, turned, convolve_after
         )
         ferry.turn_round()
     else:
-        convolve(zb, L, segment + L, taps, zz, fine, acc)
-    start = lax.axis_index("tm") * segment
-    residual_rows(rb, (signal_ref, beyond), start, acc, total_time)
-    correlate(rb, segment, taps, rr, fine, acc)
+        convolve(zb, L, segment + L, taps, zz, fine, acc, settle_tile)
+    correlate(segment, taps, rr, fine, acc)
     state = stepped_codes(state_ref[...], acc, limit_ref[...])
     state_out[...] = state
     low = state.astype(jnp.bfloat16)
@@ -458,11 +459,14 @@
 
     by_side(put, first_ref, second_ref)
     by_side(put_signal, next_first, next_second)
-    convolve(zb, L, reach, taps, zz, fine, acc)
+    start = lax.axis_index("tm") * segment
+
+    def settle_tile(tile):
+        residual_tile(tile, rb, rr, (signal_ref, beyond), start, acc, peers * segment)
+
+    convolve(zb, L, reach, taps, zz, fine, acc, settle_tile)
     ferry.turn_round()
-    start = lax.axis_index("tm") * segment
-    residual_rows(rb, (signal_ref, beyond), start, acc, peers * segment)
-    correlate(rb, segment, taps, rr, fine, acc)
+    correlate(segment, taps, rr, fine, acc)
     state = stepped_codes(state_ref[...], acc, limit_ref[...])
     low = state.astype(jnp.bfloat16)
     if not last:
@@ -472,11 +476,11 @@
     zb[:L, :] = jnp.zeros((L, K), jnp.bfloat16)
     zb[L:reach, :] = low
     zb[reach:, :] = jnp.zeros((L, K), jnp.bfloat16)
-    convolve(zb, L, reach, taps, zz, fine, acc)
     scale = (C * L) ** (-0.5)
     block = codes_out[pl.ds(first_row_of(plan_ref, step), BLOCK_ATOMS), :]
     share = channels // peers
-    for tile in range(channels // LANES):
+
+    def pack_tile(tile):
         column = slice(tile * LANES, (tile + 1) * LANES)
         value = signal_ref[:, column].astype(jnp.float32) - scale * acc[tile, :segment, :]
         if last:
@@ -486,12 +490,14 @@
             [-scale * acc[tile, segment:reach, :], jnp.zeros((segment - L, LANES), jnp.float32)], axis=0
         )
         tall[1, column, :] = spill.T
-    for peer in range(peers):
-        for part in range(2):
-            packed[peer, part * share : (part + 1) * share, :] = tall[
-                part, peer * share : (peer + 1) * share, :
-            ]
-        packed[peer, 2 * share :, :] = block
+        for peer in range(tile * LANES // share, (tile + 1) * LANES // share):
+            for part in range(2):
+                packed[peer, part * share : (part + 1) * share, :] = tall[
+                    part, peer * share : (peer + 1) * share, :
+                ]
+            packed[peer, 2 * share :, :] = block
+
+    convolve(zb, L, reach, taps, zz, fine, acc, pack_tile)
     payload_out[...] = packed[...].astype(jnp.bfloat16)
     ferry.close()
 
@@ -560,14 +566,16 @@
 
     zb[L:, :] = jnp.zeros((L, K), jnp.bfloat16)
     by_side(put, first_ref, second_ref)
-    convolve(zb, L, L, taps, zz, fine, acc)
     scale = (C * L) ** (-0.5)
-    for tile in range(channels // LANES):
+
+    def settle_tile(tile):
         column = slice(tile * LANES, (tile + 1) * LANES)
         value = jnp.concatenate(
             [partial_ref[:L, column] - scale * acc[tile], partial_ref[L:, column]], axis=0
         )
         resid_out[column, :] = value.T
+
+    convolve(zb, L, L, taps, zz, fine, acc, settle_tile)
     for store in stores:
         store.wait()
 

time: 147 us -> 147 us (level)
  no operation moved by 1% of the time
where the time goes in v14:
time: 147 us; the launch traced here: 146 us
  Pallas kernels  61.9 us (42%)
  blocking collectives  43.8 us (30%)
  starting transfers between devices  24.1 us (16%)
  waiting for transfers between devices  13.9 us (9%)
    all_to_all x2, blocking collectives, whole_channels(): blocks = lax.all_to_all(payload, 'tm', 0, 0, tiled=True)  43.8 us
    pallas_call x2, Pallas kernels, conclude(): pl.pallas_call(functools.partial(conclude_kernel, peers, step, ferry[2]),...  16.9 us
    pallas_call x2, Pallas kernels, iterate(): pl.pallas_call(functools.partial(iterate_kernel, peers * segment, step if...  16.5 us
    ppermute x14, starting transfers between devices, exchanged(): return lax.ppermute(shard, 'tm', [(i, i ^ mask) for i in range(peers)])  16.2 us
    ppermute x14, waiting for transfers between devices, exchanged(): return lax.ppermute(shard, 'tm', [(i, i ^ mask) for i in range(peers)])  13.4 us
    pallas_call x1, Pallas kernels, layout(): pl.pallas_call(layout_kernel, grid=(channels // block,), in_specs=[pl.Blo...  9.22 us
    ppermute x10, starting transfers between devices, swaps(): lax.ppermute(edge, 'tm', pair)  7.94 us
    pallas_call x2, Pallas kernels, share_gradient(): pl.pallas_call(functools.partial(gradient_kernel, share, step), in_specs=...  5.72 us
  transfers between devices with their start and end apart: 24, of which 10 were waited for; matrix products, arithmetic and copies ran while one was open for 1% of the time, Pallas kernels for 11%

profile of v14, /device:TPU:0, one launch (start us, length us, event | category | flops | bytes accessed | tf_op | source)
XLA Modules:
  0.0 146.3 jit_solution(12870705153030737096)
XLA Ops:
  2.9 9.2 %layout.1.refs_6_.refs_7_ = bf16[6,16,384,128]{3,2,1,0:T(8,128)(2,1)S(1)} custom-call(f32[128,36864]{1,0:T(8,128)} %dict_hbm.5), custom_call_target="tpu_custom_call" | custom-call | tf_op jit(solution)/shard_map/layout/pallas_call | solution.py:113
  12.2 5.1 %iterate.2 = (f32[128,128]{1,0:T(8,128)S(1)}, bf16[96,128]{1,0:T(8,128)(2,1)S(1)}, bf16[96,128]{1,0:T(8,128)(2,1)S(1)}) custom-call(s32[8]{0:T(128)S(1)} %copy-done, f32[1,128]{1,0:T(1,128)S(1)} %bitcast.13, f32[128,128]{1,0:T(8,128)S(1)} %get-tuple-element.39.refs_0_, bf16[96,512]{1,0:T(8,128)(2,1)S(1)} %collective-permute-done.refs_1_.refs_4_, ...), custom_call_target="tpu_custom_call" | custom-call | tf_op jit(solution)/shard_map/iterate/pallas_call | solution.py:398
  17.3 3.9 %collective-permute-start.2 = (bf16[96,128]{1,0:T(8,128)(2,1)S(1)}, bf16[96,128]{1,0:T(8,128)(2,1)S(1)}, u32[]{:S(2)}, u32[]{:S(2)}) collective-permute-start(bf16[96,128]{1,0:T(8,128)(2,1)S(1)} %get-tuple-element.44), channel_id=1, source_target_pairs={{0,1},{1,0},{2,3},{3,2},{4,5},{5,4},{6,7},{7,6},{8,9},{9,8},{10,11... | collective-permute-start | bytes 73736 | tf_op jit(solution)/shard_map/ppermute | solution.py:853
  22.1 8.4 %conclude.2 = (bf16[32,40,128]{2,1,0:T(8,128)(2,1)S(1)}, f32[128,128]{1,0:T(8,128)S(1)}, bf16[96,128]{1,0:T(8,128)(2,1)S(1)}, bf16[96,128]{1,0:T(8,128)(2,1)S(1)}, f32[128,36864]{1,0:T(8,128)}) custom-call(s32[8]{0:T(128)S(1)} %copy-done, f32[1,128]{1,0:T(1,128)S(1)} %bitcast.14, f32[128,128]{1,0:T(8,128)S(1)} %get-tuple-element.43.refs_0_, ...), custom_call_target="tpu_custom_call" | custom-call | tf_op jit(solution)/shard_map/conclude/pallas_call | solution.py:515
  30.5 22.7 %all_to_all.10.blocks_ref = bf16[32,40,128]{2,1,0:T(8,128)(2,1)S(1)} all-to-all(bf16[32,40,128]{2,1,0:T(8,128)(2,1)S(1)} %get-tuple-element.49), channel_id=1, replica_groups=mesh['tm'=32,'chan'=1] {'tm'}, dimensions={0} | all-to-all | bytes 655360 | tf_op jit(solution)/shard_map/all_to_all | solution.py:877
  53.2 2.9 %gradient.2 = bf16[16,1280]{1,0:T(8,128)(2,1)S(1)} custom-call(s32[8]{0:T(128)S(1)} %copy-done, bf16[32,40,128]{2,1,0:T(8,128)(2,1)S(1)} %all_to_all.10.blocks_ref, f32[128,36864]{1,0:T(8,128)} %dict_hbm.5), custom_call_target="tpu_custom_call" | custom-call | tf_op jit(solution)/shard_map/gradient/pallas_call | solution.py:686
  56.0 1.2 collective-permute-start.8
  57.3 3.2 %collective-permute-start.6 = (bf16[1,16,1280]{2,1,0:T(8,128)(2,1)S(1)}, bf16[1,16,1280]{2,1,0:T(8,128)(2,1)S(1)}, u32[]{:S(2)}, u32[]{:S(2)}) collective-permute-start(bf16[1,16,1280]{2,1,0:T(8,128)(2,1)S(1)} %bitcast.7), channel_id=1, source_target_pairs={{0,16},{1,17},{2,18},{3,19},{4,20},{5,21},{6,22},{7,23},{8,24},{9,... | collective-permute-start | bytes 122888 | tf_op jit(solution)/shard_map/ppermute | solution.py:724
  61.2 1.2 collective-permute-done.8
  62.8 2.2 %collective-permute-start.11 = (bf16[4,16,1280]{2,1,0:T(8,128)(2,1)S(1)}, bf16[4,16,1280]{2,1,0:T(8,128)(2,1)S(1)}, u32[]{:S(2)}, u32[]{:S(2)}) collective-permute-start(bf16[4,16,1280]{2,1,0:T(8,128)(2,1)S(1)} %pad_maximum_fusion.when_ref), channel_id=1, source_target_pairs={{0,6},{1,7},{2,4},{3,5},{4,2},{5,3},{6,0},{7,1},{8,14},{9,15},{10,... | collective-permute-start | bytes 491528 | tf_op jit(solution)/shard_map/ppermute | solution.py:724
  66.3 3.4 %recall.1 = (f32[16,36864]{1,0:T(8,128)S(1)}, f32[16,36864]{1,0:T(8,128)S(1)}, f32[16,128]{1,0:T(8,128)S(1)}, f32[16,128]{1,0:T(8,128)S(1)}) custom-call(s32[8]{0:T(128)S(1)} %copy-done, f32[128,36864]{1,0:T(8,128)} %dict_hbm.5, bf16[4,16,1280]{2,1,0:T(8,128)(2,1)S(1)} %pad_maximum_fusion.when_ref), custom_call_target="tpu_custom_call" | custom-call | tf_op jit(solution)/shard_map/recall/pallas_call | solution.py:765
  69.7 3.9 %collective-permute-done.9 = bf16[4,16,1280]{2,1,0:T(8,128)(2,1)S(1)} collective-permute-done((bf16[4,16,1280]{2,1,0:T(8,128)(2,1)S(1)}, bf16[4,16,1280]{2,1,0:T(8,128)(2,1)S(1)}, u32[]{:S(2)}, u32[]{:S(2)}) %collective-permute-start.9) | collective-permute-done | bytes 163872 | tf_op jit(solution)/shard_map/ppermute | solution.py:724
  73.8 2.1 %collective-permute-done.12.came_ref = bf16[16,16,1280]{2,1,0:T(8,128)(2,1)S(1)} collective-permute-done((bf16[16,16,1280]{2,1,0:T(8,128)(2,1)S(1)}, bf16[16,16,1280]{2,1,0:T(8,128)(2,1)S(1)}, u32[]{:S(2)}, u32[]{:S(2)}) %collective-permute-start.12) | collective-permute-done | bytes 655392 | tf_op jit(solution)/shard_map/ppermute | solution.py:724
  75.9 2.0 %renew.2.refs_6_.refs_0_ = f32[16,36864]{1,0:T(8,128)S(1)} custom-call(s32[8]{0:T(128)S(1)} %copy-done, bf16[16,16,1280]{2,1,0:T(8,128)(2,1)S(1)} %constant_dynamic-update-slice_fusion.held_ref, bf16[16,16,1280]{2,1,0:T(8,128)(2,1)S(1)} %collective-permute-done.12.came_ref, f32[16,36864]{1,0:T(8,128)S(1)} %get-tuple-element.52.old, ...), custom_call_target="tpu_custom_call" | custom-call | tf_op jit(solution)/shard_map/renew/pallas_call | solution.py:834
  77.9 11.4 %iterate.3 = (f32[128,128]{1,0:T(8,128)S(1)}, bf16[96,128]{1,0:T(8,128)(2,1)S(1)}, bf16[96,128]{1,0:T(8,128)(2,1)S(1)}, bf16[6,16,384,128]{3,2,1,0:T(8,128)(2,1)S(1)}, f32[128,36864]{1,0:T(8,128)}) custom-call(s32[8]{0:T(128)S(1)} %copy-done, f32[1,128]{1,0:T(1,128)S(1)} %bitcast.15, ...), custom_call_target="tpu_custom_call", output_to_operand_aliasing={{3}: (9, {}), {4}: (11, {})} | custom-call | tf_op jit(solution)/shard_map/iterate/pallas_call | solution.py:398
  90.6 8.5 %conclude.3 = (bf16[32,40,128]{2,1,0:T(8,128)(2,1)S(1)}, f32[128,384]{1,0:T(8,128)S(1)}, f32[128,128]{1,0:T(8,128)S(1)}, bf16[96,128]{1,0:T(8,128)(2,1)S(1)}, bf...) custom-call(s32[8]{0:T(128)S(1)} %copy-done, f32[1,128]{1,0:T(1,128)S(1)} %bitcast.16, ...), custom_call_target="tpu_custom_call", output_to_operand_aliasing={{5}: (10, {})} | custom-call | tf_op jit(solution)/shard_map/conclude/pallas_call | solution.py:515
  99.1 21.1 %all_to_all.11.blocks_ref = bf16[32,40,128]{2,1,0:T(8,128)(2,1)S(1)} all-to-all(bf16[32,40,128]{2,1,0:T(8,128)(2,1)S(1)} %get-tuple-element.62), channel_id=1, replica_groups=mesh['tm'=32,'chan'=1] {'tm'}, dimensions={0} | all-to-all | bytes 655360 | tf_op jit(solution)/shard_map/all_to_all | solution.py:877
  120.2 2.9 %gradient.3 = bf16[16,1280]{1,0:T(8,128)(2,1)S(1)} custom-call(s32[8]{0:T(128)S(1)} %copy-done, bf16[32,40,128]{2,1,0:T(8,128)(2,1)S(1)} %all_to_all.11.blocks_ref, f32[128,36864]{1,0:T(8,128)} %dict_hbm.5), custom_call_target="tpu_custom_call" | custom-call | tf_op jit(solution)/shard_map/gradient/pallas_call | solution.py:686
  123.0 1.2 collective-permute-start.17
  124.3 3.2 %collective-permute-start.15 = (bf16[1,16,1280]{2,1,0:T(8,128)(2,1)S(1)}, bf16[1,16,1280]{2,1,0:T(8,128)(2,1)S(1)}, u32[]{:S(2)}, u32[]{:S(2)}) collective-permute-start(bf16[1,16,1280]{2,1,0:T(8,128)(2,1)S(1)} %bitcast.11), channel_id=1, source_target_pairs={{0,16},{1,17},{2,18},{3,19},{4,20},{5,21},{6,22},{7,23},{8,24},{9,... | collective-permute-start | bytes 122888 | tf_op jit(solution)/shard_map/ppermute | solution.py:724
  129.8 2.2 %collective-permute-start.20 = (bf16[4,16,1280]{2,1,0:T(8,128)(2,1)S(1)}, bf16[4,16,1280]{2,1,0:T(8,128)(2,1)S(1)}, u32[]{:S(2)}, u32[]{:S(2)}) collective-permute-start(bf16[4,16,1280]{2,1,0:T(8,128)(2,1)S(1)} %pad_maximum_fusion.1), channel_id=1, source_target_pairs={{0,6},{1,7},{2,4},{3,5},{4,2},{5,3},{6,0},{7,1},{8,14},{9,15},{10,... | collective-permute-start | bytes 491528 | tf_op jit(solution)/shard_map/ppermute | solution.py:724
  133.4 3.8 %settle.1 = (f32[384,128]{1,0:T(8,128)S(1)}, f32[128,36864]{1,0:T(8,128)}) custom-call(s32[8]{0:T(128)S(1)} %copy-done, f32[128,384]{1,0:T(8,128)S(1)} %get-tuple-element.64.partial_ref, bf16[96,128]{1,0:T(8,128)(2,1)S(1)} %collective-permute-done.21.first_ref, ...), custom_call_target="tpu_custom_call", output_to_operand_aliasing={{1}: (6, {})} | custom-call | tf_op jit(solution)/shard_map/settle/pallas_call | solution.py:586
  137.2 3.4 %collective-permute-done.18 = bf16[4,16,1280]{2,1,0:T(8,128)(2,1)S(1)} collective-permute-done((bf16[4,16,1280]{2,1,0:T(8,128)(2,1)S(1)}, bf16[4,16,1280]{2,1,0:T(8,128)(2,1)S(1)}, u32[]{:S(2)}, u32[]{:S(2)}) %collective-permute-start.18) | collective-permute-done | bytes 163872 | tf_op jit(solution)/shard_map/ppermute | solution.py:724
  142.8 3.3 %renew.3 = f32[128,36864]{1,0:T(8,128)} custom-call(s32[8]{0:T(128)S(1)} %copy-done, bf16[16,16,1280]{2,1,0:T(8,128)(2,1)S(1)} %constant_dynamic-update-slice_fusion.7.held_ref, bf16[16,16,1280]{2,1,0:T(8,128)(2,1)S(1)} %collective-permute-done.23.came_ref, f32[16,36864]{1,0:T(8,128)S(1)} %get-tuple-element.72.old, ...), custom_call_target="tpu_custom_call", output_to_operand_aliasing={{}: (5, {})} | custom-call | tf_op jit(solution)/shard_map/renew/pallas_call | solution.py:834
  (60 shorter events, 12.9 us)
Async XLA Ops:
  1.8 10.4 %collective-permute-start = (bf16[96,512]{1,0:T(8,128)(2,1)S(1)}, bf16[96,512]{1,0:T(8,128)(2,1)S(1)}, u32[]{:S(2)}, u32[]{:S(2)}) collective-permute-start(bf16[96,512]{1,0:T(8,128)(2,1)S(1)} %get-tuple-element.40), channel_id=1, source_target_pairs={{0,1},{1,0},{2,3},{3,2},{4,5},{5,4},{6,7},{7,6},{8,9},{9,8},{10,11... | collective-permute-start | bytes 294920 | tf_op jit(solution)/shard_map/ppermute | solution.py:853
  2.3 9.9 %collective-permute-start.1 = (bf16[96,512]{1,0:T(8,128)(2,1)S(1)}, bf16[96,512]{1,0:T(8,128)(2,1)S(1)}, u32[]{:S(2)}, u32[]{:S(2)}) collective-permute-start(bf16[96,512]{1,0:T(8,128)(2,1)S(1)} %get-tuple-element.41), channel_id=1, source_target_pairs={{1,2},{2,1},{3,4},{4,3},{5,6},{6,5},{7,8},{8,7},{9,10},{10,9},{11,... | collective-permute-start | bytes 294920 | tf_op jit(solution)/shard_map/ppermute | solution.py:853
  17.3 4.8 %collective-permute-start.2 = (bf16[96,128]{1,0:T(8,128)(2,1)S(1)}, bf16[96,128]{1,0:T(8,128)(2,1)S(1)}, u32[]{:S(2)}, u32[]{:S(2)}) collective-permute-start(bf16[96,128]{1,0:T(8,128)(2,1)S(1)} %get-tuple-element.44), channel_id=1, source_target_pairs={{0,1},{1,0},{2,3},{3,2},{4,5},{5,4},{6,7},{7,6},{8,9},{9,8},{10,11... | collective-permute-start | bytes 73736 | tf_op jit(solution)/shard_map/ppermute | solution.py:853
  21.2 0.9 collective-permute-start.3
  56.0 6.3 %collective-permute-start.8 = (bf16[1,16,1280]{2,1,0:T(8,128)(2,1)S(1)}, bf16[1,16,1280]{2,1,0:T(8,128)(2,1)S(1)}, u32[]{:S(2)}, u32[]{:S(2)}) collective-permute-start(bf16[1,16,1280]{2,1,0:T(8,128)(2,1)S(1)} %bitcast.5), channel_id=1, source_target_pairs={{0,24},{1,25},{2,26},{3,27},{4,28},{5,29},{6,30},{7,31},{8,16},{9,... | collective-permute-start | bytes 122888 | tf_op jit(solution)/shard_map/ppermute | solution.py:724
  57.3 5.1 %collective-permute-start.7 = (bf16[1,16,1280]{2,1,0:T(8,128)(2,1)S(1)}, bf16[1,16,1280]{2,1,0:T(8,128)(2,1)S(1)}, u32[]{:S(2)}, u32[]{:S(2)}) collective-permute-start(bf16[1,16,1280]{2,1,0:T(8,128)(2,1)S(1)} %bitcast.6), channel_id=1, source_target_pairs={{0,8},{1,9},{2,10},{3,11},{4,12},{5,13},{6,14},{7,15},{8,0},{9,1},... | collective-permute-start | bytes 122888 | tf_op jit(solution)/shard_map/ppermute | solution.py:724
  57.3 5.5 %collective-permute-start.6 = (bf16[1,16,1280]{2,1,0:T(8,128)(2,1)S(1)}, bf16[1,16,1280]{2,1,0:T(8,128)(2,1)S(1)}, u32[]{:S(2)}, u32[]{:S(2)}) collective-permute-start(bf16[1,16,1280]{2,1,0:T(8,128)(2,1)S(1)} %bitcast.7), channel_id=1, source_target_pairs={{0,16},{1,17},{2,18},{3,19},{4,20},{5,21},{6,22},{7,23},{8,24},{9,... | collective-permute-start | bytes 122888 | tf_op jit(solution)/shard_map/ppermute | solution.py:724
  60.5 13.2 %collective-permute-start.4 = (bf16[96,128]{1,0:T(8,128)(2,1)S(1)}, bf16[96,128]{1,0:T(8,128)(2,1)S(1)}, u32[]{:S(2)}, u32[]{:S(2)}) collective-permute-start(bf16[96,128]{1,0:T(8,128)(2,1)S(1)} %get-tuple-element.50), channel_id=1, source_target_pairs={{0,1},{1,0},{2,3},{3,2},{4,5},{5,4},{6,7},{7,6},{8,9},{9,8},{10,11... | collective-permute-start | bytes 73736 | tf_op jit(solution)/shard_map/ppermute | solution.py:853
  60.5 13.2 %collective-permute-start.5 = (bf16[96,128]{1,0:T(8,128)(2,1)S(1)}, bf16[96,128]{1,0:T(8,128)(2,1)S(1)}, u32[]{:S(2)}, u32[]{:S(2)}) collective-permute-start(bf16[96,128]{1,0:T(8,128)(2,1)S(1)} %get-tuple-element.51), channel_id=1, source_target_pairs={{1,2},{2,1},{3,4},{4,3},{5,6},{6,5},{7,8},{8,7},{9,10},{10,9},{11,... | collective-permute-start | bytes 73736 | tf_op jit(solution)/shard_map/ppermute | solution.py:853
  62.8 10.9 %collective-permute-start.11 = (bf16[4,16,1280]{2,1,0:T(8,128)(2,1)S(1)}, bf16[4,16,1280]{2,1,0:T(8,128)(2,1)S(1)}, u32[]{:S(2)}, u32[]{:S(2)}) collective-permute-start(bf16[4,16,1280]{2,1,0:T(8,128)(2,1)S(1)} %pad_maximum_fusion.when_ref), channel_id=1, source_target_pairs={{0,6},{1,7},{2,4},{3,5},{4,2},{5,3},{6,0},{7,1},{8,14},{9,15},{10,... | collective-permute-start | bytes 491528 | tf_op jit(solution)/shard_map/ppermute | solution.py:724
  64.9 8.7 %collective-permute-start.10 = (bf16[4,16,1280]{2,1,0:T(8,128)(2,1)S(1)}, bf16[4,16,1280]{2,1,0:T(8,128)(2,1)S(1)}, u32[]{:S(2)}, u32[]{:S(2)}) collective-permute-start(bf16[4,16,1280]{2,1,0:T(8,128)(2,1)S(1)} %pad_maximum_fusion.when_ref), channel_id=1, source_target_pairs={{0,2},{1,3},{2,0},{3,1},{4,6},{5,7},{6,4},{7,5},{8,10},{9,11},{10,... | collective-permute-start | bytes 491528 | tf_op jit(solution)/shard_map/ppermute | solution.py:724
  65.8 7.8 %collective-permute-start.9 = (bf16[4,16,1280]{2,1,0:T(8,128)(2,1)S(1)}, bf16[4,16,1280]{2,1,0:T(8,128)(2,1)S(1)}, u32[]{:S(2)}, u32[]{:S(2)}) collective-permute-start(bf16[4,16,1280]{2,1,0:T(8,128)(2,1)S(1)} %pad_maximum_fusion.when_ref), channel_id=1, source_target_pairs={{0,4},{1,5},{2,6},{3,7},{4,0},{5,1},{6,2},{7,3},{8,12},{9,13},{10,... | collective-permute-start | bytes 491528 | tf_op jit(solution)/shard_map/ppermute | solution.py:724
  73.7 2.2 %collective-permute-start.12 = (bf16[16,16,1280]{2,1,0:T(8,128)(2,1)S(1)}, bf16[16,16,1280]{2,1,0:T(8,128)(2,1)S(1)}, u32[]{:S(2)}, u32[]{:S(2)}) collective-permute-start(bf16[16,16,1280]{2,1,0:T(8,128)(2,1)S(1)} %constant_dynamic-update-slice_fusion.held_ref), channel_id=1, source_target_pairs={{0,1},{1,0},{2,3},{3,2},{4,5},{5,4},{6,7},{7,6},{8,9},{9,8},{10,11... | collective-permute-start | bytes 1966088 | tf_op jit(solution)/shard_map/ppermute | solution.py:724
  89.3 1.3 collective-permute-start.13
  89.5 1.0 collective-permute-start.14
  123.0 6.3 %collective-permute-start.17 = (bf16[1,16,1280]{2,1,0:T(8,128)(2,1)S(1)}, bf16[1,16,1280]{2,1,0:T(8,128)(2,1)S(1)}, u32[]{:S(2)}, u32[]{:S(2)}) collective-permute-start(bf16[1,16,1280]{2,1,0:T(8,128)(2,1)S(1)} %bitcast.9), channel_id=1, source_target_pairs={{0,24},{1,25},{2,26},{3,27},{4,28},{5,29},{6,30},{7,31},{8,16},{9,... | collective-permute-start | bytes 122888 | tf_op jit(solution)/shard_map/ppermute | solution.py:724
  124.3 5.1 %collective-permute-start.16 = (bf16[1,16,1280]{2,1,0:T(8,128)(2,1)S(1)}, bf16[1,16,1280]{2,1,0:T(8,128)(2,1)S(1)}, u32[]{:S(2)}, u32[]{:S(2)}) collective-permute-start(bf16[1,16,1280]{2,1,0:T(8,128)(2,1)S(1)} %bitcast.10), channel_id=1, source_target_pairs={{0,8},{1,9},{2,10},{3,11},{4,12},{5,13},{6,14},{7,15},{8,0},{9,1},... | collective-permute-start | bytes 122888 | tf_op jit(solution)/shard_map/ppermute | solution.py:724
  124.3 5.5 %collective-permute-start.15 = (bf16[1,16,1280]{2,1,0:T(8,128)(2,1)S(1)}, bf16[1,16,1280]{2,1,0:T(8,128)(2,1)S(1)}, u32[]{:S(2)}, u32[]{:S(2)}) collective-permute-start(bf16[1,16,1280]{2,1,0:T(8,128)(2,1)S(1)} %bitcast.11), channel_id=1, source_target_pairs={{0,16},{1,17},{2,18},{3,19},{4,20},{5,21},{6,22},{7,23},{8,24},{9,... | collective-permute-start | bytes 122888 | tf_op jit(solution)/shard_map/ppermute | solution.py:724
  127.5 5.9 %collective-permute-start.21 = (bf16[96,128]{1,0:T(8,128)(2,1)S(1)}, bf16[96,128]{1,0:T(8,128)(2,1)S(1)}, u32[]{:S(2)}, u32[]{:S(2)}) collective-permute-start(bf16[96,128]{1,0:T(8,128)(2,1)S(1)} %get-tuple-element.67), channel_id=1, source_target_pairs={{0,1},{1,0},{2,3},{3,2},{4,5},{5,4},{6,7},{7,6},{8,9},{9,8},{10,11... | collective-permute-start | bytes 73736 | tf_op jit(solution)/shard_map/ppermute | solution.py:853
  127.5 5.9 %collective-permute-start.22 = (bf16[96,128]{1,0:T(8,128)(2,1)S(1)}, bf16[96,128]{1,0:T(8,128)(2,1)S(1)}, u32[]{:S(2)}, u32[]{:S(2)}) collective-permute-start(bf16[96,128]{1,0:T(8,128)(2,1)S(1)} %get-tuple-element.68), channel_id=1, source_target_pairs={{1,2},{2,1},{3,4},{4,3},{5,6},{6,5},{7,8},{8,7},{9,10},{10,9},{11,... | collective-permute-start | bytes 73736 | tf_op jit(solution)/shard_map/ppermute | solution.py:853
  129.8 10.9 %collective-permute-start.20 = (bf16[4,16,1280]{2,1,0:T(8,128)(2,1)S(1)}, bf16[4,16,1280]{2,1,0:T(8,128)(2,1)S(1)}, u32[]{:S(2)}, u32[]{:S(2)}) collective-permute-start(bf16[4,16,1280]{2,1,0:T(8,128)(2,1)S(1)} %pad_maximum_fusion.1), channel_id=1, source_target_pairs={{0,6},{1,7},{2,4},{3,5},{4,2},{5,3},{6,0},{7,1},{8,14},{9,15},{10,... | collective-permute-start | bytes 491528 | tf_op jit(solution)/shard_map/ppermute | solution.py:724
  131.9 8.7 %collective-permute-start.19 = (bf16[4,16,1280]{2,1,0:T(8,128)(2,1)S(1)}, bf16[4,16,1280]{2,1,0:T(8,128)(2,1)S(1)}, u32[]{:S(2)}, u32[]{:S(2)}) collective-permute-start(bf16[4,16,1280]{2,1,0:T(8,128)(2,1)S(1)} %pad_maximum_fusion.1), channel_id=1, source_target_pairs={{0,2},{1,3},{2,0},{3,1},{4,6},{5,7},{6,4},{7,5},{8,10},{9,11},{10,... | collective-permute-start | bytes 491528 | tf_op jit(solution)/shard_map/ppermute | solution.py:724
  132.8 7.8 %collective-permute-start.18 = (bf16[4,16,1280]{2,1,0:T(8,128)(2,1)S(1)}, bf16[4,16,1280]{2,1,0:T(8,128)(2,1)S(1)}, u32[]{:S(2)}, u32[]{:S(2)}) collective-permute-start(bf16[4,16,1280]{2,1,0:T(8,128)(2,1)S(1)} %pad_maximum_fusion.1), channel_id=1, source_target_pairs={{0,4},{1,5},{2,6},{3,7},{4,0},{5,1},{6,2},{7,3},{8,12},{9,13},{10,... | collective-permute-start | bytes 491528 | tf_op jit(solution)/shard_map/ppermute | solution.py:724
  140.7 2.2 %collective-permute-start.23 = (bf16[16,16,1280]{2,1,0:T(8,128)(2,1)S(1)}, bf16[16,16,1280]{2,1,0:T(8,128)(2,1)S(1)}, u32[]{:S(2)}, u32[]{:S(2)}) collective-permute-start(bf16[16,16,1280]{2,1,0:T(8,128)(2,1)S(1)} %constant_dynamic-update-slice_fusion.7.held_ref), channel_id=1, source_target_pairs={{0,1},{1,0},{2,3},{3,2},{4,5},{5,4},{6,7},{7,6},{8,9},{9,8},{10,11... | collective-permute-start | bytes 1966088 | tf_op jit(solution)/shard_map/ppermute | solution.py:724
  (2 other events, 23.1 us)

commit v15 on v14

--- a/solution.py
+++ b/solution.py
@@ -21,6 +21,7 @@
 ROWS = 16
 COARSE = L // ROWS
 STRIDE = L + 1
+TURNED_ROWS = -(-(ROWS + 1) * STRIDE // 8) * 8
 GROUPS = 4
 SUBLANES = 8
 COPIED = (48, 40, 40)
@@ -116,7 +117,7 @@
         in_specs=[pl.BlockSpec((K, block * L), lambda i: (0, i))],
         out_specs=vmem(),
         out_shape=pltpu.VMEM((COARSE, ROWS, channels, K), jnp.bfloat16),
-        scratch_shapes=[pltpu.VMEM((ROWS * STRIDE, K), jnp.float32)] * GROUPS,
+        scratch_shapes=[pltpu.VMEM((TURNED_ROWS, K), jnp.float32)] * GROUPS,
         compiler_params=pltpu.CompilerParams(vmem_limit_bytes=VMEM_BYTES),
         name="layout",
     )(far(dictionary))
@@ -415,7 +416,7 @@
         + (
             ferry_scratch(ferry[3], ferry[0].shape[1])
             + [pltpu.VMEM((K, GROUPS * ROWS * L), jnp.bfloat16)]
-            + [pltpu.VMEM((ROWS * STRIDE, K), jnp.float32)] * GROUPS
+            + [pltpu.VMEM((TURNED_ROWS, K), jnp.float32)] * GROUPS
         )
         * patching,
         input_output_aliases={9: 3, 11: 4} if patching else {},

time: 147 us -> 147 us (level)
  no operation moved by 1% of the time
where the time goes in v15:
time: 147 us; the launch traced here: 146 us
  Pallas kernels  61.9 us (42%)
  blocking collectives  43.8 us (30%)
  starting transfers between devices  24.1 us (16%)
  waiting for transfers between devices  13.9 us (9%)
    all_to_all x2, blocking collectives, whole_channels(): blocks = lax.all_to_all(payload, 'tm', 0, 0, tiled=True)  43.8 us
    pallas_call x2, Pallas kernels, conclude(): pl.pallas_call(functools.partial(conclude_kernel, peers, step, ferry[2]),...  16.9 us
    pallas_call x2, Pallas kernels, iterate(): pl.pallas_call(functools.partial(iterate_kernel, peers * segment, step if...  16.5 us
    ppermute x14, starting transfers between devices, exchanged(): return lax.ppermute(shard, 'tm', [(i, i ^ mask) for i in range(peers)])  16.2 us
    ppermute x14, waiting for transfers between devices, exchanged(): return lax.ppermute(shard, 'tm', [(i, i ^ mask) for i in range(peers)])  13.4 us
    pallas_call x1, Pallas kernels, layout(): pl.pallas_call(layout_kernel, grid=(channels // block,), in_specs=[pl.Blo...  9.24 us
    ppermute x10, starting transfers between devices, swaps(): lax.ppermute(edge, 'tm', pair)  7.95 us
    pallas_call x2, Pallas kernels, share_gradient(): pl.pallas_call(functools.partial(gradient_kernel, share, step), in_specs=...  5.72 us
  transfers between devices with their start and end apart: 24, of which 10 were waited for; matrix products, arithmetic and copies ran while one was open for 1% of the time, Pallas kernels for 11%

profile of v15, /device:TPU:0, one launch (start us, length us, event | category | flops | bytes accessed | tf_op | source)
XLA Modules:
  0.0 146.4 jit_solution(333235595938949309)
XLA Ops:
  2.9 9.2 %layout.1.refs_6_.refs_7_ = bf16[6,16,384,128]{3,2,1,0:T(8,128)(2,1)S(1)} custom-call(f32[128,36864]{1,0:T(8,128)} %dict_hbm.5), custom_call_target="tpu_custom_call" | custom-call | tf_op jit(solution)/shard_map/layout/pallas_call | solution.py:114
  12.2 5.1 %iterate.2 = (f32[128,128]{1,0:T(8,128)S(1)}, bf16[96,128]{1,0:T(8,128)(2,1)S(1)}, bf16[96,128]{1,0:T(8,128)(2,1)S(1)}) custom-call(s32[8]{0:T(128)S(1)} %copy-done, f32[1,128]{1,0:T(1,128)S(1)} %bitcast.13, f32[128,128]{1,0:T(8,128)S(1)} %get-tuple-element.39.refs_0_, bf16[96,512]{1,0:T(8,128)(2,1)S(1)} %collective-permute-done.refs_1_.refs_4_, ...), custom_call_target="tpu_custom_call" | custom-call | tf_op jit(solution)/shard_map/iterate/pallas_call | solution.py:399
  17.3 3.9 %collective-permute-start.2 = (bf16[96,128]{1,0:T(8,128)(2,1)S(1)}, bf16[96,128]{1,0:T(8,128)(2,1)S(1)}, u32[]{:S(2)}, u32[]{:S(2)}) collective-permute-start(bf16[96,128]{1,0:T(8,128)(2,1)S(1)} %get-tuple-element.44), channel_id=1, source_target_pairs={{0,1},{1,0},{2,3},{3,2},{4,5},{5,4},{6,7},{7,6},{8,9},{9,8},{10,11... | collective-permute-start | bytes 73736 | tf_op jit(solution)/shard_map/ppermute | solution.py:854
  22.1 8.4 %conclude.2 = (bf16[32,40,128]{2,1,0:T(8,128)(2,1)S(1)}, f32[128,128]{1,0:T(8,128)S(1)}, bf16[96,128]{1,0:T(8,128)(2,1)S(1)}, bf16[96,128]{1,0:T(8,128)(2,1)S(1)}, f32[128,36864]{1,0:T(8,128)}) custom-call(s32[8]{0:T(128)S(1)} %copy-done, f32[1,128]{1,0:T(1,128)S(1)} %bitcast.14, f32[128,128]{1,0:T(8,128)S(1)} %get-tuple-element.43.refs_0_, ...), custom_call_target="tpu_custom_call" | custom-call | tf_op jit(solution)/shard_map/conclude/pallas_call | solution.py:516
  30.5 22.7 %all_to_all.10.blocks_ref = bf16[32,40,128]{2,1,0:T(8,128)(2,1)S(1)} all-to-all(bf16[32,40,128]{2,1,0:T(8,128)(2,1)S(1)} %get-tuple-element.49), channel_id=1, replica_groups=mesh['tm'=32,'chan'=1] {'tm'}, dimensions={0} | all-to-all | bytes 655360 | tf_op jit(solution)/shard_map/all_to_all | solution.py:878
  53.2 2.9 %gradient.2 = bf16[16,1280]{1,0:T(8,128)(2,1)S(1)} custom-call(s32[8]{0:T(128)S(1)} %copy-done, bf16[32,40,128]{2,1,0:T(8,128)(2,1)S(1)} %all_to_all.10.blocks_ref, f32[128,36864]{1,0:T(8,128)} %dict_hbm.5), custom_call_target="tpu_custom_call" | custom-call | tf_op jit(solution)/shard_map/gradient/pallas_call | solution.py:687
  56.1 1.2 collective-permute-start.8
  57.3 3.2 %collective-permute-start.6 = (bf16[1,16,1280]{2,1,0:T(8,128)(2,1)S(1)}, bf16[1,16,1280]{2,1,0:T(8,128)(2,1)S(1)}, u32[]{:S(2)}, u32[]{:S(2)}) collective-permute-start(bf16[1,16,1280]{2,1,0:T(8,128)(2,1)S(1)} %bitcast.7), channel_id=1, source_target_pairs={{0,16},{1,17},{2,18},{3,19},{4,20},{5,21},{6,22},{7,23},{8,24},{9,... | collective-permute-start | bytes 122888 | tf_op jit(solution)/shard_map/ppermute | solution.py:725
  61.2 1.2 collective-permute-done.8
  62.8 2.2 %collective-permute-start.11 = (bf16[4,16,1280]{2,1,0:T(8,128)(2,1)S(1)}, bf16[4,16,1280]{2,1,0:T(8,128)(2,1)S(1)}, u32[]{:S(2)}, u32[]{:S(2)}) collective-permute-start(bf16[4,16,1280]{2,1,0:T(8,128)(2,1)S(1)} %pad_maximum_fusion.when_ref), channel_id=1, source_target_pairs={{0,6},{1,7},{2,4},{3,5},{4,2},{5,3},{6,0},{7,1},{8,14},{9,15},{10,... | collective-permute-start | bytes 491528 | tf_op jit(solution)/shard_map/ppermute | solution.py:725
  66.3 3.4 %recall.1 = (f32[16,36864]{1,0:T(8,128)S(1)}, f32[16,36864]{1,0:T(8,128)S(1)}, f32[16,128]{1,0:T(8,128)S(1)}, f32[16,128]{1,0:T(8,128)S(1)}) custom-call(s32[8]{0:T(128)S(1)} %copy-done, f32[128,36864]{1,0:T(8,128)} %dict_hbm.5, bf16[4,16,1280]{2,1,0:T(8,128)(2,1)S(1)} %pad_maximum_fusion.when_ref), custom_call_target="tpu_custom_call" | custom-call | tf_op jit(solution)/shard_map/recall/pallas_call | solution.py:766
  69.8 3.9 %collective-permute-done.9 = bf16[4,16,1280]{2,1,0:T(8,128)(2,1)S(1)} collective-permute-done((bf16[4,16,1280]{2,1,0:T(8,128)(2,1)S(1)}, bf16[4,16,1280]{2,1,0:T(8,128)(2,1)S(1)}, u32[]{:S(2)}, u32[]{:S(2)}) %collective-permute-start.9) | collective-permute-done | bytes 163872 | tf_op jit(solution)/shard_map/ppermute | solution.py:725
  73.8 2.1 %collective-permute-done.12.came_ref = bf16[16,16,1280]{2,1,0:T(8,128)(2,1)S(1)} collective-permute-done((bf16[16,16,1280]{2,1,0:T(8,128)(2,1)S(1)}, bf16[16,16,1280]{2,1,0:T(8,128)(2,1)S(1)}, u32[]{:S(2)}, u32[]{:S(2)}) %collective-permute-start.12) | collective-permute-done | bytes 655392 | tf_op jit(solution)/shard_map/ppermute | solution.py:725
  75.9 2.0 %renew.2.refs_6_.refs_0_ = f32[16,36864]{1,0:T(8,128)S(1)} custom-call(s32[8]{0:T(128)S(1)} %copy-done, bf16[16,16,1280]{2,1,0:T(8,128)(2,1)S(1)} %constant_dynamic-update-slice_fusion.held_ref, bf16[16,16,1280]{2,1,0:T(8,128)(2,1)S(1)} %collective-permute-done.12.came_ref, f32[16,36864]{1,0:T(8,128)S(1)} %get-tuple-element.52.old, ...), custom_call_target="tpu_custom_call" | custom-call | tf_op jit(solution)/shard_map/renew/pallas_call | solution.py:835
  77.9 11.4 %iterate.3 = (f32[128,128]{1,0:T(8,128)S(1)}, bf16[96,128]{1,0:T(8,128)(2,1)S(1)}, bf16[96,128]{1,0:T(8,128)(2,1)S(1)}, bf16[6,16,384,128]{3,2,1,0:T(8,128)(2,1)S(1)}, f32[128,36864]{1,0:T(8,128)}) custom-call(s32[8]{0:T(128)S(1)} %copy-done, f32[1,128]{1,0:T(1,128)S(1)} %bitcast.15, ...), custom_call_target="tpu_custom_call", output_to_operand_aliasing={{3}: (9, {}), {4}: (11, {})} | custom-call | tf_op jit(solution)/shard_map/iterate/pallas_call | solution.py:399
  90.6 8.5 %conclude.3 = (bf16[32,40,128]{2,1,0:T(8,128)(2,1)S(1)}, f32[128,384]{1,0:T(8,128)S(1)}, f32[128,128]{1,0:T(8,128)S(1)}, bf16[96,128]{1,0:T(8,128)(2,1)S(1)}, bf...) custom-call(s32[8]{0:T(128)S(1)} %copy-done, f32[1,128]{1,0:T(1,128)S(1)} %bitcast.16, ...), custom_call_target="tpu_custom_call", output_to_operand_aliasing={{5}: (10, {})} | custom-call | tf_op jit(solution)/shard_map/conclude/pallas_call | solution.py:516
  99.1 21.1 %all_to_all.11.blocks_ref = bf16[32,40,128]{2,1,0:T(8,128)(2,1)S(1)} all-to-all(bf16[32,40,128]{2,1,0:T(8,128)(2,1)S(1)} %get-tuple-element.62), channel_id=1, replica_groups=mesh['tm'=32,'chan'=1] {'tm'}, dimensions={0} | all-to-all | bytes 655360 | tf_op jit(solution)/shard_map/all_to_all | solution.py:878
  120.2 2.9 %gradient.3 = bf16[16,1280]{1,0:T(8,128)(2,1)S(1)} custom-call(s32[8]{0:T(128)S(1)} %copy-done, bf16[32,40,128]{2,1,0:T(8,128)(2,1)S(1)} %all_to_all.11.blocks_ref, f32[128,36864]{1,0:T(8,128)} %dict_hbm.5), custom_call_target="tpu_custom_call" | custom-call | tf_op jit(solution)/shard_map/gradient/pallas_call | solution.py:687
  123.1 1.2 collective-permute-start.17
  124.3 3.2 %collective-permute-start.15 = (bf16[1,16,1280]{2,1,0:T(8,128)(2,1)S(1)}, bf16[1,16,1280]{2,1,0:T(8,128)(2,1)S(1)}, u32[]{:S(2)}, u32[]{:S(2)}) collective-permute-start(bf16[1,16,1280]{2,1,0:T(8,128)(2,1)S(1)} %bitcast.11), channel_id=1, source_target_pairs={{0,16},{1,17},{2,18},{3,19},{4,20},{5,21},{6,22},{7,23},{8,24},{9,... | collective-permute-start | bytes 122888 | tf_op jit(solution)/shard_map/ppermute | solution.py:725
  129.8 2.2 %collective-permute-start.20 = (bf16[4,16,1280]{2,1,0:T(8,128)(2,1)S(1)}, bf16[4,16,1280]{2,1,0:T(8,128)(2,1)S(1)}, u32[]{:S(2)}, u32[]{:S(2)}) collective-permute-start(bf16[4,16,1280]{2,1,0:T(8,128)(2,1)S(1)} %pad_maximum_fusion.1), channel_id=1, source_target_pairs={{0,6},{1,7},{2,4},{3,5},{4,2},{5,3},{6,0},{7,1},{8,14},{9,15},{10,... | collective-permute-start | bytes 491528 | tf_op jit(solution)/shard_map/ppermute | solution.py:725
  133.4 3.8 %settle.1 = (f32[384,128]{1,0:T(8,128)S(1)}, f32[128,36864]{1,0:T(8,128)}) custom-call(s32[8]{0:T(128)S(1)} %copy-done, f32[128,384]{1,0:T(8,128)S(1)} %get-tuple-element.64.partial_ref, bf16[96,128]{1,0:T(8,128)(2,1)S(1)} %collective-permute-done.21.first_ref, ...), custom_call_target="tpu_custom_call", output_to_operand_aliasing={{1}: (6, {})} | custom-call | tf_op jit(solution)/shard_map/settle/pallas_call | solution.py:587
  137.2 3.4 %collective-permute-done.18 = bf16[4,16,1280]{2,1,0:T(8,128)(2,1)S(1)} collective-permute-done((bf16[4,16,1280]{2,1,0:T(8,128)(2,1)S(1)}, bf16[4,16,1280]{2,1,0:T(8,128)(2,1)S(1)}, u32[]{:S(2)}, u32[]{:S(2)}) %collective-permute-start.18) | collective-permute-done | bytes 163872 | tf_op jit(solution)/shard_map/ppermute | solution.py:725
  142.9 3.3 %renew.3 = f32[128,36864]{1,0:T(8,128)} custom-call(s32[8]{0:T(128)S(1)} %copy-done, bf16[16,16,1280]{2,1,0:T(8,128)(2,1)S(1)} %constant_dynamic-update-slice_fusion.7.held_ref, bf16[16,16,1280]{2,1,0:T(8,128)(2,1)S(1)} %collective-permute-done.23.came_ref, f32[16,36864]{1,0:T(8,128)S(1)} %get-tuple-element.72.old, ...), custom_call_target="tpu_custom_call", output_to_operand_aliasing={{}: (5, {})} | custom-call | tf_op jit(solution)/shard_map/renew/pallas_call | solution.py:835
  (60 shorter events, 12.9 us)
Async XLA Ops:
  1.8 10.4 %collective-permute-start = (bf16[96,512]{1,0:T(8,128)(2,1)S(1)}, bf16[96,512]{1,0:T(8,128)(2,1)S(1)}, u32[]{:S(2)}, u32[]{:S(2)}) collective-permute-start(bf16[96,512]{1,0:T(8,128)(2,1)S(1)} %get-tuple-element.40), channel_id=1, source_target_pairs={{0,1},{1,0},{2,3},{3,2},{4,5},{5,4},{6,7},{7,6},{8,9},{9,8},{10,11... | collective-permute-start | bytes 294920 | tf_op jit(solution)/shard_map/ppermute | solution.py:854
  2.3 9.9 %collective-permute-start.1 = (bf16[96,512]{1,0:T(8,128)(2,1)S(1)}, bf16[96,512]{1,0:T(8,128)(2,1)S(1)}, u32[]{:S(2)}, u32[]{:S(2)}) collective-permute-start(bf16[96,512]{1,0:T(8,128)(2,1)S(1)} %get-tuple-element.41), channel_id=1, source_target_pairs={{1,2},{2,1},{3,4},{4,3},{5,6},{6,5},{7,8},{8,7},{9,10},{10,9},{11,... | collective-permute-start | bytes 294920 | tf_op jit(solution)/shard_map/ppermute | solution.py:854
  17.3 4.8 %collective-permute-start.2 = (bf16[96,128]{1,0:T(8,128)(2,1)S(1)}, bf16[96,128]{1,0:T(8,128)(2,1)S(1)}, u32[]{:S(2)}, u32[]{:S(2)}) collective-permute-start(bf16[96,128]{1,0:T(8,128)(2,1)S(1)} %get-tuple-element.44), channel_id=1, source_target_pairs={{0,1},{1,0},{2,3},{3,2},{4,5},{5,4},{6,7},{7,6},{8,9},{9,8},{10,11... | collective-permute-start | bytes 73736 | tf_op jit(solution)/shard_map/ppermute | solution.py:854
  21.3 0.9 collective-permute-start.3
  56.1 6.3 %collective-permute-start.8 = (bf16[1,16,1280]{2,1,0:T(8,128)(2,1)S(1)}, bf16[1,16,1280]{2,1,0:T(8,128)(2,1)S(1)}, u32[]{:S(2)}, u32[]{:S(2)}) collective-permute-start(bf16[1,16,1280]{2,1,0:T(8,128)(2,1)S(1)} %bitcast.5), channel_id=1, source_target_pairs={{0,24},{1,25},{2,26},{3,27},{4,28},{5,29},{6,30},{7,31},{8,16},{9,... | collective-permute-start | bytes 122888 | tf_op jit(solution)/shard_map/ppermute | solution.py:725
  57.3 5.1 %collective-permute-start.7 = (bf16[1,16,1280]{2,1,0:T(8,128)(2,1)S(1)}, bf16[1,16,1280]{2,1,0:T(8,128)(2,1)S(1)}, u32[]{:S(2)}, u32[]{:S(2)}) collective-permute-start(bf16[1,16,1280]{2,1,0:T(8,128)(2,1)S(1)} %bitcast.6), channel_id=1, source_target_pairs={{0,8},{1,9},{2,10},{3,11},{4,12},{5,13},{6,14},{7,15},{8,0},{9,1},... | collective-permute-start | bytes 122888 | tf_op jit(solution)/shard_map/ppermute | solution.py:725
  57.3 5.5 %collective-permute-start.6 = (bf16[1,16,1280]{2,1,0:T(8,128)(2,1)S(1)}, bf16[1,16,1280]{2,1,0:T(8,128)(2,1)S(1)}, u32[]{:S(2)}, u32[]{:S(2)}) collective-permute-start(bf16[1,16,1280]{2,1,0:T(8,128)(2,1)S(1)} %bitcast.7), channel_id=1, source_target_pairs={{0,16},{1,17},{2,18},{3,19},{4,20},{5,21},{6,22},{7,23},{8,24},{9,... | collective-permute-start | bytes 122888 | tf_op jit(solution)/shard_map/ppermute | solution.py:725
  60.5 13.2 %collective-permute-start.4 = (bf16[96,128]{1,0:T(8,128)(2,1)S(1)}, bf16[96,128]{1,0:T(8,128)(2,1)S(1)}, u32[]{:S(2)}, u32[]{:S(2)}) collective-permute-start(bf16[96,128]{1,0:T(8,128)(2,1)S(1)} %get-tuple-element.50), channel_id=1, source_target_pairs={{0,1},{1,0},{2,3},{3,2},{4,5},{5,4},{6,7},{7,6},{8,9},{9,8},{10,11... | collective-permute-start | bytes 73736 | tf_op jit(solution)/shard_map/ppermute | solution.py:854
  60.5 13.2 %collective-permute-start.5 = (bf16[96,128]{1,0:T(8,128)(2,1)S(1)}, bf16[96,128]{1,0:T(8,128)(2,1)S(1)}, u32[]{:S(2)}, u32[]{:S(2)}) collective-permute-start(bf16[96,128]{1,0:T(8,128)(2,1)S(1)} %get-tuple-element.51), channel_id=1, source_target_pairs={{1,2},{2,1},{3,4},{4,3},{5,6},{6,5},{7,8},{8,7},{9,10},{10,9},{11,... | collective-permute-start | bytes 73736 | tf_op jit(solution)/shard_map/ppermute | solution.py:854
  62.8 10.9 %collective-permute-start.11 = (bf16[4,16,1280]{2,1,0:T(8,128)(2,1)S(1)}, bf16[4,16,1280]{2,1,0:T(8,128)(2,1)S(1)}, u32[]{:S(2)}, u32[]{:S(2)}) collective-permute-start(bf16[4,16,1280]{2,1,0:T(8,128)(2,1)S(1)} %pad_maximum_fusion.when_ref), channel_id=1, source_target_pairs={{0,6},{1,7},{2,4},{3,5},{4,2},{5,3},{6,0},{7,1},{8,14},{9,15},{10,... | collective-permute-start | bytes 491528 | tf_op jit(solution)/shard_map/ppermute | solution.py:725
  65.0 8.7 %collective-permute-start.10 = (bf16[4,16,1280]{2,1,0:T(8,128)(2,1)S(1)}, bf16[4,16,1280]{2,1,0:T(8,128)(2,1)S(1)}, u32[]{:S(2)}, u32[]{:S(2)}) collective-permute-start(bf16[4,16,1280]{2,1,0:T(8,128)(2,1)S(1)} %pad_maximum_fusion.when_ref), channel_id=1, source_target_pairs={{0,2},{1,3},{2,0},{3,1},{4,6},{5,7},{6,4},{7,5},{8,10},{9,11},{10,... | collective-permute-start | bytes 491528 | tf_op jit(solution)/shard_map/ppermute | solution.py:725
  65.8 7.8 %collective-permute-start.9 = (bf16[4,16,1280]{2,1,0:T(8,128)(2,1)S(1)}, bf16[4,16,1280]{2,1,0:T(8,128)(2,1)S(1)}, u32[]{:S(2)}, u32[]{:S(2)}) collective-permute-start(bf16[4,16,1280]{2,1,0:T(8,128)(2,1)S(1)} %pad_maximum_fusion.when_ref), channel_id=1, source_target_pairs={{0,4},{1,5},{2,6},{3,7},{4,0},{5,1},{6,2},{7,3},{8,12},{9,13},{10,... | collective-permute-start | bytes 491528 | tf_op jit(solution)/shard_map/ppermute | solution.py:725
  73.7 2.2 %collective-permute-start.12 = (bf16[16,16,1280]{2,1,0:T(8,128)(2,1)S(1)}, bf16[16,16,1280]{2,1,0:T(8,128)(2,1)S(1)}, u32[]{:S(2)}, u32[]{:S(2)}) collective-permute-start(bf16[16,16,1280]{2,1,0:T(8,128)(2,1)S(1)} %constant_dynamic-update-slice_fusion.held_ref), channel_id=1, source_target_pairs={{0,1},{1,0},{2,3},{3,2},{4,5},{5,4},{6,7},{7,6},{8,9},{9,8},{10,11... | collective-permute-start | bytes 1966088 | tf_op jit(solution)/shard_map/ppermute | solution.py:725
  89.3 1.3 collective-permute-start.13
  89.5 1.0 collective-permute-start.14
  123.1 6.3 %collective-permute-start.17 = (bf16[1,16,1280]{2,1,0:T(8,128)(2,1)S(1)}, bf16[1,16,1280]{2,1,0:T(8,128)(2,1)S(1)}, u32[]{:S(2)}, u32[]{:S(2)}) collective-permute-start(bf16[1,16,1280]{2,1,0:T(8,128)(2,1)S(1)} %bitcast.9), channel_id=1, source_target_pairs={{0,24},{1,25},{2,26},{3,27},{4,28},{5,29},{6,30},{7,31},{8,16},{9,... | collective-permute-start | bytes 122888 | tf_op jit(solution)/shard_map/ppermute | solution.py:725
  124.3 5.1 %collective-permute-start.16 = (bf16[1,16,1280]{2,1,0:T(8,128)(2,1)S(1)}, bf16[1,16,1280]{2,1,0:T(8,128)(2,1)S(1)}, u32[]{:S(2)}, u32[]{:S(2)}) collective-permute-start(bf16[1,16,1280]{2,1,0:T(8,128)(2,1)S(1)} %bitcast.10), channel_id=1, source_target_pairs={{0,8},{1,9},{2,10},{3,11},{4,12},{5,13},{6,14},{7,15},{8,0},{9,1},... | collective-permute-start | bytes 122888 | tf_op jit(solution)/shard_map/ppermute | solution.py:725
  124.3 5.5 %collective-permute-start.15 = (bf16[1,16,1280]{2,1,0:T(8,128)(2,1)S(1)}, bf16[1,16,1280]{2,1,0:T(8,128)(2,1)S(1)}, u32[]{:S(2)}, u32[]{:S(2)}) collective-permute-start(bf16[1,16,1280]{2,1,0:T(8,128)(2,1)S(1)} %bitcast.11), channel_id=1, source_target_pairs={{0,16},{1,17},{2,18},{3,19},{4,20},{5,21},{6,22},{7,23},{8,24},{9,... | collective-permute-start | bytes 122888 | tf_op jit(solution)/shard_map/ppermute | solution.py:725
  127.5 5.9 %collective-permute-start.21 = (bf16[96,128]{1,0:T(8,128)(2,1)S(1)}, bf16[96,128]{1,0:T(8,128)(2,1)S(1)}, u32[]{:S(2)}, u32[]{:S(2)}) collective-permute-start(bf16[96,128]{1,0:T(8,128)(2,1)S(1)} %get-tuple-element.67), channel_id=1, source_target_pairs={{0,1},{1,0},{2,3},{3,2},{4,5},{5,4},{6,7},{7,6},{8,9},{9,8},{10,11... | collective-permute-start | bytes 73736 | tf_op jit(solution)/shard_map/ppermute | solution.py:854
  127.5 5.9 %collective-permute-start.22 = (bf16[96,128]{1,0:T(8,128)(2,1)S(1)}, bf16[96,128]{1,0:T(8,128)(2,1)S(1)}, u32[]{:S(2)}, u32[]{:S(2)}) collective-permute-start(bf16[96,128]{1,0:T(8,128)(2,1)S(1)} %get-tuple-element.68), channel_id=1, source_target_pairs={{1,2},{2,1},{3,4},{4,3},{5,6},{6,5},{7,8},{8,7},{9,10},{10,9},{11,... | collective-permute-start | bytes 73736 | tf_op jit(solution)/shard_map/ppermute | solution.py:854
  129.8 10.9 %collective-permute-start.20 = (bf16[4,16,1280]{2,1,0:T(8,128)(2,1)S(1)}, bf16[4,16,1280]{2,1,0:T(8,128)(2,1)S(1)}, u32[]{:S(2)}, u32[]{:S(2)}) collective-permute-start(bf16[4,16,1280]{2,1,0:T(8,128)(2,1)S(1)} %pad_maximum_fusion.1), channel_id=1, source_target_pairs={{0,6},{1,7},{2,4},{3,5},{4,2},{5,3},{6,0},{7,1},{8,14},{9,15},{10,... | collective-permute-start | bytes 491528 | tf_op jit(solution)/shard_map/ppermute | solution.py:725
  132.0 8.7 %collective-permute-start.19 = (bf16[4,16,1280]{2,1,0:T(8,128)(2,1)S(1)}, bf16[4,16,1280]{2,1,0:T(8,128)(2,1)S(1)}, u32[]{:S(2)}, u32[]{:S(2)}) collective-permute-start(bf16[4,16,1280]{2,1,0:T(8,128)(2,1)S(1)} %pad_maximum_fusion.1), channel_id=1, source_target_pairs={{0,2},{1,3},{2,0},{3,1},{4,6},{5,7},{6,4},{7,5},{8,10},{9,11},{10,... | collective-permute-start | bytes 491528 | tf_op jit(solution)/shard_map/ppermute | solution.py:725
  132.8 7.8 %collective-permute-start.18 = (bf16[4,16,1280]{2,1,0:T(8,128)(2,1)S(1)}, bf16[4,16,1280]{2,1,0:T(8,128)(2,1)S(1)}, u32[]{:S(2)}, u32[]{:S(2)}) collective-permute-start(bf16[4,16,1280]{2,1,0:T(8,128)(2,1)S(1)} %pad_maximum_fusion.1), channel_id=1, source_target_pairs={{0,4},{1,5},{2,6},{3,7},{4,0},{5,1},{6,2},{7,3},{8,12},{9,13},{10,... | collective-permute-start | bytes 491528 | tf_op jit(solution)/shard_map/ppermute | solution.py:725
  140.7 2.2 %collective-permute-start.23 = (bf16[16,16,1280]{2,1,0:T(8,128)(2,1)S(1)}, bf16[16,16,1280]{2,1,0:T(8,128)(2,1)S(1)}, u32[]{:S(2)}, u32[]{:S(2)}) collective-permute-start(bf16[16,16,1280]{2,1,0:T(8,128)(2,1)S(1)} %constant_dynamic-update-slice_fusion.7.held_ref), channel_id=1, source_target_pairs={{0,1},{1,0},{2,3},{3,2},{4,5},{5,4},{6,7},{7,6},{8,9},{9,8},{10,11... | collective-permute-start | bytes 1966088 | tf_op jit(solution)/shard_map/ppermute | solution.py:725
  (2 other events, 23.2 us)
